TPU v7x, 32 devices: a whole 2x2x4 slice. The times are simulated.
32 devices in a mesh: groups: 2 (over y), hid: 16 (over z, x, core), mod: 1.
Axes of the slice: x: 2, y: 2, z: 4, core: 2. Of those that a mesh axis runs over, the one named last changes fastest.
Arguments:
- tokens: bfloat16 [512, 8192], P(('groups', 'hid'), 'mod'), parts along dimension 0, may hold values from -6 to 6
- out_grad: bfloat16 [512, 8192], P(('groups', 'hid'), 'mod'), parts along dimension 0, may hold values from -6 to 6
- gate_weight: bfloat16 [8192, 28672], P('mod', 'hid'), may hold values from -0.0625 to 0.0625
- up_weight: bfloat16 [8192, 28672], P('mod', 'hid'), may hold values from -0.0625 to 0.0625
- down_weight: bfloat16 [28672, 8192], P('hid', 'mod'), may hold values from -0.03125 to 0.03125
- proj_d: bfloat16 [8192, 192], P('mod'), may hold values from -0.0625 to 0.0625
- proj_ff: bfloat16 [28672, 192], P('hid'), may hold values from -0.03125 to 0.03125
- example_ids: int32 [512], P('groups'), parts along dimension 0, may hold values from 0 to 7, never falling along the last dimension, each value on 1 to 64 neighbouring positions
- test_features: bfloat16 [512, 12288], P('groups', 'hid'), parts along dimension 0, may hold values from -0.0546875 to 0.0546875
Outputs:
- features: float32 [16, 12288], P('groups', 'hid'), parts along dimension 0
- scores: float32 [16, 256], P('groups'), parts along dimension 0
There are 2 independent parts, one for each index of `groups`. A program takes and returns all parts, laid end to end along the dimension named above; an argument that names none is the same for every part. Nothing has to cross between parts.
Inputs may be any that keep to these rules, and one draw needn't show every extreme that they name: `example_ids`: example ids never fall along the tokens; each example holds 1 to 64 tokens.
All inputs are finite; a program needn't handle non-finite values.
Results may differ from a plain program's by a relative error of at most 0.003.
Values may be sent and summed in bfloat16 or wider, within the bound.
No kernel may reach another device: no remote copies, remote signals or barrier semaphores. Data moves between devices by JAX's collectives and lax.ppermute only.
A program may use at most 192 MiB of HBM per device.

v0:
```python
import jax
import jax.numpy as jnp
from jax import lax
from jax.sharding import PartitionSpec as P

R = 64
EX_TOK = 32


def project_rows(block_rows, weights):
    return jnp.dot(block_rows, weights, preferred_element_type=jnp.float32)


def local(
    tokens,
    out_grad,
    gate_weight,
    up_weight,
    down_weight,
    proj_d,
    proj_ff,
    example_ids,
    test_features,
):
    width = gate_weight.shape[1]
    input_proj = proj_d[:, : 2 * R]
    output_proj = proj_d[:, 2 * R :]
    block_rows = lax.all_gather(tokens, "hid", axis=0, tiled=True)
    forward = jnp.concatenate(
        [
            project_rows(block_rows, gate_weight),
            project_rows(block_rows, up_weight),
            project_rows(block_rows, input_proj),
        ],
        axis=1,
    )
    block_rows = lax.all_gather(out_grad, "hid", axis=0, tiled=True)
    spread = lax.dot_general(
        block_rows, down_weight, (((1,), (1,)), ((), ())), preferred_element_type=jnp.float32
    )
    backward = jnp.concatenate([spread, project_rows(block_rows, output_proj)], axis=1)
    forward = lax.psum(forward, "mod")
    backward = lax.psum(backward, "mod")
    gate_act = forward[:, :width]
    up_act = forward[:, width : 2 * width]
    input_gate = forward[:, 2 * width : 2 * width + R]
    input_up = forward[:, 2 * width + R :]
    hidden_grad = backward[:, :width]
    output_down = backward[:, width:]
    sigmoid_gate = jax.nn.sigmoid(gate_act)
    hidden = (gate_act * sigmoid_gate * up_act).astype(jnp.bfloat16)
    gate_grad = (
        hidden_grad * up_act * sigmoid_gate * (1.0 + gate_act * (1.0 - sigmoid_gate))
    ).astype(jnp.bfloat16)
    up_grad = (hidden_grad * gate_act * sigmoid_gate).astype(jnp.bfloat16)
    output_gate = project_rows(gate_grad, proj_ff[:, :R])
    output_up = project_rows(up_grad, proj_ff[:, R : 2 * R])
    input_down = project_rows(hidden, proj_ff[:, 2 * R :])
    shares = R // lax.axis_size("hid")
    offset = lax.axis_index("hid") * shares
    output_gate, output_up, input_down = lax.psum((output_gate, output_up, input_down), "hid")
    own_gate = lax.dynamic_slice_in_dim(output_gate, offset, shares, 1)
    own_up = lax.dynamic_slice_in_dim(output_up, offset, shares, 1)
    own_down = lax.dynamic_slice_in_dim(output_down, offset, shares, 1)
    outputs = jnp.stack([own_gate, own_up, own_down], axis=2)
    inputs = jnp.stack([input_gate, input_up, input_down], axis=1)
    total_rows = outputs.shape[0]
    outer = (outputs[:, :, :, None] * inputs[:, None, :, :]).reshape(total_rows, shares * 3 * R)
    examples = example_ids.shape[0] // EX_TOK
    member = (example_ids[None, :] == jnp.arange(examples, dtype=jnp.int32)[:, None]).astype(
        jnp.float32
    )
    features = jnp.dot(
        member, outer, precision=lax.Precision.HIGHEST, preferred_element_type=jnp.float32
    )
    partial_scores = jnp.dot(
        features,
        test_features.astype(jnp.float32).T,
        precision=lax.Precision.HIGHEST,
        preferred_element_type=jnp.float32,
    )
    scores = lax.psum(partial_scores, "hid")
    return (features, scores)


def solution(mesh):
    return jax.shard_map(
        local,
        mesh=mesh,
        in_specs=(
            P(("groups", "hid"), "mod"),
            P(("groups", "hid"), "mod"),
            P("mod", "hid"),
            P("mod", "hid"),
            P("hid", "mod"),
            P("mod", None),
            P("hid", None),
            P("groups"),
            P("groups", "hid"),
        ),
        out_specs=(P("groups", "hid"), P("groups", None)),
        check_vma=False,
    )
```

profile of v0, /device:TPU:0, one launch (start us, length us, event | category | flops | bytes accessed | tf_op | source)
XLA Modules:
  0.0 270.3 jit_solution(8952034810213036880)
XLA Ops:
  7.2 0.0 copy-start
  7.2 0.0 all-gather.5.cloned.1.call-start
  7.2 0.7 all-gather.5.cloned.1.call-update
  7.9 0.0 all-gather.3.cloned.1.call-start
  8.0 0.7 all-gather.3.cloned.1.call-update
  8.7 0.0 all-reduce.3.cloned.1.call-start
  8.7 54.8 %all-gather.5.cloned.1.call-done = bf16[256,8192]{1,0:T(8,128)(2,1)} async-done(((bf16[16,8192]{1,0:T(8,128)(2,1)}), bf16[256,8192]{1,0:T(8,128)(2,1)}) %all-gather.5.cloned.1.call-update) | async-done | bytes 4194320 | tf_op jit(solution)/shard_map/all_gather | solution.py:28
  63.5 0.0 copy-start.4
  63.5 19.5 %fusion.16 = f32[256,1792]{1,0:T(8,128)S(1)} fusion(bf16[256,8192]{1,0:T(8,128)(2,1)} %all-gather.5.cloned.1.call-done, bf16[8192,1792]{1,0:T(8,128)(2,1)} %param.11), kind=kOutput, calls=%fused_computation.30 | convolution fusion | flops 7516192768 | bytes 35389440 | tf_op jit(solution)/shard_map/dot_general | solution.py:11
  83.0 0.0 copy-done.4
  83.0 0.0 copy-start.6
  83.0 0.0 copy-start.5
  83.0 14.6 %fusion.15 = f32[256,1792]{1,0:T(8,128)S(1)} fusion(bf16[256,8192]{1,0:T(8,128)(2,1)S(1)} %copy-done.4, bf16[8192,1792]{1,0:T(8,128)(2,1)} %param.12), kind=kOutput, calls=%fused_computation.29 | convolution fusion | flops 7516192768 | bytes 35389440 | tf_op jit(solution)/shard_map/dot_general | solution.py:11
  97.6 0.0 copy-start.7
  97.6 1.2 copy-done.7
  98.8 0.0 copy-done.5
  98.8 1.3 convolution_bitcast_fusion
  100.1 14.6 %all-gather.3.cloned.1.call-done = bf16[256,8192]{1,0:T(8,128)(2,1)} async-done(((bf16[16,8192]{1,0:T(8,128)(2,1)}), bf16[256,8192]{1,0:T(8,128)(2,1)}) %all-gather.3.cloned.1.call-update) | async-done | bytes 4194320 | tf_op jit(solution)/shard_map/all_gather | solution.py:37
  114.7 0.0 copy-start.8
  114.7 16.7 %fusion.14 = f32[256,1792]{1,0:T(8,128)S(1)} fusion(bf16[256,8192]{1,0:T(8,128)(2,1)} %all-gather.3.cloned.1.call-done, bf16[1792,8192]{1,0:T(8,128)(2,1)} %param.13), kind=kOutput, calls=%fused_computation.28 | convolution fusion | flops 7516192768 | bytes 35389440 | tf_op jit(solution)/shard_map/dot_general | solution.py:38
  131.5 0.0 copy-done.6
  131.5 0.0 copy-done.8
  131.5 1.5 fusion.5
  133.0 0.0 copy-start.1
  133.0 2.9 %fusion.4 = f32[256,64]{0,1:T(8,128)} fusion(f32[256,1792]{1,0:T(8,128)S(1)} %fusion.14, f32[256,1792]{1,0:T(8,128)} %copy-done.6, bf16[1792,192]{0,1:T(8,128)(2,1)} %param.15), kind=kOutput, calls=%fused_computation.9 | convolution fusion | flops 61472768 | bytes 3964928 | tf_op jit(solution)/shard_map/dot_general | solution.py:11
  135.9 0.0 copy-done.1
  135.9 3.7 %fusion = f32[256,128]{0,1:T(8,128)S(1)} fusion(bf16[256,8192]{1,0:T(8,128)(2,1)} %all-gather.5.cloned.1.call-done, bf16[8192,192]{0,1:T(8,128)(2,1)S(1)} %copy-done.1), kind=kOutput, calls=%fused_computation | convolution fusion | flops 536870912 | bytes 6422528 | tf_op jit(solution)/shard_map/dot_general | solution.py:11
  139.6 0.7 slice_bitcast_fusion.1
  140.3 0.0 all-reduce.3.cloned.1.call-update
  140.3 0.0 copy-start.3
  140.3 3.6 %fusion.2 = f32[256,64]{0,1:T(8,128)S(1)} fusion(bf16[256,8192]{1,0:T(8,128)(2,1)} %all-gather.3.cloned.1.call-done, bf16[8192,192]{0,1:T(8,128)(2,1)S(1)} %copy-done.1), kind=kOutput, calls=%fused_computation.7 | convolution fusion | flops 268435456 | bytes 5308416 | tf_op jit(solution)/shard_map/dot_general | solution.py:11
  144.0 85.5 %all-reduce.3.cloned.1.call-done = (f32[256,1,64]{0,2,1:T(8,128)}, f32[256,64]{0,1:T(8,128)}, f32[256,64]{0,1:T(8,128)}) async-done(((f32[256,1,64]{0,2,1:T(8,128)}, f32[256,64]{0,1:T(8,128)}, f32[256,64]{0,1:T(8,128)}), (f32[256,1,64]{0,2,1:T(8,128)}, f32[256,64]{0,1:T(8,128)}, f32[256,64]{0,1:T(8,128)})) %all-reduce.3.cloned.1.call-update) | async-done | bytes 196624 | tf_op jit(solution)/shard_map/psum | solution.py:61
  229.4 0.7 dynamic-slice_bitcast_fusion.1
  230.2 0.9 pad_maximum_fusion
  231.1 0.1 broadcast_multiply_fusion
  231.2 0.0 copy-done.3
  231.2 0.5 fusion.9
  231.7 0.0 copy-done
  231.7 0.0 copy-start.2
  231.7 0.4 fusion.17
  232.1 31.7 %psum.37 = f32[8,256]{1,0:T(8,128)} all-reduce(f32[8,256]{1,0:T(8,128)S(1)} %fusion.17), channel_id=1, replica_groups=mesh['groups'=2,'hid'=16,'mod'=1] {'hid'}, use_global_device_ids=true, to_apply=%region_3.0 | all-reduce | flops 2048 | bytes 16384 | tf_op jit(solution)/shard_map/psum | solution.py:82
  263.7 0.0 copy-done.2
  (3 shorter events, 0.0 us)
Async XLA Ops:
  7.2 224.5 %copy-start = (bf16[256,768]{1,0:T(8,128)(2,1)S(1)}, bf16[256,768]{1,0:T(8,128)(2,1)}, u32[]{:S(2)}) copy-start(bf16[256,768]{1,0:T(8,128)(2,1)} %param.17) | copy-start | bytes 1179652
  7.2 56.3 %all-gather.5.cloned.1.call-start = ((), (), s32[]{:S(2)}) async-start(), calls=%async_computation.1 | async-start | bytes 4456448 | tf_op jit(solution)/shard_map/all_gather | solution.py:28
  7.9 106.8 %all-gather.3.cloned.1.call-start = ((), (), s32[]{:S(2)}) async-start(), calls=%async_computation | async-start | bytes 4456448 | tf_op jit(solution)/shard_map/all_gather | solution.py:37
  8.7 220.8 %all-reduce.3.cloned.1.call-start = ((), (), s32[]{:S(2)}) async-start(), calls=%async_computation.2 | async-start | bytes 393216 | tf_op jit(solution)/shard_map/psum | solution.py:61
  63.5 19.5 %copy-start.4 = (bf16[256,8192]{1,0:T(8,128)(2,1)S(1)}, bf16[256,8192]{1,0:T(8,128)(2,1)}, u32[]{:S(2)}) copy-start(bf16[256,8192]{1,0:T(8,128)(2,1)} %all-gather.5.cloned.1.call-done) | copy-start | bytes 12582916
  83.0 48.5 %copy-start.6 = (f32[256,1792]{1,0:T(8,128)}, f32[256,1792]{1,0:T(8,128)S(1)}, u32[]{:S(2)}) copy-start(f32[256,1792]{1,0:T(8,128)S(1)} %fusion.16) | copy-start | bytes 5505028
  83.0 15.8 %copy-start.5 = (bf16[1792,192]{0,1:T(8,128)(2,1)S(1)}, bf16[1792,192]{0,1:T(8,128)(2,1)}, u32[]{:S(2)}) copy-start(bf16[1792,192]{0,1:T(8,128)(2,1)} %param.15) | copy-start | bytes 2064388
  97.6 1.2 copy-start.7
  114.7 16.8 %copy-start.8 = (f32[256,1792]{1,0:T(8,128)S(1)}, f32[256,1792]{1,0:T(8,128)}, u32[]{:S(2)}) copy-start(f32[256,1792]{1,0:T(8,128)} %copy-done.7) | copy-start | bytes 5505028
  133.0 2.9 %copy-start.1 = (bf16[8192,192]{0,1:T(8,128)(2,1)S(1)}, bf16[8192,192]{0,1:T(8,128)(2,1)}, u32[]{:S(2)}) copy-start(bf16[8192,192]{0,1:T(8,128)(2,1)} %param.14) | copy-start | bytes 9437188
  140.3 90.8 %copy-start.3 = (s32[256]{0:T(256)S(1)}, s32[256]{0:T(256)}, u32[]{:S(2)}) copy-start(s32[256]{0:T(256)} %param.16) | copy-start | bytes 3076
  231.7 32.1 %copy-start.2 = (f32[8,768]{1,0:T(8,128)}, f32[8,768]{1,0:T(8,128)S(1)}, u32[]{:S(2)}) copy-start(f32[8,768]{1,0:T(8,128)S(1)} %fusion.9) | copy-start | bytes 73732
Sparse Core Ops, SparseCore 0:
  10.2 53.2 all-gather.4
  65.6 49.0 all-gather.2
  140.5 88.9 all-reduce.2
where the time goes:
time: 271 us; the launch traced here: 270 us
  waiting for transfers between devices  156 us (58%)
  matrix products  64.7 us (24%)
  blocking collectives  31.7 us (12%)
  between operations  13.9 us (5%)
    psum x1, waiting for transfers between devices, local(): lax.psum((output_gate, output_up, input_down), 'hid')  85.5 us
    all_gather x1, waiting for transfers between devices, local(): block_rows = lax.all_gather(tokens, 'hid', axis=0, tiled=True)  54.8 us
    dot_general x7, matrix products, project_rows(): return jnp.dot(block_rows, weights, preferred_element_type=jnp.float32)  47.1 us
    psum x1, blocking collectives, local(): scores = lax.psum(partial_scores, 'hid')  31.7 us
    dot_general x1, matrix products, local(): lax.dot_general(block_rows, down_weight, (((1,), (1,)), ((), ())), prefer...  16.7 us
    all_gather x1, waiting for transfers between devices, local(): block_rows = lax.all_gather(out_grad, 'hid', axis=0, tiled=True)  14.6 us
  transfers between devices with their start and end apart: 3, of which 3 were waited for; matrix products, arithmetic and copies ran while one was open for 14% of the time, Pallas kernels for 0%

commit v1 on v0

--- a/solution.py
+++ b/solution.py
@@ -1,17 +1,25 @@
+import functools
+
 import jax
 import jax.numpy as jnp
 from jax import lax
+from jax.experimental import pallas as pl
+from jax.experimental.pallas import tpu as pltpu
 from jax.sharding import PartitionSpec as P
 
 R = 64
 EX_TOK = 32
+TILE = 256
+DEPTH = 2048
+VMEM = 56 * 1024 * 1024
+HIGH = lax.Precision.HIGHEST
 
 
 def project_rows(block_rows, weights):
     return jnp.dot(block_rows, weights, preferred_element_type=jnp.float32)
 
 
-def local(
+def local_general(
     tokens,
     out_grad,
     gate_weight,
@@ -47,12 +55,7 @@
     input_up = forward[:, 2 * width + R :]
     hidden_grad = backward[:, :width]
     output_down = backward[:, width:]
-    sigmoid_gate = jax.nn.sigmoid(gate_act)
-    hidden = (gate_act * sigmoid_gate * up_act).astype(jnp.bfloat16)
-    gate_grad = (
-        hidden_grad * up_act * sigmoid_gate * (1.0 + gate_act * (1.0 - sigmoid_gate))
-    ).astype(jnp.bfloat16)
-    up_grad = (hidden_grad * gate_act * sigmoid_gate).astype(jnp.bfloat16)
+    hidden, gate_grad, up_grad = pointwise(gate_act, up_act, hidden_grad)
     output_gate = project_rows(gate_grad, proj_ff[:, :R])
     output_up = project_rows(up_grad, proj_ff[:, R : 2 * R])
     input_down = project_rows(hidden, proj_ff[:, 2 * R :])
@@ -70,22 +73,285 @@
     member = (example_ids[None, :] == jnp.arange(examples, dtype=jnp.int32)[:, None]).astype(
         jnp.float32
     )
-    features = jnp.dot(
-        member, outer, precision=lax.Precision.HIGHEST, preferred_element_type=jnp.float32
-    )
+    features = jnp.dot(member, outer, precision=HIGH, preferred_element_type=jnp.float32)
     partial_scores = jnp.dot(
         features,
         test_features.astype(jnp.float32).T,
-        precision=lax.Precision.HIGHEST,
+        precision=HIGH,
         preferred_element_type=jnp.float32,
     )
     scores = lax.psum(partial_scores, "hid")
     return (features, scores)
 
 
+def pointwise(gate_act, up_act, hidden_grad):
+    sig = jax.nn.sigmoid(gate_act)
+    hidden = (gate_act * sig * up_act).astype(jnp.bfloat16)
+    gate_grad = (hidden_grad * up_act * sig * (1.0 + gate_act * (1.0 - sig))).astype(jnp.bfloat16)
+    up_grad = (hidden_grad * gate_act * sig).astype(jnp.bfloat16)
+    return hidden, gate_grad, up_grad
+
+
+def ring_device(position, core, chips):
+    height = chips // 2
+    if isinstance(position, int):
+        back = position >= height
+        z = 2 * height - 1 - position if back else position
+        return z * 4 + int(back) * 2 + core
+    back = (position >= height).astype(jnp.int32)
+    z = position + back * (2 * height - 1 - 2 * position)
+    return z * 4 + back * 2 + core
+
+
+def ring_position(device, chips):
+    z, x = device // 4, (device // 2) % 2
+    return z + x * (chips - 1 - 2 * z)
+
+
+def ring_step(block, chips, step):
+    pairs = [
+        (ring_device(r, core, chips), ring_device((r + step) % chips, core, chips))
+        for r in range(chips)
+        for core in range(2)
+    ]
+    return lax.ppermute(block, "hid", pairs)
+
+
+def core_swap(block, chips):
+    return lax.ppermute(block, "hid", [(h, h ^ 1) for h in range(2 * chips)])
+
+
+def gather_blocks(own, chips):
+    half = own.shape[1] // 2
+    found = [(0, 0, own)]
+    ahead, behind = own, own
+    for step in range(1, chips // 2):
+        ahead = ring_step(ahead, chips, 1)
+        behind = ring_step(behind, chips, -1)
+        found += [(-step, 0, ahead), (step, 0, behind)]
+    across = chips // 2
+    found.append((across, 0, ring_step(ahead[:, :half], chips, 1)))
+    found.append((across, half, ring_step(behind[:, half:], chips, -1)))
+    places, blocks = [], []
+    for offset, column, block in found:
+        for other in range(2):
+            places.append((offset, other, column))
+            blocks.append(core_swap(block, chips) if other else block)
+    return places, blocks
+
+
+def assemble(places, chips, blocks, whole, sems):
+    device = lax.axis_index("hid")
+    position, core = ring_position(device, chips), device % 2
+    copies = []
+    for index, (offset, other, column) in enumerate(places):
+        rows, columns = blocks[index].shape
+        source_core = core + other - 2 * core * other
+        source = ring_device((position + offset + chips) % chips, source_core, chips)
+        start = pl.multiple_of(source * rows, rows)
+        target = whole.at[pl.ds(start, rows), pl.ds(column, columns)]
+        copies.append(pltpu.make_async_copy(blocks[index], target, sems.at[index]))
+    for copy in copies:
+        copy.start()
+    for copy in copies:
+        copy.wait()
+
+
+def deep_dot(left, right, transposed, columns):
+    depth = left.shape[1]
+    total = jnp.zeros((left.shape[0], columns), jnp.float32)
+    for start in range(0, depth, DEPTH):
+        part = pl.ds(start, DEPTH)
+        a = left[:, part]
+        if transposed:
+            total += lax.dot_general(
+                a, right[:, part], (((1,), (1,)), ((), ())), preferred_element_type=jnp.float32
+            )
+        else:
+            total += jnp.dot(a, right[part, :], preferred_element_type=jnp.float32)
+    return total
+
+
+def forward_kernel(places, chips, *refs):
+    count = len(places)
+    blocks, (weight, out, whole, sems) = refs[:count], refs[count:]
+
+    @pl.when(pl.program_id(0) == 0)
+    def _():
+        assemble(places, chips, blocks, whole, sems)
+
+    out[...] = deep_dot(whole, weight, False, out.shape[1])
+
+
+def forward(places, chips, blocks, weight, tile):
+    rows = blocks[0].shape[0] * chips * 2
+    depth, width = weight.shape
+    return pl.pallas_call(
+        functools.partial(forward_kernel, places, chips),
+        grid=(width // tile,),
+        out_shape=jax.ShapeDtypeStruct((rows, width), jnp.float32),
+        in_specs=[pl.BlockSpec(memory_space=pl.ANY)] * len(blocks)
+        + [pl.BlockSpec((depth, tile), lambda n: (0, n))],
+        out_specs=pl.BlockSpec((rows, tile), lambda n: (0, n)),
+        scratch_shapes=[
+            pltpu.VMEM((rows, depth), jnp.bfloat16),
+            pltpu.SemaphoreType.DMA((len(blocks),)),
+        ],
+        compiler_params=pltpu.CompilerParams(vmem_limit_bytes=VMEM),
+        cost_estimate=pl.CostEstimate(
+            flops=2 * rows * depth * width, bytes_accessed=2 * depth * width, transcendentals=0
+        ),
+    )(*blocks, weight)
+
+
+def membership(ids, examples):
+    rows = lax.broadcasted_iota(jnp.int32, (examples, ids.shape[1]), 0)
+    return (jnp.broadcast_to(ids, rows.shape) == rows).astype(jnp.float32)
+
+
+def exact_dot(a, b, contract):
+    return lax.dot_general(
+        a, b, (contract, ((), ())), precision=HIGH, preferred_element_type=jnp.float32
+    )
+
+
+def backward_kernel(places, chips, examples, *refs):
+    count = len(places)
+    blocks = refs[:count]
+    weight, gate, up, proj, proj_ff, ids, send, whole, sums, flipped, sems = refs[count:]
+    step = pl.program_id(0)
+    hid = 2 * chips
+    shares = R // hid
+
+    @pl.when(step == 0)
+    def _():
+        assemble(places, chips, blocks, whole, sems)
+        sums[...] = jnp.zeros_like(sums)
+        columns = deep_dot(whole, proj, False, R).T
+        for lanes in range(flipped.shape[0]):
+            flipped[lanes] = columns[:, lanes * 128 : (lanes + 1) * 128]
+
+    hidden_grad = deep_dot(whole, weight, True, gate.shape[1])
+    hidden, gate_grad, up_grad = pointwise(gate[...], up[...], hidden_grad)
+    for m, value in enumerate((gate_grad, up_grad, hidden)):
+        sums[m] += jnp.dot(
+            value, proj_ff[:, m * R : (m + 1) * R], preferred_element_type=jnp.float32
+        )
+
+    @pl.when(step == pl.num_programs(0) - 1)
+    def _():
+        for m in range(2):
+            columns = sums[m].T
+            for p in range(hid):
+                send[p, m * shares : (m + 1) * shares, :] = columns[p * shares : (p + 1) * shares]
+        member = membership(ids[...], examples)
+        total_rows = member.shape[1]
+        for j in range(shares):
+            every = pl.ds(j, hid, shares)
+            own = jnp.concatenate([flipped[k, every, :] for k in range(flipped.shape[0])], axis=1)
+            left = (own[:, None, :] * member[None, :, :]).reshape(hid * examples, total_rows)
+            product = exact_dot(left, sums[2], ((1,), (0,)))
+            send[:, 2 * shares :, j * R : (j + 1) * R] = product.reshape(hid, examples, R)
+
+
+def backward(places, chips, blocks, weight, gate, up, proj, proj_ff, ids, tile):
+    rows = blocks[0].shape[0] * chips * 2
+    width, depth = weight.shape
+    hid = 2 * chips
+    shares, examples = R // hid, rows // EX_TOK
+    return pl.pallas_call(
+        functools.partial(backward_kernel, places, chips, examples),
+        grid=(width // tile,),
+        out_shape=jax.ShapeDtypeStruct((hid, 2 * shares + examples, rows), jnp.float32),
+        in_specs=[pl.BlockSpec(memory_space=pl.ANY)] * len(blocks)
+        + [
+            pl.BlockSpec((tile, depth), lambda n: (n, 0)),
+            pl.BlockSpec((rows, tile), lambda n: (0, n)),
+            pl.BlockSpec((rows, tile), lambda n: (0, n)),
+            pl.BlockSpec((depth, R), lambda n: (0, 0)),
+            pl.BlockSpec((tile, 3 * R), lambda n: (n, 0)),
+            pl.BlockSpec((1, rows), lambda n: (0, 0)),
+        ],
+        out_specs=pl.BlockSpec((hid, 2 * shares + examples, rows), lambda n: (0, 0, 0)),
+        scratch_shapes=[
+            pltpu.VMEM((rows, depth), jnp.bfloat16),
+            pltpu.VMEM((3, rows, R), jnp.float32),
+            pltpu.VMEM((rows // 128, R, 128), jnp.float32),
+            pltpu.SemaphoreType.DMA((len(blocks),)),
+        ],
+        compiler_params=pltpu.CompilerParams(vmem_limit_bytes=VMEM),
+        cost_estimate=pl.CostEstimate(
+            flops=2 * rows * depth * width, bytes_accessed=2 * depth * width, transcendentals=0
+        ),
+    )(*blocks, weight, gate, up, proj, proj_ff, ids)
+
+
+def features_kernel(hid, received, inputs, ids, tests, features, partial):
+    shares = R // hid
+    examples = features.shape[0]
+    member = membership(ids[...], examples)
+    total = jnp.sum(received[...], axis=0)
+    for m in range(2):
+        own = total[m * shares : (m + 1) * shares]
+        left = (own[:, None, :] * member[None, :, :]).reshape(shares * examples, own.shape[1])
+        product = exact_dot(left, inputs[:, m * R : (m + 1) * R], ((1,), (0,)))
+        for j in range(shares):
+            start = (j * 3 + m) * R
+            features[:, start : start + R] = product[j * examples : (j + 1) * examples]
+    for j in range(shares):
+        start = (j * 3 + 2) * R
+        features[:, start : start + R] = total[2 * shares :, j * R : (j + 1) * R]
+    scores = exact_dot(features[...], tests[...].astype(jnp.float32), ((1,), (1,)))
+    partial[...] = jnp.broadcast_to(scores[None], partial.shape)
+
+
+def finish(received, inputs, ids, tests):
+    hid, _, rows = received.shape
+    examples = rows // EX_TOK
+    vmem = pl.BlockSpec(memory_space=pltpu.VMEM)
+    return pl.pallas_call(
+        functools.partial(features_kernel, hid),
+        out_shape=(
+            jax.ShapeDtypeStruct((examples, tests.shape[1]), jnp.float32),
+            jax.ShapeDtypeStruct((hid, examples, tests.shape[0]), jnp.float32),
+        ),
+        in_specs=[vmem] * 4,
+        out_specs=(vmem, vmem),
+        compiler_params=pltpu.CompilerParams(vmem_limit_bytes=VMEM),
+    )(received, inputs, ids, tests)
+
+
+def local_ring(
+    tokens,
+    out_grad,
+    gate_weight,
+    up_weight,
+    down_weight,
+    proj_d,
+    proj_ff,
+    example_ids,
+    test_features,
+):
+    chips = lax.axis_size("hid") // 2
+    ids = example_ids[None, :]
+    places, token_blocks = gather_blocks(tokens, chips)
+    _, grad_blocks = gather_blocks(out_grad, chips)
+    inputs = forward(places, chips, token_blocks, proj_d[:, : 2 * R], 2 * R)
+    gate = forward(places, chips, token_blocks, gate_weight, TILE)
+    up = forward(places, chips, token_blocks, up_weight, TILE)
+    send = backward(
+        places, chips, grad_blocks, down_weight, gate, up, proj_d[:, 2 * R :], proj_ff, ids, TILE
+    )
+    received = lax.all_to_all(send, "hid", 0, 0)
+    features, partial = finish(received, inputs, ids, test_features)
+    scores = jnp.sum(lax.all_to_all(partial, "hid", 0, 0), axis=0)
+    return features, scores
+
+
 def solution(mesh):
+    one_ring = mesh.shape["mod"] == 1 and mesh.shape["hid"] <= 16
     return jax.shard_map(
-        local,
+        local_ring if one_ring else local_general,
         mesh=mesh,
         in_specs=(
             P(("groups", "hid"), "mod"),

time: 271 us -> 148 us (0.55)
  waiting for transfers between devices: 156 us -> 27.2 us
  Pallas kernels: 0 us -> 66.7 us
  matrix products: 64.7 us -> 0 us
  starting transfers between devices: 0.11 us -> 25.7 us
  blocking collectives: 31.7 us -> 13.7 us
  between operations: 13.9 us -> 1.14 us
  local copies, waits for them, and re-layouts: 2.66 us -> 11.8 us
    psum x1 -> x0, waiting for transfers between devices: 85.5 us -> none  [local(): lax.psum((output_gate, output_up, input_down), 'hid')]
    all_gather x2 -> x0, waiting for transfers between devices: 69.4 us -> none  [the longest x1 54.8 us: local(): block_rows = lax.all_gather(tokens, 'hid', axis=0, tiled=True)]
    pallas_call x0 -> x5, Pallas kernels: none -> 66.7 us  [the longest x3 41.4 us: forward(): pl.pallas_call(functools.partial(forward_kernel, places, chips), grid=(wi...]
    dot_general x10 -> x0, matrix products: 64.7 us -> none  [the longest x7 47.1 us: project_rows(): return jnp.dot(block_rows, weights, preferred_element_type=jnp.float32)]
    psum x1 -> x0, blocking collectives: 31.7 us -> none  [local(): scores = lax.psum(partial_scores, 'hid')]
    ppermute x0 -> x34, waiting for transfers between devices: none -> 27 us  [the longest x16 27 us: ring_step(): return lax.ppermute(block, 'hid', pairs)]
    ppermute x0 -> x34, starting transfers between devices: none -> 20.7 us  [the longest x16 17.7 us: ring_step(): return lax.ppermute(block, 'hid', pairs)]
    all_to_all x0 -> x1, blocking collectives: none -> 13.7 us  [local_ring(): scores = jnp.sum(lax.all_to_all(partial, 'hid', 0, 0), axis=0)]
  transfers between devices with their start and end apart: 3 -> 35, of which waited for: 3 -> 11; matrix products, arithmetic and copies ran while one was open for 14% -> 6% of each run, Pallas kernels for 0% -> 28%
where the time goes in v1:
time: 148 us; the launch traced here: 147 us
  Pallas kernels  66.7 us (45%)
  waiting for transfers between devices  27.2 us (18%)
  starting transfers between devices  25.7 us (17%)
  blocking collectives  13.7 us (9%)
  local copies, waits for them, and re-layouts  11.8 us (8%)
    pallas_call x3, Pallas kernels, forward(): pl.pallas_call(functools.partial(forward_kernel, places, chips), grid=(wi...  41.4 us
    ppermute x16, waiting for transfers between devices, ring_step(): return lax.ppermute(block, 'hid', pairs)  27 us
    pallas_call x1, Pallas kernels, backward(): pl.pallas_call(functools.partial(backward_kernel, places, chips, examples...  22.5 us
    ppermute x16, starting transfers between devices, ring_step(): return lax.ppermute(block, 'hid', pairs)  17.7 us
    all_to_all x1, blocking collectives, local_ring(): scores = jnp.sum(lax.all_to_all(partial, 'hid', 0, 0), axis=0)  13.7 us
    unnamed x71, local copies, waits for them, and re-layouts  8.34 us
    all_to_all x1, starting transfers between devices, local_ring(): received = lax.all_to_all(send, 'hid', 0, 0)  4.97 us
    ppermute x18, starting transfers between devices, core_swap(): return lax.ppermute(block, 'hid', [(h, h ^ 1) for h in range(2 * chips)])  3.02 us
  transfers between devices with their start and end apart: 35, of which 11 were waited for; matrix products, arithmetic and copies ran while one was open for 6% of the time, Pallas kernels for 28%

profile of v1, /device:TPU:0, one launch (start us, length us, event | category | flops | bytes accessed | tf_op | source)
XLA Modules:
  0.0 146.9 jit_solution(10011189918098914547)
XLA Ops:
  0.6 0.0 slice-start
  0.6 3.1 %collective-permute-start.18 = (bf16[16,8192]{1,0:T(8,128)(2,1)}, bf16[16,8192]{1,0:T(8,128)(2,1)S(1)}, u32[]{:S(2)}, u32[]{:S(2)}) collective-permute-start(bf16[16,8192]{1,0:T(8,128)(2,1)} %refs_0_.7), channel_id=1, source_target_pairs={{0,4},{1,5},{4,8},{5,9},{8,12},{9,13},{12,14},{13,15},{14,10},{15,... | collective-permute-start | bytes 786440 | tf_op jit(solution)/shard_map/ppermute | solution.py:117
  3.7 0.0 collective-permute-start.20
  3.7 0.0 collective-permute-start.17
  3.7 2.0 %collective-permute-start.1 = (bf16[16,8192]{1,0:T(8,128)(2,1)}, bf16[16,8192]{1,0:T(8,128)(2,1)S(1)}, u32[]{:S(2)}, u32[]{:S(2)}) collective-permute-start(bf16[16,8192]{1,0:T(8,128)(2,1)} %refs_0_.6), channel_id=1, source_target_pairs={{0,4},{1,5},{4,8},{5,9},{8,12},{9,13},{12,14},{13,15},{14,10},{15,... | collective-permute-start | bytes 786440 | tf_op jit(solution)/shard_map/ppermute | solution.py:117
  5.7 0.0 collective-permute-start.3
  5.8 5.2 %collective-permute-done.18.refs_2_ = bf16[16,8192]{1,0:T(8,128)(2,1)S(1)} collective-permute-done((bf16[16,8192]{1,0:T(8,128)(2,1)}, bf16[16,8192]{1,0:T(8,128)(2,1)S(1)}, u32[]{:S(2)}, u32[]{:S(2)}) %collective-permute-start.18) | collective-permute-done | bytes 262176 | tf_op jit(solution)/shard_map/ppermute | solution.py:117
  11.0 2.1 %collective-permute-start.22 = (bf16[16,8192]{1,0:T(8,128)(2,1)S(1)}, bf16[16,8192]{1,0:T(8,128)(2,1)S(1)}, u32[]{:S(2)}, u32[]{:S(2)}) collective-permute-start(bf16[16,8192]{1,0:T(8,128)(2,1)S(1)} %collective-permute-done.18.refs_2_), channel_id=1, source_target_pairs={{0,4},{1,5},{4,8},{5,9},{8,12},{9,13},{12,14},{13,15},{14,10},{15,... | collective-permute-start | bytes 786440 | tf_op jit(solution)/shard_map/ppermute | solution.py:117
  13.1 0.0 collective-permute-done.20.refs_4_
  13.2 0.0 collective-permute-start.24
  13.2 0.1 collective-permute-start
  13.3 3.3 %collective-permute-done.1.refs_2_ = bf16[16,8192]{1,0:T(8,128)(2,1)S(1)} collective-permute-done((bf16[16,8192]{1,0:T(8,128)(2,1)}, bf16[16,8192]{1,0:T(8,128)(2,1)S(1)}, u32[]{:S(2)}, u32[]{:S(2)}) %collective-permute-start.1) | collective-permute-done | bytes 262176 | tf_op jit(solution)/shard_map/ppermute | solution.py:117
  16.6 2.1 %collective-permute-start.5 = (bf16[16,8192]{1,0:T(8,128)(2,1)S(1)}, bf16[16,8192]{1,0:T(8,128)(2,1)S(1)}, u32[]{:S(2)}, u32[]{:S(2)}) collective-permute-start(bf16[16,8192]{1,0:T(8,128)(2,1)S(1)} %collective-permute-done.1.refs_2_), channel_id=1, source_target_pairs={{0,4},{1,5},{4,8},{5,9},{8,12},{9,13},{12,14},{13,15},{14,10},{15,... | collective-permute-start | bytes 786440 | tf_op jit(solution)/shard_map/ppermute | solution.py:117
  18.7 0.0 collective-permute-done.3.refs_4_
  18.8 3.4 %collective-permute-done.22.refs_6_ = bf16[16,8192]{1,0:T(8,128)(2,1)S(1)} collective-permute-done((bf16[16,8192]{1,0:T(8,128)(2,1)S(1)}, bf16[16,8192]{1,0:T(8,128)(2,1)S(1)}, u32[]{:S(2)}, u32[]{:S(2)}) %collective-permute-start.22) | collective-permute-done | bytes 262176 | tf_op jit(solution)/shard_map/ppermute | solution.py:117
  22.2 2.1 %collective-permute-start.26 = (bf16[16,8192]{1,0:T(8,128)(2,1)S(1)}, bf16[16,8192]{1,0:T(8,128)(2,1)S(1)}, u32[]{:S(2)}, u32[]{:S(2)}) collective-permute-start(bf16[16,8192]{1,0:T(8,128)(2,1)S(1)} %collective-permute-done.22.refs_6_), channel_id=1, source_target_pairs={{0,4},{1,5},{4,8},{5,9},{8,12},{9,13},{12,14},{13,15},{14,10},{15,... | collective-permute-start | bytes 786440 | tf_op jit(solution)/shard_map/ppermute | solution.py:117
  24.4 0.0 collective-permute-done.24.refs_8_
  24.4 0.1 collective-permute-start.19
  24.5 3.3 %collective-permute-done.5.refs_6_ = bf16[16,8192]{1,0:T(8,128)(2,1)S(1)} collective-permute-done((bf16[16,8192]{1,0:T(8,128)(2,1)S(1)}, bf16[16,8192]{1,0:T(8,128)(2,1)S(1)}, u32[]{:S(2)}, u32[]{:S(2)}) %collective-permute-start.5) | collective-permute-done | bytes 262176 | tf_op jit(solution)/shard_map/ppermute | solution.py:117
  27.8 2.2 %collective-permute-done.7.refs_8_ = bf16[16,8192]{1,0:T(8,128)(2,1)S(1)} collective-permute-done((bf16[16,8192]{1,0:T(8,128)(2,1)S(1)}, bf16[16,8192]{1,0:T(8,128)(2,1)S(1)}, u32[]{:S(2)}, u32[]{:S(2)}) %collective-permute-start.7) | collective-permute-done | bytes 262176 | tf_op jit(solution)/shard_map/ppermute | solution.py:117
  30.0 2.6 %collective-permute-done.26.refs_10_ = bf16[16,8192]{1,0:T(8,128)(2,1)S(1)} collective-permute-done((bf16[16,8192]{1,0:T(8,128)(2,1)S(1)}, bf16[16,8192]{1,0:T(8,128)(2,1)S(1)}, u32[]{:S(2)}, u32[]{:S(2)}) %collective-permute-start.26) | collective-permute-done | bytes 262176 | tf_op jit(solution)/shard_map/ppermute | solution.py:117
  32.6 1.8 %collective-permute-start.9 = (bf16[16,8192]{1,0:T(8,128)(2,1)S(1)}, bf16[16,8192]{1,0:T(8,128)(2,1)S(1)}, u32[]{:S(2)}, u32[]{:S(2)}) collective-permute-start(bf16[16,8192]{1,0:T(8,128)(2,1)S(1)} %collective-permute-done.5.refs_6_), channel_id=1, source_target_pairs={{0,4},{1,5},{4,8},{5,9},{8,12},{9,13},{12,14},{13,15},{14,10},{15,... | collective-permute-start | bytes 786440 | tf_op jit(solution)/shard_map/ppermute | solution.py:117
  34.5 0.2 collective-permute-start.11
  34.8 0.1 collective-permute-start.25
  34.9 1.9 %collective-permute-start.30 = (bf16[16,4096]{1,0:T(8,128)(2,1)S(1)}, bf16[16,4096]{1,0:T(8,128)(2,1)S(1)}, u32[]{:S(2)}, u32[]{:S(2)}) collective-permute-start(bf16[16,4096]{1,0:T(8,128)(2,1)S(1)} %slice.26), channel_id=1, source_target_pairs={{0,4},{1,5},{4,8},{5,9},{8,12},{9,13},{12,14},{13,15},{14,10},{15,... | collective-permute-start | bytes 393224 | tf_op jit(solution)/shard_map/ppermute | solution.py:117
  36.7 0.2 collective-permute-start.32
  36.9 4.6 %collective-permute-done.9.refs_10_ = bf16[16,8192]{1,0:T(8,128)(2,1)S(1)} collective-permute-done((bf16[16,8192]{1,0:T(8,128)(2,1)S(1)}, bf16[16,8192]{1,0:T(8,128)(2,1)S(1)}, u32[]{:S(2)}, u32[]{:S(2)}) %collective-permute-start.9) | collective-permute-done | bytes 262176 | tf_op jit(solution)/shard_map/ppermute | solution.py:117
  41.5 1.3 collective-permute-done.11.refs_12_
  42.8 0.1 collective-permute-done.30.refs_14_
  42.9 0.5 collective-permute-start.31
  43.4 0.1 copy-done.14
  43.5 0.8 collective-permute-done.32.refs_16_
  44.3 1.8 %copy.14.refs_21_ = bf16[8192,64]{1,0:T(8,128)(2,1)} copy(bf16[8192,64]{0,1:T(8,128)(2,1)S(1)} %slice-done) | data formatting | bytes 2097152
  46.2 2.2 %copy.12.refs_22_ = bf16[1792,192]{1,0:T(8,128)(2,1)} copy(bf16[1792,192]{0,1:T(8,128)(2,1)} %param.15) | data formatting | bytes 1376256 | tf_op args[6]
  48.5 0.9 slice.24
  49.4 0.9 slice.25
  50.3 0.6 collective-permute-start.2
  50.9 0.1 collective-permute-start.4
  51.0 0.4 collective-permute-start.6
  51.4 1.6 %collective-permute-start.13 = (bf16[16,4096]{1,0:T(8,128)(2,1)S(1)}, bf16[16,4096]{1,0:T(8,128)(2,1)S(1)}, u32[]{:S(2)}, u32[]{:S(2)}) collective-permute-start(bf16[16,4096]{1,0:T(8,128)(2,1)S(1)} %slice.24), channel_id=1, source_target_pairs={{0,4},{1,5},{4,8},{5,9},{8,12},{9,13},{12,14},{13,15},{14,10},{15,... | collective-permute-start | bytes 393224 | tf_op jit(solution)/shard_map/ppermute | solution.py:117
  53.0 0.4 collective-permute-start.15
  53.5 17.8 %shard_map.105.refs_20_ = f32[256,1792]{1,0:T(8,128)} custom-call(bf16[16,8192]{1,0:T(8,128)(2,1)} %refs_0_.7, bf16[16,8192]{1,0:T(8,128)(2,1)} %copy-done.4, bf16[16,8192]{1,0:T(8,128)(2,1)} %copy-done.2, bf16[16,8192]{1,0:T(8,128)(2,1)} %copy-done.7, bf16[16,8192]{1,0:T(8,128)(2,1)} %copy-done.3, bf16[16,8192]{1,0:T(8,128)(2,1)} %copy-done.8, ...), custom_call_target="tpu_custom_call" | custom-call | flops 7516192768 | bytes 29360128 | tf_op jit(solution)/shard_map/pallas_call | solution.py:189
  71.3 0.1 collective-permute-start.8
  71.4 0.5 collective-permute-start.10
  72.0 0.1 collective-permute-start.12
  72.1 0.5 collective-permute-start.14
  72.5 0.1 collective-permute-start.16
  72.6 17.8 %shard_map.104.refs_19_ = f32[256,1792]{1,0:T(8,128)} custom-call(bf16[16,8192]{1,0:T(8,128)(2,1)} %refs_0_.7, bf16[16,8192]{1,0:T(8,128)(2,1)} %copy-done.4, bf16[16,8192]{1,0:T(8,128)(2,1)} %copy-done.2, bf16[16,8192]{1,0:T(8,128)(2,1)} %copy-done.7, bf16[16,8192]{1,0:T(8,128)(2,1)} %copy-done.3, bf16[16,8192]{1,0:T(8,128)(2,1)} %copy-done.8, ...), custom_call_target="tpu_custom_call" | custom-call | flops 7516192768 | bytes 29360128 | tf_op jit(solution)/shard_map/pallas_call | solution.py:189
  90.6 0.6 copy-done.27
  91.2 0.1 copy-done.32
  91.3 0.0 copy-done.33
  91.4 0.1 copy-done.28
  91.4 0.1 copy-done.29
  91.5 22.5 %shard_map.106 = f32[16,16,256]{2,1,0:T(8,128)} custom-call(bf16[16,8192]{1,0:T(8,128)(2,1)} %refs_0_.6, bf16[16,8192]{1,0:T(8,128)(2,1)} %collective-permute-done.refs_1_, bf16[16,8192]{1,0:T(8,128)(2,1)} %copy-done.16, bf16[16,8192]{1,0:T(8,128)(2,1)} %copy-done.24, bf16[16,8192]{1,0:T(8,128)(2,1)} %copy-done.18, bf16[16,8192]{1,0:T(8,128)(2,1)} %copy-done.25, ...), custom_call_target="tpu_custom_call" | custom-call | flops 7516192768 | bytes 29360128 | tf_op jit(solution)/shard_map/pallas_call | solution.py:262
  114.0 5.0 %all-to-all-start = ((f32[16,16,256]{2,1,0:T(8,128)}), f32[16,16,256]{2,1,0:T(8,128)S(1)}, u32[]{:S(2)}, u32[]{:S(2)}) async-start(f32[16,16,256]{2,1,0:T(8,128)} %shard_map.106), calls=%async_computation | async-start | bytes 524288 | tf_op jit(solution)/shard_map/all_to_all | solution.py:345
  119.0 0.0 slice-start.1
  119.0 1.6 %slice-done.1 = bf16[8192,128]{0,1:T(8,128)(2,1)S(1)} async-done(((bf16[8192,192]{0,1:T(8,128)(2,1)}), bf16[8192,128]{0,1:T(8,128)(2,1)S(1)}, s32[]{:S(2)}) %slice-start.1) | async-done | bytes 2097176 | tf_op jit(solution)/shard_map/slice | solution.py:339
  120.6 2.5 %copy.15.refs_18_ = bf16[8192,128]{1,0:T(8,128)(2,1)} copy(bf16[8192,128]{0,1:T(8,128)(2,1)S(1)} %slice-done.1) | data formatting | bytes 4194304
  123.0 5.8 %shard_map.107.inputs = f32[256,128]{1,0:T(8,128)} custom-call(bf16[16,8192]{1,0:T(8,128)(2,1)} %refs_0_.7, bf16[16,8192]{1,0:T(8,128)(2,1)} %copy-done.4, bf16[16,8192]{1,0:T(8,128)(2,1)} %copy-done.2, bf16[16,8192]{1,0:T(8,128)(2,1)} %copy-done.7, bf16[16,8192]{1,0:T(8,128)(2,1)} %copy-done.3, bf16[16,8192]{1,0:T(8,128)(2,1)} %copy-done.8, ...), custom_call_target="tpu_custom_call" | custom-call | flops 536870912 | bytes 2097152 | tf_op jit(solution)/shard_map/pallas_call | solution.py:189
  128.8 0.2 all-to-all-done.received
  129.0 0.7 copy-done.11
  129.7 2.8 %shard_map.108 = (f32[8,768]{1,0:T(8,128)}, f32[16,8,256]{2,1,0:T(8,128)}) custom-call(f32[16,16,256]{2,1,0:T(8,128)} %copy-done.11, f32[256,128]{1,0:T(8,128)} %shard_map.107.inputs, s32[1,256]{1,0:T(1,128)} %bitcast.2, bf16[256,768]{1,0:T(8,128)(2,1)} %tests.1), custom_call_target="tpu_custom_call" | custom-call | tf_op jit(solution)/shard_map/pallas_call | solution.py:312
  132.6 13.7 %all_to_all.10 = f32[16,8,256]{2,1,0:T(8,128)S(1)} all-to-all(f32[16,8,256]{2,1,0:T(8,128)} %get-tuple-element.5), channel_id=1, replica_groups=mesh['groups'=2,'hid'=16,'mod'=1] {'hid'}, dimensions={0} | all-to-all | bytes 262144 | tf_op jit(solution)/shard_map/all_to_all | solution.py:347
  146.3 0.6 reduce_sum.9
  (92 shorter events, 0.2 us)
Async XLA Ops:
  0.6 43.7 %slice-start = ((bf16[8192,192]{0,1:T(8,128)(2,1)}), bf16[8192,64]{0,1:T(8,128)(2,1)S(1)}, s32[]{:S(2)}) async-start(bf16[8192,192]{0,1:T(8,128)(2,1)} %param.14), calls=%async_computation.2 | async-start | bytes 2097152 | tf_op jit(solution)/shard_map/slice | solution.py:343
  0.6 10.3 %collective-permute-start.18 = (bf16[16,8192]{1,0:T(8,128)(2,1)}, bf16[16,8192]{1,0:T(8,128)(2,1)S(1)}, u32[]{:S(2)}, u32[]{:S(2)}) collective-permute-start(bf16[16,8192]{1,0:T(8,128)(2,1)} %refs_0_.7), channel_id=1, source_target_pairs={{0,4},{1,5},{4,8},{5,9},{8,12},{9,13},{12,14},{13,15},{14,10},{15,... | collective-permute-start | bytes 786440 | tf_op jit(solution)/shard_map/ppermute | solution.py:117
  3.7 9.4 %collective-permute-start.20 = (bf16[16,8192]{1,0:T(8,128)(2,1)}, bf16[16,8192]{1,0:T(8,128)(2,1)S(1)}, u32[]{:S(2)}, u32[]{:S(2)}) collective-permute-start(bf16[16,8192]{1,0:T(8,128)(2,1)} %refs_0_.7), channel_id=1, source_target_pairs={{0,2},{1,3},{4,0},{5,1},{8,4},{9,5},{12,8},{13,9},{14,12},{15,13},... | collective-permute-start | bytes 786440 | tf_op jit(solution)/shard_map/ppermute | solution.py:117
  3.7 9.4 %collective-permute-start.17 = (bf16[16,8192]{1,0:T(8,128)(2,1)}, bf16[16,8192]{1,0:T(8,128)(2,1)S(1)}, u32[]{:S(2)}, u32[]{:S(2)}) collective-permute-start(bf16[16,8192]{1,0:T(8,128)(2,1)} %refs_0_.7), channel_id=1, source_target_pairs={{0,1},{1,0},{2,3},{3,2},{4,5},{5,4},{6,7},{7,6},{8,9},{9,8},{10,11... | collective-permute-start | bytes 786440 | tf_op jit(solution)/shard_map/ppermute | solution.py:121
  3.7 12.9 %collective-permute-start.1 = (bf16[16,8192]{1,0:T(8,128)(2,1)}, bf16[16,8192]{1,0:T(8,128)(2,1)S(1)}, u32[]{:S(2)}, u32[]{:S(2)}) collective-permute-start(bf16[16,8192]{1,0:T(8,128)(2,1)} %refs_0_.6), channel_id=1, source_target_pairs={{0,4},{1,5},{4,8},{5,9},{8,12},{9,13},{12,14},{13,15},{14,10},{15,... | collective-permute-start | bytes 786440 | tf_op jit(solution)/shard_map/ppermute | solution.py:117
  5.7 13.0 %collective-permute-start.3 = (bf16[16,8192]{1,0:T(8,128)(2,1)}, bf16[16,8192]{1,0:T(8,128)(2,1)S(1)}, u32[]{:S(2)}, u32[]{:S(2)}) collective-permute-start(bf16[16,8192]{1,0:T(8,128)(2,1)} %refs_0_.6), channel_id=1, source_target_pairs={{0,2},{1,3},{4,0},{5,1},{8,4},{9,5},{12,8},{13,9},{14,12},{15,13},... | collective-permute-start | bytes 786440 | tf_op jit(solution)/shard_map/ppermute | solution.py:117
  11.0 35.1 %copy-start.2 = (bf16[16,8192]{1,0:T(8,128)(2,1)}, bf16[16,8192]{1,0:T(8,128)(2,1)S(1)}, u32[]{:S(2)}) copy-start(bf16[16,8192]{1,0:T(8,128)(2,1)S(1)} %collective-permute-done.18.refs_2_) | copy-start | bytes 786436
  11.0 11.2 %collective-permute-start.22 = (bf16[16,8192]{1,0:T(8,128)(2,1)S(1)}, bf16[16,8192]{1,0:T(8,128)(2,1)S(1)}, u32[]{:S(2)}, u32[]{:S(2)}) collective-permute-start(bf16[16,8192]{1,0:T(8,128)(2,1)S(1)} %collective-permute-done.18.refs_2_), channel_id=1, source_target_pairs={{0,4},{1,5},{4,8},{5,9},{8,12},{9,13},{12,14},{13,15},{14,10},{15,... | collective-permute-start | bytes 786440 | tf_op jit(solution)/shard_map/ppermute | solution.py:117
  13.2 33.0 %copy-start.3 = (bf16[16,8192]{1,0:T(8,128)(2,1)}, bf16[16,8192]{1,0:T(8,128)(2,1)S(1)}, u32[]{:S(2)}) copy-start(bf16[16,8192]{1,0:T(8,128)(2,1)S(1)} %collective-permute-done.20.refs_4_) | copy-start | bytes 786436
  13.2 11.2 %collective-permute-start.24 = (bf16[16,8192]{1,0:T(8,128)(2,1)S(1)}, bf16[16,8192]{1,0:T(8,128)(2,1)S(1)}, u32[]{:S(2)}, u32[]{:S(2)}) collective-permute-start(bf16[16,8192]{1,0:T(8,128)(2,1)S(1)} %collective-permute-done.20.refs_4_), channel_id=1, source_target_pairs={{0,2},{1,3},{4,0},{5,1},{8,4},{9,5},{12,8},{13,9},{14,12},{15,13},... | collective-permute-start | bytes 786440 | tf_op jit(solution)/shard_map/ppermute | solution.py:117
  13.2 32.9 %copy-start.4 = (bf16[16,8192]{1,0:T(8,128)(2,1)}, bf16[16,8192]{1,0:T(8,128)(2,1)S(1)}, u32[]{:S(2)}) copy-start(bf16[16,8192]{1,0:T(8,128)(2,1)S(1)} %collective-permute-done.17.refs_1_) | copy-start | bytes 786436
  13.2 11.2 %collective-permute-start = (bf16[16,8192]{1,0:T(8,128)(2,1)}, bf16[16,8192]{1,0:T(8,128)(2,1)}, u32[]{:S(2)}, u32[]{:S(2)}) collective-permute-start(bf16[16,8192]{1,0:T(8,128)(2,1)} %refs_0_.6), channel_id=1, source_target_pairs={{0,1},{1,0},{2,3},{3,2},{4,5},{5,4},{6,7},{7,6},{8,9},{9,8},{10,11... | collective-permute-start | bytes 786440 | tf_op jit(solution)/shard_map/ppermute | solution.py:121
  16.6 7.9 %copy-start.16 = (bf16[16,8192]{1,0:T(8,128)(2,1)}, bf16[16,8192]{1,0:T(8,128)(2,1)S(1)}, u32[]{:S(2)}) copy-start(bf16[16,8192]{1,0:T(8,128)(2,1)S(1)} %collective-permute-done.1.refs_2_) | copy-start | bytes 786436
  16.6 11.2 %collective-permute-start.5 = (bf16[16,8192]{1,0:T(8,128)(2,1)S(1)}, bf16[16,8192]{1,0:T(8,128)(2,1)S(1)}, u32[]{:S(2)}, u32[]{:S(2)}) collective-permute-start(bf16[16,8192]{1,0:T(8,128)(2,1)S(1)} %collective-permute-done.1.refs_2_), channel_id=1, source_target_pairs={{0,4},{1,5},{4,8},{5,9},{8,12},{9,13},{12,14},{13,15},{14,10},{15,... | collective-permute-start | bytes 786440 | tf_op jit(solution)/shard_map/ppermute | solution.py:117
  18.8 15.7 %copy-start.18 = (bf16[16,8192]{1,0:T(8,128)(2,1)}, bf16[16,8192]{1,0:T(8,128)(2,1)S(1)}, u32[]{:S(2)}) copy-start(bf16[16,8192]{1,0:T(8,128)(2,1)S(1)} %collective-permute-done.3.refs_4_) | copy-start | bytes 786436
  18.8 11.2 %collective-permute-start.7 = (bf16[16,8192]{1,0:T(8,128)(2,1)S(1)}, bf16[16,8192]{1,0:T(8,128)(2,1)S(1)}, u32[]{:S(2)}, u32[]{:S(2)}) collective-permute-start(bf16[16,8192]{1,0:T(8,128)(2,1)S(1)} %collective-permute-done.3.refs_4_), channel_id=1, source_target_pairs={{0,2},{1,3},{4,0},{5,1},{8,4},{9,5},{12,8},{13,9},{14,12},{15,13},... | collective-permute-start | bytes 786440 | tf_op jit(solution)/shard_map/ppermute | solution.py:117
  22.2 23.9 %copy-start.5 = (bf16[16,8192]{1,0:T(8,128)(2,1)}, bf16[16,8192]{1,0:T(8,128)(2,1)S(1)}, u32[]{:S(2)}) copy-start(bf16[16,8192]{1,0:T(8,128)(2,1)S(1)} %collective-permute-done.22.refs_6_) | copy-start | bytes 786436
  22.2 10.4 %collective-permute-start.26 = (bf16[16,8192]{1,0:T(8,128)(2,1)S(1)}, bf16[16,8192]{1,0:T(8,128)(2,1)S(1)}, u32[]{:S(2)}, u32[]{:S(2)}) collective-permute-start(bf16[16,8192]{1,0:T(8,128)(2,1)S(1)} %collective-permute-done.22.refs_6_), channel_id=1, source_target_pairs={{0,4},{1,5},{4,8},{5,9},{8,12},{9,13},{12,14},{13,15},{14,10},{15,... | collective-permute-start | bytes 786440 | tf_op jit(solution)/shard_map/ppermute | solution.py:117
  24.4 21.7 %copy-start.6 = (bf16[16,8192]{1,0:T(8,128)(2,1)}, bf16[16,8192]{1,0:T(8,128)(2,1)S(1)}, u32[]{:S(2)}) copy-start(bf16[16,8192]{1,0:T(8,128)(2,1)S(1)} %collective-permute-done.24.refs_8_) | copy-start | bytes 786436
  24.4 10.1 %collective-permute-start.28 = (bf16[16,8192]{1,0:T(8,128)(2,1)S(1)}, bf16[16,8192]{1,0:T(8,128)(2,1)S(1)}, u32[]{:S(2)}, u32[]{:S(2)}) collective-permute-start(bf16[16,8192]{1,0:T(8,128)(2,1)S(1)} %collective-permute-done.24.refs_8_), channel_id=1, source_target_pairs={{0,2},{1,3},{4,0},{5,1},{8,4},{9,5},{12,8},{13,9},{14,12},{15,13},... | collective-permute-start | bytes 786440 | tf_op jit(solution)/shard_map/ppermute | solution.py:117
  24.4 10.3 %collective-permute-start.19 = (bf16[16,8192]{1,0:T(8,128)(2,1)S(1)}, bf16[16,8192]{1,0:T(8,128)(2,1)S(1)}, u32[]{:S(2)}, u32[]{:S(2)}) collective-permute-start(bf16[16,8192]{1,0:T(8,128)(2,1)S(1)} %collective-permute-done.18.refs_2_), channel_id=1, source_target_pairs={{0,1},{1,0},{2,3},{3,2},{4,5},{5,4},{6,7},{7,6},{8,9},{9,8},{10,11... | collective-permute-start | bytes 786440 | tf_op jit(solution)/shard_map/ppermute | solution.py:121
  27.8 16.5 %copy-start.20 = (bf16[16,8192]{1,0:T(8,128)(2,1)}, bf16[16,8192]{1,0:T(8,128)(2,1)S(1)}, u32[]{:S(2)}) copy-start(bf16[16,8192]{1,0:T(8,128)(2,1)S(1)} %collective-permute-done.5.refs_6_) | copy-start | bytes 786436
  27.8 7.0 %collective-permute-start.21 = (bf16[16,8192]{1,0:T(8,128)(2,1)S(1)}, bf16[16,8192]{1,0:T(8,128)(2,1)S(1)}, u32[]{:S(2)}, u32[]{:S(2)}) collective-permute-start(bf16[16,8192]{1,0:T(8,128)(2,1)S(1)} %collective-permute-done.20.refs_4_), channel_id=1, source_target_pairs={{0,1},{1,0},{2,3},{3,2},{4,5},{5,4},{6,7},{7,6},{8,9},{9,8},{10,11... | collective-permute-start | bytes 786440 | tf_op jit(solution)/shard_map/ppermute | solution.py:121
  30.0 14.3 %copy-start.22 = (bf16[16,8192]{1,0:T(8,128)(2,1)}, bf16[16,8192]{1,0:T(8,128)(2,1)S(1)}, u32[]{:S(2)}) copy-start(bf16[16,8192]{1,0:T(8,128)(2,1)S(1)} %collective-permute-done.7.refs_8_) | copy-start | bytes 786436
  30.0 6.7 %collective-permute-start.23 = (bf16[16,8192]{1,0:T(8,128)(2,1)S(1)}, bf16[16,8192]{1,0:T(8,128)(2,1)S(1)}, u32[]{:S(2)}, u32[]{:S(2)}) collective-permute-start(bf16[16,8192]{1,0:T(8,128)(2,1)S(1)} %collective-permute-done.22.refs_6_), channel_id=1, source_target_pairs={{0,1},{1,0},{2,3},{3,2},{4,5},{5,4},{6,7},{7,6},{8,9},{9,8},{10,11... | collective-permute-start | bytes 786440 | tf_op jit(solution)/shard_map/ppermute | solution.py:121
  32.6 13.5 %copy-start = (bf16[16,8192]{1,0:T(8,128)(2,1)}, bf16[16,8192]{1,0:T(8,128)(2,1)S(1)}, u32[]{:S(2)}) copy-start(bf16[16,8192]{1,0:T(8,128)(2,1)S(1)} %collective-permute-done.26.refs_10_) | copy-start | bytes 786436
  32.6 8.9 %collective-permute-start.9 = (bf16[16,8192]{1,0:T(8,128)(2,1)S(1)}, bf16[16,8192]{1,0:T(8,128)(2,1)S(1)}, u32[]{:S(2)}, u32[]{:S(2)}) collective-permute-start(bf16[16,8192]{1,0:T(8,128)(2,1)S(1)} %collective-permute-done.5.refs_6_), channel_id=1, source_target_pairs={{0,4},{1,5},{4,8},{5,9},{8,12},{9,13},{12,14},{13,15},{14,10},{15,... | collective-permute-start | bytes 786440 | tf_op jit(solution)/shard_map/ppermute | solution.py:117
  34.5 11.7 %copy-start.1 = (bf16[16,8192]{1,0:T(8,128)(2,1)}, bf16[16,8192]{1,0:T(8,128)(2,1)S(1)}, u32[]{:S(2)}) copy-start(bf16[16,8192]{1,0:T(8,128)(2,1)S(1)} %collective-permute-done.28.refs_12_) | copy-start | bytes 786436
  34.5 8.3 %collective-permute-start.11 = (bf16[16,8192]{1,0:T(8,128)(2,1)S(1)}, bf16[16,8192]{1,0:T(8,128)(2,1)S(1)}, u32[]{:S(2)}, u32[]{:S(2)}) collective-permute-start(bf16[16,8192]{1,0:T(8,128)(2,1)S(1)} %collective-permute-done.7.refs_8_), channel_id=1, source_target_pairs={{0,2},{1,3},{4,0},{5,1},{8,4},{9,5},{12,8},{13,9},{14,12},{15,13},... | collective-permute-start | bytes 786440 | tf_op jit(solution)/shard_map/ppermute | solution.py:117
  34.7 11.4 %copy-start.7 = (bf16[16,8192]{1,0:T(8,128)(2,1)}, bf16[16,8192]{1,0:T(8,128)(2,1)S(1)}, u32[]{:S(2)}) copy-start(bf16[16,8192]{1,0:T(8,128)(2,1)S(1)} %collective-permute-done.19.refs_3_) | copy-start | bytes 786436
  34.8 15.6 %collective-permute-start.25 = (bf16[16,8192]{1,0:T(8,128)(2,1)S(1)}, bf16[16,8192]{1,0:T(8,128)(2,1)}, u32[]{:S(2)}, u32[]{:S(2)}) collective-permute-start(bf16[16,8192]{1,0:T(8,128)(2,1)S(1)} %collective-permute-done.24.refs_8_), channel_id=1, source_target_pairs={{0,1},{1,0},{2,3},{3,2},{4,5},{5,4},{6,7},{7,6},{8,9},{9,8},{10,11... | collective-permute-start | bytes 786440 | tf_op jit(solution)/shard_map/ppermute | solution.py:121
  34.8 11.3 %copy-start.8 = (bf16[16,8192]{1,0:T(8,128)(2,1)}, bf16[16,8192]{1,0:T(8,128)(2,1)S(1)}, u32[]{:S(2)}) copy-start(bf16[16,8192]{1,0:T(8,128)(2,1)S(1)} %collective-permute-done.21.refs_5_) | copy-start | bytes 786436
  34.9 8.1 %collective-permute-start.30 = (bf16[16,4096]{1,0:T(8,128)(2,1)S(1)}, bf16[16,4096]{1,0:T(8,128)(2,1)S(1)}, u32[]{:S(2)}, u32[]{:S(2)}) collective-permute-start(bf16[16,4096]{1,0:T(8,128)(2,1)S(1)} %slice.26), channel_id=1, source_target_pairs={{0,4},{1,5},{4,8},{5,9},{8,12},{9,13},{12,14},{13,15},{14,10},{15,... | collective-permute-start | bytes 393224 | tf_op jit(solution)/shard_map/ppermute | solution.py:117
  36.7 4.8 %copy-start.9 = (bf16[16,8192]{1,0:T(8,128)(2,1)}, bf16[16,8192]{1,0:T(8,128)(2,1)S(1)}, u32[]{:S(2)}) copy-start(bf16[16,8192]{1,0:T(8,128)(2,1)S(1)} %collective-permute-done.23.refs_7_) | copy-start | bytes 786436
  36.7 7.6 %collective-permute-start.32 = (bf16[16,4096]{1,0:T(8,128)(2,1)S(1)}, bf16[16,4096]{1,0:T(8,128)(2,1)}, u32[]{:S(2)}, u32[]{:S(2)}) collective-permute-start(bf16[16,4096]{1,0:T(8,128)(2,1)S(1)} %slice.27), channel_id=1, source_target_pairs={{0,2},{1,3},{4,0},{5,1},{8,4},{9,5},{12,8},{13,9},{14,12},{15,13},... | collective-permute-start | bytes 393224 | tf_op jit(solution)/shard_map/ppermute | solution.py:117
  41.5 1.4 copy-start.12
  41.5 9.9 %collective-permute-start.27 = (bf16[16,8192]{1,0:T(8,128)(2,1)S(1)}, bf16[16,8192]{1,0:T(8,128)(2,1)}, u32[]{:S(2)}, u32[]{:S(2)}) collective-permute-start(bf16[16,8192]{1,0:T(8,128)(2,1)S(1)} %collective-permute-done.26.refs_10_), channel_id=1, source_target_pairs={{0,1},{1,0},{2,3},{3,2},{4,5},{5,4},{6,7},{7,6},{8,9},{9,8},{10,11... | collective-permute-start | bytes 786440 | tf_op jit(solution)/shard_map/ppermute | solution.py:121
  42.8 10.2 %collective-permute-start.29 = (bf16[16,8192]{1,0:T(8,128)(2,1)S(1)}, bf16[16,8192]{1,0:T(8,128)(2,1)}, u32[]{:S(2)}, u32[]{:S(2)}) collective-permute-start(bf16[16,8192]{1,0:T(8,128)(2,1)S(1)} %collective-permute-done.28.refs_12_), channel_id=1, source_target_pairs={{0,1},{1,0},{2,3},{3,2},{4,5},{5,4},{6,7},{7,6},{8,9},{9,8},{10,11... | collective-permute-start | bytes 786440 | tf_op jit(solution)/shard_map/ppermute | solution.py:121
  42.9 3.3 %copy-start.10 = (bf16[16,4096]{1,0:T(8,128)(2,1)}, bf16[16,4096]{1,0:T(8,128)(2,1)S(1)}, u32[]{:S(2)}) copy-start(bf16[16,4096]{1,0:T(8,128)(2,1)S(1)} %collective-permute-done.30.refs_14_) | copy-start | bytes 393220
  42.9 8.0 %collective-permute-start.31 = (bf16[16,4096]{1,0:T(8,128)(2,1)S(1)}, bf16[16,4096]{1,0:T(8,128)(2,1)}, u32[]{:S(2)}, u32[]{:S(2)}) collective-permute-start(bf16[16,4096]{1,0:T(8,128)(2,1)S(1)} %collective-permute-done.30.refs_14_), channel_id=1, source_target_pairs={{0,1},{1,0},{2,3},{3,2},{4,5},{5,4},{6,7},{7,6},{8,9},{9,8},{10,11... | collective-permute-start | bytes 393224 | tf_op jit(solution)/shard_map/ppermute | solution.py:121
  44.3 6.7 %collective-permute-start.33 = (bf16[16,4096]{1,0:T(8,128)(2,1)}, bf16[16,4096]{1,0:T(8,128)(2,1)}, u32[]{:S(2)}, u32[]{:S(2)}) collective-permute-start(bf16[16,4096]{1,0:T(8,128)(2,1)} %collective-permute-done.32.refs_16_), channel_id=1, source_target_pairs={{0,1},{1,0},{2,3},{3,2},{4,5},{5,4},{6,7},{7,6},{8,9},{9,8},{10,11... | collective-permute-start | bytes 393224 | tf_op jit(solution)/shard_map/ppermute | solution.py:121
  46.2 4.1 %copy-start.17 = (bf16[16,8192]{1,0:T(8,128)(2,1)S(1)}, bf16[16,8192]{1,0:T(8,128)(2,1)}, u32[]{:S(2)}) copy-start(bf16[16,8192]{1,0:T(8,128)(2,1)} %copy-done.16) | copy-start | bytes 786436
  46.2 4.7 %copy-start.19 = (bf16[16,8192]{1,0:T(8,128)(2,1)S(1)}, bf16[16,8192]{1,0:T(8,128)(2,1)}, u32[]{:S(2)}) copy-start(bf16[16,8192]{1,0:T(8,128)(2,1)} %copy-done.18) | copy-start | bytes 786436
  46.2 4.8 %copy-start.21 = (bf16[16,8192]{1,0:T(8,128)(2,1)S(1)}, bf16[16,8192]{1,0:T(8,128)(2,1)}, u32[]{:S(2)}) copy-start(bf16[16,8192]{1,0:T(8,128)(2,1)} %copy-done.20) | copy-start | bytes 786436
  50.3 21.0 %copy-start.23 = (bf16[16,8192]{1,0:T(8,128)(2,1)S(1)}, bf16[16,8192]{1,0:T(8,128)(2,1)}, u32[]{:S(2)}) copy-start(bf16[16,8192]{1,0:T(8,128)(2,1)} %copy-done.22) | copy-start | bytes 786436
  50.3 21.1 %copy-start.13 = (bf16[16,8192]{1,0:T(8,128)(2,1)S(1)}, bf16[16,8192]{1,0:T(8,128)(2,1)}, u32[]{:S(2)}) copy-start(bf16[16,8192]{1,0:T(8,128)(2,1)} %copy-done.12) | copy-start | bytes 786436
  50.3 21.6 %copy-start.15 = (bf16[16,8192]{1,0:T(8,128)(2,1)S(1)}, bf16[16,8192]{1,0:T(8,128)(2,1)}, u32[]{:S(2)}) copy-start(bf16[16,8192]{1,0:T(8,128)(2,1)} %copy-done.14) | copy-start | bytes 786436
  50.3 20.9 %collective-permute-start.2 = (bf16[16,8192]{1,0:T(8,128)(2,1)S(1)}, bf16[16,8192]{1,0:T(8,128)(2,1)S(1)}, u32[]{:S(2)}, u32[]{:S(2)}) collective-permute-start(bf16[16,8192]{1,0:T(8,128)(2,1)S(1)} %copy-done.17), channel_id=1, source_target_pairs={{0,1},{1,0},{2,3},{3,2},{4,5},{5,4},{6,7},{7,6},{8,9},{9,8},{10,11... | collective-permute-start | bytes 786440 | tf_op jit(solution)/shard_map/ppermute | solution.py:121
  50.9 20.5 %collective-permute-start.4 = (bf16[16,8192]{1,0:T(8,128)(2,1)S(1)}, bf16[16,8192]{1,0:T(8,128)(2,1)S(1)}, u32[]{:S(2)}, u32[]{:S(2)}) collective-permute-start(bf16[16,8192]{1,0:T(8,128)(2,1)S(1)} %copy-done.19), channel_id=1, source_target_pairs={{0,1},{1,0},{2,3},{3,2},{4,5},{5,4},{6,7},{7,6},{8,9},{9,8},{10,11... | collective-permute-start | bytes 786440 | tf_op jit(solution)/shard_map/ppermute | solution.py:121
  51.0 21.0 %collective-permute-start.6 = (bf16[16,8192]{1,0:T(8,128)(2,1)S(1)}, bf16[16,8192]{1,0:T(8,128)(2,1)S(1)}, u32[]{:S(2)}, u32[]{:S(2)}) collective-permute-start(bf16[16,8192]{1,0:T(8,128)(2,1)S(1)} %copy-done.21), channel_id=1, source_target_pairs={{0,1},{1,0},{2,3},{3,2},{4,5},{5,4},{6,7},{7,6},{8,9},{9,8},{10,11... | collective-permute-start | bytes 786440 | tf_op jit(solution)/shard_map/ppermute | solution.py:121
  51.4 20.6 %collective-permute-start.13 = (bf16[16,4096]{1,0:T(8,128)(2,1)S(1)}, bf16[16,4096]{1,0:T(8,128)(2,1)S(1)}, u32[]{:S(2)}, u32[]{:S(2)}) collective-permute-start(bf16[16,4096]{1,0:T(8,128)(2,1)S(1)} %slice.24), channel_id=1, source_target_pairs={{0,4},{1,5},{4,8},{5,9},{8,12},{9,13},{12,14},{13,15},{14,10},{15,... | collective-permute-start | bytes 393224 | tf_op jit(solution)/shard_map/ppermute | solution.py:117
  53.0 19.5 %collective-permute-start.15 = (bf16[16,4096]{1,0:T(8,128)(2,1)S(1)}, bf16[16,4096]{1,0:T(8,128)(2,1)S(1)}, u32[]{:S(2)}, u32[]{:S(2)}) collective-permute-start(bf16[16,4096]{1,0:T(8,128)(2,1)S(1)} %slice.25), channel_id=1, source_target_pairs={{0,2},{1,3},{4,0},{5,1},{8,4},{9,5},{12,8},{13,9},{14,12},{15,13},... | collective-permute-start | bytes 393224 | tf_op jit(solution)/shard_map/ppermute | solution.py:117
  71.3 19.2 %copy-start.24 = (bf16[16,8192]{1,0:T(8,128)(2,1)}, bf16[16,8192]{1,0:T(8,128)(2,1)S(1)}, u32[]{:S(2)}) copy-start(bf16[16,8192]{1,0:T(8,128)(2,1)S(1)} %collective-permute-done.2.refs_3_) | copy-start | bytes 786436
  71.3 19.2 %collective-permute-start.8 = (bf16[16,8192]{1,0:T(8,128)(2,1)S(1)}, bf16[16,8192]{1,0:T(8,128)(2,1)S(1)}, u32[]{:S(2)}, u32[]{:S(2)}) collective-permute-start(bf16[16,8192]{1,0:T(8,128)(2,1)S(1)} %copy-done.23), channel_id=1, source_target_pairs={{0,1},{1,0},{2,3},{3,2},{4,5},{5,4},{6,7},{7,6},{8,9},{9,8},{10,11... | collective-permute-start | bytes 786440 | tf_op jit(solution)/shard_map/ppermute | solution.py:121
  71.4 19.1 %copy-start.25 = (bf16[16,8192]{1,0:T(8,128)(2,1)}, bf16[16,8192]{1,0:T(8,128)(2,1)S(1)}, u32[]{:S(2)}) copy-start(bf16[16,8192]{1,0:T(8,128)(2,1)S(1)} %collective-permute-done.4.refs_5_) | copy-start | bytes 786436
  71.4 19.2 %collective-permute-start.10 = (bf16[16,8192]{1,0:T(8,128)(2,1)S(1)}, bf16[16,8192]{1,0:T(8,128)(2,1)S(1)}, u32[]{:S(2)}, u32[]{:S(2)}) collective-permute-start(bf16[16,8192]{1,0:T(8,128)(2,1)S(1)} %copy-done.13), channel_id=1, source_target_pairs={{0,1},{1,0},{2,3},{3,2},{4,5},{5,4},{6,7},{7,6},{8,9},{9,8},{10,11... | collective-permute-start | bytes 786440 | tf_op jit(solution)/shard_map/ppermute | solution.py:121
  72.0 18.5 %copy-start.26 = (bf16[16,8192]{1,0:T(8,128)(2,1)}, bf16[16,8192]{1,0:T(8,128)(2,1)S(1)}, u32[]{:S(2)}) copy-start(bf16[16,8192]{1,0:T(8,128)(2,1)S(1)} %collective-permute-done.6.refs_7_) | copy-start | bytes 786436
  72.0 18.6 %collective-permute-start.12 = (bf16[16,8192]{1,0:T(8,128)(2,1)S(1)}, bf16[16,8192]{1,0:T(8,128)(2,1)S(1)}, u32[]{:S(2)}, u32[]{:S(2)}) collective-permute-start(bf16[16,8192]{1,0:T(8,128)(2,1)S(1)} %copy-done.15), channel_id=1, source_target_pairs={{0,1},{1,0},{2,3},{3,2},{4,5},{5,4},{6,7},{7,6},{8,9},{9,8},{10,11... | collective-permute-start | bytes 786440 | tf_op jit(solution)/shard_map/ppermute | solution.py:121
  72.1 18.4 %copy-start.30 = (bf16[16,4096]{1,0:T(8,128)(2,1)}, bf16[16,4096]{1,0:T(8,128)(2,1)S(1)}, u32[]{:S(2)}) copy-start(bf16[16,4096]{1,0:T(8,128)(2,1)S(1)} %collective-permute-done.13.refs_14_) | copy-start | bytes 393220
  72.1 18.5 %collective-permute-start.14 = (bf16[16,4096]{1,0:T(8,128)(2,1)S(1)}, bf16[16,4096]{1,0:T(8,128)(2,1)S(1)}, u32[]{:S(2)}, u32[]{:S(2)}) collective-permute-start(bf16[16,4096]{1,0:T(8,128)(2,1)S(1)} %collective-permute-done.13.refs_14_), channel_id=1, source_target_pairs={{0,1},{1,0},{2,3},{3,2},{4,5},{5,4},{6,7},{7,6},{8,9},{9,8},{10,11... | collective-permute-start | bytes 393224 | tf_op jit(solution)/shard_map/ppermute | solution.py:121
  72.5 18.0 %copy-start.31 = (bf16[16,4096]{1,0:T(8,128)(2,1)}, bf16[16,4096]{1,0:T(8,128)(2,1)S(1)}, u32[]{:S(2)}) copy-start(bf16[16,4096]{1,0:T(8,128)(2,1)S(1)} %collective-permute-done.15.refs_16_) | copy-start | bytes 393220
  72.5 18.0 %collective-permute-start.16 = (bf16[16,4096]{1,0:T(8,128)(2,1)S(1)}, bf16[16,4096]{1,0:T(8,128)(2,1)S(1)}, u32[]{:S(2)}, u32[]{:S(2)}) collective-permute-start(bf16[16,4096]{1,0:T(8,128)(2,1)S(1)} %collective-permute-done.15.refs_16_), channel_id=1, source_target_pairs={{0,1},{1,0},{2,3},{3,2},{4,5},{5,4},{6,7},{7,6},{8,9},{9,8},{10,11... | collective-permute-start | bytes 393224 | tf_op jit(solution)/shard_map/ppermute | solution.py:121
  114.0 15.0 %all-to-all-start = ((f32[16,16,256]{2,1,0:T(8,128)}), f32[16,16,256]{2,1,0:T(8,128)S(1)}, u32[]{:S(2)}, u32[]{:S(2)}) async-start(f32[16,16,256]{2,1,0:T(8,128)} %shard_map.106), calls=%async_computation | async-start | bytes 524288 | tf_op jit(solution)/shard_map/all_to_all | solution.py:345
  119.0 1.6 %slice-start.1 = ((bf16[8192,192]{0,1:T(8,128)(2,1)}), bf16[8192,128]{0,1:T(8,128)(2,1)S(1)}, s32[]{:S(2)}) async-start(bf16[8192,192]{0,1:T(8,128)(2,1)} %param.14), calls=%async_computation.3 | async-start | bytes 4194304 | tf_op jit(solution)/shard_map/slice | solution.py:339
  (7 other events, 5.4 us)

commit v2 on v1

--- a/solution.py
+++ b/solution.py
@@ -164,15 +164,17 @@
         part = pl.ds(start, DEPTH)
         a = left[:, part]
         if transposed:
-            total += lax.dot_general(
-                a, right[:, part], (((1,), (1,)), ((), ())), preferred_element_type=jnp.float32
-            )
+            total += last_dot(a, right[:, part])
         else:
             total += jnp.dot(a, right[part, :], preferred_element_type=jnp.float32)
     return total
 
 
-def forward_kernel(places, chips, *refs):
+def last_dot(a, b):
+    return lax.dot_general(a, b, (((1,), (1,)), ((), ())), preferred_element_type=jnp.float32)
+
+
+def tiled_kernel(places, chips, *refs):
     count = len(places)
     blocks, (weight, out, whole, sems) = refs[:count], refs[count:]
 
@@ -183,11 +185,11 @@
     out[...] = deep_dot(whole, weight, False, out.shape[1])
 
 
-def forward(places, chips, blocks, weight, tile):
+def tiled_forward(places, chips, blocks, weight, tile):
     rows = blocks[0].shape[0] * chips * 2
     depth, width = weight.shape
     return pl.pallas_call(
-        functools.partial(forward_kernel, places, chips),
+        functools.partial(tiled_kernel, places, chips),
         grid=(width // tile,),
         out_shape=jax.ShapeDtypeStruct((rows, width), jnp.float32),
         in_specs=[pl.BlockSpec(memory_space=pl.ANY)] * len(blocks)
@@ -204,6 +206,53 @@
     )(*blocks, weight)
 
 
+def deep_kernel(places, chips, *refs):
+    count = len(places)
+    blocks, (weight, proj, out, inputs, whole, sems) = refs[:count], refs[count:]
+    step = pl.program_id(0)
+
+    @pl.when(step == 0)
+    def _():
+        assemble(places, chips, blocks, whole, sems)
+        out[...] = jnp.zeros_like(out)
+        inputs[...] = jnp.zeros_like(inputs)
+
+    depth = weight.shape[0]
+    x = whole[:, pl.ds(pl.multiple_of(step * depth, depth), depth)]
+    out[...] += jnp.dot(x, weight[...], preferred_element_type=jnp.float32)
+    inputs[...] += last_dot(x, proj[: 2 * R, :])
+
+
+def deep_forward(places, chips, blocks, weight, proj, depth_tile):
+    rows = blocks[0].shape[0] * chips * 2
+    depth, width = weight.shape
+    return pl.pallas_call(
+        functools.partial(deep_kernel, places, chips),
+        grid=(depth // depth_tile,),
+        out_shape=(
+            jax.ShapeDtypeStruct((rows, width), jnp.float32),
+            jax.ShapeDtypeStruct((rows, 2 * R), jnp.float32),
+        ),
+        in_specs=[pl.BlockSpec(memory_space=pl.ANY)] * len(blocks)
+        + [
+            pl.BlockSpec((depth_tile, width), lambda k: (k, 0)),
+            pl.BlockSpec((3 * R, depth_tile), lambda k: (0, k)),
+        ],
+        out_specs=(
+            pl.BlockSpec((rows, width), lambda k: (0, 0)),
+            pl.BlockSpec((rows, 2 * R), lambda k: (0, 0)),
+        ),
+        scratch_shapes=[
+            pltpu.VMEM((rows, depth), jnp.bfloat16),
+            pltpu.SemaphoreType.DMA((len(blocks),)),
+        ],
+        compiler_params=pltpu.CompilerParams(vmem_limit_bytes=VMEM),
+        cost_estimate=pl.CostEstimate(
+            flops=2 * rows * depth * width, bytes_accessed=2 * depth * width, transcendentals=0
+        ),
+    )(*blocks, weight, proj)
+
+
 def membership(ids, examples):
     rows = lax.broadcasted_iota(jnp.int32, (examples, ids.shape[1]), 0)
     return (jnp.broadcast_to(ids, rows.shape) == rows).astype(jnp.float32)
@@ -227,30 +276,31 @@
     def _():
         assemble(places, chips, blocks, whole, sems)
         sums[...] = jnp.zeros_like(sums)
-        columns = deep_dot(whole, proj, False, R).T
+        columns = jnp.zeros((R, whole.shape[0]), jnp.float32)
+        for start in range(0, whole.shape[1], DEPTH):
+            part = pl.ds(start, DEPTH)
+            columns += last_dot(proj[2 * R :, part], whole[:, part])
         for lanes in range(flipped.shape[0]):
             flipped[lanes] = columns[:, lanes * 128 : (lanes + 1) * 128]
 
     hidden_grad = deep_dot(whole, weight, True, gate.shape[1])
     hidden, gate_grad, up_grad = pointwise(gate[...], up[...], hidden_grad)
     for m, value in enumerate((gate_grad, up_grad, hidden)):
-        sums[m] += jnp.dot(
-            value, proj_ff[:, m * R : (m + 1) * R], preferred_element_type=jnp.float32
-        )
+        sums[m * R : (m + 1) * R, :] += last_dot(proj_ff[m * R : (m + 1) * R, :], value)
 
     @pl.when(step == pl.num_programs(0) - 1)
     def _():
         for m in range(2):
-            columns = sums[m].T
             for p in range(hid):
-                send[p, m * shares : (m + 1) * shares, :] = columns[p * shares : (p + 1) * shares]
+                own = sums[m * R + p * shares : m * R + (p + 1) * shares, :]
+                send[p, m * shares : (m + 1) * shares, :] = own
         member = membership(ids[...], examples)
         total_rows = member.shape[1]
         for j in range(shares):
             every = pl.ds(j, hid, shares)
             own = jnp.concatenate([flipped[k, every, :] for k in range(flipped.shape[0])], axis=1)
             left = (own[:, None, :] * member[None, :, :]).reshape(hid * examples, total_rows)
-            product = exact_dot(left, sums[2], ((1,), (0,)))
+            product = exact_dot(left, sums[2 * R :, :], ((1,), (1,)))
             send[:, 2 * shares :, j * R : (j + 1) * R] = product.reshape(hid, examples, R)
 
 
@@ -268,14 +318,14 @@
             pl.BlockSpec((tile, depth), lambda n: (n, 0)),
             pl.BlockSpec((rows, tile), lambda n: (0, n)),
             pl.BlockSpec((rows, tile), lambda n: (0, n)),
-            pl.BlockSpec((depth, R), lambda n: (0, 0)),
-            pl.BlockSpec((tile, 3 * R), lambda n: (n, 0)),
+            pl.BlockSpec((3 * R, depth), lambda n: (0, 0)),
+            pl.BlockSpec((3 * R, tile), lambda n: (0, n)),
             pl.BlockSpec((1, rows), lambda n: (0, 0)),
         ],
         out_specs=pl.BlockSpec((hid, 2 * shares + examples, rows), lambda n: (0, 0, 0)),
         scratch_shapes=[
             pltpu.VMEM((rows, depth), jnp.bfloat16),
-            pltpu.VMEM((3, rows, R), jnp.float32),
+            pltpu.VMEM((3 * R, rows), jnp.float32),
             pltpu.VMEM((rows // 128, R, 128), jnp.float32),
             pltpu.SemaphoreType.DMA((len(blocks),)),
         ],
@@ -336,11 +386,10 @@
     ids = example_ids[None, :]
     places, token_blocks = gather_blocks(tokens, chips)
     _, grad_blocks = gather_blocks(out_grad, chips)
-    inputs = forward(places, chips, token_blocks, proj_d[:, : 2 * R], 2 * R)
-    gate = forward(places, chips, token_blocks, gate_weight, TILE)
-    up = forward(places, chips, token_blocks, up_weight, TILE)
+    gate, inputs = deep_forward(places, chips, token_blocks, gate_weight, proj_d.T, 1024)
+    up = tiled_forward(places, chips, token_blocks, up_weight, up_weight.shape[1] // 2)
     send = backward(
-        places, chips, grad_blocks, down_weight, gate, up, proj_d[:, 2 * R :], proj_ff, ids, TILE
+        places, chips, grad_blocks, down_weight, gate, up, proj_d.T, proj_ff.T, ids, TILE
     )
     received = lax.all_to_all(send, "hid", 0, 0)
     features, partial = finish(received, inputs, ids, test_features)

time: 148 us -> 143 us (0.966)
  blocking collectives: 13.7 us -> 26.5 us
  local copies, waits for them, and re-layouts: 11.8 us -> 1.11 us
  starting transfers between devices: 25.7 us -> 20.3 us
    all_to_all x0 -> x1, blocking collectives: none -> 15.1 us  [local_ring(): received = lax.all_to_all(send, 'hid', 0, 0)]
    unnamed x71 -> x68, local copies, waits for them, and re-layouts: 8.34 us -> 1.07 us
    all_to_all x1 -> x0, starting transfers between devices: 4.97 us -> none  [local_ring(): received = lax.all_to_all(send, 'hid', 0, 0)]
    all_to_all x1, blocking collectives: 13.7 us -> 11.4 us  [local_ring(): scores = jnp.sum(lax.all_to_all(partial, 'hid', 0, 0), axis=0)]
    slice x4 -> x0, local copies, waits for them, and re-layouts: 1.6 us -> none  [the longest x2 1.59 us: local_ring(): inputs = forward(places, chips, token_blocks, proj_d[:, :2 * R], 2 * R)]
    pallas_call x3 -> x2, Pallas kernels: 41.4 us -> 40.1 us  [the longest x1 20.8 us: tiled_forward(): pl.pallas_call(functools.partial(tiled_kernel, places, chips), grid=(widt...]
  transfers between devices with their start and end apart: 35 -> 34, of which waited for: 11 -> 11; matrix products, arithmetic and copies ran while one was open for 6% -> 0% of each run, Pallas kernels for 28% -> 28%
where the time goes in v2:
time: 143 us
  Pallas kernels  65.6 us (46%)
  waiting for transfers between devices  27.8 us (19%)
  blocking collectives  26.5 us (19%)
  starting transfers between devices  20.3 us (14%)
    ppermute x16, waiting for transfers between devices, ring_step(): return lax.ppermute(block, 'hid', pairs)  27.1 us
    pallas_call x1, Pallas kernels, backward(): pl.pallas_call(functools.partial(backward_kernel, places, chips, examples...  22.6 us
    pallas_call x1, Pallas kernels, tiled_forward(): pl.pallas_call(functools.partial(tiled_kernel, places, chips), grid=(widt...  20.8 us
    pallas_call x1, Pallas kernels, deep_forward(): pl.pallas_call(functools.partial(deep_kernel, places, chips), grid=(depth...  19.3 us
    ppermute x16, starting transfers between devices, ring_step(): return lax.ppermute(block, 'hid', pairs)  17.7 us
    all_to_all x1, blocking collectives, local_ring(): received = lax.all_to_all(send, 'hid', 0, 0)  15.1 us
    all_to_all x1, blocking collectives, local_ring(): scores = jnp.sum(lax.all_to_all(partial, 'hid', 0, 0), axis=0)  11.4 us
  transfers between devices with their start and end apart: 34, of which 11 were waited for; matrix products, arithmetic and copies ran while one was open for 0% of the time, Pallas kernels for 28%

profile of v2, /device:TPU:0, one launch (start us, length us, event | category | flops | bytes accessed | tf_op | source)
XLA Modules:
  0.0 142.9 jit_solution(6130342868786522088)
XLA Ops:
  0.6 3.1 %collective-permute-start.18 = (bf16[16,8192]{1,0:T(8,128)(2,1)}, bf16[16,8192]{1,0:T(8,128)(2,1)S(1)}, u32[]{:S(2)}, u32[]{:S(2)}) collective-permute-start(bf16[16,8192]{1,0:T(8,128)(2,1)} %refs_0_.4), channel_id=1, source_target_pairs={{0,4},{1,5},{4,8},{5,9},{8,12},{9,13},{12,14},{13,15},{14,10},{15,... | collective-permute-start | bytes 786440 | tf_op jit(solution)/shard_map/ppermute | solution.py:117
  3.7 0.0 collective-permute-start.20
  3.7 0.0 collective-permute-start.17
  3.7 2.0 %collective-permute-start.1 = (bf16[16,8192]{1,0:T(8,128)(2,1)}, bf16[16,8192]{1,0:T(8,128)(2,1)S(1)}, u32[]{:S(2)}, u32[]{:S(2)}) collective-permute-start(bf16[16,8192]{1,0:T(8,128)(2,1)} %refs_0_.5), channel_id=1, source_target_pairs={{0,4},{1,5},{4,8},{5,9},{8,12},{9,13},{12,14},{13,15},{14,10},{15,... | collective-permute-start | bytes 786440 | tf_op jit(solution)/shard_map/ppermute | solution.py:117
  5.7 0.0 collective-permute-start.3
  5.7 5.2 %collective-permute-done.18.refs_2_ = bf16[16,8192]{1,0:T(8,128)(2,1)S(1)} collective-permute-done((bf16[16,8192]{1,0:T(8,128)(2,1)}, bf16[16,8192]{1,0:T(8,128)(2,1)S(1)}, u32[]{:S(2)}, u32[]{:S(2)}) %collective-permute-start.18) | collective-permute-done | bytes 262176 | tf_op jit(solution)/shard_map/ppermute | solution.py:117
  11.0 2.1 %collective-permute-start.22 = (bf16[16,8192]{1,0:T(8,128)(2,1)S(1)}, bf16[16,8192]{1,0:T(8,128)(2,1)S(1)}, u32[]{:S(2)}, u32[]{:S(2)}) collective-permute-start(bf16[16,8192]{1,0:T(8,128)(2,1)S(1)} %collective-permute-done.18.refs_2_), channel_id=1, source_target_pairs={{0,4},{1,5},{4,8},{5,9},{8,12},{9,13},{12,14},{13,15},{14,10},{15,... | collective-permute-start | bytes 786440 | tf_op jit(solution)/shard_map/ppermute | solution.py:117
  13.1 0.0 collective-permute-done.20.refs_4_
  13.1 0.0 collective-permute-start.24
  13.2 0.0 collective-permute-done.17.refs_1_
  13.2 0.1 collective-permute-start
  13.2 3.3 %collective-permute-done.1.refs_2_ = bf16[16,8192]{1,0:T(8,128)(2,1)S(1)} collective-permute-done((bf16[16,8192]{1,0:T(8,128)(2,1)}, bf16[16,8192]{1,0:T(8,128)(2,1)S(1)}, u32[]{:S(2)}, u32[]{:S(2)}) %collective-permute-start.1) | collective-permute-done | bytes 262176 | tf_op jit(solution)/shard_map/ppermute | solution.py:117
  16.6 2.1 %collective-permute-start.5 = (bf16[16,8192]{1,0:T(8,128)(2,1)S(1)}, bf16[16,8192]{1,0:T(8,128)(2,1)S(1)}, u32[]{:S(2)}, u32[]{:S(2)}) collective-permute-start(bf16[16,8192]{1,0:T(8,128)(2,1)S(1)} %collective-permute-done.1.refs_2_), channel_id=1, source_target_pairs={{0,4},{1,5},{4,8},{5,9},{8,12},{9,13},{12,14},{13,15},{14,10},{15,... | collective-permute-start | bytes 786440 | tf_op jit(solution)/shard_map/ppermute | solution.py:117
  18.7 0.0 collective-permute-done.3.refs_4_
  18.8 0.0 collective-permute-start.7
  18.8 3.4 %collective-permute-done.22.refs_6_ = bf16[16,8192]{1,0:T(8,128)(2,1)S(1)} collective-permute-done((bf16[16,8192]{1,0:T(8,128)(2,1)S(1)}, bf16[16,8192]{1,0:T(8,128)(2,1)S(1)}, u32[]{:S(2)}, u32[]{:S(2)}) %collective-permute-start.22) | collective-permute-done | bytes 262176 | tf_op jit(solution)/shard_map/ppermute | solution.py:117
  22.2 2.1 %collective-permute-start.26 = (bf16[16,8192]{1,0:T(8,128)(2,1)S(1)}, bf16[16,8192]{1,0:T(8,128)(2,1)S(1)}, u32[]{:S(2)}, u32[]{:S(2)}) collective-permute-start(bf16[16,8192]{1,0:T(8,128)(2,1)S(1)} %collective-permute-done.22.refs_6_), channel_id=1, source_target_pairs={{0,4},{1,5},{4,8},{5,9},{8,12},{9,13},{12,14},{13,15},{14,10},{15,... | collective-permute-start | bytes 786440 | tf_op jit(solution)/shard_map/ppermute | solution.py:117
  24.3 0.0 collective-permute-done.24.refs_8_
  24.4 0.0 collective-permute-done.refs_1_
  24.4 0.1 collective-permute-start.19
  24.5 3.3 %collective-permute-done.5.refs_6_ = bf16[16,8192]{1,0:T(8,128)(2,1)S(1)} collective-permute-done((bf16[16,8192]{1,0:T(8,128)(2,1)S(1)}, bf16[16,8192]{1,0:T(8,128)(2,1)S(1)}, u32[]{:S(2)}, u32[]{:S(2)}) %collective-permute-start.5) | collective-permute-done | bytes 262176 | tf_op jit(solution)/shard_map/ppermute | solution.py:117
  27.8 0.0 collective-permute-start.21
  27.8 2.2 %collective-permute-done.7.refs_8_ = bf16[16,8192]{1,0:T(8,128)(2,1)S(1)} collective-permute-done((bf16[16,8192]{1,0:T(8,128)(2,1)S(1)}, bf16[16,8192]{1,0:T(8,128)(2,1)S(1)}, u32[]{:S(2)}, u32[]{:S(2)}) %collective-permute-start.7) | collective-permute-done | bytes 262176 | tf_op jit(solution)/shard_map/ppermute | solution.py:117
  30.0 0.0 collective-permute-start.23
  30.0 2.6 %collective-permute-done.26.refs_10_ = bf16[16,8192]{1,0:T(8,128)(2,1)S(1)} collective-permute-done((bf16[16,8192]{1,0:T(8,128)(2,1)S(1)}, bf16[16,8192]{1,0:T(8,128)(2,1)S(1)}, u32[]{:S(2)}, u32[]{:S(2)}) %collective-permute-start.26) | collective-permute-done | bytes 262176 | tf_op jit(solution)/shard_map/ppermute | solution.py:117
  32.6 1.8 %collective-permute-start.9 = (bf16[16,8192]{1,0:T(8,128)(2,1)S(1)}, bf16[16,8192]{1,0:T(8,128)(2,1)S(1)}, u32[]{:S(2)}, u32[]{:S(2)}) collective-permute-start(bf16[16,8192]{1,0:T(8,128)(2,1)S(1)} %collective-permute-done.5.refs_6_), channel_id=1, source_target_pairs={{0,4},{1,5},{4,8},{5,9},{8,12},{9,13},{12,14},{13,15},{14,10},{15,... | collective-permute-start | bytes 786440 | tf_op jit(solution)/shard_map/ppermute | solution.py:117
  34.4 0.0 collective-permute-done.28.refs_12_
  34.4 0.2 collective-permute-start.11
  34.7 0.0 collective-permute-done.19.refs_3_
  34.7 0.1 collective-permute-start.25
  34.8 1.9 %collective-permute-start.30 = (bf16[16,4096]{1,0:T(8,128)(2,1)S(1)}, bf16[16,4096]{1,0:T(8,128)(2,1)S(1)}, u32[]{:S(2)}, u32[]{:S(2)}) collective-permute-start(bf16[16,4096]{1,0:T(8,128)(2,1)S(1)} %slice.18), channel_id=1, source_target_pairs={{0,4},{1,5},{4,8},{5,9},{8,12},{9,13},{12,14},{13,15},{14,10},{15,... | collective-permute-start | bytes 393224 | tf_op jit(solution)/shard_map/ppermute | solution.py:117
  36.7 0.2 collective-permute-start.32
  36.9 4.6 %collective-permute-done.9.refs_10_ = bf16[16,8192]{1,0:T(8,128)(2,1)S(1)} collective-permute-done((bf16[16,8192]{1,0:T(8,128)(2,1)S(1)}, bf16[16,8192]{1,0:T(8,128)(2,1)S(1)}, u32[]{:S(2)}, u32[]{:S(2)}) %collective-permute-start.9) | collective-permute-done | bytes 262176 | tf_op jit(solution)/shard_map/ppermute | solution.py:117
  41.5 1.2 collective-permute-done.11.refs_12_
  42.7 0.2 collective-permute-done.30.refs_14_
  42.9 0.3 collective-permute-start.31
  43.3 0.9 collective-permute-done.32.refs_16_
  44.1 0.0 collective-permute-start.33
  44.2 0.0 collective-permute-done.25.refs_9_
  44.2 0.6 collective-permute-start.2
  44.8 0.1 collective-permute-start.4
  44.9 0.6 collective-permute-done.33.refs_17_
  45.5 0.1 collective-permute-start.6
  45.6 0.0 collective-permute-done.27.refs_11_
  45.7 1.6 %collective-permute-start.13 = (bf16[16,4096]{1,0:T(8,128)(2,1)S(1)}, bf16[16,4096]{1,0:T(8,128)(2,1)S(1)}, u32[]{:S(2)}, u32[]{:S(2)}) collective-permute-start(bf16[16,4096]{1,0:T(8,128)(2,1)S(1)} %slice.16), channel_id=1, source_target_pairs={{0,4},{1,5},{4,8},{5,9},{8,12},{9,13},{12,14},{13,15},{14,10},{15,... | collective-permute-start | bytes 393224 | tf_op jit(solution)/shard_map/ppermute | solution.py:117
  47.2 0.4 collective-permute-start.15
  47.8 0.1 copy-done.12
  48.0 20.8 %shard_map.105.refs_20_ = f32[256,1792]{1,0:T(8,128)} custom-call(bf16[16,8192]{1,0:T(8,128)(2,1)} %refs_0_.4, bf16[16,8192]{1,0:T(8,128)(2,1)} %copy-done.4, bf16[16,8192]{1,0:T(8,128)(2,1)} %copy-done.2, bf16[16,8192]{1,0:T(8,128)(2,1)} %copy-done.7, bf16[16,8192]{1,0:T(8,128)(2,1)} %copy-done.3, bf16[16,8192]{1,0:T(8,128)(2,1)} %copy-done.8, ...), custom_call_target="tpu_custom_call" | custom-call | flops 7516192768 | bytes 29360128 | tf_op jit(solution)/shard_map/pallas_call | solution.py:191
  68.8 0.1 collective-permute-start.8
  69.0 0.4 collective-permute-start.10
  69.4 0.1 collective-permute-start.12
  69.5 0.4 collective-permute-start.14
  69.9 0.1 collective-permute-start.16
  70.0 19.3 %shard_map.104 = (f32[256,1792]{1,0:T(8,128)}, f32[256,128]{1,0:T(8,128)}) custom-call(bf16[16,8192]{1,0:T(8,128)(2,1)} %refs_0_.4, bf16[16,8192]{1,0:T(8,128)(2,1)} %copy-done.4, bf16[16,8192]{1,0:T(8,128)(2,1)} %copy-done.2, bf16[16,8192]{1,0:T(8,128)(2,1)} %copy-done.7, bf16[16,8192]{1,0:T(8,128)(2,1)} %copy-done.3, bf16[16,8192]{1,0:T(8,128)(2,1)} %copy-done.8, ...), custom_call_target="tpu_custom_call" | custom-call | flops 7516192768 | bytes 29360128 | tf_op jit(solution)/shard_map/pallas_call | solution.py:229
  89.6 0.5 copy-done.27
  90.0 0.0 copy-done.32
  90.1 0.1 copy-done.33
  90.2 0.1 copy-done.28
  90.3 0.1 copy-done.29
  90.4 22.6 %shard_map.106 = f32[16,16,256]{2,1,0:T(8,128)} custom-call(bf16[16,8192]{1,0:T(8,128)(2,1)} %refs_0_.5, bf16[16,8192]{1,0:T(8,128)(2,1)} %copy-done.21, bf16[16,8192]{1,0:T(8,128)(2,1)} %copy-done.19, bf16[16,8192]{1,0:T(8,128)(2,1)} %copy-done.24, bf16[16,8192]{1,0:T(8,128)(2,1)} %copy-done.20, bf16[16,8192]{1,0:T(8,128)(2,1)} %copy-done.25, ...), custom_call_target="tpu_custom_call" | custom-call | flops 7516192768 | bytes 29360128 | tf_op jit(solution)/shard_map/pallas_call | solution.py:312
  113.0 15.1 %all_to_all.10.received = f32[16,16,256]{2,1,0:T(8,128)} all-to-all(f32[16,16,256]{2,1,0:T(8,128)} %shard_map.106), channel_id=1, replica_groups=mesh['groups'=2,'hid'=16,'mod'=1] {'hid'}, dimensions={0} | all-to-all | bytes 524288 | tf_op jit(solution)/shard_map/all_to_all | solution.py:394
  128.1 2.8 %shard_map.107 = (f32[8,768]{1,0:T(8,128)}, f32[16,8,256]{2,1,0:T(8,128)}) custom-call(f32[16,16,256]{2,1,0:T(8,128)} %all_to_all.10.received, f32[256,128]{1,0:T(8,128)} %get-tuple-element.7.inputs, s32[1,256]{1,0:T(1,128)} %bitcast.7, bf16[256,768]{1,0:T(8,128)(2,1)} %tests.1), custom_call_target="tpu_custom_call" | custom-call | tf_op jit(solution)/shard_map/pallas_call | solution.py:362
  130.9 11.4 %all_to_all.11 = f32[16,8,256]{2,1,0:T(8,128)S(1)} all-to-all(f32[16,8,256]{2,1,0:T(8,128)} %get-tuple-element.9), channel_id=1, replica_groups=mesh['groups'=2,'hid'=16,'mod'=1] {'hid'}, dimensions={0} | all-to-all | bytes 262144 | tf_op jit(solution)/shard_map/all_to_all | solution.py:396
  142.3 0.6 reduce_sum.9
  (83 shorter events, 0.2 us)
Async XLA Ops:
  0.6 10.3 %collective-permute-start.18 = (bf16[16,8192]{1,0:T(8,128)(2,1)}, bf16[16,8192]{1,0:T(8,128)(2,1)S(1)}, u32[]{:S(2)}, u32[]{:S(2)}) collective-permute-start(bf16[16,8192]{1,0:T(8,128)(2,1)} %refs_0_.4), channel_id=1, source_target_pairs={{0,4},{1,5},{4,8},{5,9},{8,12},{9,13},{12,14},{13,15},{14,10},{15,... | collective-permute-start | bytes 786440 | tf_op jit(solution)/shard_map/ppermute | solution.py:117
  3.7 9.4 %collective-permute-start.20 = (bf16[16,8192]{1,0:T(8,128)(2,1)}, bf16[16,8192]{1,0:T(8,128)(2,1)S(1)}, u32[]{:S(2)}, u32[]{:S(2)}) collective-permute-start(bf16[16,8192]{1,0:T(8,128)(2,1)} %refs_0_.4), channel_id=1, source_target_pairs={{0,2},{1,3},{4,0},{5,1},{8,4},{9,5},{12,8},{13,9},{14,12},{15,13},... | collective-permute-start | bytes 786440 | tf_op jit(solution)/shard_map/ppermute | solution.py:117
  3.7 9.4 %collective-permute-start.17 = (bf16[16,8192]{1,0:T(8,128)(2,1)}, bf16[16,8192]{1,0:T(8,128)(2,1)S(1)}, u32[]{:S(2)}, u32[]{:S(2)}) collective-permute-start(bf16[16,8192]{1,0:T(8,128)(2,1)} %refs_0_.4), channel_id=1, source_target_pairs={{0,1},{1,0},{2,3},{3,2},{4,5},{5,4},{6,7},{7,6},{8,9},{9,8},{10,11... | collective-permute-start | bytes 786440 | tf_op jit(solution)/shard_map/ppermute | solution.py:121
  3.7 12.9 %collective-permute-start.1 = (bf16[16,8192]{1,0:T(8,128)(2,1)}, bf16[16,8192]{1,0:T(8,128)(2,1)S(1)}, u32[]{:S(2)}, u32[]{:S(2)}) collective-permute-start(bf16[16,8192]{1,0:T(8,128)(2,1)} %refs_0_.5), channel_id=1, source_target_pairs={{0,4},{1,5},{4,8},{5,9},{8,12},{9,13},{12,14},{13,15},{14,10},{15,... | collective-permute-start | bytes 786440 | tf_op jit(solution)/shard_map/ppermute | solution.py:117
  5.7 13.0 %collective-permute-start.3 = (bf16[16,8192]{1,0:T(8,128)(2,1)}, bf16[16,8192]{1,0:T(8,128)(2,1)S(1)}, u32[]{:S(2)}, u32[]{:S(2)}) collective-permute-start(bf16[16,8192]{1,0:T(8,128)(2,1)} %refs_0_.5), channel_id=1, source_target_pairs={{0,2},{1,3},{4,0},{5,1},{8,4},{9,5},{12,8},{13,9},{14,12},{15,13},... | collective-permute-start | bytes 786440 | tf_op jit(solution)/shard_map/ppermute | solution.py:117
  11.0 36.7 %copy-start.2 = (bf16[16,8192]{1,0:T(8,128)(2,1)}, bf16[16,8192]{1,0:T(8,128)(2,1)S(1)}, u32[]{:S(2)}) copy-start(bf16[16,8192]{1,0:T(8,128)(2,1)S(1)} %collective-permute-done.18.refs_2_) | copy-start | bytes 786436
  11.0 11.2 %collective-permute-start.22 = (bf16[16,8192]{1,0:T(8,128)(2,1)S(1)}, bf16[16,8192]{1,0:T(8,128)(2,1)S(1)}, u32[]{:S(2)}, u32[]{:S(2)}) collective-permute-start(bf16[16,8192]{1,0:T(8,128)(2,1)S(1)} %collective-permute-done.18.refs_2_), channel_id=1, source_target_pairs={{0,4},{1,5},{4,8},{5,9},{8,12},{9,13},{12,14},{13,15},{14,10},{15,... | collective-permute-start | bytes 786440 | tf_op jit(solution)/shard_map/ppermute | solution.py:117
  13.1 34.6 %copy-start.3 = (bf16[16,8192]{1,0:T(8,128)(2,1)}, bf16[16,8192]{1,0:T(8,128)(2,1)S(1)}, u32[]{:S(2)}) copy-start(bf16[16,8192]{1,0:T(8,128)(2,1)S(1)} %collective-permute-done.20.refs_4_) | copy-start | bytes 786436
  13.1 11.2 %collective-permute-start.24 = (bf16[16,8192]{1,0:T(8,128)(2,1)S(1)}, bf16[16,8192]{1,0:T(8,128)(2,1)S(1)}, u32[]{:S(2)}, u32[]{:S(2)}) collective-permute-start(bf16[16,8192]{1,0:T(8,128)(2,1)S(1)} %collective-permute-done.20.refs_4_), channel_id=1, source_target_pairs={{0,2},{1,3},{4,0},{5,1},{8,4},{9,5},{12,8},{13,9},{14,12},{15,13},... | collective-permute-start | bytes 786440 | tf_op jit(solution)/shard_map/ppermute | solution.py:117
  13.2 34.5 %copy-start.4 = (bf16[16,8192]{1,0:T(8,128)(2,1)}, bf16[16,8192]{1,0:T(8,128)(2,1)S(1)}, u32[]{:S(2)}) copy-start(bf16[16,8192]{1,0:T(8,128)(2,1)S(1)} %collective-permute-done.17.refs_1_) | copy-start | bytes 786436
  13.2 11.2 %collective-permute-start = (bf16[16,8192]{1,0:T(8,128)(2,1)}, bf16[16,8192]{1,0:T(8,128)(2,1)S(1)}, u32[]{:S(2)}, u32[]{:S(2)}) collective-permute-start(bf16[16,8192]{1,0:T(8,128)(2,1)} %refs_0_.5), channel_id=1, source_target_pairs={{0,1},{1,0},{2,3},{3,2},{4,5},{5,4},{6,7},{7,6},{8,9},{9,8},{10,11... | collective-permute-start | bytes 786440 | tf_op jit(solution)/shard_map/ppermute | solution.py:121
  16.6 72.8 %copy-start.19 = (bf16[16,8192]{1,0:T(8,128)(2,1)}, bf16[16,8192]{1,0:T(8,128)(2,1)S(1)}, u32[]{:S(2)}) copy-start(bf16[16,8192]{1,0:T(8,128)(2,1)S(1)} %collective-permute-done.1.refs_2_) | copy-start | bytes 786436
  16.6 11.2 %collective-permute-start.5 = (bf16[16,8192]{1,0:T(8,128)(2,1)S(1)}, bf16[16,8192]{1,0:T(8,128)(2,1)S(1)}, u32[]{:S(2)}, u32[]{:S(2)}) collective-permute-start(bf16[16,8192]{1,0:T(8,128)(2,1)S(1)} %collective-permute-done.1.refs_2_), channel_id=1, source_target_pairs={{0,4},{1,5},{4,8},{5,9},{8,12},{9,13},{12,14},{13,15},{14,10},{15,... | collective-permute-start | bytes 786440 | tf_op jit(solution)/shard_map/ppermute | solution.py:117
  18.8 70.7 %copy-start.20 = (bf16[16,8192]{1,0:T(8,128)(2,1)}, bf16[16,8192]{1,0:T(8,128)(2,1)S(1)}, u32[]{:S(2)}) copy-start(bf16[16,8192]{1,0:T(8,128)(2,1)S(1)} %collective-permute-done.3.refs_4_) | copy-start | bytes 786436
  18.8 11.2 %collective-permute-start.7 = (bf16[16,8192]{1,0:T(8,128)(2,1)S(1)}, bf16[16,8192]{1,0:T(8,128)(2,1)S(1)}, u32[]{:S(2)}, u32[]{:S(2)}) collective-permute-start(bf16[16,8192]{1,0:T(8,128)(2,1)S(1)} %collective-permute-done.3.refs_4_), channel_id=1, source_target_pairs={{0,2},{1,3},{4,0},{5,1},{8,4},{9,5},{12,8},{13,9},{14,12},{15,13},... | collective-permute-start | bytes 786440 | tf_op jit(solution)/shard_map/ppermute | solution.py:117
  22.2 25.5 %copy-start.5 = (bf16[16,8192]{1,0:T(8,128)(2,1)}, bf16[16,8192]{1,0:T(8,128)(2,1)S(1)}, u32[]{:S(2)}) copy-start(bf16[16,8192]{1,0:T(8,128)(2,1)S(1)} %collective-permute-done.22.refs_6_) | copy-start | bytes 786436
  22.2 10.4 %collective-permute-start.26 = (bf16[16,8192]{1,0:T(8,128)(2,1)S(1)}, bf16[16,8192]{1,0:T(8,128)(2,1)S(1)}, u32[]{:S(2)}, u32[]{:S(2)}) collective-permute-start(bf16[16,8192]{1,0:T(8,128)(2,1)S(1)} %collective-permute-done.22.refs_6_), channel_id=1, source_target_pairs={{0,4},{1,5},{4,8},{5,9},{8,12},{9,13},{12,14},{13,15},{14,10},{15,... | collective-permute-start | bytes 786440 | tf_op jit(solution)/shard_map/ppermute | solution.py:117
  24.4 23.3 %copy-start.6 = (bf16[16,8192]{1,0:T(8,128)(2,1)}, bf16[16,8192]{1,0:T(8,128)(2,1)S(1)}, u32[]{:S(2)}) copy-start(bf16[16,8192]{1,0:T(8,128)(2,1)S(1)} %collective-permute-done.24.refs_8_) | copy-start | bytes 786436
  24.4 10.1 %collective-permute-start.28 = (bf16[16,8192]{1,0:T(8,128)(2,1)S(1)}, bf16[16,8192]{1,0:T(8,128)(2,1)S(1)}, u32[]{:S(2)}, u32[]{:S(2)}) collective-permute-start(bf16[16,8192]{1,0:T(8,128)(2,1)S(1)} %collective-permute-done.24.refs_8_), channel_id=1, source_target_pairs={{0,2},{1,3},{4,0},{5,1},{8,4},{9,5},{12,8},{13,9},{14,12},{15,13},... | collective-permute-start | bytes 786440 | tf_op jit(solution)/shard_map/ppermute | solution.py:117
  24.4 65.1 %copy-start.21 = (bf16[16,8192]{1,0:T(8,128)(2,1)}, bf16[16,8192]{1,0:T(8,128)(2,1)S(1)}, u32[]{:S(2)}) copy-start(bf16[16,8192]{1,0:T(8,128)(2,1)S(1)} %collective-permute-done.refs_1_) | copy-start | bytes 786436
  24.4 10.3 %collective-permute-start.19 = (bf16[16,8192]{1,0:T(8,128)(2,1)S(1)}, bf16[16,8192]{1,0:T(8,128)(2,1)S(1)}, u32[]{:S(2)}, u32[]{:S(2)}) collective-permute-start(bf16[16,8192]{1,0:T(8,128)(2,1)S(1)} %collective-permute-done.18.refs_2_), channel_id=1, source_target_pairs={{0,1},{1,0},{2,3},{3,2},{4,5},{5,4},{6,7},{7,6},{8,9},{9,8},{10,11... | collective-permute-start | bytes 786440 | tf_op jit(solution)/shard_map/ppermute | solution.py:121
  27.8 61.6 %copy-start.22 = (bf16[16,8192]{1,0:T(8,128)(2,1)}, bf16[16,8192]{1,0:T(8,128)(2,1)S(1)}, u32[]{:S(2)}) copy-start(bf16[16,8192]{1,0:T(8,128)(2,1)S(1)} %collective-permute-done.5.refs_6_) | copy-start | bytes 786436
  27.8 7.0 %collective-permute-start.21 = (bf16[16,8192]{1,0:T(8,128)(2,1)S(1)}, bf16[16,8192]{1,0:T(8,128)(2,1)S(1)}, u32[]{:S(2)}, u32[]{:S(2)}) collective-permute-start(bf16[16,8192]{1,0:T(8,128)(2,1)S(1)} %collective-permute-done.20.refs_4_), channel_id=1, source_target_pairs={{0,1},{1,0},{2,3},{3,2},{4,5},{5,4},{6,7},{7,6},{8,9},{9,8},{10,11... | collective-permute-start | bytes 786440 | tf_op jit(solution)/shard_map/ppermute | solution.py:121
  30.0 59.5 %copy-start.23 = (bf16[16,8192]{1,0:T(8,128)(2,1)}, bf16[16,8192]{1,0:T(8,128)(2,1)S(1)}, u32[]{:S(2)}) copy-start(bf16[16,8192]{1,0:T(8,128)(2,1)S(1)} %collective-permute-done.7.refs_8_) | copy-start | bytes 786436
  30.0 6.7 %collective-permute-start.23 = (bf16[16,8192]{1,0:T(8,128)(2,1)S(1)}, bf16[16,8192]{1,0:T(8,128)(2,1)S(1)}, u32[]{:S(2)}, u32[]{:S(2)}) collective-permute-start(bf16[16,8192]{1,0:T(8,128)(2,1)S(1)} %collective-permute-done.22.refs_6_), channel_id=1, source_target_pairs={{0,1},{1,0},{2,3},{3,2},{4,5},{5,4},{6,7},{7,6},{8,9},{9,8},{10,11... | collective-permute-start | bytes 786440 | tf_op jit(solution)/shard_map/ppermute | solution.py:121
  32.6 15.1 %copy-start = (bf16[16,8192]{1,0:T(8,128)(2,1)}, bf16[16,8192]{1,0:T(8,128)(2,1)S(1)}, u32[]{:S(2)}) copy-start(bf16[16,8192]{1,0:T(8,128)(2,1)S(1)} %collective-permute-done.26.refs_10_) | copy-start | bytes 786436
  32.6 8.9 %collective-permute-start.9 = (bf16[16,8192]{1,0:T(8,128)(2,1)S(1)}, bf16[16,8192]{1,0:T(8,128)(2,1)S(1)}, u32[]{:S(2)}, u32[]{:S(2)}) collective-permute-start(bf16[16,8192]{1,0:T(8,128)(2,1)S(1)} %collective-permute-done.5.refs_6_), channel_id=1, source_target_pairs={{0,4},{1,5},{4,8},{5,9},{8,12},{9,13},{12,14},{13,15},{14,10},{15,... | collective-permute-start | bytes 786440 | tf_op jit(solution)/shard_map/ppermute | solution.py:117
  34.4 13.3 %copy-start.1 = (bf16[16,8192]{1,0:T(8,128)(2,1)}, bf16[16,8192]{1,0:T(8,128)(2,1)S(1)}, u32[]{:S(2)}) copy-start(bf16[16,8192]{1,0:T(8,128)(2,1)S(1)} %collective-permute-done.28.refs_12_) | copy-start | bytes 786436
  34.4 8.3 %collective-permute-start.11 = (bf16[16,8192]{1,0:T(8,128)(2,1)S(1)}, bf16[16,8192]{1,0:T(8,128)(2,1)S(1)}, u32[]{:S(2)}, u32[]{:S(2)}) collective-permute-start(bf16[16,8192]{1,0:T(8,128)(2,1)S(1)} %collective-permute-done.7.refs_8_), channel_id=1, source_target_pairs={{0,2},{1,3},{4,0},{5,1},{8,4},{9,5},{12,8},{13,9},{14,12},{15,13},... | collective-permute-start | bytes 786440 | tf_op jit(solution)/shard_map/ppermute | solution.py:117
  34.7 13.1 %copy-start.7 = (bf16[16,8192]{1,0:T(8,128)(2,1)}, bf16[16,8192]{1,0:T(8,128)(2,1)S(1)}, u32[]{:S(2)}) copy-start(bf16[16,8192]{1,0:T(8,128)(2,1)S(1)} %collective-permute-done.19.refs_3_) | copy-start | bytes 786436
  34.7 9.5 %collective-permute-start.25 = (bf16[16,8192]{1,0:T(8,128)(2,1)S(1)}, bf16[16,8192]{1,0:T(8,128)(2,1)S(1)}, u32[]{:S(2)}, u32[]{:S(2)}) collective-permute-start(bf16[16,8192]{1,0:T(8,128)(2,1)S(1)} %collective-permute-done.24.refs_8_), channel_id=1, source_target_pairs={{0,1},{1,0},{2,3},{3,2},{4,5},{5,4},{6,7},{7,6},{8,9},{9,8},{10,11... | collective-permute-start | bytes 786440 | tf_op jit(solution)/shard_map/ppermute | solution.py:121
  34.8 13.0 %copy-start.8 = (bf16[16,8192]{1,0:T(8,128)(2,1)}, bf16[16,8192]{1,0:T(8,128)(2,1)S(1)}, u32[]{:S(2)}) copy-start(bf16[16,8192]{1,0:T(8,128)(2,1)S(1)} %collective-permute-done.21.refs_5_) | copy-start | bytes 786436
  34.8 8.1 %collective-permute-start.30 = (bf16[16,4096]{1,0:T(8,128)(2,1)S(1)}, bf16[16,4096]{1,0:T(8,128)(2,1)S(1)}, u32[]{:S(2)}, u32[]{:S(2)}) collective-permute-start(bf16[16,4096]{1,0:T(8,128)(2,1)S(1)} %slice.18), channel_id=1, source_target_pairs={{0,4},{1,5},{4,8},{5,9},{8,12},{9,13},{12,14},{13,15},{14,10},{15,... | collective-permute-start | bytes 393224 | tf_op jit(solution)/shard_map/ppermute | solution.py:117
  36.7 11.1 %copy-start.9 = (bf16[16,8192]{1,0:T(8,128)(2,1)}, bf16[16,8192]{1,0:T(8,128)(2,1)S(1)}, u32[]{:S(2)}) copy-start(bf16[16,8192]{1,0:T(8,128)(2,1)S(1)} %collective-permute-done.23.refs_7_) | copy-start | bytes 786436
  36.7 7.5 %collective-permute-start.32 = (bf16[16,4096]{1,0:T(8,128)(2,1)S(1)}, bf16[16,4096]{1,0:T(8,128)(2,1)S(1)}, u32[]{:S(2)}, u32[]{:S(2)}) collective-permute-start(bf16[16,4096]{1,0:T(8,128)(2,1)S(1)} %slice.19), channel_id=1, source_target_pairs={{0,2},{1,3},{4,0},{5,1},{8,4},{9,5},{12,8},{13,9},{14,12},{15,13},... | collective-permute-start | bytes 393224 | tf_op jit(solution)/shard_map/ppermute | solution.py:117
  41.5 48.0 %copy-start.13 = (bf16[16,8192]{1,0:T(8,128)(2,1)}, bf16[16,8192]{1,0:T(8,128)(2,1)S(1)}, u32[]{:S(2)}) copy-start(bf16[16,8192]{1,0:T(8,128)(2,1)S(1)} %collective-permute-done.9.refs_10_) | copy-start | bytes 786436
  41.5 4.1 %collective-permute-start.27 = (bf16[16,8192]{1,0:T(8,128)(2,1)S(1)}, bf16[16,8192]{1,0:T(8,128)(2,1)S(1)}, u32[]{:S(2)}, u32[]{:S(2)}) collective-permute-start(bf16[16,8192]{1,0:T(8,128)(2,1)S(1)} %collective-permute-done.26.refs_10_), channel_id=1, source_target_pairs={{0,1},{1,0},{2,3},{3,2},{4,5},{5,4},{6,7},{7,6},{8,9},{9,8},{10,11... | collective-permute-start | bytes 786440 | tf_op jit(solution)/shard_map/ppermute | solution.py:121
  42.7 46.8 %copy-start.14 = (bf16[16,8192]{1,0:T(8,128)(2,1)}, bf16[16,8192]{1,0:T(8,128)(2,1)S(1)}, u32[]{:S(2)}) copy-start(bf16[16,8192]{1,0:T(8,128)(2,1)S(1)} %collective-permute-done.11.refs_12_) | copy-start | bytes 786436
  42.7 4.5 %collective-permute-start.29 = (bf16[16,8192]{1,0:T(8,128)(2,1)S(1)}, bf16[16,8192]{1,0:T(8,128)(2,1)S(1)}, u32[]{:S(2)}, u32[]{:S(2)}) collective-permute-start(bf16[16,8192]{1,0:T(8,128)(2,1)S(1)} %collective-permute-done.28.refs_12_), channel_id=1, source_target_pairs={{0,1},{1,0},{2,3},{3,2},{4,5},{5,4},{6,7},{7,6},{8,9},{9,8},{10,11... | collective-permute-start | bytes 786440 | tf_op jit(solution)/shard_map/ppermute | solution.py:121
  42.9 4.9 %copy-start.15 = (bf16[16,4096]{1,0:T(8,128)(2,1)}, bf16[16,4096]{1,0:T(8,128)(2,1)S(1)}, u32[]{:S(2)}) copy-start(bf16[16,4096]{1,0:T(8,128)(2,1)S(1)} %collective-permute-done.30.refs_14_) | copy-start | bytes 393220
  42.9 1.9 %collective-permute-start.31 = (bf16[16,4096]{1,0:T(8,128)(2,1)S(1)}, bf16[16,4096]{1,0:T(8,128)(2,1)S(1)}, u32[]{:S(2)}, u32[]{:S(2)}) collective-permute-start(bf16[16,4096]{1,0:T(8,128)(2,1)S(1)} %collective-permute-done.30.refs_14_), channel_id=1, source_target_pairs={{0,1},{1,0},{2,3},{3,2},{4,5},{5,4},{6,7},{7,6},{8,9},{9,8},{10,11... | collective-permute-start | bytes 393224 | tf_op jit(solution)/shard_map/ppermute | solution.py:121
  44.1 3.6 %copy-start.16 = (bf16[16,4096]{1,0:T(8,128)(2,1)}, bf16[16,4096]{1,0:T(8,128)(2,1)S(1)}, u32[]{:S(2)}) copy-start(bf16[16,4096]{1,0:T(8,128)(2,1)S(1)} %collective-permute-done.32.refs_16_) | copy-start | bytes 393220
  44.1 1.3 collective-permute-start.33
  44.2 3.6 %copy-start.10 = (bf16[16,8192]{1,0:T(8,128)(2,1)}, bf16[16,8192]{1,0:T(8,128)(2,1)S(1)}, u32[]{:S(2)}) copy-start(bf16[16,8192]{1,0:T(8,128)(2,1)S(1)} %collective-permute-done.25.refs_9_) | copy-start | bytes 786436
  44.2 24.6 %collective-permute-start.2 = (bf16[16,8192]{1,0:T(8,128)(2,1)S(1)}, bf16[16,8192]{1,0:T(8,128)(2,1)S(1)}, u32[]{:S(2)}, u32[]{:S(2)}) collective-permute-start(bf16[16,8192]{1,0:T(8,128)(2,1)S(1)} %collective-permute-done.1.refs_2_), channel_id=1, source_target_pairs={{0,1},{1,0},{2,3},{3,2},{4,5},{5,4},{6,7},{7,6},{8,9},{9,8},{10,11... | collective-permute-start | bytes 786440 | tf_op jit(solution)/shard_map/ppermute | solution.py:121
  44.8 3.0 %copy-start.17 = (bf16[16,4096]{1,0:T(8,128)(2,1)}, bf16[16,4096]{1,0:T(8,128)(2,1)S(1)}, u32[]{:S(2)}) copy-start(bf16[16,4096]{1,0:T(8,128)(2,1)S(1)} %collective-permute-done.31.refs_15_) | copy-start | bytes 393220
  44.8 24.2 %collective-permute-start.4 = (bf16[16,8192]{1,0:T(8,128)(2,1)S(1)}, bf16[16,8192]{1,0:T(8,128)(2,1)S(1)}, u32[]{:S(2)}, u32[]{:S(2)}) collective-permute-start(bf16[16,8192]{1,0:T(8,128)(2,1)S(1)} %collective-permute-done.3.refs_4_), channel_id=1, source_target_pairs={{0,1},{1,0},{2,3},{3,2},{4,5},{5,4},{6,7},{7,6},{8,9},{9,8},{10,11... | collective-permute-start | bytes 786440 | tf_op jit(solution)/shard_map/ppermute | solution.py:121
  45.5 2.3 %copy-start.18 = (bf16[16,4096]{1,0:T(8,128)(2,1)}, bf16[16,4096]{1,0:T(8,128)(2,1)S(1)}, u32[]{:S(2)}) copy-start(bf16[16,4096]{1,0:T(8,128)(2,1)S(1)} %collective-permute-done.33.refs_17_) | copy-start | bytes 393220
  45.5 23.9 %collective-permute-start.6 = (bf16[16,8192]{1,0:T(8,128)(2,1)S(1)}, bf16[16,8192]{1,0:T(8,128)(2,1)S(1)}, u32[]{:S(2)}, u32[]{:S(2)}) collective-permute-start(bf16[16,8192]{1,0:T(8,128)(2,1)S(1)} %collective-permute-done.5.refs_6_), channel_id=1, source_target_pairs={{0,1},{1,0},{2,3},{3,2},{4,5},{5,4},{6,7},{7,6},{8,9},{9,8},{10,11... | collective-permute-start | bytes 786440 | tf_op jit(solution)/shard_map/ppermute | solution.py:121
  45.6 2.2 %copy-start.11 = (bf16[16,8192]{1,0:T(8,128)(2,1)}, bf16[16,8192]{1,0:T(8,128)(2,1)S(1)}, u32[]{:S(2)}) copy-start(bf16[16,8192]{1,0:T(8,128)(2,1)S(1)} %collective-permute-done.27.refs_11_) | copy-start | bytes 786436
  45.7 23.9 %collective-permute-start.13 = (bf16[16,4096]{1,0:T(8,128)(2,1)S(1)}, bf16[16,4096]{1,0:T(8,128)(2,1)S(1)}, u32[]{:S(2)}, u32[]{:S(2)}) collective-permute-start(bf16[16,4096]{1,0:T(8,128)(2,1)S(1)} %slice.16), channel_id=1, source_target_pairs={{0,4},{1,5},{4,8},{5,9},{8,12},{9,13},{12,14},{13,15},{14,10},{15,... | collective-permute-start | bytes 393224 | tf_op jit(solution)/shard_map/ppermute | solution.py:117
  47.2 22.7 %collective-permute-start.15 = (bf16[16,4096]{1,0:T(8,128)(2,1)S(1)}, bf16[16,4096]{1,0:T(8,128)(2,1)S(1)}, u32[]{:S(2)}, u32[]{:S(2)}) collective-permute-start(bf16[16,4096]{1,0:T(8,128)(2,1)S(1)} %slice.17), channel_id=1, source_target_pairs={{0,2},{1,3},{4,0},{5,1},{8,4},{9,5},{12,8},{13,9},{14,12},{15,13},... | collective-permute-start | bytes 393224 | tf_op jit(solution)/shard_map/ppermute | solution.py:117
  68.8 20.7 %copy-start.24 = (bf16[16,8192]{1,0:T(8,128)(2,1)}, bf16[16,8192]{1,0:T(8,128)(2,1)S(1)}, u32[]{:S(2)}) copy-start(bf16[16,8192]{1,0:T(8,128)(2,1)S(1)} %collective-permute-done.2.refs_3_) | copy-start | bytes 786436
  68.8 20.5 %collective-permute-start.8 = (bf16[16,8192]{1,0:T(8,128)(2,1)S(1)}, bf16[16,8192]{1,0:T(8,128)(2,1)S(1)}, u32[]{:S(2)}, u32[]{:S(2)}) collective-permute-start(bf16[16,8192]{1,0:T(8,128)(2,1)S(1)} %collective-permute-done.7.refs_8_), channel_id=1, source_target_pairs={{0,1},{1,0},{2,3},{3,2},{4,5},{5,4},{6,7},{7,6},{8,9},{9,8},{10,11... | collective-permute-start | bytes 786440 | tf_op jit(solution)/shard_map/ppermute | solution.py:121
  69.0 20.6 %copy-start.25 = (bf16[16,8192]{1,0:T(8,128)(2,1)}, bf16[16,8192]{1,0:T(8,128)(2,1)S(1)}, u32[]{:S(2)}) copy-start(bf16[16,8192]{1,0:T(8,128)(2,1)S(1)} %collective-permute-done.4.refs_5_) | copy-start | bytes 786436
  69.0 20.4 %collective-permute-start.10 = (bf16[16,8192]{1,0:T(8,128)(2,1)S(1)}, bf16[16,8192]{1,0:T(8,128)(2,1)S(1)}, u32[]{:S(2)}, u32[]{:S(2)}) collective-permute-start(bf16[16,8192]{1,0:T(8,128)(2,1)S(1)} %collective-permute-done.9.refs_10_), channel_id=1, source_target_pairs={{0,1},{1,0},{2,3},{3,2},{4,5},{5,4},{6,7},{7,6},{8,9},{9,8},{10,11... | collective-permute-start | bytes 786440 | tf_op jit(solution)/shard_map/ppermute | solution.py:121
  69.4 20.1 %copy-start.26 = (bf16[16,8192]{1,0:T(8,128)(2,1)}, bf16[16,8192]{1,0:T(8,128)(2,1)S(1)}, u32[]{:S(2)}) copy-start(bf16[16,8192]{1,0:T(8,128)(2,1)S(1)} %collective-permute-done.6.refs_7_) | copy-start | bytes 786436
  69.4 20.0 %collective-permute-start.12 = (bf16[16,8192]{1,0:T(8,128)(2,1)S(1)}, bf16[16,8192]{1,0:T(8,128)(2,1)S(1)}, u32[]{:S(2)}, u32[]{:S(2)}) collective-permute-start(bf16[16,8192]{1,0:T(8,128)(2,1)S(1)} %collective-permute-done.11.refs_12_), channel_id=1, source_target_pairs={{0,1},{1,0},{2,3},{3,2},{4,5},{5,4},{6,7},{7,6},{8,9},{9,8},{10,11... | collective-permute-start | bytes 786440 | tf_op jit(solution)/shard_map/ppermute | solution.py:121
  69.5 20.0 %copy-start.30 = (bf16[16,4096]{1,0:T(8,128)(2,1)}, bf16[16,4096]{1,0:T(8,128)(2,1)S(1)}, u32[]{:S(2)}) copy-start(bf16[16,4096]{1,0:T(8,128)(2,1)S(1)} %collective-permute-done.13.refs_14_) | copy-start | bytes 393220
  69.5 19.8 %collective-permute-start.14 = (bf16[16,4096]{1,0:T(8,128)(2,1)S(1)}, bf16[16,4096]{1,0:T(8,128)(2,1)S(1)}, u32[]{:S(2)}, u32[]{:S(2)}) collective-permute-start(bf16[16,4096]{1,0:T(8,128)(2,1)S(1)} %collective-permute-done.13.refs_14_), channel_id=1, source_target_pairs={{0,1},{1,0},{2,3},{3,2},{4,5},{5,4},{6,7},{7,6},{8,9},{9,8},{10,11... | collective-permute-start | bytes 393224 | tf_op jit(solution)/shard_map/ppermute | solution.py:121
  69.9 19.6 %copy-start.31 = (bf16[16,4096]{1,0:T(8,128)(2,1)}, bf16[16,4096]{1,0:T(8,128)(2,1)S(1)}, u32[]{:S(2)}) copy-start(bf16[16,4096]{1,0:T(8,128)(2,1)S(1)} %collective-permute-done.15.refs_16_) | copy-start | bytes 393220
  69.9 19.4 %collective-permute-start.16 = (bf16[16,4096]{1,0:T(8,128)(2,1)S(1)}, bf16[16,4096]{1,0:T(8,128)(2,1)S(1)}, u32[]{:S(2)}, u32[]{:S(2)}) collective-permute-start(bf16[16,4096]{1,0:T(8,128)(2,1)S(1)} %collective-permute-done.15.refs_16_), channel_id=1, source_target_pairs={{0,1},{1,0},{2,3},{3,2},{4,5},{5,4},{6,7},{7,6},{8,9},{9,8},{10,11... | collective-permute-start | bytes 393224 | tf_op jit(solution)/shard_map/ppermute | solution.py:121
  89.4 0.9 copy-start.28
  89.4 1.0 copy-start.29
  (4 other events, 2.9 us)

commit v3 on v1

--- a/solution.py
+++ b/solution.py
@@ -11,6 +11,7 @@
 EX_TOK = 32
 TILE = 256
 DEPTH = 2048
+NEAR = 4
 VMEM = 56 * 1024 * 1024
 HIGH = lax.Precision.HIGHEST
 
@@ -164,44 +165,65 @@
         part = pl.ds(start, DEPTH)
         a = left[:, part]
         if transposed:
-            total += lax.dot_general(
-                a, right[:, part], (((1,), (1,)), ((), ())), preferred_element_type=jnp.float32
-            )
+            total += last_dot(a, right[:, part])
         else:
             total += jnp.dot(a, right[part, :], preferred_element_type=jnp.float32)
     return total
 
 
+def last_dot(a, b):
+    return lax.dot_general(a, b, (((1,), (1,)), ((), ())), preferred_element_type=jnp.float32)
+
+
 def forward_kernel(places, chips, *refs):
     count = len(places)
-    blocks, (weight, out, whole, sems) = refs[:count], refs[count:]
+    blocks, refs = refs[:count], refs[count:]
+    weight, proj = refs[0], refs[1] if len(refs) == 6 else None
+    out, whole, sems = refs[-4 if proj is not None else -3], refs[-2], refs[-1]
 
     @pl.when(pl.program_id(0) == 0)
     def _():
         assemble(places, chips, blocks, whole, sems)
-
-    out[...] = deep_dot(whole, weight, False, out.shape[1])
-
-
-def forward(places, chips, blocks, weight, tile):
+        if proj is not None:
+            total = jnp.zeros(refs[3].shape, jnp.float32)
+            for start in range(0, whole.shape[1], DEPTH):
+                part = pl.ds(start, DEPTH)
+                total += last_dot(proj[: 2 * R, part], whole[:, part])
+            refs[3][...] = total
+
+    out[...] = deep_dot(whole, weight, False, out.shape[0]).T
+
+
+def forward(places, chips, blocks, weight, tile, first, tiles, proj=None):
     rows = blocks[0].shape[0] * chips * 2
-    depth, width = weight.shape
+    depth = weight.shape[0]
+    in_specs = [pl.BlockSpec(memory_space=pl.ANY)] * len(blocks)
+    in_specs.append(pl.BlockSpec((depth, tile), lambda n: (0, n + first)))
+    out_shape = [jax.ShapeDtypeStruct((tiles * tile, rows), jnp.float32)]
+    out_specs = [pl.BlockSpec((tile, rows), lambda n: (n, 0))]
+    operands = [*blocks, weight]
+    if proj is not None:
+        in_specs.append(pl.BlockSpec((3 * R, depth), lambda n: (0, 0)))
+        out_shape.append(jax.ShapeDtypeStruct((2 * R, rows), jnp.float32))
+        out_specs.append(pl.BlockSpec((2 * R, rows), lambda n: (0, 0)))
+        operands.append(proj)
     return pl.pallas_call(
         functools.partial(forward_kernel, places, chips),
-        grid=(width // tile,),
-        out_shape=jax.ShapeDtypeStruct((rows, width), jnp.float32),
-        in_specs=[pl.BlockSpec(memory_space=pl.ANY)] * len(blocks)
-        + [pl.BlockSpec((depth, tile), lambda n: (0, n))],
-        out_specs=pl.BlockSpec((rows, tile), lambda n: (0, n)),
+        grid=(tiles,),
+        out_shape=out_shape,
+        in_specs=in_specs,
+        out_specs=out_specs,
         scratch_shapes=[
             pltpu.VMEM((rows, depth), jnp.bfloat16),
             pltpu.SemaphoreType.DMA((len(blocks),)),
         ],
         compiler_params=pltpu.CompilerParams(vmem_limit_bytes=VMEM),
         cost_estimate=pl.CostEstimate(
-            flops=2 * rows * depth * width, bytes_accessed=2 * depth * width, transcendentals=0
+            flops=4 * rows * depth * tiles * tile,
+            bytes_accessed=2 * depth * tiles * tile,
+            transcendentals=0,
         ),
-    )(*blocks, weight)
+    )(*operands)
 
 
 def membership(ids, examples):
@@ -215,110 +237,171 @@
     )
 
 
-def backward_kernel(places, chips, examples, *refs):
+def backward_kernel(places, chips, examples, tile, parts, *refs):
     count = len(places)
-    blocks = refs[:count]
-    weight, gate, up, proj, proj_ff, ids, send, whole, sums, flipped, sems = refs[count:]
+    blocks, refs = refs[:count], refs[count:]
+    weight, proj, proj_ff, ids = refs[:4]
+    gates, ups = refs[4 : 4 + parts], refs[4 + parts : 4 + 2 * parts]
+    sends, (whole, spread, flipped, sums, ready, sems) = refs[4 + 2 * parts : -6], refs[-6:]
     step = pl.program_id(0)
     hid = 2 * chips
     shares = R // hid
+    near = len(sends)
 
     @pl.when(step == 0)
     def _():
         assemble(places, chips, blocks, whole, sems)
-        sums[...] = jnp.zeros_like(sums)
-        columns = deep_dot(whole, proj, False, R).T
-        for lanes in range(flipped.shape[0]):
-            flipped[lanes] = columns[:, lanes * 128 : (lanes + 1) * 128]
-
-    hidden_grad = deep_dot(whole, weight, True, gate.shape[1])
-    hidden, gate_grad, up_grad = pointwise(gate[...], up[...], hidden_grad)
-    for m, value in enumerate((gate_grad, up_grad, hidden)):
-        sums[m] += jnp.dot(
-            value, proj_ff[:, m * R : (m + 1) * R], preferred_element_type=jnp.float32
-        )
+        spread[...] = jnp.zeros_like(spread)
+        flipped[...] = jnp.zeros_like(flipped)
+
+    depth = weight.shape[1]
+    x = whole[:, pl.ds(pl.multiple_of(step * depth, depth), depth)]
+    spread[...] += last_dot(weight[...], x)
+    turned = last_dot(proj[2 * R :, :], x)
+    for lanes in range(flipped.shape[0]):
+        flipped[lanes] += turned[:, lanes * 128 : (lanes + 1) * 128]
 
     @pl.when(step == pl.num_programs(0) - 1)
     def _():
+        sums[...] = jnp.zeros_like(sums)
+        start = 0
+        for gate, up in zip(gates, ups):
+            for local in range(0, gate.shape[0], tile):
+                part = pl.ds(local, tile)
+                hidden, gate_grad, up_grad = pointwise(
+                    gate[part, :], up[part, :], spread[start : start + tile, :]
+                )
+                for m, value in enumerate((gate_grad, up_grad, hidden)):
+                    sums[m * R : (m + 1) * R, :] += jnp.dot(
+                        proj_ff[m * R : (m + 1) * R, start : start + tile],
+                        value,
+                        preferred_element_type=jnp.float32,
+                    )
+                start += tile
         for m in range(2):
-            columns = sums[m].T
             for p in range(hid):
-                send[p, m * shares : (m + 1) * shares, :] = columns[p * shares : (p + 1) * shares]
+                own = sums[m * R + p * shares : m * R + (p + 1) * shares, :]
+                ready[p, m * shares : (m + 1) * shares, :] = own
         member = membership(ids[...], examples)
         total_rows = member.shape[1]
         for j in range(shares):
             every = pl.ds(j, hid, shares)
             own = jnp.concatenate([flipped[k, every, :] for k in range(flipped.shape[0])], axis=1)
             left = (own[:, None, :] * member[None, :, :]).reshape(hid * examples, total_rows)
-            product = exact_dot(left, sums[2], ((1,), (0,)))
-            send[:, 2 * shares :, j * R : (j + 1) * R] = product.reshape(hid, examples, R)
-
-
-def backward(places, chips, blocks, weight, gate, up, proj, proj_ff, ids, tile):
+            product = exact_dot(left, sums[2 * R :, :], ((1,), (1,)))
+            ready[:, 2 * shares :, j * R : (j + 1) * R] = product.reshape(hid, examples, R)
+        mine = lax.rem(lax.axis_index("hid"), near)
+        for d in range(near):
+            partner = mine + d - 2 * (mine & d)
+            for z in range(hid // near):
+                sends[d][z] = ready[z * near + partner]
+
+
+def backward(places, chips, blocks, weight, gates, ups, proj, proj_ff, ids, depth_tile, tile):
     rows = blocks[0].shape[0] * chips * 2
     width, depth = weight.shape
     hid = 2 * chips
     shares, examples = R // hid, rows // EX_TOK
+    deep = 2 * shares + examples
+
+    def stay(*shape):
+        return pl.BlockSpec(shape, lambda k: (0,) * len(shape))
+
     return pl.pallas_call(
-        functools.partial(backward_kernel, places, chips, examples),
-        grid=(width // tile,),
-        out_shape=jax.ShapeDtypeStruct((hid, 2 * shares + examples, rows), jnp.float32),
+        functools.partial(backward_kernel, places, chips, examples, tile, len(gates)),
+        grid=(depth // depth_tile,),
+        out_shape=[jax.ShapeDtypeStruct((hid // NEAR, deep, rows), jnp.float32)] * NEAR,
         in_specs=[pl.BlockSpec(memory_space=pl.ANY)] * len(blocks)
         + [
-            pl.BlockSpec((tile, depth), lambda n: (n, 0)),
-            pl.BlockSpec((rows, tile), lambda n: (0, n)),
-            pl.BlockSpec((rows, tile), lambda n: (0, n)),
-            pl.BlockSpec((depth, R), lambda n: (0, 0)),
-            pl.BlockSpec((tile, 3 * R), lambda n: (n, 0)),
-            pl.BlockSpec((1, rows), lambda n: (0, 0)),
-        ],
-        out_specs=pl.BlockSpec((hid, 2 * shares + examples, rows), lambda n: (0, 0, 0)),
+            pl.BlockSpec((width, depth_tile), lambda k: (0, k)),
+            pl.BlockSpec((3 * R, depth_tile), lambda k: (0, k)),
+            stay(3 * R, width),
+            stay(1, rows),
+        ]
+        + [stay(*value.shape) for value in (*gates, *ups)],
+        out_specs=[stay(hid // NEAR, deep, rows)] * NEAR,
         scratch_shapes=[
             pltpu.VMEM((rows, depth), jnp.bfloat16),
-            pltpu.VMEM((3, rows, R), jnp.float32),
+            pltpu.VMEM((width, rows), jnp.float32),
             pltpu.VMEM((rows // 128, R, 128), jnp.float32),
+            pltpu.VMEM((3 * R, rows), jnp.float32),
+            pltpu.VMEM((hid, deep, rows), jnp.float32),
             pltpu.SemaphoreType.DMA((len(blocks),)),
         ],
         compiler_params=pltpu.CompilerParams(vmem_limit_bytes=VMEM),
         cost_estimate=pl.CostEstimate(
             flops=2 * rows * depth * width, bytes_accessed=2 * depth * width, transcendentals=0
         ),
-    )(*blocks, weight, gate, up, proj, proj_ff, ids)
-
-
-def features_kernel(hid, received, inputs, ids, tests, features, partial):
+    )(*blocks, weight, proj, proj_ff, ids, *gates, *ups)
+
+
+def exchange_near(sends):
+    hid = lax.axis_size("hid")
+    return [sends[0]] + [
+        lax.ppermute(sends[d], "hid", [(h, h ^ d) for h in range(hid)]) for d in range(1, NEAR)
+    ]
+
+
+def exchange_far(sends):
+    hid = lax.axis_size("hid")
+    return [sends[0]] + [
+        lax.ppermute(sends[e], "hid", [(h, h ^ (e * NEAR)) for h in range(hid)])
+        for e in range(1, hid // NEAR)
+    ]
+
+
+def combine_kernel(count, *refs):
+    parts, sends = refs[:count], refs[count:]
+    mine = lax.axis_index("hid") // NEAR
+    for e in range(len(sends)):
+        partner = mine + e - 2 * (mine & e)
+        sends[e][...] = sum(part[partner] for part in parts[1:]) + parts[0][partner]
+
+
+def combine(parts):
+    far = parts[0].shape[0]
+    vmem = pl.BlockSpec(memory_space=pltpu.VMEM)
+    return pl.pallas_call(
+        functools.partial(combine_kernel, len(parts)),
+        out_shape=[jax.ShapeDtypeStruct(parts[0].shape[1:], jnp.float32)] * far,
+        in_specs=[vmem] * len(parts),
+        out_specs=[vmem] * far,
+        compiler_params=pltpu.CompilerParams(vmem_limit_bytes=VMEM),
+    )(*parts)
+
+
+def features_kernel(hid, count, *refs):
+    received, (inputs, ids, tests, features, partial) = refs[:count], refs[count:]
     shares = R // hid
     examples = features.shape[0]
     member = membership(ids[...], examples)
-    total = jnp.sum(received[...], axis=0)
+    total = sum(part[...] for part in received[1:]) + received[0][...]
     for m in range(2):
         own = total[m * shares : (m + 1) * shares]
         left = (own[:, None, :] * member[None, :, :]).reshape(shares * examples, own.shape[1])
-        product = exact_dot(left, inputs[:, m * R : (m + 1) * R], ((1,), (0,)))
+        product = exact_dot(left, inputs[m * R : (m + 1) * R, :], ((1,), (1,)))
         for j in range(shares):
             start = (j * 3 + m) * R
             features[:, start : start + R] = product[j * examples : (j + 1) * examples]
     for j in range(shares):
         start = (j * 3 + 2) * R
         features[:, start : start + R] = total[2 * shares :, j * R : (j + 1) * R]
-    scores = exact_dot(features[...], tests[...].astype(jnp.float32), ((1,), (1,)))
-    partial[...] = jnp.broadcast_to(scores[None], partial.shape)
-
-
-def finish(received, inputs, ids, tests):
-    hid, _, rows = received.shape
-    examples = rows // EX_TOK
+    partial[...] = exact_dot(features[...], tests[...].astype(jnp.float32), ((1,), (1,)))
+
+
+def finish(hid, received, inputs, ids, tests):
+    examples = ids.shape[1] // EX_TOK
     vmem = pl.BlockSpec(memory_space=pltpu.VMEM)
     return pl.pallas_call(
-        functools.partial(features_kernel, hid),
+        functools.partial(features_kernel, hid, len(received)),
         out_shape=(
             jax.ShapeDtypeStruct((examples, tests.shape[1]), jnp.float32),
-            jax.ShapeDtypeStruct((hid, examples, tests.shape[0]), jnp.float32),
+            jax.ShapeDtypeStruct((examples, tests.shape[0]), jnp.float32),
         ),
-        in_specs=[vmem] * 4,
+        in_specs=[vmem] * (len(received) + 3),
         out_specs=(vmem, vmem),
         compiler_params=pltpu.CompilerParams(vmem_limit_bytes=VMEM),
-    )(received, inputs, ids, tests)
+    )(*received, inputs, ids, tests)
 
 
 def local_ring(
@@ -336,15 +419,16 @@
     ids = example_ids[None, :]
     places, token_blocks = gather_blocks(tokens, chips)
     _, grad_blocks = gather_blocks(out_grad, chips)
-    inputs = forward(places, chips, token_blocks, proj_d[:, : 2 * R], 2 * R)
-    gate = forward(places, chips, token_blocks, gate_weight, TILE)
-    up = forward(places, chips, token_blocks, up_weight, TILE)
-    send = backward(
-        places, chips, grad_blocks, down_weight, gate, up, proj_d[:, 2 * R :], proj_ff, ids, TILE
-    )
-    received = lax.all_to_all(send, "hid", 0, 0)
-    features, partial = finish(received, inputs, ids, test_features)
-    scores = jnp.sum(lax.all_to_all(partial, "hid", 0, 0), axis=0)
+    tiles = gate_weight.shape[1] // TILE
+    gate, inputs = forward(places, chips, token_blocks, gate_weight, TILE, 0, tiles, proj_d.T)
+    (up,) = forward(places, chips, token_blocks, up_weight, TILE, 0, tiles)
+    sends = backward(
+        places, chips, grad_blocks, down_weight, [gate], [up], proj_d.T, proj_ff.T, ids, 1024, TILE
+    )
+    received = exchange_far(combine(exchange_near(sends)))
+    features, partial = finish(2 * chips, received, inputs, ids, test_features)
+    near = sum(exchange_near([partial] * NEAR))
+    scores = sum(exchange_far([near] * (2 * chips // NEAR)))
     return features, scores
 
 

time: 148 us -> 145 us (0.980)
  waiting for transfers between devices: 27.2 us -> 41.7 us
  blocking collectives: 13.7 us -> 0 us
  local copies, waits for them, and re-layouts: 11.8 us -> 2.46 us
  starting transfers between devices: 25.7 us -> 32.8 us
  Pallas kernels: 66.7 us -> 65 us
    ppermute x0 -> x12, waiting for transfers between devices: none -> 13.9 us  [the longest x6 7.52 us: exchange_far(): lax.ppermute(sends[e], 'hid', [(h, h ^ e * NEAR) for h in range(hid)])]
    all_to_all x1 -> x0, blocking collectives: 13.7 us -> none  [local_ring(): scores = jnp.sum(lax.all_to_all(partial, 'hid', 0, 0), axis=0)]
    ppermute x0 -> x12, starting transfers between devices: none -> 12.6 us  [the longest x6 8.77 us: exchange_far(): lax.ppermute(sends[e], 'hid', [(h, h ^ e * NEAR) for h in range(hid)])]
    unnamed x71 -> x80, local copies, waits for them, and re-layouts: 8.34 us -> 2.42 us
    all_to_all x1 -> x0, starting transfers between devices: 4.97 us -> none  [local_ring(): received = lax.all_to_all(send, 'hid', 0, 0)]
    slice x4 -> x0, local copies, waits for them, and re-layouts: 1.6 us -> none  [the longest x2 1.59 us: local_ring(): inputs = forward(places, chips, token_blocks, proj_d[:, :2 * R], 2 * R)]
    pallas_call x4, Pallas kernels: 44.2 us -> 42.7 us  [the longest x2 38.4 us: forward(): pl.pallas_call(functools.partial(forward_kernel, places, chips), grid=(ti...]
  transfers between devices with their start and end apart: 35 -> 46, of which waited for: 11 -> 18; matrix products, arithmetic and copies ran while one was open for 6% -> 0% of each run, Pallas kernels for 28% -> 27%
where the time goes in v3:
time: 145 us; the launch traced here: 144 us
  Pallas kernels  65 us (45%)
  waiting for transfers between devices  41.7 us (29%)
  starting transfers between devices  32.8 us (23%)
  local copies, waits for them, and re-layouts  2.46 us (2%)
    pallas_call x2, Pallas kernels, forward(): pl.pallas_call(functools.partial(forward_kernel, places, chips), grid=(ti...  38.4 us
    ppermute x16, waiting for transfers between devices, ring_step(): return lax.ppermute(block, 'hid', pairs)  27.1 us
    pallas_call x1, Pallas kernels, backward(): pl.pallas_call(functools.partial(backward_kernel, places, chips, examples...  22.3 us
    ppermute x16, starting transfers between devices, ring_step(): return lax.ppermute(block, 'hid', pairs)  17.7 us
    ppermute x6, starting transfers between devices, exchange_far(): lax.ppermute(sends[e], 'hid', [(h, h ^ e * NEAR) for h in range(hid)])  8.77 us
    ppermute x6, waiting for transfers between devices, exchange_far(): lax.ppermute(sends[e], 'hid', [(h, h ^ e * NEAR) for h in range(hid)])  7.52 us
    ppermute x6, waiting for transfers between devices, exchange_near(): lax.ppermute(sends[d], 'hid', [(h, h ^ d) for h in range(hid)])  6.42 us
    ppermute x6, starting transfers between devices, exchange_near(): lax.ppermute(sends[d], 'hid', [(h, h ^ d) for h in range(hid)])  3.79 us
  transfers between devices with their start and end apart: 46, of which 18 were waited for; matrix products, arithmetic and copies ran while one was open for 0% of the time, Pallas kernels for 27%

profile of v3, /device:TPU:0, one launch (start us, length us, event | category | flops | bytes accessed | tf_op | source)
XLA Modules:
  0.0 144.5 jit_solution(10624571294691719930)
XLA Ops:
  0.6 3.1 %collective-permute-start.18 = (bf16[16,8192]{1,0:T(8,128)(2,1)}, bf16[16,8192]{1,0:T(8,128)(2,1)S(1)}, u32[]{:S(2)}, u32[]{:S(2)}) collective-permute-start(bf16[16,8192]{1,0:T(8,128)(2,1)} %refs_0_.4), channel_id=1, source_target_pairs={{0,4},{1,5},{4,8},{5,9},{8,12},{9,13},{12,14},{13,15},{14,10},{15,... | collective-permute-start | bytes 786440 | tf_op jit(solution)/shard_map/ppermute | solution.py:118
  3.7 2.0 %collective-permute-start.1 = (bf16[16,8192]{1,0:T(8,128)(2,1)}, bf16[16,8192]{1,0:T(8,128)(2,1)S(1)}, u32[]{:S(2)}, u32[]{:S(2)}) collective-permute-start(bf16[16,8192]{1,0:T(8,128)(2,1)} %refs_0_.5), channel_id=1, source_target_pairs={{0,4},{1,5},{4,8},{5,9},{8,12},{9,13},{12,14},{13,15},{14,10},{15,... | collective-permute-start | bytes 786440 | tf_op jit(solution)/shard_map/ppermute | solution.py:118
  5.7 5.2 %collective-permute-done.18.refs_2_ = bf16[16,8192]{1,0:T(8,128)(2,1)S(1)} collective-permute-done((bf16[16,8192]{1,0:T(8,128)(2,1)}, bf16[16,8192]{1,0:T(8,128)(2,1)S(1)}, u32[]{:S(2)}, u32[]{:S(2)}) %collective-permute-start.18) | collective-permute-done | bytes 262176 | tf_op jit(solution)/shard_map/ppermute | solution.py:118
  11.0 2.1 %collective-permute-start.22 = (bf16[16,8192]{1,0:T(8,128)(2,1)S(1)}, bf16[16,8192]{1,0:T(8,128)(2,1)S(1)}, u32[]{:S(2)}, u32[]{:S(2)}) collective-permute-start(bf16[16,8192]{1,0:T(8,128)(2,1)S(1)} %collective-permute-done.18.refs_2_), channel_id=1, source_target_pairs={{0,4},{1,5},{4,8},{5,9},{8,12},{9,13},{12,14},{13,15},{14,10},{15,... | collective-permute-start | bytes 786440 | tf_op jit(solution)/shard_map/ppermute | solution.py:118
  13.2 0.1 collective-permute-start
  13.2 3.3 %collective-permute-done.1.refs_2_ = bf16[16,8192]{1,0:T(8,128)(2,1)S(1)} collective-permute-done((bf16[16,8192]{1,0:T(8,128)(2,1)}, bf16[16,8192]{1,0:T(8,128)(2,1)S(1)}, u32[]{:S(2)}, u32[]{:S(2)}) %collective-permute-start.1) | collective-permute-done | bytes 262176 | tf_op jit(solution)/shard_map/ppermute | solution.py:118
  16.6 2.1 %collective-permute-start.5 = (bf16[16,8192]{1,0:T(8,128)(2,1)S(1)}, bf16[16,8192]{1,0:T(8,128)(2,1)S(1)}, u32[]{:S(2)}, u32[]{:S(2)}) collective-permute-start(bf16[16,8192]{1,0:T(8,128)(2,1)S(1)} %collective-permute-done.1.refs_2_), channel_id=1, source_target_pairs={{0,4},{1,5},{4,8},{5,9},{8,12},{9,13},{12,14},{13,15},{14,10},{15,... | collective-permute-start | bytes 786440 | tf_op jit(solution)/shard_map/ppermute | solution.py:118
  18.8 3.4 %collective-permute-done.22.refs_6_ = bf16[16,8192]{1,0:T(8,128)(2,1)S(1)} collective-permute-done((bf16[16,8192]{1,0:T(8,128)(2,1)S(1)}, bf16[16,8192]{1,0:T(8,128)(2,1)S(1)}, u32[]{:S(2)}, u32[]{:S(2)}) %collective-permute-start.22) | collective-permute-done | bytes 262176 | tf_op jit(solution)/shard_map/ppermute | solution.py:118
  22.2 2.1 %collective-permute-start.26 = (bf16[16,8192]{1,0:T(8,128)(2,1)S(1)}, bf16[16,8192]{1,0:T(8,128)(2,1)S(1)}, u32[]{:S(2)}, u32[]{:S(2)}) collective-permute-start(bf16[16,8192]{1,0:T(8,128)(2,1)S(1)} %collective-permute-done.22.refs_6_), channel_id=1, source_target_pairs={{0,4},{1,5},{4,8},{5,9},{8,12},{9,13},{12,14},{13,15},{14,10},{15,... | collective-permute-start | bytes 786440 | tf_op jit(solution)/shard_map/ppermute | solution.py:118
  24.4 0.1 collective-permute-start.19
  24.5 3.3 %collective-permute-done.5.refs_6_ = bf16[16,8192]{1,0:T(8,128)(2,1)S(1)} collective-permute-done((bf16[16,8192]{1,0:T(8,128)(2,1)S(1)}, bf16[16,8192]{1,0:T(8,128)(2,1)S(1)}, u32[]{:S(2)}, u32[]{:S(2)}) %collective-permute-start.5) | collective-permute-done | bytes 262176 | tf_op jit(solution)/shard_map/ppermute | solution.py:118
  27.8 2.2 %collective-permute-done.7.refs_8_ = bf16[16,8192]{1,0:T(8,128)(2,1)S(1)} collective-permute-done((bf16[16,8192]{1,0:T(8,128)(2,1)S(1)}, bf16[16,8192]{1,0:T(8,128)(2,1)S(1)}, u32[]{:S(2)}, u32[]{:S(2)}) %collective-permute-start.7) | collective-permute-done | bytes 262176 | tf_op jit(solution)/shard_map/ppermute | solution.py:118
  30.0 2.6 %collective-permute-done.26.refs_10_ = bf16[16,8192]{1,0:T(8,128)(2,1)S(1)} collective-permute-done((bf16[16,8192]{1,0:T(8,128)(2,1)S(1)}, bf16[16,8192]{1,0:T(8,128)(2,1)S(1)}, u32[]{:S(2)}, u32[]{:S(2)}) %collective-permute-start.26) | collective-permute-done | bytes 262176 | tf_op jit(solution)/shard_map/ppermute | solution.py:118
  32.6 1.8 %collective-permute-start.9 = (bf16[16,8192]{1,0:T(8,128)(2,1)S(1)}, bf16[16,8192]{1,0:T(8,128)(2,1)S(1)}, u32[]{:S(2)}, u32[]{:S(2)}) collective-permute-start(bf16[16,8192]{1,0:T(8,128)(2,1)S(1)} %collective-permute-done.5.refs_6_), channel_id=1, source_target_pairs={{0,4},{1,5},{4,8},{5,9},{8,12},{9,13},{12,14},{13,15},{14,10},{15,... | collective-permute-start | bytes 786440 | tf_op jit(solution)/shard_map/ppermute | solution.py:118
  34.4 0.2 collective-permute-start.11
  34.8 1.9 %collective-permute-start.30 = (bf16[16,4096]{1,0:T(8,128)(2,1)S(1)}, bf16[16,4096]{1,0:T(8,128)(2,1)S(1)}, u32[]{:S(2)}, u32[]{:S(2)}) collective-permute-start(bf16[16,4096]{1,0:T(8,128)(2,1)S(1)} %slice.18), channel_id=1, source_target_pairs={{0,4},{1,5},{4,8},{5,9},{8,12},{9,13},{12,14},{13,15},{14,10},{15,... | collective-permute-start | bytes 393224 | tf_op jit(solution)/shard_map/ppermute | solution.py:118
  36.7 0.2 collective-permute-start.32
  36.9 4.6 %collective-permute-done.9.refs_10_ = bf16[16,8192]{1,0:T(8,128)(2,1)S(1)} collective-permute-done((bf16[16,8192]{1,0:T(8,128)(2,1)S(1)}, bf16[16,8192]{1,0:T(8,128)(2,1)S(1)}, u32[]{:S(2)}, u32[]{:S(2)}) %collective-permute-start.9) | collective-permute-done | bytes 262176 | tf_op jit(solution)/shard_map/ppermute | solution.py:118
  41.5 1.2 collective-permute-done.11.refs_12_
  42.7 0.2 collective-permute-done.30.refs_14_
  42.9 0.3 collective-permute-start.31
  43.3 0.9 collective-permute-done.32.refs_16_
  44.2 0.6 collective-permute-start.2
  44.8 0.1 collective-permute-start.4
  44.9 0.6 collective-permute-done.33.refs_17_
  45.5 0.1 collective-permute-start.6
  45.7 1.6 %collective-permute-start.13 = (bf16[16,4096]{1,0:T(8,128)(2,1)S(1)}, bf16[16,4096]{1,0:T(8,128)(2,1)S(1)}, u32[]{:S(2)}, u32[]{:S(2)}) collective-permute-start(bf16[16,4096]{1,0:T(8,128)(2,1)S(1)} %slice.16), channel_id=1, source_target_pairs={{0,4},{1,5},{4,8},{5,9},{8,12},{9,13},{12,14},{13,15},{14,10},{15,... | collective-permute-start | bytes 393224 | tf_op jit(solution)/shard_map/ppermute | solution.py:118
  47.2 0.4 collective-permute-start.15
  47.8 0.1 copy-done.35
  48.0 18.0 %shard_map.105.refs_23_ = f32[1792,256]{1,0:T(8,128)} custom-call(bf16[16,8192]{1,0:T(8,128)(2,1)} %refs_0_.4, bf16[16,8192]{1,0:T(8,128)(2,1)} %copy-done.27, bf16[16,8192]{1,0:T(8,128)(2,1)} %copy-done.25, bf16[16,8192]{1,0:T(8,128)(2,1)} %copy-done.30, bf16[16,8192]{1,0:T(8,128)(2,1)} %copy-done.26, bf16[16,8192]{1,0:T(8,128)(2,1)} %copy-done.31, ...), custom_call_target="tpu_custom_call" | custom-call | flops 15032385536 | bytes 29360128 | tf_op jit(solution)/shard_map/pallas_call | solution.py:210
  66.0 0.1 collective-permute-start.8
  66.1 0.4 collective-permute-start.10
  66.6 0.1 collective-permute-start.12
  66.7 0.4 collective-permute-start.14
  67.1 0.1 collective-permute-start.16
  67.2 20.4 %shard_map.104 = (f32[1792,256]{1,0:T(8,128)}, f32[128,256]{1,0:T(8,128)}) custom-call(bf16[16,8192]{1,0:T(8,128)(2,1)} %refs_0_.4, bf16[16,8192]{1,0:T(8,128)(2,1)} %copy-done.27, bf16[16,8192]{1,0:T(8,128)(2,1)} %copy-done.25, bf16[16,8192]{1,0:T(8,128)(2,1)} %copy-done.30, bf16[16,8192]{1,0:T(8,128)(2,1)} %copy-done.26, bf16[16,8192]{1,0:T(8,128)(2,1)} %copy-done.31, ...), custom_call_target="tpu_custom_call" | custom-call | flops 15032385536 | bytes 29360128 | tf_op jit(solution)/shard_map/pallas_call | solution.py:210
  87.9 0.6 copy-done.10
  88.5 0.1 copy-done.16
  88.5 0.1 copy-done.11
  88.7 0.1 copy-done.12
  88.8 22.3 %shard_map.106 = (f32[4,16,256]{2,1,0:T(8,128)}, f32[4,16,256]{2,1,0:T(8,128)}, f32[4,16,256]{2,1,0:T(8,128)}, f32[4,16,256]{2,1,0:T(8,128)}) custom-call(bf16[16,8192]{1,0:T(8,128)(2,1)} %refs_0_.5, bf16[16,8192]{1,0:T(8,128)(2,1)} %copy-done.4, bf16[16,8192]{1,0:T(8,128)(2,1)} %copy-done.2, bf16[16,8192]{1,0:T(8,128)(2,1)} %copy-done.7, ...), custom_call_target="tpu_custom_call" | custom-call | flops 7516192768 | bytes 29360128 | tf_op jit(solution)/shard_map/pallas_call | solution.py:310
  111.1 0.5 collective-permute-start.34
  111.6 0.4 collective-permute-start.35
  112.0 1.0 collective-permute-start.36
  113.0 3.6 %collective-permute-done.35.refs_2_ = f32[4,16,256]{2,1,0:T(8,128)S(1)} collective-permute-done((f32[4,16,256]{2,1,0:T(8,128)}, f32[4,16,256]{2,1,0:T(8,128)S(1)}, u32[]{:S(2)}, u32[]{:S(2)}) %collective-permute-start.35) | collective-permute-done | bytes 65568 | tf_op jit(solution)/shard_map/ppermute | solution.py:341
  116.7 0.6 copy-done.20
  117.3 1.6 %shard_map.107 = (f32[16,256]{1,0:T(8,128)}, f32[16,256]{1,0:T(8,128)}, f32[16,256]{1,0:T(8,128)}, f32[16,256]{1,0:T(8,128)}) custom-call(f32[4,16,256]{2,1,0:T(8,128)} %get-tuple-element.15.refs_0_, f32[4,16,256]{2,1,0:T(8,128)} %copy-done.19, f32[4,16,256]{2,1,0:T(8,128)} %copy-done.20, f32[4,16,256]{2,1,0:T(8,128)} %copy-done.21), custom_call_target="tpu_custom_call" | custom-call | tf_op jit(solution)/shard_map/pallas_call | solution.py:364
  118.9 1.6 %collective-permute-start.37 = (f32[16,256]{1,0:T(8,128)}, f32[16,256]{1,0:T(8,128)S(1)}, u32[]{:S(2)}, u32[]{:S(2)}) collective-permute-start(f32[16,256]{1,0:T(8,128)} %get-tuple-element.20), channel_id=1, source_target_pairs={{0,4},{1,5},{2,6},{3,7},{4,0},{5,1},{6,2},{7,3},{8,12},{9,13},{10,... | collective-permute-start | bytes 49160 | tf_op jit(solution)/shard_map/ppermute | solution.py:348
  120.4 2.6 %collective-permute-start.38 = (f32[16,256]{1,0:T(8,128)}, f32[16,256]{1,0:T(8,128)S(1)}, u32[]{:S(2)}, u32[]{:S(2)}) collective-permute-start(f32[16,256]{1,0:T(8,128)} %get-tuple-element.21), channel_id=1, source_target_pairs={{0,8},{1,9},{2,10},{3,11},{4,12},{5,13},{6,14},{7,15},{8,0},{9,1},... | collective-permute-start | bytes 49160 | tf_op jit(solution)/shard_map/ppermute | solution.py:348
  123.0 0.2 collective-permute-start.39
  123.3 2.1 %collective-permute-done.38.refs_2_ = f32[16,256]{1,0:T(8,128)S(1)} collective-permute-done((f32[16,256]{1,0:T(8,128)}, f32[16,256]{1,0:T(8,128)S(1)}, u32[]{:S(2)}, u32[]{:S(2)}) %collective-permute-start.38) | collective-permute-done | bytes 16416 | tf_op jit(solution)/shard_map/ppermute | solution.py:348
  125.4 3.4 %collective-permute-done.39.refs_3_ = f32[16,256]{1,0:T(8,128)S(1)} collective-permute-done((f32[16,256]{1,0:T(8,128)}, f32[16,256]{1,0:T(8,128)S(1)}, u32[]{:S(2)}, u32[]{:S(2)}) %collective-permute-start.39) | collective-permute-done | bytes 16416 | tf_op jit(solution)/shard_map/ppermute | solution.py:348
  128.8 0.6 copy-done.24
  129.4 2.7 %shard_map.108 = (f32[8,768]{1,0:T(8,128)}, f32[8,256]{1,0:T(8,128)}) custom-call(f32[16,256]{1,0:T(8,128)} %get-tuple-element.19.refs_0_, f32[16,256]{1,0:T(8,128)} %copy-done.22, f32[16,256]{1,0:T(8,128)} %copy-done.23, f32[16,256]{1,0:T(8,128)} %copy-done.24, f32[128,256]{1,0:T(8,128)} %get-tuple-element.23.refs_4_, s32[1,256]{1,0:T(1,128)} %bitcast.7, ...), custom_call_target="tpu_custom_call" | custom-call | tf_op jit(solution)/shard_map/pallas_call | solution.py:395
  132.1 1.4 collective-permute-start.41
  133.5 0.5 collective-permute-start.42
  133.9 2.0 %collective-permute-done.41 = f32[8,256]{1,0:T(8,128)S(1)} collective-permute-done((f32[8,256]{1,0:T(8,128)}, f32[8,256]{1,0:T(8,128)S(1)}, u32[]{:S(2)}, u32[]{:S(2)}) %collective-permute-start.41) | collective-permute-done | bytes 8224 | tf_op jit(solution)/shard_map/ppermute | solution.py:341
  135.9 0.8 collective-permute-done.42
  136.7 0.7 add_add_fusion.1
  137.5 1.0 collective-permute-start.44
  138.4 3.4 %collective-permute-start.45 = (f32[8,256]{1,0:T(8,128)S(1)}, f32[8,256]{1,0:T(8,128)S(1)}, u32[]{:S(2)}, u32[]{:S(2)}) collective-permute-start(f32[8,256]{1,0:T(8,128)S(1)} %add_add_fusion.1), channel_id=1, source_target_pairs={{0,12},{1,13},{2,14},{3,15},{4,8},{5,9},{6,10},{7,11},{8,4},{9,5},... | collective-permute-start | bytes 24584 | tf_op jit(solution)/shard_map/ppermute | solution.py:348
  141.8 0.2 collective-permute-done.44
  142.0 1.9 %collective-permute-done.45 = f32[8,256]{1,0:T(8,128)S(1)} collective-permute-done((f32[8,256]{1,0:T(8,128)S(1)}, f32[8,256]{1,0:T(8,128)S(1)}, u32[]{:S(2)}, u32[]{:S(2)}) %collective-permute-start.45) | collective-permute-done | bytes 8224 | tf_op jit(solution)/shard_map/ppermute | solution.py:348
  143.9 0.6 add_add_fusion
  (119 shorter events, 0.5 us)
Async XLA Ops:
  0.6 10.3 %collective-permute-start.18 = (bf16[16,8192]{1,0:T(8,128)(2,1)}, bf16[16,8192]{1,0:T(8,128)(2,1)S(1)}, u32[]{:S(2)}, u32[]{:S(2)}) collective-permute-start(bf16[16,8192]{1,0:T(8,128)(2,1)} %refs_0_.4), channel_id=1, source_target_pairs={{0,4},{1,5},{4,8},{5,9},{8,12},{9,13},{12,14},{13,15},{14,10},{15,... | collective-permute-start | bytes 786440 | tf_op jit(solution)/shard_map/ppermute | solution.py:118
  3.7 9.4 %collective-permute-start.20 = (bf16[16,8192]{1,0:T(8,128)(2,1)}, bf16[16,8192]{1,0:T(8,128)(2,1)S(1)}, u32[]{:S(2)}, u32[]{:S(2)}) collective-permute-start(bf16[16,8192]{1,0:T(8,128)(2,1)} %refs_0_.4), channel_id=1, source_target_pairs={{0,2},{1,3},{4,0},{5,1},{8,4},{9,5},{12,8},{13,9},{14,12},{15,13},... | collective-permute-start | bytes 786440 | tf_op jit(solution)/shard_map/ppermute | solution.py:118
  3.7 9.4 %collective-permute-start.17 = (bf16[16,8192]{1,0:T(8,128)(2,1)}, bf16[16,8192]{1,0:T(8,128)(2,1)S(1)}, u32[]{:S(2)}, u32[]{:S(2)}) collective-permute-start(bf16[16,8192]{1,0:T(8,128)(2,1)} %refs_0_.4), channel_id=1, source_target_pairs={{0,1},{1,0},{2,3},{3,2},{4,5},{5,4},{6,7},{7,6},{8,9},{9,8},{10,11... | collective-permute-start | bytes 786440 | tf_op jit(solution)/shard_map/ppermute | solution.py:122
  3.7 12.9 %collective-permute-start.1 = (bf16[16,8192]{1,0:T(8,128)(2,1)}, bf16[16,8192]{1,0:T(8,128)(2,1)S(1)}, u32[]{:S(2)}, u32[]{:S(2)}) collective-permute-start(bf16[16,8192]{1,0:T(8,128)(2,1)} %refs_0_.5), channel_id=1, source_target_pairs={{0,4},{1,5},{4,8},{5,9},{8,12},{9,13},{12,14},{13,15},{14,10},{15,... | collective-permute-start | bytes 786440 | tf_op jit(solution)/shard_map/ppermute | solution.py:118
  5.7 13.0 %collective-permute-start.3 = (bf16[16,8192]{1,0:T(8,128)(2,1)}, bf16[16,8192]{1,0:T(8,128)(2,1)S(1)}, u32[]{:S(2)}, u32[]{:S(2)}) collective-permute-start(bf16[16,8192]{1,0:T(8,128)(2,1)} %refs_0_.5), channel_id=1, source_target_pairs={{0,2},{1,3},{4,0},{5,1},{8,4},{9,5},{12,8},{13,9},{14,12},{15,13},... | collective-permute-start | bytes 786440 | tf_op jit(solution)/shard_map/ppermute | solution.py:118
  11.0 36.7 %copy-start.25 = (bf16[16,8192]{1,0:T(8,128)(2,1)}, bf16[16,8192]{1,0:T(8,128)(2,1)S(1)}, u32[]{:S(2)}) copy-start(bf16[16,8192]{1,0:T(8,128)(2,1)S(1)} %collective-permute-done.18.refs_2_) | copy-start | bytes 786436
  11.0 11.2 %collective-permute-start.22 = (bf16[16,8192]{1,0:T(8,128)(2,1)S(1)}, bf16[16,8192]{1,0:T(8,128)(2,1)S(1)}, u32[]{:S(2)}, u32[]{:S(2)}) collective-permute-start(bf16[16,8192]{1,0:T(8,128)(2,1)S(1)} %collective-permute-done.18.refs_2_), channel_id=1, source_target_pairs={{0,4},{1,5},{4,8},{5,9},{8,12},{9,13},{12,14},{13,15},{14,10},{15,... | collective-permute-start | bytes 786440 | tf_op jit(solution)/shard_map/ppermute | solution.py:118
  13.1 34.6 %copy-start.26 = (bf16[16,8192]{1,0:T(8,128)(2,1)}, bf16[16,8192]{1,0:T(8,128)(2,1)S(1)}, u32[]{:S(2)}) copy-start(bf16[16,8192]{1,0:T(8,128)(2,1)S(1)} %collective-permute-done.20.refs_4_) | copy-start | bytes 786436
  13.1 11.2 %collective-permute-start.24 = (bf16[16,8192]{1,0:T(8,128)(2,1)S(1)}, bf16[16,8192]{1,0:T(8,128)(2,1)S(1)}, u32[]{:S(2)}, u32[]{:S(2)}) collective-permute-start(bf16[16,8192]{1,0:T(8,128)(2,1)S(1)} %collective-permute-done.20.refs_4_), channel_id=1, source_target_pairs={{0,2},{1,3},{4,0},{5,1},{8,4},{9,5},{12,8},{13,9},{14,12},{15,13},... | collective-permute-start | bytes 786440 | tf_op jit(solution)/shard_map/ppermute | solution.py:118
  13.2 34.5 %copy-start.27 = (bf16[16,8192]{1,0:T(8,128)(2,1)}, bf16[16,8192]{1,0:T(8,128)(2,1)S(1)}, u32[]{:S(2)}) copy-start(bf16[16,8192]{1,0:T(8,128)(2,1)S(1)} %collective-permute-done.17.refs_1_) | copy-start | bytes 786436
  13.2 11.2 %collective-permute-start = (bf16[16,8192]{1,0:T(8,128)(2,1)}, bf16[16,8192]{1,0:T(8,128)(2,1)S(1)}, u32[]{:S(2)}, u32[]{:S(2)}) collective-permute-start(bf16[16,8192]{1,0:T(8,128)(2,1)} %refs_0_.5), channel_id=1, source_target_pairs={{0,1},{1,0},{2,3},{3,2},{4,5},{5,4},{6,7},{7,6},{8,9},{9,8},{10,11... | collective-permute-start | bytes 786440 | tf_op jit(solution)/shard_map/ppermute | solution.py:122
  16.6 71.1 %copy-start.2 = (bf16[16,8192]{1,0:T(8,128)(2,1)}, bf16[16,8192]{1,0:T(8,128)(2,1)S(1)}, u32[]{:S(2)}) copy-start(bf16[16,8192]{1,0:T(8,128)(2,1)S(1)} %collective-permute-done.1.refs_2_) | copy-start | bytes 786436
  16.6 11.2 %collective-permute-start.5 = (bf16[16,8192]{1,0:T(8,128)(2,1)S(1)}, bf16[16,8192]{1,0:T(8,128)(2,1)S(1)}, u32[]{:S(2)}, u32[]{:S(2)}) collective-permute-start(bf16[16,8192]{1,0:T(8,128)(2,1)S(1)} %collective-permute-done.1.refs_2_), channel_id=1, source_target_pairs={{0,4},{1,5},{4,8},{5,9},{8,12},{9,13},{12,14},{13,15},{14,10},{15,... | collective-permute-start | bytes 786440 | tf_op jit(solution)/shard_map/ppermute | solution.py:118
  18.8 68.9 %copy-start.3 = (bf16[16,8192]{1,0:T(8,128)(2,1)}, bf16[16,8192]{1,0:T(8,128)(2,1)S(1)}, u32[]{:S(2)}) copy-start(bf16[16,8192]{1,0:T(8,128)(2,1)S(1)} %collective-permute-done.3.refs_4_) | copy-start | bytes 786436
  18.8 11.2 %collective-permute-start.7 = (bf16[16,8192]{1,0:T(8,128)(2,1)S(1)}, bf16[16,8192]{1,0:T(8,128)(2,1)S(1)}, u32[]{:S(2)}, u32[]{:S(2)}) collective-permute-start(bf16[16,8192]{1,0:T(8,128)(2,1)S(1)} %collective-permute-done.3.refs_4_), channel_id=1, source_target_pairs={{0,2},{1,3},{4,0},{5,1},{8,4},{9,5},{12,8},{13,9},{14,12},{15,13},... | collective-permute-start | bytes 786440 | tf_op jit(solution)/shard_map/ppermute | solution.py:118
  22.2 25.5 %copy-start.28 = (bf16[16,8192]{1,0:T(8,128)(2,1)}, bf16[16,8192]{1,0:T(8,128)(2,1)S(1)}, u32[]{:S(2)}) copy-start(bf16[16,8192]{1,0:T(8,128)(2,1)S(1)} %collective-permute-done.22.refs_6_) | copy-start | bytes 786436
  22.2 10.4 %collective-permute-start.26 = (bf16[16,8192]{1,0:T(8,128)(2,1)S(1)}, bf16[16,8192]{1,0:T(8,128)(2,1)S(1)}, u32[]{:S(2)}, u32[]{:S(2)}) collective-permute-start(bf16[16,8192]{1,0:T(8,128)(2,1)S(1)} %collective-permute-done.22.refs_6_), channel_id=1, source_target_pairs={{0,4},{1,5},{4,8},{5,9},{8,12},{9,13},{12,14},{13,15},{14,10},{15,... | collective-permute-start | bytes 786440 | tf_op jit(solution)/shard_map/ppermute | solution.py:118
  24.4 23.3 %copy-start.29 = (bf16[16,8192]{1,0:T(8,128)(2,1)}, bf16[16,8192]{1,0:T(8,128)(2,1)S(1)}, u32[]{:S(2)}) copy-start(bf16[16,8192]{1,0:T(8,128)(2,1)S(1)} %collective-permute-done.24.refs_8_) | copy-start | bytes 786436
  24.4 10.1 %collective-permute-start.28 = (bf16[16,8192]{1,0:T(8,128)(2,1)S(1)}, bf16[16,8192]{1,0:T(8,128)(2,1)S(1)}, u32[]{:S(2)}, u32[]{:S(2)}) collective-permute-start(bf16[16,8192]{1,0:T(8,128)(2,1)S(1)} %collective-permute-done.24.refs_8_), channel_id=1, source_target_pairs={{0,2},{1,3},{4,0},{5,1},{8,4},{9,5},{12,8},{13,9},{14,12},{15,13},... | collective-permute-start | bytes 786440 | tf_op jit(solution)/shard_map/ppermute | solution.py:118
  24.4 63.3 %copy-start.4 = (bf16[16,8192]{1,0:T(8,128)(2,1)}, bf16[16,8192]{1,0:T(8,128)(2,1)S(1)}, u32[]{:S(2)}) copy-start(bf16[16,8192]{1,0:T(8,128)(2,1)S(1)} %collective-permute-done.refs_1_) | copy-start | bytes 786436
  24.4 10.3 %collective-permute-start.19 = (bf16[16,8192]{1,0:T(8,128)(2,1)S(1)}, bf16[16,8192]{1,0:T(8,128)(2,1)S(1)}, u32[]{:S(2)}, u32[]{:S(2)}) collective-permute-start(bf16[16,8192]{1,0:T(8,128)(2,1)S(1)} %collective-permute-done.18.refs_2_), channel_id=1, source_target_pairs={{0,1},{1,0},{2,3},{3,2},{4,5},{5,4},{6,7},{7,6},{8,9},{9,8},{10,11... | collective-permute-start | bytes 786440 | tf_op jit(solution)/shard_map/ppermute | solution.py:122
  27.8 59.9 %copy-start.5 = (bf16[16,8192]{1,0:T(8,128)(2,1)}, bf16[16,8192]{1,0:T(8,128)(2,1)S(1)}, u32[]{:S(2)}) copy-start(bf16[16,8192]{1,0:T(8,128)(2,1)S(1)} %collective-permute-done.5.refs_6_) | copy-start | bytes 786436
  27.8 7.0 %collective-permute-start.21 = (bf16[16,8192]{1,0:T(8,128)(2,1)S(1)}, bf16[16,8192]{1,0:T(8,128)(2,1)S(1)}, u32[]{:S(2)}, u32[]{:S(2)}) collective-permute-start(bf16[16,8192]{1,0:T(8,128)(2,1)S(1)} %collective-permute-done.20.refs_4_), channel_id=1, source_target_pairs={{0,1},{1,0},{2,3},{3,2},{4,5},{5,4},{6,7},{7,6},{8,9},{9,8},{10,11... | collective-permute-start | bytes 786440 | tf_op jit(solution)/shard_map/ppermute | solution.py:122
  30.0 57.7 %copy-start.6 = (bf16[16,8192]{1,0:T(8,128)(2,1)}, bf16[16,8192]{1,0:T(8,128)(2,1)S(1)}, u32[]{:S(2)}) copy-start(bf16[16,8192]{1,0:T(8,128)(2,1)S(1)} %collective-permute-done.7.refs_8_) | copy-start | bytes 786436
  30.0 6.7 %collective-permute-start.23 = (bf16[16,8192]{1,0:T(8,128)(2,1)S(1)}, bf16[16,8192]{1,0:T(8,128)(2,1)S(1)}, u32[]{:S(2)}, u32[]{:S(2)}) collective-permute-start(bf16[16,8192]{1,0:T(8,128)(2,1)S(1)} %collective-permute-done.22.refs_6_), channel_id=1, source_target_pairs={{0,1},{1,0},{2,3},{3,2},{4,5},{5,4},{6,7},{7,6},{8,9},{9,8},{10,11... | collective-permute-start | bytes 786440 | tf_op jit(solution)/shard_map/ppermute | solution.py:122
  32.6 15.1 %copy-start.17 = (bf16[16,8192]{1,0:T(8,128)(2,1)}, bf16[16,8192]{1,0:T(8,128)(2,1)S(1)}, u32[]{:S(2)}) copy-start(bf16[16,8192]{1,0:T(8,128)(2,1)S(1)} %collective-permute-done.26.refs_10_) | copy-start | bytes 786436
  32.6 8.9 %collective-permute-start.9 = (bf16[16,8192]{1,0:T(8,128)(2,1)S(1)}, bf16[16,8192]{1,0:T(8,128)(2,1)S(1)}, u32[]{:S(2)}, u32[]{:S(2)}) collective-permute-start(bf16[16,8192]{1,0:T(8,128)(2,1)S(1)} %collective-permute-done.5.refs_6_), channel_id=1, source_target_pairs={{0,4},{1,5},{4,8},{5,9},{8,12},{9,13},{12,14},{13,15},{14,10},{15,... | collective-permute-start | bytes 786440 | tf_op jit(solution)/shard_map/ppermute | solution.py:118
  34.4 8.3 %collective-permute-start.11 = (bf16[16,8192]{1,0:T(8,128)(2,1)S(1)}, bf16[16,8192]{1,0:T(8,128)(2,1)S(1)}, u32[]{:S(2)}, u32[]{:S(2)}) collective-permute-start(bf16[16,8192]{1,0:T(8,128)(2,1)S(1)} %collective-permute-done.7.refs_8_), channel_id=1, source_target_pairs={{0,2},{1,3},{4,0},{5,1},{8,4},{9,5},{12,8},{13,9},{14,12},{15,13},... | collective-permute-start | bytes 786440 | tf_op jit(solution)/shard_map/ppermute | solution.py:118
  34.7 9.5 %collective-permute-start.25 = (bf16[16,8192]{1,0:T(8,128)(2,1)S(1)}, bf16[16,8192]{1,0:T(8,128)(2,1)S(1)}, u32[]{:S(2)}, u32[]{:S(2)}) collective-permute-start(bf16[16,8192]{1,0:T(8,128)(2,1)S(1)} %collective-permute-done.24.refs_8_), channel_id=1, source_target_pairs={{0,1},{1,0},{2,3},{3,2},{4,5},{5,4},{6,7},{7,6},{8,9},{9,8},{10,11... | collective-permute-start | bytes 786440 | tf_op jit(solution)/shard_map/ppermute | solution.py:122
  34.8 8.1 %collective-permute-start.30 = (bf16[16,4096]{1,0:T(8,128)(2,1)S(1)}, bf16[16,4096]{1,0:T(8,128)(2,1)S(1)}, u32[]{:S(2)}, u32[]{:S(2)}) collective-permute-start(bf16[16,4096]{1,0:T(8,128)(2,1)S(1)} %slice.18), channel_id=1, source_target_pairs={{0,4},{1,5},{4,8},{5,9},{8,12},{9,13},{12,14},{13,15},{14,10},{15,... | collective-permute-start | bytes 393224 | tf_op jit(solution)/shard_map/ppermute | solution.py:118
  36.7 7.5 %collective-permute-start.32 = (bf16[16,4096]{1,0:T(8,128)(2,1)S(1)}, bf16[16,4096]{1,0:T(8,128)(2,1)S(1)}, u32[]{:S(2)}, u32[]{:S(2)}) collective-permute-start(bf16[16,4096]{1,0:T(8,128)(2,1)S(1)} %slice.19), channel_id=1, source_target_pairs={{0,2},{1,3},{4,0},{5,1},{8,4},{9,5},{12,8},{13,9},{14,12},{15,13},... | collective-permute-start | bytes 393224 | tf_op jit(solution)/shard_map/ppermute | solution.py:118
  41.5 46.2 %copy-start = (bf16[16,8192]{1,0:T(8,128)(2,1)}, bf16[16,8192]{1,0:T(8,128)(2,1)S(1)}, u32[]{:S(2)}) copy-start(bf16[16,8192]{1,0:T(8,128)(2,1)S(1)} %collective-permute-done.9.refs_10_) | copy-start | bytes 786436
  41.5 4.1 %collective-permute-start.27 = (bf16[16,8192]{1,0:T(8,128)(2,1)S(1)}, bf16[16,8192]{1,0:T(8,128)(2,1)S(1)}, u32[]{:S(2)}, u32[]{:S(2)}) collective-permute-start(bf16[16,8192]{1,0:T(8,128)(2,1)S(1)} %collective-permute-done.26.refs_10_), channel_id=1, source_target_pairs={{0,1},{1,0},{2,3},{3,2},{4,5},{5,4},{6,7},{7,6},{8,9},{9,8},{10,11... | collective-permute-start | bytes 786440 | tf_op jit(solution)/shard_map/ppermute | solution.py:122
  42.7 45.0 %copy-start.1 = (bf16[16,8192]{1,0:T(8,128)(2,1)}, bf16[16,8192]{1,0:T(8,128)(2,1)S(1)}, u32[]{:S(2)}) copy-start(bf16[16,8192]{1,0:T(8,128)(2,1)S(1)} %collective-permute-done.11.refs_12_) | copy-start | bytes 786436
  42.7 4.5 %collective-permute-start.29 = (bf16[16,8192]{1,0:T(8,128)(2,1)S(1)}, bf16[16,8192]{1,0:T(8,128)(2,1)S(1)}, u32[]{:S(2)}, u32[]{:S(2)}) collective-permute-start(bf16[16,8192]{1,0:T(8,128)(2,1)S(1)} %collective-permute-done.28.refs_12_), channel_id=1, source_target_pairs={{0,1},{1,0},{2,3},{3,2},{4,5},{5,4},{6,7},{7,6},{8,9},{9,8},{10,11... | collective-permute-start | bytes 786440 | tf_op jit(solution)/shard_map/ppermute | solution.py:122
  42.9 1.9 %collective-permute-start.31 = (bf16[16,4096]{1,0:T(8,128)(2,1)S(1)}, bf16[16,4096]{1,0:T(8,128)(2,1)S(1)}, u32[]{:S(2)}, u32[]{:S(2)}) collective-permute-start(bf16[16,4096]{1,0:T(8,128)(2,1)S(1)} %collective-permute-done.30.refs_14_), channel_id=1, source_target_pairs={{0,1},{1,0},{2,3},{3,2},{4,5},{5,4},{6,7},{7,6},{8,9},{9,8},{10,11... | collective-permute-start | bytes 393224 | tf_op jit(solution)/shard_map/ppermute | solution.py:122
  44.1 1.3 collective-permute-start.33
  44.2 21.8 %collective-permute-start.2 = (bf16[16,8192]{1,0:T(8,128)(2,1)S(1)}, bf16[16,8192]{1,0:T(8,128)(2,1)S(1)}, u32[]{:S(2)}, u32[]{:S(2)}) collective-permute-start(bf16[16,8192]{1,0:T(8,128)(2,1)S(1)} %collective-permute-done.1.refs_2_), channel_id=1, source_target_pairs={{0,1},{1,0},{2,3},{3,2},{4,5},{5,4},{6,7},{7,6},{8,9},{9,8},{10,11... | collective-permute-start | bytes 786440 | tf_op jit(solution)/shard_map/ppermute | solution.py:122
  44.8 21.4 %collective-permute-start.4 = (bf16[16,8192]{1,0:T(8,128)(2,1)S(1)}, bf16[16,8192]{1,0:T(8,128)(2,1)S(1)}, u32[]{:S(2)}, u32[]{:S(2)}) collective-permute-start(bf16[16,8192]{1,0:T(8,128)(2,1)S(1)} %collective-permute-done.3.refs_4_), channel_id=1, source_target_pairs={{0,1},{1,0},{2,3},{3,2},{4,5},{5,4},{6,7},{7,6},{8,9},{9,8},{10,11... | collective-permute-start | bytes 786440 | tf_op jit(solution)/shard_map/ppermute | solution.py:122
  45.5 21.1 %collective-permute-start.6 = (bf16[16,8192]{1,0:T(8,128)(2,1)S(1)}, bf16[16,8192]{1,0:T(8,128)(2,1)S(1)}, u32[]{:S(2)}, u32[]{:S(2)}) collective-permute-start(bf16[16,8192]{1,0:T(8,128)(2,1)S(1)} %collective-permute-done.5.refs_6_), channel_id=1, source_target_pairs={{0,1},{1,0},{2,3},{3,2},{4,5},{5,4},{6,7},{7,6},{8,9},{9,8},{10,11... | collective-permute-start | bytes 786440 | tf_op jit(solution)/shard_map/ppermute | solution.py:122
  45.7 21.0 %collective-permute-start.13 = (bf16[16,4096]{1,0:T(8,128)(2,1)S(1)}, bf16[16,4096]{1,0:T(8,128)(2,1)S(1)}, u32[]{:S(2)}, u32[]{:S(2)}) collective-permute-start(bf16[16,4096]{1,0:T(8,128)(2,1)S(1)} %slice.16), channel_id=1, source_target_pairs={{0,4},{1,5},{4,8},{5,9},{8,12},{9,13},{12,14},{13,15},{14,10},{15,... | collective-permute-start | bytes 393224 | tf_op jit(solution)/shard_map/ppermute | solution.py:118
  47.2 19.9 %collective-permute-start.15 = (bf16[16,4096]{1,0:T(8,128)(2,1)S(1)}, bf16[16,4096]{1,0:T(8,128)(2,1)S(1)}, u32[]{:S(2)}, u32[]{:S(2)}) collective-permute-start(bf16[16,4096]{1,0:T(8,128)(2,1)S(1)} %slice.17), channel_id=1, source_target_pairs={{0,2},{1,3},{4,0},{5,1},{8,4},{9,5},{12,8},{13,9},{14,12},{15,13},... | collective-permute-start | bytes 393224 | tf_op jit(solution)/shard_map/ppermute | solution.py:118
  66.0 21.8 %copy-start.7 = (bf16[16,8192]{1,0:T(8,128)(2,1)}, bf16[16,8192]{1,0:T(8,128)(2,1)S(1)}, u32[]{:S(2)}) copy-start(bf16[16,8192]{1,0:T(8,128)(2,1)S(1)} %collective-permute-done.2.refs_3_) | copy-start | bytes 786436
  66.0 21.7 %collective-permute-start.8 = (bf16[16,8192]{1,0:T(8,128)(2,1)S(1)}, bf16[16,8192]{1,0:T(8,128)(2,1)S(1)}, u32[]{:S(2)}, u32[]{:S(2)}) collective-permute-start(bf16[16,8192]{1,0:T(8,128)(2,1)S(1)} %collective-permute-done.7.refs_8_), channel_id=1, source_target_pairs={{0,1},{1,0},{2,3},{3,2},{4,5},{5,4},{6,7},{7,6},{8,9},{9,8},{10,11... | collective-permute-start | bytes 786440 | tf_op jit(solution)/shard_map/ppermute | solution.py:122
  66.1 21.7 %copy-start.8 = (bf16[16,8192]{1,0:T(8,128)(2,1)}, bf16[16,8192]{1,0:T(8,128)(2,1)S(1)}, u32[]{:S(2)}) copy-start(bf16[16,8192]{1,0:T(8,128)(2,1)S(1)} %collective-permute-done.4.refs_5_) | copy-start | bytes 786436
  66.1 21.6 %collective-permute-start.10 = (bf16[16,8192]{1,0:T(8,128)(2,1)S(1)}, bf16[16,8192]{1,0:T(8,128)(2,1)S(1)}, u32[]{:S(2)}, u32[]{:S(2)}) collective-permute-start(bf16[16,8192]{1,0:T(8,128)(2,1)S(1)} %collective-permute-done.9.refs_10_), channel_id=1, source_target_pairs={{0,1},{1,0},{2,3},{3,2},{4,5},{5,4},{6,7},{7,6},{8,9},{9,8},{10,11... | collective-permute-start | bytes 786440 | tf_op jit(solution)/shard_map/ppermute | solution.py:122
  66.6 21.3 %copy-start.9 = (bf16[16,8192]{1,0:T(8,128)(2,1)}, bf16[16,8192]{1,0:T(8,128)(2,1)S(1)}, u32[]{:S(2)}) copy-start(bf16[16,8192]{1,0:T(8,128)(2,1)S(1)} %collective-permute-done.6.refs_7_) | copy-start | bytes 786436
  66.6 21.2 %collective-permute-start.12 = (bf16[16,8192]{1,0:T(8,128)(2,1)S(1)}, bf16[16,8192]{1,0:T(8,128)(2,1)S(1)}, u32[]{:S(2)}, u32[]{:S(2)}) collective-permute-start(bf16[16,8192]{1,0:T(8,128)(2,1)S(1)} %collective-permute-done.11.refs_12_), channel_id=1, source_target_pairs={{0,1},{1,0},{2,3},{3,2},{4,5},{5,4},{6,7},{7,6},{8,9},{9,8},{10,11... | collective-permute-start | bytes 786440 | tf_op jit(solution)/shard_map/ppermute | solution.py:122
  66.7 21.2 %copy-start.13 = (bf16[16,4096]{1,0:T(8,128)(2,1)}, bf16[16,4096]{1,0:T(8,128)(2,1)S(1)}, u32[]{:S(2)}) copy-start(bf16[16,4096]{1,0:T(8,128)(2,1)S(1)} %collective-permute-done.13.refs_14_) | copy-start | bytes 393220
  66.7 21.1 %collective-permute-start.14 = (bf16[16,4096]{1,0:T(8,128)(2,1)S(1)}, bf16[16,4096]{1,0:T(8,128)(2,1)S(1)}, u32[]{:S(2)}, u32[]{:S(2)}) collective-permute-start(bf16[16,4096]{1,0:T(8,128)(2,1)S(1)} %collective-permute-done.13.refs_14_), channel_id=1, source_target_pairs={{0,1},{1,0},{2,3},{3,2},{4,5},{5,4},{6,7},{7,6},{8,9},{9,8},{10,11... | collective-permute-start | bytes 393224 | tf_op jit(solution)/shard_map/ppermute | solution.py:122
  67.1 20.8 %copy-start.14 = (bf16[16,4096]{1,0:T(8,128)(2,1)}, bf16[16,4096]{1,0:T(8,128)(2,1)S(1)}, u32[]{:S(2)}) copy-start(bf16[16,4096]{1,0:T(8,128)(2,1)S(1)} %collective-permute-done.15.refs_16_) | copy-start | bytes 393220
  67.1 20.6 %collective-permute-start.16 = (bf16[16,4096]{1,0:T(8,128)(2,1)S(1)}, bf16[16,4096]{1,0:T(8,128)(2,1)S(1)}, u32[]{:S(2)}, u32[]{:S(2)}) collective-permute-start(bf16[16,4096]{1,0:T(8,128)(2,1)S(1)} %collective-permute-done.15.refs_16_), channel_id=1, source_target_pairs={{0,1},{1,0},{2,3},{3,2},{4,5},{5,4},{6,7},{7,6},{8,9},{9,8},{10,11... | collective-permute-start | bytes 393224 | tf_op jit(solution)/shard_map/ppermute | solution.py:122
  111.1 1.9 %collective-permute-start.34 = (f32[4,16,256]{2,1,0:T(8,128)}, f32[4,16,256]{2,1,0:T(8,128)S(1)}, u32[]{:S(2)}, u32[]{:S(2)}) collective-permute-start(f32[4,16,256]{2,1,0:T(8,128)} %get-tuple-element.16), channel_id=1, source_target_pairs={{0,1},{1,0},{2,3},{3,2},{4,5},{5,4},{6,7},{7,6},{8,9},{9,8},{10,11... | collective-permute-start | bytes 196616 | tf_op jit(solution)/shard_map/ppermute | solution.py:341
  111.6 5.1 %collective-permute-start.35 = (f32[4,16,256]{2,1,0:T(8,128)}, f32[4,16,256]{2,1,0:T(8,128)S(1)}, u32[]{:S(2)}, u32[]{:S(2)}) collective-permute-start(f32[4,16,256]{2,1,0:T(8,128)} %get-tuple-element.17), channel_id=1, source_target_pairs={{0,2},{1,3},{2,0},{3,1},{4,6},{5,7},{6,4},{7,5},{8,10},{9,11},{10,... | collective-permute-start | bytes 196616 | tf_op jit(solution)/shard_map/ppermute | solution.py:341
  112.0 4.6 %collective-permute-start.36 = (f32[4,16,256]{2,1,0:T(8,128)}, f32[4,16,256]{2,1,0:T(8,128)S(1)}, u32[]{:S(2)}, u32[]{:S(2)}) collective-permute-start(f32[4,16,256]{2,1,0:T(8,128)} %get-tuple-element.18), channel_id=1, source_target_pairs={{0,3},{1,2},{2,1},{3,0},{4,7},{5,6},{6,5},{7,4},{8,11},{9,10},{10,... | collective-permute-start | bytes 196616 | tf_op jit(solution)/shard_map/ppermute | solution.py:341
  118.9 4.4 %collective-permute-start.37 = (f32[16,256]{1,0:T(8,128)}, f32[16,256]{1,0:T(8,128)S(1)}, u32[]{:S(2)}, u32[]{:S(2)}) collective-permute-start(f32[16,256]{1,0:T(8,128)} %get-tuple-element.20), channel_id=1, source_target_pairs={{0,4},{1,5},{2,6},{3,7},{4,0},{5,1},{6,2},{7,3},{8,12},{9,13},{10,... | collective-permute-start | bytes 49160 | tf_op jit(solution)/shard_map/ppermute | solution.py:348
  120.4 4.9 %collective-permute-start.38 = (f32[16,256]{1,0:T(8,128)}, f32[16,256]{1,0:T(8,128)S(1)}, u32[]{:S(2)}, u32[]{:S(2)}) collective-permute-start(f32[16,256]{1,0:T(8,128)} %get-tuple-element.21), channel_id=1, source_target_pairs={{0,8},{1,9},{2,10},{3,11},{4,12},{5,13},{6,14},{7,15},{8,0},{9,1},... | collective-permute-start | bytes 49160 | tf_op jit(solution)/shard_map/ppermute | solution.py:348
  123.0 5.7 %collective-permute-start.39 = (f32[16,256]{1,0:T(8,128)}, f32[16,256]{1,0:T(8,128)S(1)}, u32[]{:S(2)}, u32[]{:S(2)}) collective-permute-start(f32[16,256]{1,0:T(8,128)} %get-tuple-element.22), channel_id=1, source_target_pairs={{0,12},{1,13},{2,14},{3,15},{4,8},{5,9},{6,10},{7,11},{8,4},{9,5},... | collective-permute-start | bytes 49160 | tf_op jit(solution)/shard_map/ppermute | solution.py:348
  132.1 1.9 %collective-permute-start.40 = (f32[8,256]{1,0:T(8,128)}, f32[8,256]{1,0:T(8,128)S(1)}, u32[]{:S(2)}, u32[]{:S(2)}) collective-permute-start(f32[8,256]{1,0:T(8,128)} %get-tuple-element.25), channel_id=1, source_target_pairs={{0,1},{1,0},{2,3},{3,2},{4,5},{5,4},{6,7},{7,6},{8,9},{9,8},{10,11... | collective-permute-start | bytes 24584 | tf_op jit(solution)/shard_map/ppermute | solution.py:341
  132.1 3.9 %collective-permute-start.41 = (f32[8,256]{1,0:T(8,128)}, f32[8,256]{1,0:T(8,128)S(1)}, u32[]{:S(2)}, u32[]{:S(2)}) collective-permute-start(f32[8,256]{1,0:T(8,128)} %get-tuple-element.25), channel_id=1, source_target_pairs={{0,2},{1,3},{2,0},{3,1},{4,6},{5,7},{6,4},{7,5},{8,10},{9,11},{10,... | collective-permute-start | bytes 24584 | tf_op jit(solution)/shard_map/ppermute | solution.py:341
  133.5 3.3 %collective-permute-start.42 = (f32[8,256]{1,0:T(8,128)}, f32[8,256]{1,0:T(8,128)S(1)}, u32[]{:S(2)}, u32[]{:S(2)}) collective-permute-start(f32[8,256]{1,0:T(8,128)} %get-tuple-element.25), channel_id=1, source_target_pairs={{0,3},{1,2},{2,1},{3,0},{4,7},{5,6},{6,5},{7,4},{8,11},{9,10},{10,... | collective-permute-start | bytes 24584 | tf_op jit(solution)/shard_map/ppermute | solution.py:341
  137.5 4.4 %collective-permute-start.43 = (f32[8,256]{1,0:T(8,128)S(1)}, f32[8,256]{1,0:T(8,128)S(1)}, u32[]{:S(2)}, u32[]{:S(2)}) collective-permute-start(f32[8,256]{1,0:T(8,128)S(1)} %add_add_fusion.1), channel_id=1, source_target_pairs={{0,4},{1,5},{2,6},{3,7},{4,0},{5,1},{6,2},{7,3},{8,12},{9,13},{10,... | collective-permute-start | bytes 24584 | tf_op jit(solution)/shard_map/ppermute | solution.py:348
  137.5 4.5 %collective-permute-start.44 = (f32[8,256]{1,0:T(8,128)S(1)}, f32[8,256]{1,0:T(8,128)S(1)}, u32[]{:S(2)}, u32[]{:S(2)}) collective-permute-start(f32[8,256]{1,0:T(8,128)S(1)} %add_add_fusion.1), channel_id=1, source_target_pairs={{0,8},{1,9},{2,10},{3,11},{4,12},{5,13},{6,14},{7,15},{8,0},{9,1},... | collective-permute-start | bytes 24584 | tf_op jit(solution)/shard_map/ppermute | solution.py:348
  138.4 5.4 %collective-permute-start.45 = (f32[8,256]{1,0:T(8,128)S(1)}, f32[8,256]{1,0:T(8,128)S(1)}, u32[]{:S(2)}, u32[]{:S(2)}) collective-permute-start(f32[8,256]{1,0:T(8,128)S(1)} %add_add_fusion.1), channel_id=1, source_target_pairs={{0,12},{1,13},{2,14},{3,15},{4,8},{5,9},{6,10},{7,11},{8,4},{9,5},... | collective-permute-start | bytes 24584 | tf_op jit(solution)/shard_map/ppermute | solution.py:348
  (22 other events, 89.2 us)

commit v4 on v1

--- a/solution.py
+++ b/solution.py
@@ -11,6 +11,7 @@
 EX_TOK = 32
 TILE = 256
 DEPTH = 2048
+SPLIT = 4
 VMEM = 56 * 1024 * 1024
 HIGH = lax.Precision.HIGHEST
 
@@ -121,23 +122,31 @@
     return lax.ppermute(block, "hid", [(h, h ^ 1) for h in range(2 * chips)])
 
 
-def gather_blocks(own, chips):
+def gather_blocks(own, chips, base=0):
     half = own.shape[1] // 2
-    found = [(0, 0, own)]
+    places, blocks, steps = [], [], []
+
+    def found(offset, column, block):
+        for other in range(2):
+            places.append((offset, other, base + column))
+            blocks.append(core_swap(block, chips) if other else block)
+
+    found(0, 0, own)
     ahead, behind = own, own
     for step in range(1, chips // 2):
         ahead = ring_step(ahead, chips, 1)
         behind = ring_step(behind, chips, -1)
-        found += [(-step, 0, ahead), (step, 0, behind)]
+        found(-step, 0, ahead)
+        found(step, 0, behind)
+        steps.append((ahead, behind))
     across = chips // 2
-    found.append((across, 0, ring_step(ahead[:, :half], chips, 1)))
-    found.append((across, half, ring_step(behind[:, half:], chips, -1)))
-    places, blocks = [], []
-    for offset, column, block in found:
-        for other in range(2):
-            places.append((offset, other, column))
-            blocks.append(core_swap(block, chips) if other else block)
-    return places, blocks
+    found(across, 0, ring_step(ahead[:, :half], chips, 1))
+    found(across, half, ring_step(behind[:, half:], chips, -1))
+    return places, blocks, steps
+
+
+def after(value, *others):
+    return lax.optimization_barrier((value, *others))[0]
 
 
 def assemble(places, chips, blocks, whole, sems):
@@ -157,51 +166,89 @@
         copy.wait()
 
 
-def deep_dot(left, right, transposed, columns):
-    depth = left.shape[1]
-    total = jnp.zeros((left.shape[0], columns), jnp.float32)
-    for start in range(0, depth, DEPTH):
-        part = pl.ds(start, DEPTH)
-        a = left[:, part]
-        if transposed:
-            total += lax.dot_general(
-                a, right[:, part], (((1,), (1,)), ((), ())), preferred_element_type=jnp.float32
-            )
-        else:
-            total += jnp.dot(a, right[part, :], preferred_element_type=jnp.float32)
+def last_dot(a, b):
+    return lax.dot_general(a, b, (((1,), (1,)), ((), ())), preferred_element_type=jnp.float32)
+
+
+def deep_dot(left, rights):
+    total, start = None, 0
+    for right in rights:
+        part = pl.ds(start, right.shape[0])
+        term = jnp.dot(left[:, part], right[...], preferred_element_type=jnp.float32)
+        total = term if total is None else total + term
+        start += right.shape[0]
     return total
 
 
 def forward_kernel(places, chips, *refs):
     count = len(places)
-    blocks, (weight, out, whole, sems) = refs[:count], refs[count:]
+    blocks, refs = refs[:count], refs[count:]
+    (gate, up, whole, sems), weights = refs[-4:], refs[: 2 * SPLIT]
 
     @pl.when(pl.program_id(0) == 0)
     def _():
         assemble(places, chips, blocks, whole, sems)
 
-    out[...] = deep_dot(whole, weight, False, out.shape[1])
-
-
-def forward(places, chips, blocks, weight, tile):
+    gate[...] = deep_dot(whole, weights[:SPLIT]).T
+    up[...] = deep_dot(whole, weights[SPLIT:]).T
+
+
+def forward(places, chips, blocks, gate_weight, up_weight, tile, first, tiles, waits):
+    depth = gate_weight.shape[0]
     rows = blocks[0].shape[0] * chips * 2
-    depth, width = weight.shape
     return pl.pallas_call(
         functools.partial(forward_kernel, places, chips),
-        grid=(width // tile,),
-        out_shape=jax.ShapeDtypeStruct((rows, width), jnp.float32),
+        grid=(tiles,),
+        out_shape=[jax.ShapeDtypeStruct((tiles * tile, rows), jnp.float32)] * 2,
         in_specs=[pl.BlockSpec(memory_space=pl.ANY)] * len(blocks)
-        + [pl.BlockSpec((depth, tile), lambda n: (0, n))],
-        out_specs=pl.BlockSpec((rows, tile), lambda n: (0, n)),
+        + [
+            pl.BlockSpec((depth // SPLIT, tile), lambda n, q=q: (q, n + first))
+            for q in range(SPLIT)
+        ]
+        * 2
+        + [pl.BlockSpec(memory_space=pl.ANY)] * len(waits),
+        out_specs=[pl.BlockSpec((tile, rows), lambda n: (n, 0))] * 2,
         scratch_shapes=[
             pltpu.VMEM((rows, depth), jnp.bfloat16),
             pltpu.SemaphoreType.DMA((len(blocks),)),
         ],
         compiler_params=pltpu.CompilerParams(vmem_limit_bytes=VMEM),
         cost_estimate=pl.CostEstimate(
-            flops=2 * rows * depth * width, bytes_accessed=2 * depth * width, transcendentals=0
+            flops=8 * rows * depth * tiles * tile,
+            bytes_accessed=8 * depth * tiles * tile,
+            transcendentals=0,
         ),
-    )(*blocks, weight)
+    )(*blocks, *[gate_weight] * SPLIT, *[up_weight] * SPLIT, *waits)
+
+
+def inputs_kernel(places, chips, *refs):
+    count = len(places)
+    blocks, (proj, out, whole, sems) = refs[:count], refs[count:]
+    assemble(places, chips, blocks, whole, sems)
+    total = jnp.zeros(out.shape, jnp.float32)
+    for start in range(0, whole.shape[1], DEPTH):
+        part = pl.ds(start, DEPTH)
+        total += last_dot(proj[: 2 * R, part], whole[:, part])
+    out[...] = total
+
+
+def project_inputs(places, chips, blocks, proj):
+    rows, depth = blocks[0].shape[0] * chips * 2, proj.shape[1]
+    vmem = pl.BlockSpec(memory_space=pltpu.VMEM)
+    return pl.pallas_call(
+        functools.partial(inputs_kernel, places, chips),
+        out_shape=jax.ShapeDtypeStruct((2 * R, rows), jnp.float32),
+        in_specs=[pl.BlockSpec(memory_space=pl.ANY)] * len(blocks) + [vmem],
+        out_specs=vmem,
+        scratch_shapes=[
+            pltpu.VMEM((rows, depth), jnp.bfloat16),
+            pltpu.SemaphoreType.DMA((len(blocks),)),
+        ],
+        compiler_params=pltpu.CompilerParams(vmem_limit_bytes=VMEM),
+        cost_estimate=pl.CostEstimate(
+            flops=16 * R * rows * depth, bytes_accessed=8 * R * depth, transcendentals=0
+        ),
+    )(*blocks, proj)
 
 
 def membership(ids, examples):
@@ -215,10 +262,13 @@
     )
 
 
-def backward_kernel(places, chips, examples, *refs):
+def backward_kernel(places, chips, examples, tile, parts, *refs):
     count = len(places)
-    blocks = refs[:count]
-    weight, gate, up, proj, proj_ff, ids, send, whole, sums, flipped, sems = refs[count:]
+    blocks, refs = refs[:count], refs[count:]
+    weights, refs = refs[:SPLIT], refs[SPLIT:]
+    proj, proj_ff, ids = refs[:3]
+    gates, ups = refs[3 : 3 + parts], refs[3 + parts : 3 + 2 * parts]
+    ready, whole, spread, flipped, sums, sems = refs[3 + 2 * parts :]
     step = pl.program_id(0)
     hid = 2 * chips
     shares = R // hid
@@ -226,64 +276,86 @@
     @pl.when(step == 0)
     def _():
         assemble(places, chips, blocks, whole, sems)
-        sums[...] = jnp.zeros_like(sums)
-        columns = deep_dot(whole, proj, False, R).T
-        for lanes in range(flipped.shape[0]):
-            flipped[lanes] = columns[:, lanes * 128 : (lanes + 1) * 128]
-
-    hidden_grad = deep_dot(whole, weight, True, gate.shape[1])
-    hidden, gate_grad, up_grad = pointwise(gate[...], up[...], hidden_grad)
-    for m, value in enumerate((gate_grad, up_grad, hidden)):
-        sums[m] += jnp.dot(
-            value, proj_ff[:, m * R : (m + 1) * R], preferred_element_type=jnp.float32
-        )
+        spread[...] = jnp.zeros_like(spread)
+        flipped[...] = jnp.zeros_like(flipped)
+
+    height, depth = weights[0].shape
+    x = whole[:, pl.ds(pl.multiple_of(step * depth, depth), depth)]
+    for q, weight in enumerate(weights):
+        spread[q * height : (q + 1) * height, :] += last_dot(weight[...], x)
+    turned = last_dot(proj[2 * R :, :], x)
+    for lanes in range(flipped.shape[0]):
+        flipped[lanes] += turned[:, lanes * 128 : (lanes + 1) * 128]
 
     @pl.when(step == pl.num_programs(0) - 1)
     def _():
+        sums[...] = jnp.zeros_like(sums)
+        start = 0
+        for gate, up in zip(gates, ups):
+            for local in range(0, gate.shape[0], tile):
+                part = pl.ds(local, tile)
+                hidden, gate_grad, up_grad = pointwise(
+                    gate[part, :], up[part, :], spread[start : start + tile, :]
+                )
+                for m, value in enumerate((gate_grad, up_grad, hidden)):
+                    sums[m * R : (m + 1) * R, :] += jnp.dot(
+                        proj_ff[m * R : (m + 1) * R, start : start + tile],
+                        value,
+                        preferred_element_type=jnp.float32,
+                    )
+                start += tile
         for m in range(2):
-            columns = sums[m].T
             for p in range(hid):
-                send[p, m * shares : (m + 1) * shares, :] = columns[p * shares : (p + 1) * shares]
+                own = sums[m * R + p * shares : m * R + (p + 1) * shares, :]
+                ready[p, m * shares : (m + 1) * shares, :] = own
         member = membership(ids[...], examples)
         total_rows = member.shape[1]
         for j in range(shares):
             every = pl.ds(j, hid, shares)
             own = jnp.concatenate([flipped[k, every, :] for k in range(flipped.shape[0])], axis=1)
             left = (own[:, None, :] * member[None, :, :]).reshape(hid * examples, total_rows)
-            product = exact_dot(left, sums[2], ((1,), (0,)))
-            send[:, 2 * shares :, j * R : (j + 1) * R] = product.reshape(hid, examples, R)
-
-
-def backward(places, chips, blocks, weight, gate, up, proj, proj_ff, ids, tile):
+            product = exact_dot(left, sums[2 * R :, :], ((1,), (1,)))
+            ready[:, 2 * shares :, j * R : (j + 1) * R] = product.reshape(hid, examples, R)
+
+
+def backward(places, chips, blocks, weight, gates, ups, proj, proj_ff, ids, depth_tile, tile):
     rows = blocks[0].shape[0] * chips * 2
     width, depth = weight.shape
     hid = 2 * chips
     shares, examples = R // hid, rows // EX_TOK
+    deep = 2 * shares + examples
+
+    def stay(*shape):
+        return pl.BlockSpec(shape, lambda k: (0,) * len(shape))
+
     return pl.pallas_call(
-        functools.partial(backward_kernel, places, chips, examples),
-        grid=(width // tile,),
-        out_shape=jax.ShapeDtypeStruct((hid, 2 * shares + examples, rows), jnp.float32),
+        functools.partial(backward_kernel, places, chips, examples, tile, len(gates)),
+        grid=(depth // depth_tile,),
+        out_shape=jax.ShapeDtypeStruct((hid, deep, rows), jnp.float32),
         in_specs=[pl.BlockSpec(memory_space=pl.ANY)] * len(blocks)
         + [
-            pl.BlockSpec((tile, depth), lambda n: (n, 0)),
-            pl.BlockSpec((rows, tile), lambda n: (0, n)),
-            pl.BlockSpec((rows, tile), lambda n: (0, n)),
-            pl.BlockSpec((depth, R), lambda n: (0, 0)),
-            pl.BlockSpec((tile, 3 * R), lambda n: (n, 0)),
-            pl.BlockSpec((1, rows), lambda n: (0, 0)),
-        ],
-        out_specs=pl.BlockSpec((hid, 2 * shares + examples, rows), lambda n: (0, 0, 0)),
+            pl.BlockSpec((width // SPLIT, depth_tile), lambda k, q=q: (q, k))
+            for q in range(SPLIT)
+        ]
+        + [
+            pl.BlockSpec((3 * R, depth_tile), lambda k: (0, k)),
+            stay(3 * R, width),
+            stay(1, rows),
+        ]
+        + [stay(*value.shape) for value in (*gates, *ups)],
+        out_specs=stay(hid, deep, rows),
         scratch_shapes=[
             pltpu.VMEM((rows, depth), jnp.bfloat16),
-            pltpu.VMEM((3, rows, R), jnp.float32),
+            pltpu.VMEM((width, rows), jnp.float32),
             pltpu.VMEM((rows // 128, R, 128), jnp.float32),
+            pltpu.VMEM((3 * R, rows), jnp.float32),
             pltpu.SemaphoreType.DMA((len(blocks),)),
         ],
         compiler_params=pltpu.CompilerParams(vmem_limit_bytes=VMEM),
         cost_estimate=pl.CostEstimate(
             flops=2 * rows * depth * width, bytes_accessed=2 * depth * width, transcendentals=0
         ),
-    )(*blocks, weight, gate, up, proj, proj_ff, ids)
+    )(*blocks, *[weight] * SPLIT, proj, proj_ff, ids, *gates, *ups)
 
 
 def features_kernel(hid, received, inputs, ids, tests, features, partial):
@@ -294,7 +366,7 @@
     for m in range(2):
         own = total[m * shares : (m + 1) * shares]
         left = (own[:, None, :] * member[None, :, :]).reshape(shares * examples, own.shape[1])
-        product = exact_dot(left, inputs[:, m * R : (m + 1) * R], ((1,), (0,)))
+        product = exact_dot(left, inputs[m * R : (m + 1) * R, :], ((1,), (1,)))
         for j in range(shares):
             start = (j * 3 + m) * R
             features[:, start : start + R] = product[j * examples : (j + 1) * examples]
@@ -306,8 +378,8 @@
 
 
 def finish(received, inputs, ids, tests):
-    hid, _, rows = received.shape
-    examples = rows // EX_TOK
+    hid = received.shape[0]
+    examples = ids.shape[1] // EX_TOK
     vmem = pl.BlockSpec(memory_space=pltpu.VMEM)
     return pl.pallas_call(
         functools.partial(features_kernel, hid),
@@ -334,15 +406,33 @@
 ):
     chips = lax.axis_size("hid") // 2
     ids = example_ids[None, :]
-    places, token_blocks = gather_blocks(tokens, chips)
-    _, grad_blocks = gather_blocks(out_grad, chips)
-    inputs = forward(places, chips, token_blocks, proj_d[:, : 2 * R], 2 * R)
-    gate = forward(places, chips, token_blocks, gate_weight, TILE)
-    up = forward(places, chips, token_blocks, up_weight, TILE)
+    half = tokens.shape[1] // 2
+    places, token_blocks, _ = gather_blocks(tokens[:, :half], chips)
+    more_places, more_blocks, steps = gather_blocks(tokens[:, half:], chips, half)
+    places, token_blocks = places + more_places, token_blocks + more_blocks
+    grad_places, grad_blocks, grad_steps = gather_blocks(after(out_grad, *steps[-1]), chips)
+    tiles = gate_weight.shape[1] // TILE
+    shares = -(-tiles // len(grad_steps))
+    gates, ups = [], []
+    for index, first in enumerate(range(0, tiles, shares)):
+        gate, up = forward(
+            places,
+            chips,
+            token_blocks,
+            gate_weight,
+            up_weight,
+            TILE,
+            first,
+            min(shares, tiles - first),
+            grad_steps[index],
+        )
+        gates.append(gate)
+        ups.append(up)
     send = backward(
-        places, chips, grad_blocks, down_weight, gate, up, proj_d[:, 2 * R :], proj_ff, ids, TILE
+        grad_places, chips, grad_blocks, down_weight, gates, ups, proj_d.T, proj_ff.T, ids, 1024, TILE
     )
     received = lax.all_to_all(send, "hid", 0, 0)
+    inputs = project_inputs(places, chips, token_blocks, proj_d.T)
     features, partial = finish(received, inputs, ids, test_features)
     scores = jnp.sum(lax.all_to_all(partial, "hid", 0, 0), axis=0)
     return features, scores

time: 148 us -> 153 us (1.034)
  Pallas kernels: 66.7 us -> 75.8 us
  local copies, waits for them, and re-layouts: 11.8 us -> 2.81 us
  starting transfers between devices: 25.7 us -> 33.8 us
  blocking collectives: 13.7 us -> 11.4 us
    pallas_call x3 -> x4, Pallas kernels: 41.4 us -> 50.4 us  [the longest x3 43.9 us: forward(): pl.pallas_call(functools.partial(forward_kernel, places, chips), grid=(ti...]
    ppermute x16 -> x24, starting transfers between devices: 17.7 us -> 26 us  [ring_step(): return lax.ppermute(block, 'hid', pairs)]
    unnamed x71 -> x108, local copies, waits for them, and re-layouts: 8.34 us -> 1.78 us
    ppermute x16 -> x24, waiting for transfers between devices: 27 us -> 22 us  [ring_step(): return lax.ppermute(block, 'hid', pairs)]
    all_to_all x1, waiting for transfers between devices: 0.21 us -> 3.45 us  [local_ring(): received = lax.all_to_all(send, 'hid', 0, 0)]
    slice x8 -> x7, local copies, waits for them, and re-layouts: 3.44 us -> 1.03 us  [the longest x1 0.99 us: local_ring(): places, token_blocks, _ = gather_blocks(tokens[:, :half], chips)]
    all_to_all x1, blocking collectives: 13.7 us -> 11.4 us  [local_ring(): scores = jnp.sum(lax.all_to_all(partial, 'hid', 0, 0), axis=0)]
    ppermute x18 -> x27, waiting for transfers between devices: 0.05 us -> 1.6 us  [core_swap(): return lax.ppermute(block, 'hid', [(h, h ^ 1) for h in range(2 * chips)])]
  transfers between devices with their start and end apart: 35 -> 52, of which waited for: 11 -> 17; matrix products, arithmetic and copies ran while one was open for 6% -> 0% of each run, Pallas kernels for 28% -> 33%
where the time goes in v4:
time: 153 us
  Pallas kernels  75.8 us (50%)
  starting transfers between devices  33.8 us (22%)
  waiting for transfers between devices  27.1 us (18%)
  blocking collectives  11.4 us (7%)
  local copies, waits for them, and re-layouts  2.81 us (2%)
    pallas_call x3, Pallas kernels, forward(): pl.pallas_call(functools.partial(forward_kernel, places, chips), grid=(ti...  43.9 us
    ppermute x24, starting transfers between devices, ring_step(): return lax.ppermute(block, 'hid', pairs)  26 us
    pallas_call x1, Pallas kernels, backward(): pl.pallas_call(functools.partial(backward_kernel, places, chips, examples...  22.6 us
    ppermute x24, waiting for transfers between devices, ring_step(): return lax.ppermute(block, 'hid', pairs)  22 us
    all_to_all x1, blocking collectives, local_ring(): scores = jnp.sum(lax.all_to_all(partial, 'hid', 0, 0), axis=0)  11.4 us
    pallas_call x1, Pallas kernels, project_inputs(): pl.pallas_call(functools.partial(inputs_kernel, places, chips), out_shape...  6.59 us
    ppermute x27, starting transfers between devices, core_swap(): return lax.ppermute(block, 'hid', [(h, h ^ 1) for h in range(2 * chips)])  4.14 us
    all_to_all x1, starting transfers between devices, local_ring(): received = lax.all_to_all(send, 'hid', 0, 0)  3.71 us
  transfers between devices with their start and end apart: 52, of which 17 were waited for; matrix products, arithmetic and copies ran while one was open for 0% of the time, Pallas kernels for 33%

profile of v4, /device:TPU:0, one launch (start us, length us, event | category | flops | bytes accessed | tf_op | source)
XLA Modules:
  0.0 153.0 jit_solution(14760904157788982803)
XLA Ops:
  0.6 1.0 fusion
  1.6 3.1 %collective-permute-start = (bf16[16,4096]{1,0:T(8,128)(2,1)S(1)}, bf16[16,4096]{1,0:T(8,128)(2,1)S(1)}, u32[]{:S(2)}, u32[]{:S(2)}) collective-permute-start(bf16[16,4096]{1,0:T(8,128)(2,1)S(1)} %get-tuple-element.21.refs_18_), channel_id=1, source_target_pairs={{0,4},{1,5},{4,8},{5,9},{8,12},{9,13},{12,14},{13,15},{14,10},{15,... | collective-permute-start | bytes 393224 | tf_op jit(solution)/shard_map/ppermute | solution.py:118
  4.7 2.0 %collective-permute-start.24 = (bf16[16,4096]{1,0:T(8,128)(2,1)S(1)}, bf16[16,4096]{1,0:T(8,128)(2,1)S(1)}, u32[]{:S(2)}, u32[]{:S(2)}) collective-permute-start(bf16[16,4096]{1,0:T(8,128)(2,1)S(1)} %get-tuple-element.20.refs_0_), channel_id=1, source_target_pairs={{0,4},{1,5},{4,8},{5,9},{8,12},{9,13},{12,14},{13,15},{14,10},{15,... | collective-permute-start | bytes 393224 | tf_op jit(solution)/shard_map/ppermute | solution.py:118
  6.7 2.2 %collective-permute-done.refs_20_ = bf16[16,4096]{1,0:T(8,128)(2,1)S(1)} collective-permute-done((bf16[16,4096]{1,0:T(8,128)(2,1)S(1)}, bf16[16,4096]{1,0:T(8,128)(2,1)S(1)}, u32[]{:S(2)}, u32[]{:S(2)}) %collective-permute-start) | collective-permute-done | bytes 131104 | tf_op jit(solution)/shard_map/ppermute | solution.py:118
  9.0 2.1 %collective-permute-done.3.refs_22_ = bf16[16,4096]{1,0:T(8,128)(2,1)S(1)} collective-permute-done((bf16[16,4096]{1,0:T(8,128)(2,1)S(1)}, bf16[16,4096]{1,0:T(8,128)(2,1)S(1)}, u32[]{:S(2)}, u32[]{:S(2)}) %collective-permute-start.3) | collective-permute-done | bytes 131104 | tf_op jit(solution)/shard_map/ppermute | solution.py:118
  11.0 1.6 %collective-permute-start.1 = (bf16[16,4096]{1,0:T(8,128)(2,1)S(1)}, bf16[16,4096]{1,0:T(8,128)(2,1)S(1)}, u32[]{:S(2)}, u32[]{:S(2)}) collective-permute-start(bf16[16,4096]{1,0:T(8,128)(2,1)S(1)} %collective-permute-done.refs_20_), channel_id=1, source_target_pairs={{0,4},{1,5},{4,8},{5,9},{8,12},{9,13},{12,14},{13,15},{14,10},{15,... | collective-permute-start | bytes 393224 | tf_op jit(solution)/shard_map/ppermute | solution.py:118
  12.6 0.5 collective-permute-start.4
  13.1 1.6 %collective-permute-start.28 = (bf16[16,4096]{1,0:T(8,128)(2,1)S(1)}, bf16[16,4096]{1,0:T(8,128)(2,1)S(1)}, u32[]{:S(2)}, u32[]{:S(2)}) collective-permute-start(bf16[16,4096]{1,0:T(8,128)(2,1)S(1)} %collective-permute-done.24.refs_2_), channel_id=1, source_target_pairs={{0,4},{1,5},{4,8},{5,9},{8,12},{9,13},{12,14},{13,15},{14,10},{15,... | collective-permute-start | bytes 393224 | tf_op jit(solution)/shard_map/ppermute | solution.py:118
  14.7 0.5 collective-permute-start.30
  15.1 1.7 %collective-permute-done.1.refs_24_ = bf16[16,4096]{1,0:T(8,128)(2,1)S(1)} collective-permute-done((bf16[16,4096]{1,0:T(8,128)(2,1)S(1)}, bf16[16,4096]{1,0:T(8,128)(2,1)S(1)}, u32[]{:S(2)}, u32[]{:S(2)}) %collective-permute-start.1) | collective-permute-done | bytes 131104 | tf_op jit(solution)/shard_map/ppermute | solution.py:118
  16.8 1.4 collective-permute-done.4.refs_26_
  18.2 1.7 %collective-permute-start.2 = (bf16[16,4096]{1,0:T(8,128)(2,1)S(1)}, bf16[16,4096]{1,0:T(8,128)(2,1)S(1)}, u32[]{:S(2)}, u32[]{:S(2)}) collective-permute-start(bf16[16,4096]{1,0:T(8,128)(2,1)S(1)} %collective-permute-done.1.refs_24_), channel_id=1, source_target_pairs={{0,4},{1,5},{4,8},{5,9},{8,12},{9,13},{12,14},{13,15},{14,10},{15,... | collective-permute-start | bytes 393224 | tf_op jit(solution)/shard_map/ppermute | solution.py:118
  19.9 0.4 collective-permute-start.5
  20.4 1.7 %collective-permute-start.32 = (bf16[16,4096]{1,0:T(8,128)(2,1)S(1)}, bf16[16,4096]{1,0:T(8,128)(2,1)S(1)}, u32[]{:S(2)}, u32[]{:S(2)}) collective-permute-start(bf16[16,4096]{1,0:T(8,128)(2,1)S(1)} %collective-permute-done.28.refs_6_), channel_id=1, source_target_pairs={{0,4},{1,5},{4,8},{5,9},{8,12},{9,13},{12,14},{13,15},{14,10},{15,... | collective-permute-start | bytes 393224 | tf_op jit(solution)/shard_map/ppermute | solution.py:118
  22.0 0.4 collective-permute-start.34
  22.4 2.1 %collective-permute-done.2.refs_28_ = bf16[16,4096]{1,0:T(8,128)(2,1)S(1)} collective-permute-done((bf16[16,4096]{1,0:T(8,128)(2,1)S(1)}, bf16[16,4096]{1,0:T(8,128)(2,1)S(1)}, u32[]{:S(2)}, u32[]{:S(2)}) %collective-permute-start.2) | collective-permute-done | bytes 131104 | tf_op jit(solution)/shard_map/ppermute | solution.py:118
  24.6 1.5 collective-permute-done.5.refs_30_
  26.1 1.6 %collective-permute-start.7 = (bf16[16,8192]{1,0:T(8,128)(2,1)}, bf16[16,8192]{1,0:T(8,128)(2,1)S(1)}, u32[]{:S(2)}, u32[]{:S(2)}) collective-permute-start(bf16[16,8192]{1,0:T(8,128)(2,1)} %refs_0_), channel_id=1, source_target_pairs={{0,4},{1,5},{4,8},{5,9},{8,12},{9,13},{12,14},{13,15},{14,10},{15,... | collective-permute-start | bytes 786440 | tf_op jit(solution)/shard_map/ppermute | solution.py:118
  27.8 0.4 collective-permute-start.9
  28.3 0.5 collective-permute-start.44
  28.8 1.6 %collective-permute-start.47 = (bf16[16,2048]{1,0:T(8,128)(2,1)S(1)}, bf16[16,2048]{1,0:T(8,128)(2,1)S(1)}, u32[]{:S(2)}, u32[]{:S(2)}) collective-permute-start(bf16[16,2048]{1,0:T(8,128)(2,1)S(1)} %slice.36), channel_id=1, source_target_pairs={{0,4},{1,5},{4,8},{5,9},{8,12},{9,13},{12,14},{13,15},{14,10},{15,... | collective-permute-start | bytes 196616 | tf_op jit(solution)/shard_map/ppermute | solution.py:118
  30.5 0.5 collective-permute-start.49
  31.0 1.6 %collective-permute-start.36 = (bf16[16,2048]{1,0:T(8,128)(2,1)S(1)}, bf16[16,2048]{1,0:T(8,128)(2,1)S(1)}, u32[]{:S(2)}, u32[]{:S(2)}) collective-permute-start(bf16[16,2048]{1,0:T(8,128)(2,1)S(1)} %slice.34), channel_id=1, source_target_pairs={{0,4},{1,5},{4,8},{5,9},{8,12},{9,13},{12,14},{13,15},{14,10},{15,... | collective-permute-start | bytes 196616 | tf_op jit(solution)/shard_map/ppermute | solution.py:118
  32.6 4.3 %collective-permute-done.47.refs_32_ = bf16[16,2048]{1,0:T(8,128)(2,1)S(1)} collective-permute-done((bf16[16,2048]{1,0:T(8,128)(2,1)S(1)}, bf16[16,2048]{1,0:T(8,128)(2,1)S(1)}, u32[]{:S(2)}, u32[]{:S(2)}) %collective-permute-start.47) | collective-permute-done | bytes 65568 | tf_op jit(solution)/shard_map/ppermute | solution.py:118
  36.9 0.5 collective-permute-start.38
  37.4 0.4 collective-permute-done.49.refs_34_
  37.8 0.1 collective-permute-done.36.refs_14_
  37.9 0.4 collective-permute-start.50
  38.3 2.9 %collective-permute-done.38.refs_16_ = bf16[16,2048]{1,0:T(8,128)(2,1)S(1)} collective-permute-done((bf16[16,2048]{1,0:T(8,128)(2,1)S(1)}, bf16[16,2048]{1,0:T(8,128)(2,1)S(1)}, u32[]{:S(2)}, u32[]{:S(2)}) %collective-permute-start.38) | collective-permute-done | bytes 65568 | tf_op jit(solution)/shard_map/ppermute | solution.py:118
  41.2 1.6 %collective-permute-start.11 = (bf16[16,8192]{1,0:T(8,128)(2,1)S(1)}, bf16[16,8192]{1,0:T(8,128)(2,1)S(1)}, u32[]{:S(2)}, u32[]{:S(2)}) collective-permute-start(bf16[16,8192]{1,0:T(8,128)(2,1)S(1)} %collective-permute-done.7.refs_44_.refs_2_), channel_id=1, source_target_pairs={{0,4},{1,5},{4,8},{5,9},{8,12},{9,13},{12,14},{13,15},{14,10},{15,... | collective-permute-start | bytes 786440 | tf_op jit(solution)/shard_map/ppermute | solution.py:118
  42.8 0.4 collective-permute-start.13
  43.3 0.5 collective-permute-start.39
  43.8 0.7 collective-permute-done.37.refs_15_
  44.5 0.2 collective-permute-start.46
  44.7 0.1 collective-permute-done.39.refs_17_
  44.8 0.4 collective-permute-start.33
  45.2 0.2 collective-permute-start.35
  45.3 0.5 collective-permute-done.46.refs_31_
  45.9 0.2 collective-permute-start.6
  46.0 0.1 collective-permute-done.33.refs_11_
  46.2 0.4 collective-permute-start.10
  46.5 0.2 collective-permute-start.8
  46.7 3.2 %collective-permute-done.11.refs_44_.refs_6_ = bf16[16,8192]{1,0:T(8,128)(2,1)S(1)} collective-permute-done((bf16[16,8192]{1,0:T(8,128)(2,1)S(1)}, bf16[16,8192]{1,0:T(8,128)(2,1)S(1)}, u32[]{:S(2)}, u32[]{:S(2)}) %collective-permute-start.11) | collective-permute-done | bytes 262176 | tf_op jit(solution)/shard_map/ppermute | solution.py:118
  49.9 1.6 %collective-permute-start.15 = (bf16[16,8192]{1,0:T(8,128)(2,1)S(1)}, bf16[16,8192]{1,0:T(8,128)(2,1)S(1)}, u32[]{:S(2)}, u32[]{:S(2)}) collective-permute-start(bf16[16,8192]{1,0:T(8,128)(2,1)S(1)} %collective-permute-done.11.refs_44_.refs_6_), channel_id=1, source_target_pairs={{0,4},{1,5},{4,8},{5,9},{8,12},{9,13},{12,14},{13,15},{14,10},{15,... | collective-permute-start | bytes 786440 | tf_op jit(solution)/shard_map/ppermute | solution.py:118
  51.5 0.4 collective-permute-start.17
  52.3 17.4 %shard_map.104 = (f32[768,256]{1,0:T(8,128)}, f32[768,256]{1,0:T(8,128)}) custom-call(bf16[16,4096]{1,0:T(8,128)(2,1)} %copy-done, bf16[16,4096]{1,0:T(8,128)(2,1)} %copy-done.12, bf16[16,4096]{1,0:T(8,128)(2,1)} %copy-done.10, bf16[16,4096]{1,0:T(8,128)(2,1)} %copy-done.18, bf16[16,4096]{1,0:T(8,128)(2,1)} %copy-done.11, bf16[16,4096]{1,0:T(8,128)(2,1)} %copy-done.19, ...), custom_call_target="tpu_custom_call" | custom-call | flops 12884901888 | bytes 50331648 | tf_op jit(solution)/shard_map/pallas_call | solution.py:199
  69.8 1.6 %collective-permute-start.19 = (bf16[16,4096]{1,0:T(8,128)(2,1)S(1)}, bf16[16,4096]{1,0:T(8,128)(2,1)S(1)}, u32[]{:S(2)}, u32[]{:S(2)}) collective-permute-start(bf16[16,4096]{1,0:T(8,128)(2,1)S(1)} %slice.32), channel_id=1, source_target_pairs={{0,4},{1,5},{4,8},{5,9},{8,12},{9,13},{12,14},{13,15},{14,10},{15,... | collective-permute-start | bytes 393224 | tf_op jit(solution)/shard_map/ppermute | solution.py:118
  71.5 0.7 collective-permute-start.21
  72.2 17.2 %shard_map.105 = (f32[768,256]{1,0:T(8,128)}, f32[768,256]{1,0:T(8,128)}) custom-call(bf16[16,4096]{1,0:T(8,128)(2,1)} %copy-done, bf16[16,4096]{1,0:T(8,128)(2,1)} %copy-done.12, bf16[16,4096]{1,0:T(8,128)(2,1)} %copy-done.10, bf16[16,4096]{1,0:T(8,128)(2,1)} %copy-done.18, bf16[16,4096]{1,0:T(8,128)(2,1)} %copy-done.11, bf16[16,4096]{1,0:T(8,128)(2,1)} %copy-done.19, ...), custom_call_target="tpu_custom_call" | custom-call | flops 12884901888 | bytes 50331648 | tf_op jit(solution)/shard_map/pallas_call | solution.py:199
  89.6 0.5 collective-permute-start.16
  90.1 0.1 collective-permute-start.18
  90.2 0.5 collective-permute-start.20
  90.7 0.1 collective-permute-start.22
  90.8 9.3 %shard_map.106 = (f32[256,256]{1,0:T(8,128)}, f32[256,256]{1,0:T(8,128)}) custom-call(bf16[16,4096]{1,0:T(8,128)(2,1)} %copy-done, bf16[16,4096]{1,0:T(8,128)(2,1)} %copy-done.12, bf16[16,4096]{1,0:T(8,128)(2,1)} %copy-done.10, bf16[16,4096]{1,0:T(8,128)(2,1)} %copy-done.18, bf16[16,4096]{1,0:T(8,128)(2,1)} %copy-done.11, bf16[16,4096]{1,0:T(8,128)(2,1)} %copy-done.19, ...), custom_call_target="tpu_custom_call" | custom-call | flops 4294967296 | bytes 16777216 | tf_op jit(solution)/shard_map/pallas_call | solution.py:199
  100.2 0.6 copy-done.47
  100.9 0.1 copy-done.48
  101.1 22.6 %shard_map.107 = f32[16,16,256]{2,1,0:T(8,128)} custom-call(bf16[16,8192]{1,0:T(8,128)(2,1)} %refs_0_, bf16[16,8192]{1,0:T(8,128)(2,1)} %copy-done.43, bf16[16,8192]{1,0:T(8,128)(2,1)} %copy-done.30, bf16[16,8192]{1,0:T(8,128)(2,1)} %copy-done.45, bf16[16,8192]{1,0:T(8,128)(2,1)} %copy-done.31, bf16[16,8192]{1,0:T(8,128)(2,1)} %copy-done.44, ...), custom_call_target="tpu_custom_call" | custom-call | flops 7516192768 | bytes 29360128 | tf_op jit(solution)/shard_map/pallas_call | solution.py:331
  123.7 3.7 %all-to-all-start = ((f32[16,16,256]{2,1,0:T(8,128)}), f32[16,16,256]{2,1,0:T(8,128)S(1)}, u32[]{:S(2)}, u32[]{:S(2)}) async-start(f32[16,16,256]{2,1,0:T(8,128)} %shard_map.107), calls=%async_computation | async-start | bytes 524288 | tf_op jit(solution)/shard_map/all_to_all | solution.py:434
  127.4 6.6 %shard_map.108.inputs = f32[128,256]{1,0:T(8,128)} custom-call(bf16[16,4096]{1,0:T(8,128)(2,1)} %copy-done, bf16[16,4096]{1,0:T(8,128)(2,1)} %copy-done.12, bf16[16,4096]{1,0:T(8,128)(2,1)} %copy-done.10, bf16[16,4096]{1,0:T(8,128)(2,1)} %copy-done.18, bf16[16,4096]{1,0:T(8,128)(2,1)} %copy-done.11, bf16[16,4096]{1,0:T(8,128)(2,1)} %copy-done.19, ...), custom_call_target="tpu_custom_call" | custom-call | flops 2147483648 | bytes 4194304 | tf_op jit(solution)/shard_map/pallas_call | solution.py:238
  134.0 3.5 %all-to-all-done.received = f32[16,16,256]{2,1,0:T(8,128)S(1)} async-done(((f32[16,16,256]{2,1,0:T(8,128)}), f32[16,16,256]{2,1,0:T(8,128)S(1)}, u32[]{:S(2)}, u32[]{:S(2)}) %all-to-all-start) | async-done | bytes 262176 | tf_op jit(solution)/shard_map/all_to_all | solution.py:434
  137.4 0.7 copy-done.35
  138.1 2.8 %shard_map.109 = (f32[8,768]{1,0:T(8,128)}, f32[16,8,256]{2,1,0:T(8,128)}) custom-call(f32[16,16,256]{2,1,0:T(8,128)} %copy-done.35, f32[128,256]{1,0:T(8,128)} %shard_map.108.inputs, s32[1,256]{1,0:T(1,128)} %bitcast.7, bf16[256,768]{1,0:T(8,128)(2,1)} %tests.1), custom_call_target="tpu_custom_call" | custom-call | tf_op jit(solution)/shard_map/pallas_call | solution.py:384
  140.9 11.4 %all_to_all.10 = f32[16,8,256]{2,1,0:T(8,128)S(1)} all-to-all(f32[16,8,256]{2,1,0:T(8,128)} %get-tuple-element.19), channel_id=1, replica_groups=mesh['groups'=2,'hid'=16,'mod'=1] {'hid'}, dimensions={0} | all-to-all | bytes 262144 | tf_op jit(solution)/shard_map/all_to_all | solution.py:437
  152.3 0.6 reduce_sum.9
  (163 shorter events, 0.7 us)
Async XLA Ops:
  1.6 50.3 %copy-start = (bf16[16,4096]{1,0:T(8,128)(2,1)}, bf16[16,4096]{1,0:T(8,128)(2,1)S(1)}, u32[]{:S(2)}) copy-start(bf16[16,4096]{1,0:T(8,128)(2,1)S(1)} %get-tuple-element.20.refs_0_) | copy-start | bytes 393220
  1.6 50.3 %copy-start.1 = (bf16[16,4096]{1,0:T(8,128)(2,1)}, bf16[16,4096]{1,0:T(8,128)(2,1)S(1)}, u32[]{:S(2)}) copy-start(bf16[16,4096]{1,0:T(8,128)(2,1)S(1)} %get-tuple-element.21.refs_18_) | copy-start | bytes 393220
  1.6 7.3 %collective-permute-start = (bf16[16,4096]{1,0:T(8,128)(2,1)S(1)}, bf16[16,4096]{1,0:T(8,128)(2,1)S(1)}, u32[]{:S(2)}, u32[]{:S(2)}) collective-permute-start(bf16[16,4096]{1,0:T(8,128)(2,1)S(1)} %get-tuple-element.21.refs_18_), channel_id=1, source_target_pairs={{0,4},{1,5},{4,8},{5,9},{8,12},{9,13},{12,14},{13,15},{14,10},{15,... | collective-permute-start | bytes 393224 | tf_op jit(solution)/shard_map/ppermute | solution.py:118
  4.7 6.3 %collective-permute-start.3 = (bf16[16,4096]{1,0:T(8,128)(2,1)S(1)}, bf16[16,4096]{1,0:T(8,128)(2,1)S(1)}, u32[]{:S(2)}, u32[]{:S(2)}) collective-permute-start(bf16[16,4096]{1,0:T(8,128)(2,1)S(1)} %get-tuple-element.21.refs_18_), channel_id=1, source_target_pairs={{0,2},{1,3},{4,0},{5,1},{8,4},{9,5},{12,8},{13,9},{14,12},{15,13},... | collective-permute-start | bytes 393224 | tf_op jit(solution)/shard_map/ppermute | solution.py:118
  4.7 7.9 %collective-permute-start.24 = (bf16[16,4096]{1,0:T(8,128)(2,1)S(1)}, bf16[16,4096]{1,0:T(8,128)(2,1)S(1)}, u32[]{:S(2)}, u32[]{:S(2)}) collective-permute-start(bf16[16,4096]{1,0:T(8,128)(2,1)S(1)} %get-tuple-element.20.refs_0_), channel_id=1, source_target_pairs={{0,4},{1,5},{4,8},{5,9},{8,12},{9,13},{12,14},{13,15},{14,10},{15,... | collective-permute-start | bytes 393224 | tf_op jit(solution)/shard_map/ppermute | solution.py:118
  6.7 6.4 %collective-permute-start.26 = (bf16[16,4096]{1,0:T(8,128)(2,1)S(1)}, bf16[16,4096]{1,0:T(8,128)(2,1)S(1)}, u32[]{:S(2)}, u32[]{:S(2)}) collective-permute-start(bf16[16,4096]{1,0:T(8,128)(2,1)S(1)} %get-tuple-element.20.refs_0_), channel_id=1, source_target_pairs={{0,2},{1,3},{4,0},{5,1},{8,4},{9,5},{12,8},{13,9},{14,12},{15,13},... | collective-permute-start | bytes 393224 | tf_op jit(solution)/shard_map/ppermute | solution.py:118
  6.7 7.9 %collective-permute-start.23 = (bf16[16,4096]{1,0:T(8,128)(2,1)S(1)}, bf16[16,4096]{1,0:T(8,128)(2,1)S(1)}, u32[]{:S(2)}, u32[]{:S(2)}) collective-permute-start(bf16[16,4096]{1,0:T(8,128)(2,1)S(1)} %get-tuple-element.20.refs_0_), channel_id=1, source_target_pairs={{0,1},{1,0},{2,3},{3,2},{4,5},{5,4},{6,7},{7,6},{8,9},{9,8},{10,11... | collective-permute-start | bytes 393224 | tf_op jit(solution)/shard_map/ppermute | solution.py:122
  9.0 43.0 %copy-start.8 = (bf16[16,4096]{1,0:T(8,128)(2,1)}, bf16[16,4096]{1,0:T(8,128)(2,1)S(1)}, u32[]{:S(2)}) copy-start(bf16[16,4096]{1,0:T(8,128)(2,1)S(1)} %collective-permute-done.refs_20_) | copy-start | bytes 393220
  9.0 6.2 %collective-permute-start.40 = (bf16[16,4096]{1,0:T(8,128)(2,1)S(1)}, bf16[16,4096]{1,0:T(8,128)(2,1)S(1)}, u32[]{:S(2)}, u32[]{:S(2)}) collective-permute-start(bf16[16,4096]{1,0:T(8,128)(2,1)S(1)} %get-tuple-element.21.refs_18_), channel_id=1, source_target_pairs={{0,1},{1,0},{2,3},{3,2},{4,5},{5,4},{6,7},{7,6},{8,9},{9,8},{10,11... | collective-permute-start | bytes 393224 | tf_op jit(solution)/shard_map/ppermute | solution.py:122
  11.0 40.9 %copy-start.9 = (bf16[16,4096]{1,0:T(8,128)(2,1)}, bf16[16,4096]{1,0:T(8,128)(2,1)S(1)}, u32[]{:S(2)}) copy-start(bf16[16,4096]{1,0:T(8,128)(2,1)S(1)} %collective-permute-done.3.refs_22_) | copy-start | bytes 393220
  11.0 5.8 %collective-permute-start.1 = (bf16[16,4096]{1,0:T(8,128)(2,1)S(1)}, bf16[16,4096]{1,0:T(8,128)(2,1)S(1)}, u32[]{:S(2)}, u32[]{:S(2)}) collective-permute-start(bf16[16,4096]{1,0:T(8,128)(2,1)S(1)} %collective-permute-done.refs_20_), channel_id=1, source_target_pairs={{0,4},{1,5},{4,8},{5,9},{8,12},{9,13},{12,14},{13,15},{14,10},{15,... | collective-permute-start | bytes 393224 | tf_op jit(solution)/shard_map/ppermute | solution.py:118
  12.6 39.3 %copy-start.10 = (bf16[16,4096]{1,0:T(8,128)(2,1)}, bf16[16,4096]{1,0:T(8,128)(2,1)S(1)}, u32[]{:S(2)}) copy-start(bf16[16,4096]{1,0:T(8,128)(2,1)S(1)} %collective-permute-done.24.refs_2_) | copy-start | bytes 393220
  12.6 5.6 %collective-permute-start.4 = (bf16[16,4096]{1,0:T(8,128)(2,1)S(1)}, bf16[16,4096]{1,0:T(8,128)(2,1)S(1)}, u32[]{:S(2)}, u32[]{:S(2)}) collective-permute-start(bf16[16,4096]{1,0:T(8,128)(2,1)S(1)} %collective-permute-done.3.refs_22_), channel_id=1, source_target_pairs={{0,2},{1,3},{4,0},{5,1},{8,4},{9,5},{12,8},{13,9},{14,12},{15,13},... | collective-permute-start | bytes 393224 | tf_op jit(solution)/shard_map/ppermute | solution.py:118
  13.1 38.9 %copy-start.11 = (bf16[16,4096]{1,0:T(8,128)(2,1)}, bf16[16,4096]{1,0:T(8,128)(2,1)S(1)}, u32[]{:S(2)}) copy-start(bf16[16,4096]{1,0:T(8,128)(2,1)S(1)} %collective-permute-done.26.refs_4_) | copy-start | bytes 393220
  13.1 5.1 %collective-permute-start.28 = (bf16[16,4096]{1,0:T(8,128)(2,1)S(1)}, bf16[16,4096]{1,0:T(8,128)(2,1)S(1)}, u32[]{:S(2)}, u32[]{:S(2)}) collective-permute-start(bf16[16,4096]{1,0:T(8,128)(2,1)S(1)} %collective-permute-done.24.refs_2_), channel_id=1, source_target_pairs={{0,4},{1,5},{4,8},{5,9},{8,12},{9,13},{12,14},{13,15},{14,10},{15,... | collective-permute-start | bytes 393224 | tf_op jit(solution)/shard_map/ppermute | solution.py:118
  14.7 37.3 %copy-start.12 = (bf16[16,4096]{1,0:T(8,128)(2,1)}, bf16[16,4096]{1,0:T(8,128)(2,1)S(1)}, u32[]{:S(2)}) copy-start(bf16[16,4096]{1,0:T(8,128)(2,1)S(1)} %collective-permute-done.23.refs_1_) | copy-start | bytes 393220
  14.7 5.3 %collective-permute-start.30 = (bf16[16,4096]{1,0:T(8,128)(2,1)S(1)}, bf16[16,4096]{1,0:T(8,128)(2,1)S(1)}, u32[]{:S(2)}, u32[]{:S(2)}) collective-permute-start(bf16[16,4096]{1,0:T(8,128)(2,1)S(1)} %collective-permute-done.26.refs_4_), channel_id=1, source_target_pairs={{0,2},{1,3},{4,0},{5,1},{8,4},{9,5},{12,8},{13,9},{14,12},{15,13},... | collective-permute-start | bytes 393224 | tf_op jit(solution)/shard_map/ppermute | solution.py:118
  15.1 36.8 %copy-start.13 = (bf16[16,4096]{1,0:T(8,128)(2,1)}, bf16[16,4096]{1,0:T(8,128)(2,1)S(1)}, u32[]{:S(2)}) copy-start(bf16[16,4096]{1,0:T(8,128)(2,1)S(1)} %collective-permute-done.40.refs_19_) | copy-start | bytes 393220
  15.1 5.2 %collective-permute-start.25 = (bf16[16,4096]{1,0:T(8,128)(2,1)S(1)}, bf16[16,4096]{1,0:T(8,128)(2,1)S(1)}, u32[]{:S(2)}, u32[]{:S(2)}) collective-permute-start(bf16[16,4096]{1,0:T(8,128)(2,1)S(1)} %collective-permute-done.24.refs_2_), channel_id=1, source_target_pairs={{0,1},{1,0},{2,3},{3,2},{4,5},{5,4},{6,7},{7,6},{8,9},{9,8},{10,11... | collective-permute-start | bytes 393224 | tf_op jit(solution)/shard_map/ppermute | solution.py:122
  16.8 35.2 %copy-start.14 = (bf16[16,4096]{1,0:T(8,128)(2,1)}, bf16[16,4096]{1,0:T(8,128)(2,1)S(1)}, u32[]{:S(2)}) copy-start(bf16[16,4096]{1,0:T(8,128)(2,1)S(1)} %collective-permute-done.1.refs_24_) | copy-start | bytes 393220
  16.8 3.5 %collective-permute-start.27 = (bf16[16,4096]{1,0:T(8,128)(2,1)S(1)}, bf16[16,4096]{1,0:T(8,128)(2,1)S(1)}, u32[]{:S(2)}, u32[]{:S(2)}) collective-permute-start(bf16[16,4096]{1,0:T(8,128)(2,1)S(1)} %collective-permute-done.26.refs_4_), channel_id=1, source_target_pairs={{0,1},{1,0},{2,3},{3,2},{4,5},{5,4},{6,7},{7,6},{8,9},{9,8},{10,11... | collective-permute-start | bytes 393224 | tf_op jit(solution)/shard_map/ppermute | solution.py:122
  18.2 33.8 %copy-start.15 = (bf16[16,4096]{1,0:T(8,128)(2,1)}, bf16[16,4096]{1,0:T(8,128)(2,1)S(1)}, u32[]{:S(2)}) copy-start(bf16[16,4096]{1,0:T(8,128)(2,1)S(1)} %collective-permute-done.4.refs_26_) | copy-start | bytes 393220
  18.2 3.8 %collective-permute-start.41 = (bf16[16,4096]{1,0:T(8,128)(2,1)S(1)}, bf16[16,4096]{1,0:T(8,128)(2,1)S(1)}, u32[]{:S(2)}, u32[]{:S(2)}) collective-permute-start(bf16[16,4096]{1,0:T(8,128)(2,1)S(1)} %collective-permute-done.refs_20_), channel_id=1, source_target_pairs={{0,1},{1,0},{2,3},{3,2},{4,5},{5,4},{6,7},{7,6},{8,9},{9,8},{10,11... | collective-permute-start | bytes 393224 | tf_op jit(solution)/shard_map/ppermute | solution.py:122
  18.2 33.8 %copy-start.16 = (bf16[16,4096]{1,0:T(8,128)(2,1)}, bf16[16,4096]{1,0:T(8,128)(2,1)S(1)}, u32[]{:S(2)}) copy-start(bf16[16,4096]{1,0:T(8,128)(2,1)S(1)} %collective-permute-done.28.refs_6_) | copy-start | bytes 393220
  18.2 6.3 %collective-permute-start.2 = (bf16[16,4096]{1,0:T(8,128)(2,1)S(1)}, bf16[16,4096]{1,0:T(8,128)(2,1)S(1)}, u32[]{:S(2)}, u32[]{:S(2)}) collective-permute-start(bf16[16,4096]{1,0:T(8,128)(2,1)S(1)} %collective-permute-done.1.refs_24_), channel_id=1, source_target_pairs={{0,4},{1,5},{4,8},{5,9},{8,12},{9,13},{12,14},{13,15},{14,10},{15,... | collective-permute-start | bytes 393224 | tf_op jit(solution)/shard_map/ppermute | solution.py:118
  19.9 32.1 %copy-start.17 = (bf16[16,4096]{1,0:T(8,128)(2,1)}, bf16[16,4096]{1,0:T(8,128)(2,1)S(1)}, u32[]{:S(2)}) copy-start(bf16[16,4096]{1,0:T(8,128)(2,1)S(1)} %collective-permute-done.30.refs_8_) | copy-start | bytes 393220
  19.9 6.2 %collective-permute-start.5 = (bf16[16,4096]{1,0:T(8,128)(2,1)S(1)}, bf16[16,4096]{1,0:T(8,128)(2,1)S(1)}, u32[]{:S(2)}, u32[]{:S(2)}) collective-permute-start(bf16[16,4096]{1,0:T(8,128)(2,1)S(1)} %collective-permute-done.4.refs_26_), channel_id=1, source_target_pairs={{0,2},{1,3},{4,0},{5,1},{8,4},{9,5},{12,8},{13,9},{14,12},{15,13},... | collective-permute-start | bytes 393224 | tf_op jit(solution)/shard_map/ppermute | solution.py:118
  20.3 5.8 %collective-permute-start.42 = (bf16[16,4096]{1,0:T(8,128)(2,1)S(1)}, bf16[16,4096]{1,0:T(8,128)(2,1)S(1)}, u32[]{:S(2)}, u32[]{:S(2)}) collective-permute-start(bf16[16,4096]{1,0:T(8,128)(2,1)S(1)} %collective-permute-done.3.refs_22_), channel_id=1, source_target_pairs={{0,1},{1,0},{2,3},{3,2},{4,5},{5,4},{6,7},{7,6},{8,9},{9,8},{10,11... | collective-permute-start | bytes 393224 | tf_op jit(solution)/shard_map/ppermute | solution.py:122
  20.4 7.4 %collective-permute-start.32 = (bf16[16,4096]{1,0:T(8,128)(2,1)S(1)}, bf16[16,4096]{1,0:T(8,128)(2,1)S(1)}, u32[]{:S(2)}, u32[]{:S(2)}) collective-permute-start(bf16[16,4096]{1,0:T(8,128)(2,1)S(1)} %collective-permute-done.28.refs_6_), channel_id=1, source_target_pairs={{0,4},{1,5},{4,8},{5,9},{8,12},{9,13},{12,14},{13,15},{14,10},{15,... | collective-permute-start | bytes 393224 | tf_op jit(solution)/shard_map/ppermute | solution.py:118
  22.0 6.2 %collective-permute-start.34 = (bf16[16,4096]{1,0:T(8,128)(2,1)S(1)}, bf16[16,4096]{1,0:T(8,128)(2,1)S(1)}, u32[]{:S(2)}, u32[]{:S(2)}) collective-permute-start(bf16[16,4096]{1,0:T(8,128)(2,1)S(1)} %collective-permute-done.30.refs_8_), channel_id=1, source_target_pairs={{0,2},{1,3},{4,0},{5,1},{8,4},{9,5},{12,8},{13,9},{14,12},{15,13},... | collective-permute-start | bytes 393224 | tf_op jit(solution)/shard_map/ppermute | solution.py:118
  24.6 3.7 %collective-permute-start.29 = (bf16[16,4096]{1,0:T(8,128)(2,1)S(1)}, bf16[16,4096]{1,0:T(8,128)(2,1)S(1)}, u32[]{:S(2)}, u32[]{:S(2)}) collective-permute-start(bf16[16,4096]{1,0:T(8,128)(2,1)S(1)} %collective-permute-done.28.refs_6_), channel_id=1, source_target_pairs={{0,1},{1,0},{2,3},{3,2},{4,5},{5,4},{6,7},{7,6},{8,9},{9,8},{10,11... | collective-permute-start | bytes 393224 | tf_op jit(solution)/shard_map/ppermute | solution.py:122
  26.1 2.7 %collective-permute-start.31 = (bf16[16,4096]{1,0:T(8,128)(2,1)S(1)}, bf16[16,4096]{1,0:T(8,128)(2,1)S(1)}, u32[]{:S(2)}, u32[]{:S(2)}) collective-permute-start(bf16[16,4096]{1,0:T(8,128)(2,1)S(1)} %collective-permute-done.30.refs_8_), channel_id=1, source_target_pairs={{0,1},{1,0},{2,3},{3,2},{4,5},{5,4},{6,7},{7,6},{8,9},{9,8},{10,11... | collective-permute-start | bytes 393224 | tf_op jit(solution)/shard_map/ppermute | solution.py:122
  26.1 15.1 %collective-permute-start.7 = (bf16[16,8192]{1,0:T(8,128)(2,1)}, bf16[16,8192]{1,0:T(8,128)(2,1)S(1)}, u32[]{:S(2)}, u32[]{:S(2)}) collective-permute-start(bf16[16,8192]{1,0:T(8,128)(2,1)} %refs_0_), channel_id=1, source_target_pairs={{0,4},{1,5},{4,8},{5,9},{8,12},{9,13},{12,14},{13,15},{14,10},{15,... | collective-permute-start | bytes 786440 | tf_op jit(solution)/shard_map/ppermute | solution.py:118
  27.8 15.1 %collective-permute-start.9 = (bf16[16,8192]{1,0:T(8,128)(2,1)}, bf16[16,8192]{1,0:T(8,128)(2,1)S(1)}, u32[]{:S(2)}, u32[]{:S(2)}) collective-permute-start(bf16[16,8192]{1,0:T(8,128)(2,1)} %refs_0_), channel_id=1, source_target_pairs={{0,2},{1,3},{4,0},{5,1},{8,4},{9,5},{12,8},{13,9},{14,12},{15,13},... | collective-permute-start | bytes 786440 | tf_op jit(solution)/shard_map/ppermute | solution.py:118
  28.3 2.2 %collective-permute-start.43 = (bf16[16,4096]{1,0:T(8,128)(2,1)S(1)}, bf16[16,4096]{1,0:T(8,128)(2,1)S(1)}, u32[]{:S(2)}, u32[]{:S(2)}) collective-permute-start(bf16[16,4096]{1,0:T(8,128)(2,1)S(1)} %collective-permute-done.1.refs_24_), channel_id=1, source_target_pairs={{0,1},{1,0},{2,3},{3,2},{4,5},{5,4},{6,7},{7,6},{8,9},{9,8},{10,11... | collective-permute-start | bytes 393224 | tf_op jit(solution)/shard_map/ppermute | solution.py:122
  28.3 2.7 %collective-permute-start.44 = (bf16[16,4096]{1,0:T(8,128)(2,1)S(1)}, bf16[16,4096]{1,0:T(8,128)(2,1)S(1)}, u32[]{:S(2)}, u32[]{:S(2)}) collective-permute-start(bf16[16,4096]{1,0:T(8,128)(2,1)S(1)} %collective-permute-done.4.refs_26_), channel_id=1, source_target_pairs={{0,1},{1,0},{2,3},{3,2},{4,5},{5,4},{6,7},{7,6},{8,9},{9,8},{10,11... | collective-permute-start | bytes 393224 | tf_op jit(solution)/shard_map/ppermute | solution.py:122
  28.8 8.1 %collective-permute-start.47 = (bf16[16,2048]{1,0:T(8,128)(2,1)S(1)}, bf16[16,2048]{1,0:T(8,128)(2,1)S(1)}, u32[]{:S(2)}, u32[]{:S(2)}) collective-permute-start(bf16[16,2048]{1,0:T(8,128)(2,1)S(1)} %slice.36), channel_id=1, source_target_pairs={{0,4},{1,5},{4,8},{5,9},{8,12},{9,13},{12,14},{13,15},{14,10},{15,... | collective-permute-start | bytes 196616 | tf_op jit(solution)/shard_map/ppermute | solution.py:118
  30.5 7.3 %collective-permute-start.49 = (bf16[16,2048]{1,0:T(8,128)(2,1)S(1)}, bf16[16,2048]{1,0:T(8,128)(2,1)S(1)}, u32[]{:S(2)}, u32[]{:S(2)}) collective-permute-start(bf16[16,2048]{1,0:T(8,128)(2,1)S(1)} %slice.37), channel_id=1, source_target_pairs={{0,2},{1,3},{4,0},{5,1},{8,4},{9,5},{12,8},{13,9},{14,12},{15,13},... | collective-permute-start | bytes 196616 | tf_op jit(solution)/shard_map/ppermute | solution.py:118
  31.0 6.9 %collective-permute-start.36 = (bf16[16,2048]{1,0:T(8,128)(2,1)S(1)}, bf16[16,2048]{1,0:T(8,128)(2,1)S(1)}, u32[]{:S(2)}, u32[]{:S(2)}) collective-permute-start(bf16[16,2048]{1,0:T(8,128)(2,1)S(1)} %slice.34), channel_id=1, source_target_pairs={{0,4},{1,5},{4,8},{5,9},{8,12},{9,13},{12,14},{13,15},{14,10},{15,... | collective-permute-start | bytes 196616 | tf_op jit(solution)/shard_map/ppermute | solution.py:118
  36.9 4.3 %collective-permute-start.38 = (bf16[16,2048]{1,0:T(8,128)(2,1)S(1)}, bf16[16,2048]{1,0:T(8,128)(2,1)S(1)}, u32[]{:S(2)}, u32[]{:S(2)}) collective-permute-start(bf16[16,2048]{1,0:T(8,128)(2,1)S(1)} %slice.35), channel_id=1, source_target_pairs={{0,2},{1,3},{4,0},{5,1},{8,4},{9,5},{12,8},{13,9},{14,12},{15,13},... | collective-permute-start | bytes 196616 | tf_op jit(solution)/shard_map/ppermute | solution.py:118
  37.8 5.5 %collective-permute-start.48 = (bf16[16,2048]{1,0:T(8,128)(2,1)S(1)}, bf16[16,2048]{1,0:T(8,128)(2,1)S(1)}, u32[]{:S(2)}, u32[]{:S(2)}) collective-permute-start(bf16[16,2048]{1,0:T(8,128)(2,1)S(1)} %collective-permute-done.47.refs_32_), channel_id=1, source_target_pairs={{0,1},{1,0},{2,3},{3,2},{4,5},{5,4},{6,7},{7,6},{8,9},{9,8},{10,11... | collective-permute-start | bytes 196616 | tf_op jit(solution)/shard_map/ppermute | solution.py:122
  37.9 5.4 %collective-permute-start.50 = (bf16[16,2048]{1,0:T(8,128)(2,1)S(1)}, bf16[16,2048]{1,0:T(8,128)(2,1)S(1)}, u32[]{:S(2)}, u32[]{:S(2)}) collective-permute-start(bf16[16,2048]{1,0:T(8,128)(2,1)S(1)} %collective-permute-done.49.refs_34_), channel_id=1, source_target_pairs={{0,1},{1,0},{2,3},{3,2},{4,5},{5,4},{6,7},{7,6},{8,9},{9,8},{10,11... | collective-permute-start | bytes 196616 | tf_op jit(solution)/shard_map/ppermute | solution.py:122
  41.2 4.0 %collective-permute-start.45 = (bf16[16,4096]{1,0:T(8,128)(2,1)S(1)}, bf16[16,4096]{1,0:T(8,128)(2,1)S(1)}, u32[]{:S(2)}, u32[]{:S(2)}) collective-permute-start(bf16[16,4096]{1,0:T(8,128)(2,1)S(1)} %collective-permute-done.2.refs_28_), channel_id=1, source_target_pairs={{0,1},{1,0},{2,3},{3,2},{4,5},{5,4},{6,7},{7,6},{8,9},{9,8},{10,11... | collective-permute-start | bytes 393224 | tf_op jit(solution)/shard_map/ppermute | solution.py:122
  41.2 8.7 %collective-permute-start.11 = (bf16[16,8192]{1,0:T(8,128)(2,1)S(1)}, bf16[16,8192]{1,0:T(8,128)(2,1)S(1)}, u32[]{:S(2)}, u32[]{:S(2)}) collective-permute-start(bf16[16,8192]{1,0:T(8,128)(2,1)S(1)} %collective-permute-done.7.refs_44_.refs_2_), channel_id=1, source_target_pairs={{0,4},{1,5},{4,8},{5,9},{8,12},{9,13},{12,14},{13,15},{14,10},{15,... | collective-permute-start | bytes 786440 | tf_op jit(solution)/shard_map/ppermute | solution.py:118
  42.8 8.7 %collective-permute-start.13 = (bf16[16,8192]{1,0:T(8,128)(2,1)S(1)}, bf16[16,8192]{1,0:T(8,128)(2,1)S(1)}, u32[]{:S(2)}, u32[]{:S(2)}) collective-permute-start(bf16[16,8192]{1,0:T(8,128)(2,1)S(1)} %collective-permute-done.9.refs_45_.refs_4_), channel_id=1, source_target_pairs={{0,2},{1,3},{4,0},{5,1},{8,4},{9,5},{12,8},{13,9},{14,12},{15,13},... | collective-permute-start | bytes 786440 | tf_op jit(solution)/shard_map/ppermute | solution.py:118
  43.3 1.3 collective-permute-start.37
  43.3 1.5 collective-permute-start.39
  44.5 1.3 collective-permute-start.46
  44.8 1.3 collective-permute-start.33
  45.2 1.3 collective-permute-start.35
  45.9 25.6 %collective-permute-start.6 = (bf16[16,8192]{1,0:T(8,128)(2,1)}, bf16[16,8192]{1,0:T(8,128)(2,1)S(1)}, u32[]{:S(2)}, u32[]{:S(2)}) collective-permute-start(bf16[16,8192]{1,0:T(8,128)(2,1)} %refs_0_), channel_id=1, source_target_pairs={{0,1},{1,0},{2,3},{3,2},{4,5},{5,4},{6,7},{7,6},{8,9},{9,8},{10,11... | collective-permute-start | bytes 786440 | tf_op jit(solution)/shard_map/ppermute | solution.py:122
  46.2 43.2 %collective-permute-start.10 = (bf16[16,8192]{1,0:T(8,128)(2,1)S(1)}, bf16[16,8192]{1,0:T(8,128)(2,1)S(1)}, u32[]{:S(2)}, u32[]{:S(2)}) collective-permute-start(bf16[16,8192]{1,0:T(8,128)(2,1)S(1)} %collective-permute-done.9.refs_45_.refs_4_), channel_id=1, source_target_pairs={{0,1},{1,0},{2,3},{3,2},{4,5},{5,4},{6,7},{7,6},{8,9},{9,8},{10,11... | collective-permute-start | bytes 786440 | tf_op jit(solution)/shard_map/ppermute | solution.py:122
  46.5 43.0 %collective-permute-start.8 = (bf16[16,8192]{1,0:T(8,128)(2,1)S(1)}, bf16[16,8192]{1,0:T(8,128)(2,1)S(1)}, u32[]{:S(2)}, u32[]{:S(2)}) collective-permute-start(bf16[16,8192]{1,0:T(8,128)(2,1)S(1)} %collective-permute-done.7.refs_44_.refs_2_), channel_id=1, source_target_pairs={{0,1},{1,0},{2,3},{3,2},{4,5},{5,4},{6,7},{7,6},{8,9},{9,8},{10,11... | collective-permute-start | bytes 786440 | tf_op jit(solution)/shard_map/ppermute | solution.py:122
  49.9 19.8 %collective-permute-start.15 = (bf16[16,8192]{1,0:T(8,128)(2,1)S(1)}, bf16[16,8192]{1,0:T(8,128)(2,1)S(1)}, u32[]{:S(2)}, u32[]{:S(2)}) collective-permute-start(bf16[16,8192]{1,0:T(8,128)(2,1)S(1)} %collective-permute-done.11.refs_44_.refs_6_), channel_id=1, source_target_pairs={{0,4},{1,5},{4,8},{5,9},{8,12},{9,13},{12,14},{13,15},{14,10},{15,... | collective-permute-start | bytes 786440 | tf_op jit(solution)/shard_map/ppermute | solution.py:118
  51.5 18.3 %collective-permute-start.17 = (bf16[16,8192]{1,0:T(8,128)(2,1)S(1)}, bf16[16,8192]{1,0:T(8,128)(2,1)S(1)}, u32[]{:S(2)}, u32[]{:S(2)}) collective-permute-start(bf16[16,8192]{1,0:T(8,128)(2,1)S(1)} %collective-permute-done.13.refs_45_.refs_8_), channel_id=1, source_target_pairs={{0,2},{1,3},{4,0},{5,1},{8,4},{9,5},{12,8},{13,9},{14,12},{15,13},... | collective-permute-start | bytes 786440 | tf_op jit(solution)/shard_map/ppermute | solution.py:118
  69.7 20.4 %collective-permute-start.12 = (bf16[16,8192]{1,0:T(8,128)(2,1)S(1)}, bf16[16,8192]{1,0:T(8,128)(2,1)S(1)}, u32[]{:S(2)}, u32[]{:S(2)}) collective-permute-start(bf16[16,8192]{1,0:T(8,128)(2,1)S(1)} %collective-permute-done.11.refs_44_.refs_6_), channel_id=1, source_target_pairs={{0,1},{1,0},{2,3},{3,2},{4,5},{5,4},{6,7},{7,6},{8,9},{9,8},{10,11... | collective-permute-start | bytes 786440 | tf_op jit(solution)/shard_map/ppermute | solution.py:122
  69.8 20.4 %collective-permute-start.19 = (bf16[16,4096]{1,0:T(8,128)(2,1)S(1)}, bf16[16,4096]{1,0:T(8,128)(2,1)S(1)}, u32[]{:S(2)}, u32[]{:S(2)}) collective-permute-start(bf16[16,4096]{1,0:T(8,128)(2,1)S(1)} %slice.32), channel_id=1, source_target_pairs={{0,4},{1,5},{4,8},{5,9},{8,12},{9,13},{12,14},{13,15},{14,10},{15,... | collective-permute-start | bytes 393224 | tf_op jit(solution)/shard_map/ppermute | solution.py:118
  71.5 19.2 %collective-permute-start.21 = (bf16[16,4096]{1,0:T(8,128)(2,1)S(1)}, bf16[16,4096]{1,0:T(8,128)(2,1)S(1)}, u32[]{:S(2)}, u32[]{:S(2)}) collective-permute-start(bf16[16,4096]{1,0:T(8,128)(2,1)S(1)} %slice.33), channel_id=1, source_target_pairs={{0,2},{1,3},{4,0},{5,1},{8,4},{9,5},{12,8},{13,9},{14,12},{15,13},... | collective-permute-start | bytes 393224 | tf_op jit(solution)/shard_map/ppermute | solution.py:118
  89.4 10.7 %collective-permute-start.14 = (bf16[16,8192]{1,0:T(8,128)(2,1)S(1)}, bf16[16,8192]{1,0:T(8,128)(2,1)S(1)}, u32[]{:S(2)}, u32[]{:S(2)}) collective-permute-start(bf16[16,8192]{1,0:T(8,128)(2,1)S(1)} %copy-done.34), channel_id=1, source_target_pairs={{0,1},{1,0},{2,3},{3,2},{4,5},{5,4},{6,7},{7,6},{8,9},{9,8},{10,11... | collective-permute-start | bytes 786440 | tf_op jit(solution)/shard_map/ppermute | solution.py:122
  89.6 10.6 %collective-permute-start.16 = (bf16[16,8192]{1,0:T(8,128)(2,1)S(1)}, bf16[16,8192]{1,0:T(8,128)(2,1)S(1)}, u32[]{:S(2)}, u32[]{:S(2)}) collective-permute-start(bf16[16,8192]{1,0:T(8,128)(2,1)S(1)} %collective-permute-done.15.refs_44_.refs_10_), channel_id=1, source_target_pairs={{0,1},{1,0},{2,3},{3,2},{4,5},{5,4},{6,7},{7,6},{8,9},{9,8},{10,11... | collective-permute-start | bytes 786440 | tf_op jit(solution)/shard_map/ppermute | solution.py:122
  90.1 10.1 %collective-permute-start.18 = (bf16[16,8192]{1,0:T(8,128)(2,1)S(1)}, bf16[16,8192]{1,0:T(8,128)(2,1)S(1)}, u32[]{:S(2)}, u32[]{:S(2)}) collective-permute-start(bf16[16,8192]{1,0:T(8,128)(2,1)S(1)} %collective-permute-done.17.refs_45_.refs_12_), channel_id=1, source_target_pairs={{0,1},{1,0},{2,3},{3,2},{4,5},{5,4},{6,7},{7,6},{8,9},{9,8},{10,11... | collective-permute-start | bytes 786440 | tf_op jit(solution)/shard_map/ppermute | solution.py:122
  90.2 9.9 %collective-permute-start.20 = (bf16[16,4096]{1,0:T(8,128)(2,1)S(1)}, bf16[16,4096]{1,0:T(8,128)(2,1)S(1)}, u32[]{:S(2)}, u32[]{:S(2)}) collective-permute-start(bf16[16,4096]{1,0:T(8,128)(2,1)S(1)} %collective-permute-done.19.refs_14_), channel_id=1, source_target_pairs={{0,1},{1,0},{2,3},{3,2},{4,5},{5,4},{6,7},{7,6},{8,9},{9,8},{10,11... | collective-permute-start | bytes 393224 | tf_op jit(solution)/shard_map/ppermute | solution.py:122
  90.7 9.5 %collective-permute-start.22 = (bf16[16,4096]{1,0:T(8,128)(2,1)S(1)}, bf16[16,4096]{1,0:T(8,128)(2,1)S(1)}, u32[]{:S(2)}, u32[]{:S(2)}) collective-permute-start(bf16[16,4096]{1,0:T(8,128)(2,1)S(1)} %collective-permute-done.21.refs_16_), channel_id=1, source_target_pairs={{0,1},{1,0},{2,3},{3,2},{4,5},{5,4},{6,7},{7,6},{8,9},{9,8},{10,11... | collective-permute-start | bytes 393224 | tf_op jit(solution)/shard_map/ppermute | solution.py:122
  123.7 13.8 %all-to-all-start = ((f32[16,16,256]{2,1,0:T(8,128)}), f32[16,16,256]{2,1,0:T(8,128)S(1)}, u32[]{:S(2)}, u32[]{:S(2)}) async-start(f32[16,16,256]{2,1,0:T(8,128)} %shard_map.107), calls=%async_computation | async-start | bytes 524288 | tf_op jit(solution)/shard_map/all_to_all | solution.py:434
  (42 other events, 606.1 us)

commit v5 on v4

--- a/solution.py
+++ b/solution.py
@@ -12,7 +12,7 @@
 TILE = 256
 DEPTH = 2048
 SPLIT = 4
-VMEM = 56 * 1024 * 1024
+MEBI = 1024 * 1024
 HIGH = lax.Precision.HIGHEST
 
 
@@ -122,13 +122,13 @@
     return lax.ppermute(block, "hid", [(h, h ^ 1) for h in range(2 * chips)])
 
 
-def gather_blocks(own, chips, base=0):
+def gather_blocks(own, chips):
     half = own.shape[1] // 2
-    places, blocks, steps = [], [], []
+    places, blocks = [], []
 
     def found(offset, column, block):
         for other in range(2):
-            places.append((offset, other, base + column))
+            places.append((offset, other, column))
             blocks.append(core_swap(block, chips) if other else block)
 
     found(0, 0, own)
@@ -138,15 +138,10 @@
         behind = ring_step(behind, chips, -1)
         found(-step, 0, ahead)
         found(step, 0, behind)
-        steps.append((ahead, behind))
     across = chips // 2
     found(across, 0, ring_step(ahead[:, :half], chips, 1))
     found(across, half, ring_step(behind[:, half:], chips, -1))
-    return places, blocks, steps
-
-
-def after(value, *others):
-    return lax.optimization_barrier((value, *others))[0]
+    return places, blocks
 
 
 def assemble(places, chips, blocks, whole, sems):
@@ -170,55 +165,53 @@
     return lax.dot_general(a, b, (((1,), (1,)), ((), ())), preferred_element_type=jnp.float32)
 
 
-def deep_dot(left, rights):
-    total, start = None, 0
-    for right in rights:
-        part = pl.ds(start, right.shape[0])
-        term = jnp.dot(left[:, part], right[...], preferred_element_type=jnp.float32)
-        total = term if total is None else total + term
-        start += right.shape[0]
-    return total
-
-
 def forward_kernel(places, chips, *refs):
     count = len(places)
     blocks, refs = refs[:count], refs[count:]
-    (gate, up, whole, sems), weights = refs[-4:], refs[: 2 * SPLIT]
-
-    @pl.when(pl.program_id(0) == 0)
+    gate_weight, up_weight, gate, up, gate_sum, up_sum, whole, sems = refs
+    n, k = pl.program_id(0), pl.program_id(1)
+
+    @pl.when((n == 0) & (k == 0))
     def _():
         assemble(places, chips, blocks, whole, sems)
 
-    gate[...] = deep_dot(whole, weights[:SPLIT]).T
-    up[...] = deep_dot(whole, weights[SPLIT:]).T
-
-
-def forward(places, chips, blocks, gate_weight, up_weight, tile, first, tiles, waits):
     depth = gate_weight.shape[0]
+    x = whole[:, pl.ds(pl.multiple_of(k * depth, depth), depth)]
+    gate_part = jnp.dot(x, gate_weight[...], preferred_element_type=jnp.float32)
+    up_part = jnp.dot(x, up_weight[...], preferred_element_type=jnp.float32)
+
+    @pl.when(k == 0)
+    def _():
+        gate_sum[...] = gate_part
+        up_sum[...] = up_part
+
+    @pl.when(k == 1)
+    def _():
+        gate[...] = (gate_sum[...] + gate_part).T
+        up[...] = (up_sum[...] + up_part).T
+
+
+def forward(places, chips, blocks, gate_weight, up_weight, tile):
+    depth, width = gate_weight.shape
     rows = blocks[0].shape[0] * chips * 2
     return pl.pallas_call(
         functools.partial(forward_kernel, places, chips),
-        grid=(tiles,),
-        out_shape=[jax.ShapeDtypeStruct((tiles * tile, rows), jnp.float32)] * 2,
+        grid=(width // tile, 2),
+        out_shape=[jax.ShapeDtypeStruct((width, rows), jnp.float32)] * 2,
         in_specs=[pl.BlockSpec(memory_space=pl.ANY)] * len(blocks)
-        + [
-            pl.BlockSpec((depth // SPLIT, tile), lambda n, q=q: (q, n + first))
-            for q in range(SPLIT)
-        ]
-        * 2
-        + [pl.BlockSpec(memory_space=pl.ANY)] * len(waits),
-        out_specs=[pl.BlockSpec((tile, rows), lambda n: (n, 0))] * 2,
+        + [pl.BlockSpec((depth // 2, tile), lambda n, k: (k, n))] * 2,
+        out_specs=[pl.BlockSpec((tile, rows), lambda n, k: (n, 0))] * 2,
         scratch_shapes=[
+            pltpu.VMEM((rows, tile), jnp.float32),
+            pltpu.VMEM((rows, tile), jnp.float32),
             pltpu.VMEM((rows, depth), jnp.bfloat16),
             pltpu.SemaphoreType.DMA((len(blocks),)),
         ],
-        compiler_params=pltpu.CompilerParams(vmem_limit_bytes=VMEM),
+        compiler_params=pltpu.CompilerParams(vmem_limit_bytes=20 * MEBI),
         cost_estimate=pl.CostEstimate(
-            flops=8 * rows * depth * tiles * tile,
-            bytes_accessed=8 * depth * tiles * tile,
-            transcendentals=0,
+            flops=4 * rows * depth * width, bytes_accessed=4 * depth * width, transcendentals=0
         ),
-    )(*blocks, *[gate_weight] * SPLIT, *[up_weight] * SPLIT, *waits)
+    )(*blocks, gate_weight, up_weight)
 
 
 def inputs_kernel(places, chips, *refs):
@@ -244,7 +237,7 @@
             pltpu.VMEM((rows, depth), jnp.bfloat16),
             pltpu.SemaphoreType.DMA((len(blocks),)),
         ],
-        compiler_params=pltpu.CompilerParams(vmem_limit_bytes=VMEM),
+        compiler_params=pltpu.CompilerParams(vmem_limit_bytes=24 * MEBI),
         cost_estimate=pl.CostEstimate(
             flops=16 * R * rows * depth, bytes_accessed=8 * R * depth, transcendentals=0
         ),
@@ -351,7 +344,7 @@
             pltpu.VMEM((3 * R, rows), jnp.float32),
             pltpu.SemaphoreType.DMA((len(blocks),)),
         ],
-        compiler_params=pltpu.CompilerParams(vmem_limit_bytes=VMEM),
+        compiler_params=pltpu.CompilerParams(vmem_limit_bytes=32 * MEBI),
         cost_estimate=pl.CostEstimate(
             flops=2 * rows * depth * width, bytes_accessed=2 * depth * width, transcendentals=0
         ),
@@ -389,7 +382,7 @@
         ),
         in_specs=[vmem] * 4,
         out_specs=(vmem, vmem),
-        compiler_params=pltpu.CompilerParams(vmem_limit_bytes=VMEM),
+        compiler_params=pltpu.CompilerParams(vmem_limit_bytes=24 * MEBI),
     )(received, inputs, ids, tests)
 
 
@@ -406,30 +399,11 @@
 ):
     chips = lax.axis_size("hid") // 2
     ids = example_ids[None, :]
-    half = tokens.shape[1] // 2
-    places, token_blocks, _ = gather_blocks(tokens[:, :half], chips)
-    more_places, more_blocks, steps = gather_blocks(tokens[:, half:], chips, half)
-    places, token_blocks = places + more_places, token_blocks + more_blocks
-    grad_places, grad_blocks, grad_steps = gather_blocks(after(out_grad, *steps[-1]), chips)
-    tiles = gate_weight.shape[1] // TILE
-    shares = -(-tiles // len(grad_steps))
-    gates, ups = [], []
-    for index, first in enumerate(range(0, tiles, shares)):
-        gate, up = forward(
-            places,
-            chips,
-            token_blocks,
-            gate_weight,
-            up_weight,
-            TILE,
-            first,
-            min(shares, tiles - first),
-            grad_steps[index],
-        )
-        gates.append(gate)
-        ups.append(up)
+    places, token_blocks = gather_blocks(tokens, chips)
+    _, grad_blocks = gather_blocks(out_grad, chips)
+    gate, up = forward(places, chips, token_blocks, gate_weight, up_weight, TILE)
     send = backward(
-        grad_places, chips, grad_blocks, down_weight, gates, ups, proj_d.T, proj_ff.T, ids, 1024, TILE
+        places, chips, grad_blocks, down_weight, [gate], [up], proj_d.T, proj_ff.T, ids, 1024, TILE
     )
     received = lax.all_to_all(send, "hid", 0, 0)
     inputs = project_inputs(places, chips, token_blocks, proj_d.T)

time: 153 us -> 143 us (0.935)
  Pallas kernels: 75.8 us -> 50.9 us
  local copies, waits for them, and re-layouts: 2.81 us -> 19.6 us
  starting transfers between devices: 33.8 us -> 30.6 us
  blocking collectives: 11.4 us -> 13.7 us
  waiting for transfers between devices: 27.1 us -> 25.5 us
    unnamed x108 -> x82, local copies, waits for them, and re-layouts: 1.78 us -> 19.6 us
    pallas_call x3 -> x1, Pallas kernels: 43.9 us -> 28.6 us  [forward(): pl.pallas_call(functools.partial(forward_kernel, places, chips), grid=(wi...]
    pallas_call x1, Pallas kernels: 6.59 us -> 2.37 us  [project_inputs(): pl.pallas_call(functools.partial(inputs_kernel, places, chips), out_shape...]
    pallas_call x1, Pallas kernels: 22.6 us -> 18.9 us  [backward(): pl.pallas_call(functools.partial(backward_kernel, places, chips, examples...]
    ppermute x24 -> x16, waiting for transfers between devices: 22 us -> 25.5 us  [ring_step(): return lax.ppermute(block, 'hid', pairs)]
    all_to_all x1, waiting for transfers between devices: 3.45 us -> 0.01 us  [local_ring(): received = lax.all_to_all(send, 'hid', 0, 0)]
    ppermute x24 -> x16, starting transfers between devices: 26 us -> 22.6 us  [ring_step(): return lax.ppermute(block, 'hid', pairs)]
    all_to_all x1, blocking collectives: 11.4 us -> 13.7 us  [local_ring(): scores = jnp.sum(lax.all_to_all(partial, 'hid', 0, 0), axis=0)]
  transfers between devices with their start and end apart: 52 -> 35, of which waited for: 17 -> 13; matrix products, arithmetic and copies ran while one was open for 0% -> 0% of each run, Pallas kernels for 33% -> 22%
where the time goes in v5:
time: 143 us; the launch traced here: 142 us
  Pallas kernels  50.9 us (36%)
  starting transfers between devices  30.6 us (21%)
  waiting for transfers between devices  25.5 us (18%)
  local copies, waits for them, and re-layouts  19.6 us (14%)
  blocking collectives  13.7 us (10%)
    pallas_call x1, Pallas kernels, forward(): pl.pallas_call(functools.partial(forward_kernel, places, chips), grid=(wi...  28.6 us
    ppermute x16, waiting for transfers between devices, ring_step(): return lax.ppermute(block, 'hid', pairs)  25.5 us
    ppermute x16, starting transfers between devices, ring_step(): return lax.ppermute(block, 'hid', pairs)  22.6 us
    unnamed x82, local copies, waits for them, and re-layouts  19.6 us
    pallas_call x1, Pallas kernels, backward(): pl.pallas_call(functools.partial(backward_kernel, places, chips, examples...  18.9 us
    all_to_all x1, blocking collectives, local_ring(): scores = jnp.sum(lax.all_to_all(partial, 'hid', 0, 0), axis=0)  13.7 us
    all_to_all x1, starting transfers between devices, local_ring(): received = lax.all_to_all(send, 'hid', 0, 0)  5.81 us
  transfers between devices with their start and end apart: 35, of which 13 were waited for; matrix products, arithmetic and copies ran while one was open for 0% of the time, Pallas kernels for 22%

profile of v5, /device:TPU:0, one launch (start us, length us, event | category | flops | bytes accessed | tf_op | source)
XLA Modules:
  0.0 142.0 jit_solution(14278315911883584278)
XLA Ops:
  0.6 3.1 %collective-permute-start.18 = (bf16[16,8192]{1,0:T(8,128)(2,1)}, bf16[16,8192]{1,0:T(8,128)(2,1)S(1)}, u32[]{:S(2)}, u32[]{:S(2)}) collective-permute-start(bf16[16,8192]{1,0:T(8,128)(2,1)} %refs_0_.5), channel_id=1, source_target_pairs={{0,4},{1,5},{4,8},{5,9},{8,12},{9,13},{12,14},{13,15},{14,10},{15,... | collective-permute-start | bytes 786440 | tf_op jit(solution)/shard_map/ppermute | solution.py:118
  3.7 2.0 %collective-permute-start.1 = (bf16[16,8192]{1,0:T(8,128)(2,1)}, bf16[16,8192]{1,0:T(8,128)(2,1)S(1)}, u32[]{:S(2)}, u32[]{:S(2)}) collective-permute-start(bf16[16,8192]{1,0:T(8,128)(2,1)} %refs_0_.4), channel_id=1, source_target_pairs={{0,4},{1,5},{4,8},{5,9},{8,12},{9,13},{12,14},{13,15},{14,10},{15,... | collective-permute-start | bytes 786440 | tf_op jit(solution)/shard_map/ppermute | solution.py:118
  5.7 5.2 %collective-permute-done.18.refs_2_ = bf16[16,8192]{1,0:T(8,128)(2,1)S(1)} collective-permute-done((bf16[16,8192]{1,0:T(8,128)(2,1)}, bf16[16,8192]{1,0:T(8,128)(2,1)S(1)}, u32[]{:S(2)}, u32[]{:S(2)}) %collective-permute-start.18) | collective-permute-done | bytes 262176 | tf_op jit(solution)/shard_map/ppermute | solution.py:118
  11.0 2.2 %collective-permute-done.20.refs_4_ = bf16[16,8192]{1,0:T(8,128)(2,1)S(1)} collective-permute-done((bf16[16,8192]{1,0:T(8,128)(2,1)}, bf16[16,8192]{1,0:T(8,128)(2,1)S(1)}, u32[]{:S(2)}, u32[]{:S(2)}) %collective-permute-start.20) | collective-permute-done | bytes 262176 | tf_op jit(solution)/shard_map/ppermute | solution.py:118
  13.1 1.6 %collective-permute-start.22 = (bf16[16,8192]{1,0:T(8,128)(2,1)S(1)}, bf16[16,8192]{1,0:T(8,128)(2,1)S(1)}, u32[]{:S(2)}, u32[]{:S(2)}) collective-permute-start(bf16[16,8192]{1,0:T(8,128)(2,1)S(1)} %collective-permute-done.18.refs_2_), channel_id=1, source_target_pairs={{0,4},{1,5},{4,8},{5,9},{8,12},{9,13},{12,14},{13,15},{14,10},{15,... | collective-permute-start | bytes 786440 | tf_op jit(solution)/shard_map/ppermute | solution.py:118
  14.7 0.4 collective-permute-start.24
  15.2 1.4 collective-permute-done.1.refs_2_
  16.6 2.0 %collective-permute-done.3.refs_4_ = bf16[16,8192]{1,0:T(8,128)(2,1)S(1)} collective-permute-done((bf16[16,8192]{1,0:T(8,128)(2,1)}, bf16[16,8192]{1,0:T(8,128)(2,1)S(1)}, u32[]{:S(2)}, u32[]{:S(2)}) %collective-permute-start.3) | collective-permute-done | bytes 262176 | tf_op jit(solution)/shard_map/ppermute | solution.py:118
  18.6 1.6 %collective-permute-start.5 = (bf16[16,8192]{1,0:T(8,128)(2,1)S(1)}, bf16[16,8192]{1,0:T(8,128)(2,1)S(1)}, u32[]{:S(2)}, u32[]{:S(2)}) collective-permute-start(bf16[16,8192]{1,0:T(8,128)(2,1)S(1)} %collective-permute-done.1.refs_2_), channel_id=1, source_target_pairs={{0,4},{1,5},{4,8},{5,9},{8,12},{9,13},{12,14},{13,15},{14,10},{15,... | collective-permute-start | bytes 786440 | tf_op jit(solution)/shard_map/ppermute | solution.py:118
  20.2 1.2 collective-permute-done.22.refs_6_
  21.4 2.9 %collective-permute-start.7 = (bf16[16,8192]{1,0:T(8,128)(2,1)S(1)}, bf16[16,8192]{1,0:T(8,128)(2,1)S(1)}, u32[]{:S(2)}, u32[]{:S(2)}) collective-permute-start(bf16[16,8192]{1,0:T(8,128)(2,1)S(1)} %collective-permute-done.3.refs_4_), channel_id=1, source_target_pairs={{0,2},{1,3},{4,0},{5,1},{8,4},{9,5},{12,8},{13,9},{14,12},{15,13},... | collective-permute-start | bytes 786440 | tf_op jit(solution)/shard_map/ppermute | solution.py:118
  24.3 0.3 collective-permute-start.26
  24.6 1.8 %collective-permute-start.28 = (bf16[16,8192]{1,0:T(8,128)(2,1)S(1)}, bf16[16,8192]{1,0:T(8,128)(2,1)S(1)}, u32[]{:S(2)}, u32[]{:S(2)}) collective-permute-start(bf16[16,8192]{1,0:T(8,128)(2,1)S(1)} %collective-permute-done.24.refs_8_), channel_id=1, source_target_pairs={{0,2},{1,3},{4,0},{5,1},{8,4},{9,5},{12,8},{13,9},{14,12},{15,13},... | collective-permute-start | bytes 786440 | tf_op jit(solution)/shard_map/ppermute | solution.py:118
  26.4 0.9 collective-permute-done.5.refs_6_
  27.3 2.0 %collective-permute-start.9 = (bf16[16,8192]{1,0:T(8,128)(2,1)S(1)}, bf16[16,8192]{1,0:T(8,128)(2,1)S(1)}, u32[]{:S(2)}, u32[]{:S(2)}) collective-permute-start(bf16[16,8192]{1,0:T(8,128)(2,1)S(1)} %collective-permute-done.5.refs_6_), channel_id=1, source_target_pairs={{0,4},{1,5},{4,8},{5,9},{8,12},{9,13},{12,14},{13,15},{14,10},{15,... | collective-permute-start | bytes 786440 | tf_op jit(solution)/shard_map/ppermute | solution.py:118
  29.3 0.6 collective-permute-done.7.refs_8_
  29.8 0.5 collective-permute-start.23
  30.3 3.1 %collective-permute-done.26.refs_10_ = bf16[16,8192]{1,0:T(8,128)(2,1)S(1)} collective-permute-done((bf16[16,8192]{1,0:T(8,128)(2,1)S(1)}, bf16[16,8192]{1,0:T(8,128)(2,1)S(1)}, u32[]{:S(2)}, u32[]{:S(2)}) %collective-permute-start.26) | collective-permute-done | bytes 262176 | tf_op jit(solution)/shard_map/ppermute | solution.py:118
  33.5 0.8 collective-permute-done.28.refs_12_
  34.3 2.0 %collective-permute-start.11 = (bf16[16,8192]{1,0:T(8,128)(2,1)S(1)}, bf16[16,8192]{1,0:T(8,128)(2,1)S(1)}, u32[]{:S(2)}, u32[]{:S(2)}) collective-permute-start(bf16[16,8192]{1,0:T(8,128)(2,1)S(1)} %collective-permute-done.7.refs_8_), channel_id=1, source_target_pairs={{0,2},{1,3},{4,0},{5,1},{8,4},{9,5},{12,8},{13,9},{14,12},{15,13},... | collective-permute-start | bytes 786440 | tf_op jit(solution)/shard_map/ppermute | solution.py:118
  36.3 2.4 %collective-permute-done.9.refs_10_ = bf16[16,8192]{1,0:T(8,128)(2,1)S(1)} collective-permute-done((bf16[16,8192]{1,0:T(8,128)(2,1)S(1)}, bf16[16,8192]{1,0:T(8,128)(2,1)S(1)}, u32[]{:S(2)}, u32[]{:S(2)}) %collective-permute-start.9) | collective-permute-done | bytes 262176 | tf_op jit(solution)/shard_map/ppermute | solution.py:118
  38.7 1.6 %collective-permute-start.30 = (bf16[16,4096]{1,0:T(8,128)(2,1)S(1)}, bf16[16,4096]{1,0:T(8,128)(2,1)S(1)}, u32[]{:S(2)}, u32[]{:S(2)}) collective-permute-start(bf16[16,4096]{1,0:T(8,128)(2,1)S(1)} %slice.18), channel_id=1, source_target_pairs={{0,4},{1,5},{4,8},{5,9},{8,12},{9,13},{12,14},{13,15},{14,10},{15,... | collective-permute-start | bytes 393224 | tf_op jit(solution)/shard_map/ppermute | solution.py:118
  40.2 0.5 collective-permute-start.32
  40.8 1.5 %collective-permute-start.13 = (bf16[16,4096]{1,0:T(8,128)(2,1)S(1)}, bf16[16,4096]{1,0:T(8,128)(2,1)S(1)}, u32[]{:S(2)}, u32[]{:S(2)}) collective-permute-start(bf16[16,4096]{1,0:T(8,128)(2,1)S(1)} %slice.16), channel_id=1, source_target_pairs={{0,4},{1,5},{4,8},{5,9},{8,12},{9,13},{12,14},{13,15},{14,10},{15,... | collective-permute-start | bytes 393224 | tf_op jit(solution)/shard_map/ppermute | solution.py:118
  42.3 0.5 collective-permute-start.29
  42.8 0.0 copy-start
  42.8 0.0 copy-start.1
  42.8 0.0 copy-start.7
  42.8 2.2 %collective-permute-done.30.refs_14_ = bf16[16,4096]{1,0:T(8,128)(2,1)S(1)} collective-permute-done((bf16[16,4096]{1,0:T(8,128)(2,1)S(1)}, bf16[16,4096]{1,0:T(8,128)(2,1)S(1)}, u32[]{:S(2)}, u32[]{:S(2)}) %collective-permute-start.30) | collective-permute-done | bytes 131104 | tf_op jit(solution)/shard_map/ppermute | solution.py:118
  45.0 1.4 %collective-permute-start.15 = (bf16[16,4096]{1,0:T(8,128)(2,1)S(1)}, bf16[16,4096]{1,0:T(8,128)(2,1)S(1)}, u32[]{:S(2)}, u32[]{:S(2)}) collective-permute-start(bf16[16,4096]{1,0:T(8,128)(2,1)S(1)} %slice.17), channel_id=1, source_target_pairs={{0,2},{1,3},{4,0},{5,1},{8,4},{9,5},{12,8},{13,9},{14,12},{15,13},... | collective-permute-start | bytes 393224 | tf_op jit(solution)/shard_map/ppermute | solution.py:118
  46.5 1.0 collective-permute-done.13.refs_14_
  47.4 2.5 %collective-permute-done.15.refs_16_ = bf16[16,4096]{1,0:T(8,128)(2,1)S(1)} collective-permute-done((bf16[16,4096]{1,0:T(8,128)(2,1)S(1)}, bf16[16,4096]{1,0:T(8,128)(2,1)S(1)}, u32[]{:S(2)}, u32[]{:S(2)}) %collective-permute-start.15) | collective-permute-done | bytes 131104 | tf_op jit(solution)/shard_map/ppermute | solution.py:118
  50.0 0.5 collective-permute-start.10
  50.5 0.1 collective-permute-start.12
  50.6 0.4 collective-permute-start.14
  51.0 0.1 collective-permute-start.16
  51.1 1.0 copy-done.8
  52.1 28.6 %shard_map.104 = (f32[1792,256]{1,0:T(8,128)S(1)}, f32[1792,256]{1,0:T(8,128)S(1)}) custom-call(bf16[16,8192]{1,0:T(8,128)(2,1)S(1)} %copy-done.8, bf16[16,8192]{1,0:T(8,128)(2,1)S(1)} %collective-permute-done.17.refs_1_, bf16[16,8192]{1,0:T(8,128)(2,1)S(1)} %collective-permute-done.18.refs_2_, bf16[16,8192]{1,0:T(8,128)(2,1)S(1)} %collective-permute-done.19.refs_3_, ...), custom_call_target="tpu_custom_call" | custom-call | flops 15032385536 | bytes 58720256 | tf_op jit(solution)/shard_map/pallas_call | solution.py:197
  80.9 18.9 %shard_map.105 = f32[16,16,256]{2,1,0:T(8,128)} custom-call(bf16[16,8192]{1,0:T(8,128)(2,1)S(1)} %copy-done.7, bf16[16,8192]{1,0:T(8,128)(2,1)S(1)} %collective-permute-done.refs_1_, bf16[16,8192]{1,0:T(8,128)(2,1)S(1)} %collective-permute-done.1.refs_2_, bf16[16,8192]{1,0:T(8,128)(2,1)S(1)} %collective-permute-done.2.refs_3_, ...), custom_call_target="tpu_custom_call" | custom-call | flops 7516192768 | bytes 29360128 | tf_op jit(solution)/shard_map/pallas_call | solution.py:324
  99.8 5.8 %all-to-all-start = ((f32[16,16,256]{2,1,0:T(8,128)}), f32[16,16,256]{2,1,0:T(8,128)S(1)}, u32[]{:S(2)}, u32[]{:S(2)}) async-start(f32[16,16,256]{2,1,0:T(8,128)} %shard_map.105), calls=%async_computation | async-start | bytes 524288 | tf_op jit(solution)/shard_map/all_to_all | solution.py:408
  105.6 0.9 copy-done.3
  106.6 0.9 copy-done.5
  107.5 0.9 copy-done.9
  108.5 0.9 copy-done.11
  109.4 0.9 copy-done.13
  110.4 0.9 copy-done.15
  111.3 0.9 copy-done.17
  112.3 0.9 copy-done.19
  113.2 0.9 copy-done.21
  114.2 0.9 copy-done.23
  115.1 0.9 copy-done.25
  116.1 0.9 copy-done.27
  117.0 0.9 copy-done.29
  118.0 0.9 copy-done.31
  118.9 0.9 copy-done.33
  119.8 0.9 copy-done.35
  120.7 0.9 copy-done.37
  121.6 2.4 %shard_map.106.inputs = f32[128,256]{1,0:T(8,128)S(1)} custom-call(bf16[16,8192]{1,0:T(8,128)(2,1)S(1)} %copy-done.9, bf16[16,8192]{1,0:T(8,128)(2,1)S(1)} %copy-done.15, bf16[16,8192]{1,0:T(8,128)(2,1)S(1)} %copy-done.11, bf16[16,8192]{1,0:T(8,128)(2,1)S(1)} %copy-done.21, bf16[16,8192]{1,0:T(8,128)(2,1)S(1)} %copy-done.13, ...), custom_call_target="tpu_custom_call" | custom-call | flops 2147483648 | bytes 4194304 | tf_op jit(solution)/shard_map/pallas_call | solution.py:231
  124.0 0.6 copy-done.38
  124.7 1.0 copy-done.6
  125.7 0.9 copy-done.39
  126.6 1.1 shard_map.107
  127.7 13.7 %all_to_all.10 = f32[16,8,256]{2,1,0:T(8,128)S(1)} all-to-all(f32[16,8,256]{2,1,0:T(8,128)S(1)} %get-tuple-element.9), channel_id=1, replica_groups=mesh['groups'=2,'hid'=16,'mod'=1] {'hid'}, dimensions={0} | all-to-all | bytes 262144 | tf_op jit(solution)/shard_map/all_to_all | solution.py:411
  141.4 0.6 reduce_sum.9
  (98 shorter events, 0.2 us)
Async XLA Ops:
  0.6 10.3 %collective-permute-start.18 = (bf16[16,8192]{1,0:T(8,128)(2,1)}, bf16[16,8192]{1,0:T(8,128)(2,1)S(1)}, u32[]{:S(2)}, u32[]{:S(2)}) collective-permute-start(bf16[16,8192]{1,0:T(8,128)(2,1)} %refs_0_.5), channel_id=1, source_target_pairs={{0,4},{1,5},{4,8},{5,9},{8,12},{9,13},{12,14},{13,15},{14,10},{15,... | collective-permute-start | bytes 786440 | tf_op jit(solution)/shard_map/ppermute | solution.py:118
  3.7 9.4 %collective-permute-start.20 = (bf16[16,8192]{1,0:T(8,128)(2,1)}, bf16[16,8192]{1,0:T(8,128)(2,1)S(1)}, u32[]{:S(2)}, u32[]{:S(2)}) collective-permute-start(bf16[16,8192]{1,0:T(8,128)(2,1)} %refs_0_.5), channel_id=1, source_target_pairs={{0,2},{1,3},{4,0},{5,1},{8,4},{9,5},{12,8},{13,9},{14,12},{15,13},... | collective-permute-start | bytes 786440 | tf_op jit(solution)/shard_map/ppermute | solution.py:118
  3.7 11.0 %collective-permute-start.17 = (bf16[16,8192]{1,0:T(8,128)(2,1)}, bf16[16,8192]{1,0:T(8,128)(2,1)S(1)}, u32[]{:S(2)}, u32[]{:S(2)}) collective-permute-start(bf16[16,8192]{1,0:T(8,128)(2,1)} %refs_0_.5), channel_id=1, source_target_pairs={{0,1},{1,0},{2,3},{3,2},{4,5},{5,4},{6,7},{7,6},{8,9},{9,8},{10,11... | collective-permute-start | bytes 786440 | tf_op jit(solution)/shard_map/ppermute | solution.py:122
  3.7 12.9 %collective-permute-start.1 = (bf16[16,8192]{1,0:T(8,128)(2,1)}, bf16[16,8192]{1,0:T(8,128)(2,1)S(1)}, u32[]{:S(2)}, u32[]{:S(2)}) collective-permute-start(bf16[16,8192]{1,0:T(8,128)(2,1)} %refs_0_.4), channel_id=1, source_target_pairs={{0,4},{1,5},{4,8},{5,9},{8,12},{9,13},{12,14},{13,15},{14,10},{15,... | collective-permute-start | bytes 786440 | tf_op jit(solution)/shard_map/ppermute | solution.py:118
  5.7 12.8 %collective-permute-start.3 = (bf16[16,8192]{1,0:T(8,128)(2,1)}, bf16[16,8192]{1,0:T(8,128)(2,1)S(1)}, u32[]{:S(2)}, u32[]{:S(2)}) collective-permute-start(bf16[16,8192]{1,0:T(8,128)(2,1)} %refs_0_.4), channel_id=1, source_target_pairs={{0,2},{1,3},{4,0},{5,1},{8,4},{9,5},{12,8},{13,9},{14,12},{15,13},... | collective-permute-start | bytes 786440 | tf_op jit(solution)/shard_map/ppermute | solution.py:118
  11.0 69.7 %copy-start.10 = (bf16[16,8192]{1,0:T(8,128)(2,1)}, bf16[16,8192]{1,0:T(8,128)(2,1)S(1)}, u32[]{:S(2)}) copy-start(bf16[16,8192]{1,0:T(8,128)(2,1)S(1)} %collective-permute-done.18.refs_2_) | copy-start | bytes 786436
  11.0 7.6 %collective-permute-start = (bf16[16,8192]{1,0:T(8,128)(2,1)}, bf16[16,8192]{1,0:T(8,128)(2,1)S(1)}, u32[]{:S(2)}, u32[]{:S(2)}) collective-permute-start(bf16[16,8192]{1,0:T(8,128)(2,1)} %refs_0_.4), channel_id=1, source_target_pairs={{0,1},{1,0},{2,3},{3,2},{4,5},{5,4},{6,7},{7,6},{8,9},{9,8},{10,11... | collective-permute-start | bytes 786440 | tf_op jit(solution)/shard_map/ppermute | solution.py:122
  13.1 67.5 %copy-start.12 = (bf16[16,8192]{1,0:T(8,128)(2,1)}, bf16[16,8192]{1,0:T(8,128)(2,1)S(1)}, u32[]{:S(2)}) copy-start(bf16[16,8192]{1,0:T(8,128)(2,1)S(1)} %collective-permute-done.20.refs_4_) | copy-start | bytes 786436
  13.1 8.2 %collective-permute-start.22 = (bf16[16,8192]{1,0:T(8,128)(2,1)S(1)}, bf16[16,8192]{1,0:T(8,128)(2,1)S(1)}, u32[]{:S(2)}, u32[]{:S(2)}) collective-permute-start(bf16[16,8192]{1,0:T(8,128)(2,1)S(1)} %collective-permute-done.18.refs_2_), channel_id=1, source_target_pairs={{0,4},{1,5},{4,8},{5,9},{8,12},{9,13},{12,14},{13,15},{14,10},{15,... | collective-permute-start | bytes 786440 | tf_op jit(solution)/shard_map/ppermute | solution.py:118
  14.7 66.0 %copy-start.14 = (bf16[16,8192]{1,0:T(8,128)(2,1)}, bf16[16,8192]{1,0:T(8,128)(2,1)S(1)}, u32[]{:S(2)}) copy-start(bf16[16,8192]{1,0:T(8,128)(2,1)S(1)} %collective-permute-done.17.refs_1_) | copy-start | bytes 786436
  14.7 9.5 %collective-permute-start.24 = (bf16[16,8192]{1,0:T(8,128)(2,1)S(1)}, bf16[16,8192]{1,0:T(8,128)(2,1)S(1)}, u32[]{:S(2)}, u32[]{:S(2)}) collective-permute-start(bf16[16,8192]{1,0:T(8,128)(2,1)S(1)} %collective-permute-done.20.refs_4_), channel_id=1, source_target_pairs={{0,2},{1,3},{4,0},{5,1},{8,4},{9,5},{12,8},{13,9},{14,12},{15,13},... | collective-permute-start | bytes 786440 | tf_op jit(solution)/shard_map/ppermute | solution.py:118
  16.6 7.7 %collective-permute-start.19 = (bf16[16,8192]{1,0:T(8,128)(2,1)S(1)}, bf16[16,8192]{1,0:T(8,128)(2,1)S(1)}, u32[]{:S(2)}, u32[]{:S(2)}) collective-permute-start(bf16[16,8192]{1,0:T(8,128)(2,1)S(1)} %collective-permute-done.18.refs_2_), channel_id=1, source_target_pairs={{0,1},{1,0},{2,3},{3,2},{4,5},{5,4},{6,7},{7,6},{8,9},{9,8},{10,11... | collective-permute-start | bytes 786440 | tf_op jit(solution)/shard_map/ppermute | solution.py:122
  18.6 6.0 %collective-permute-start.21 = (bf16[16,8192]{1,0:T(8,128)(2,1)S(1)}, bf16[16,8192]{1,0:T(8,128)(2,1)S(1)}, u32[]{:S(2)}, u32[]{:S(2)}) collective-permute-start(bf16[16,8192]{1,0:T(8,128)(2,1)S(1)} %collective-permute-done.20.refs_4_), channel_id=1, source_target_pairs={{0,1},{1,0},{2,3},{3,2},{4,5},{5,4},{6,7},{7,6},{8,9},{9,8},{10,11... | collective-permute-start | bytes 786440 | tf_op jit(solution)/shard_map/ppermute | solution.py:122
  18.6 8.7 %collective-permute-start.5 = (bf16[16,8192]{1,0:T(8,128)(2,1)S(1)}, bf16[16,8192]{1,0:T(8,128)(2,1)S(1)}, u32[]{:S(2)}, u32[]{:S(2)}) collective-permute-start(bf16[16,8192]{1,0:T(8,128)(2,1)S(1)} %collective-permute-done.1.refs_2_), channel_id=1, source_target_pairs={{0,4},{1,5},{4,8},{5,9},{8,12},{9,13},{12,14},{13,15},{14,10},{15,... | collective-permute-start | bytes 786440 | tf_op jit(solution)/shard_map/ppermute | solution.py:118
  21.4 59.3 %copy-start.16 = (bf16[16,8192]{1,0:T(8,128)(2,1)}, bf16[16,8192]{1,0:T(8,128)(2,1)S(1)}, u32[]{:S(2)}) copy-start(bf16[16,8192]{1,0:T(8,128)(2,1)S(1)} %collective-permute-done.22.refs_6_) | copy-start | bytes 786436
  21.4 8.5 %collective-permute-start.7 = (bf16[16,8192]{1,0:T(8,128)(2,1)S(1)}, bf16[16,8192]{1,0:T(8,128)(2,1)S(1)}, u32[]{:S(2)}, u32[]{:S(2)}) collective-permute-start(bf16[16,8192]{1,0:T(8,128)(2,1)S(1)} %collective-permute-done.3.refs_4_), channel_id=1, source_target_pairs={{0,2},{1,3},{4,0},{5,1},{8,4},{9,5},{12,8},{13,9},{14,12},{15,13},... | collective-permute-start | bytes 786440 | tf_op jit(solution)/shard_map/ppermute | solution.py:118
  24.3 56.5 %copy-start.18 = (bf16[16,8192]{1,0:T(8,128)(2,1)}, bf16[16,8192]{1,0:T(8,128)(2,1)S(1)}, u32[]{:S(2)}) copy-start(bf16[16,8192]{1,0:T(8,128)(2,1)S(1)} %collective-permute-done.24.refs_8_) | copy-start | bytes 786436
  24.3 5.6 %collective-permute-start.2 = (bf16[16,8192]{1,0:T(8,128)(2,1)S(1)}, bf16[16,8192]{1,0:T(8,128)(2,1)S(1)}, u32[]{:S(2)}, u32[]{:S(2)}) collective-permute-start(bf16[16,8192]{1,0:T(8,128)(2,1)S(1)} %collective-permute-done.1.refs_2_), channel_id=1, source_target_pairs={{0,1},{1,0},{2,3},{3,2},{4,5},{5,4},{6,7},{7,6},{8,9},{9,8},{10,11... | collective-permute-start | bytes 786440 | tf_op jit(solution)/shard_map/ppermute | solution.py:122
  24.3 56.4 %copy-start.20 = (bf16[16,8192]{1,0:T(8,128)(2,1)}, bf16[16,8192]{1,0:T(8,128)(2,1)S(1)}, u32[]{:S(2)}) copy-start(bf16[16,8192]{1,0:T(8,128)(2,1)S(1)} %collective-permute-done.19.refs_3_) | copy-start | bytes 786436
  24.3 9.2 %collective-permute-start.26 = (bf16[16,8192]{1,0:T(8,128)(2,1)S(1)}, bf16[16,8192]{1,0:T(8,128)(2,1)S(1)}, u32[]{:S(2)}, u32[]{:S(2)}) collective-permute-start(bf16[16,8192]{1,0:T(8,128)(2,1)S(1)} %collective-permute-done.22.refs_6_), channel_id=1, source_target_pairs={{0,4},{1,5},{4,8},{5,9},{8,12},{9,13},{12,14},{13,15},{14,10},{15,... | collective-permute-start | bytes 786440 | tf_op jit(solution)/shard_map/ppermute | solution.py:118
  24.6 56.2 %copy-start.22 = (bf16[16,8192]{1,0:T(8,128)(2,1)}, bf16[16,8192]{1,0:T(8,128)(2,1)S(1)}, u32[]{:S(2)}) copy-start(bf16[16,8192]{1,0:T(8,128)(2,1)S(1)} %collective-permute-done.21.refs_5_) | copy-start | bytes 786436
  24.6 9.7 %collective-permute-start.28 = (bf16[16,8192]{1,0:T(8,128)(2,1)S(1)}, bf16[16,8192]{1,0:T(8,128)(2,1)S(1)}, u32[]{:S(2)}, u32[]{:S(2)}) collective-permute-start(bf16[16,8192]{1,0:T(8,128)(2,1)S(1)} %collective-permute-done.24.refs_8_), channel_id=1, source_target_pairs={{0,2},{1,3},{4,0},{5,1},{8,4},{9,5},{12,8},{13,9},{14,12},{15,13},... | collective-permute-start | bytes 786440 | tf_op jit(solution)/shard_map/ppermute | solution.py:118
  27.3 11.3 %collective-permute-start.9 = (bf16[16,8192]{1,0:T(8,128)(2,1)S(1)}, bf16[16,8192]{1,0:T(8,128)(2,1)S(1)}, u32[]{:S(2)}, u32[]{:S(2)}) collective-permute-start(bf16[16,8192]{1,0:T(8,128)(2,1)S(1)} %collective-permute-done.5.refs_6_), channel_id=1, source_target_pairs={{0,4},{1,5},{4,8},{5,9},{8,12},{9,13},{12,14},{13,15},{14,10},{15,... | collective-permute-start | bytes 786440 | tf_op jit(solution)/shard_map/ppermute | solution.py:118
  29.8 8.8 %collective-permute-start.4 = (bf16[16,8192]{1,0:T(8,128)(2,1)S(1)}, bf16[16,8192]{1,0:T(8,128)(2,1)S(1)}, u32[]{:S(2)}, u32[]{:S(2)}) collective-permute-start(bf16[16,8192]{1,0:T(8,128)(2,1)S(1)} %collective-permute-done.3.refs_4_), channel_id=1, source_target_pairs={{0,1},{1,0},{2,3},{3,2},{4,5},{5,4},{6,7},{7,6},{8,9},{9,8},{10,11... | collective-permute-start | bytes 786440 | tf_op jit(solution)/shard_map/ppermute | solution.py:122
  29.8 10.4 %collective-permute-start.23 = (bf16[16,8192]{1,0:T(8,128)(2,1)S(1)}, bf16[16,8192]{1,0:T(8,128)(2,1)S(1)}, u32[]{:S(2)}, u32[]{:S(2)}) collective-permute-start(bf16[16,8192]{1,0:T(8,128)(2,1)S(1)} %collective-permute-done.22.refs_6_), channel_id=1, source_target_pairs={{0,1},{1,0},{2,3},{3,2},{4,5},{5,4},{6,7},{7,6},{8,9},{9,8},{10,11... | collective-permute-start | bytes 786440 | tf_op jit(solution)/shard_map/ppermute | solution.py:122
  33.5 47.3 %copy-start.2 = (bf16[16,8192]{1,0:T(8,128)(2,1)}, bf16[16,8192]{1,0:T(8,128)(2,1)S(1)}, u32[]{:S(2)}) copy-start(bf16[16,8192]{1,0:T(8,128)(2,1)S(1)} %collective-permute-done.26.refs_10_) | copy-start | bytes 786436
  33.5 7.3 %collective-permute-start.25 = (bf16[16,8192]{1,0:T(8,128)(2,1)S(1)}, bf16[16,8192]{1,0:T(8,128)(2,1)S(1)}, u32[]{:S(2)}, u32[]{:S(2)}) collective-permute-start(bf16[16,8192]{1,0:T(8,128)(2,1)S(1)} %collective-permute-done.24.refs_8_), channel_id=1, source_target_pairs={{0,1},{1,0},{2,3},{3,2},{4,5},{5,4},{6,7},{7,6},{8,9},{9,8},{10,11... | collective-permute-start | bytes 786440 | tf_op jit(solution)/shard_map/ppermute | solution.py:122
  34.3 46.5 %copy-start.4 = (bf16[16,8192]{1,0:T(8,128)(2,1)}, bf16[16,8192]{1,0:T(8,128)(2,1)S(1)}, u32[]{:S(2)}) copy-start(bf16[16,8192]{1,0:T(8,128)(2,1)S(1)} %collective-permute-done.28.refs_12_) | copy-start | bytes 786436
  34.3 8.0 %collective-permute-start.11 = (bf16[16,8192]{1,0:T(8,128)(2,1)S(1)}, bf16[16,8192]{1,0:T(8,128)(2,1)S(1)}, u32[]{:S(2)}, u32[]{:S(2)}) collective-permute-start(bf16[16,8192]{1,0:T(8,128)(2,1)S(1)} %collective-permute-done.7.refs_8_), channel_id=1, source_target_pairs={{0,2},{1,3},{4,0},{5,1},{8,4},{9,5},{12,8},{13,9},{14,12},{15,13},... | collective-permute-start | bytes 786440 | tf_op jit(solution)/shard_map/ppermute | solution.py:118
  38.6 3.7 %collective-permute-start.6 = (bf16[16,8192]{1,0:T(8,128)(2,1)S(1)}, bf16[16,8192]{1,0:T(8,128)(2,1)S(1)}, u32[]{:S(2)}, u32[]{:S(2)}) collective-permute-start(bf16[16,8192]{1,0:T(8,128)(2,1)S(1)} %collective-permute-done.5.refs_6_), channel_id=1, source_target_pairs={{0,1},{1,0},{2,3},{3,2},{4,5},{5,4},{6,7},{7,6},{8,9},{9,8},{10,11... | collective-permute-start | bytes 786440 | tf_op jit(solution)/shard_map/ppermute | solution.py:122
  38.7 6.3 %collective-permute-start.30 = (bf16[16,4096]{1,0:T(8,128)(2,1)S(1)}, bf16[16,4096]{1,0:T(8,128)(2,1)S(1)}, u32[]{:S(2)}, u32[]{:S(2)}) collective-permute-start(bf16[16,4096]{1,0:T(8,128)(2,1)S(1)} %slice.18), channel_id=1, source_target_pairs={{0,4},{1,5},{4,8},{5,9},{8,12},{9,13},{12,14},{13,15},{14,10},{15,... | collective-permute-start | bytes 393224 | tf_op jit(solution)/shard_map/ppermute | solution.py:118
  40.2 40.5 %copy-start.24 = (bf16[16,8192]{1,0:T(8,128)(2,1)}, bf16[16,8192]{1,0:T(8,128)(2,1)S(1)}, u32[]{:S(2)}) copy-start(bf16[16,8192]{1,0:T(8,128)(2,1)S(1)} %collective-permute-done.23.refs_7_) | copy-start | bytes 786436
  40.2 6.2 %collective-permute-start.32 = (bf16[16,4096]{1,0:T(8,128)(2,1)S(1)}, bf16[16,4096]{1,0:T(8,128)(2,1)S(1)}, u32[]{:S(2)}, u32[]{:S(2)}) collective-permute-start(bf16[16,4096]{1,0:T(8,128)(2,1)S(1)} %slice.19), channel_id=1, source_target_pairs={{0,2},{1,3},{4,0},{5,1},{8,4},{9,5},{12,8},{13,9},{14,12},{15,13},... | collective-permute-start | bytes 393224 | tf_op jit(solution)/shard_map/ppermute | solution.py:118
  40.8 40.0 %copy-start.26 = (bf16[16,8192]{1,0:T(8,128)(2,1)}, bf16[16,8192]{1,0:T(8,128)(2,1)S(1)}, u32[]{:S(2)}) copy-start(bf16[16,8192]{1,0:T(8,128)(2,1)S(1)} %collective-permute-done.25.refs_9_) | copy-start | bytes 786436
  40.8 6.7 %collective-permute-start.13 = (bf16[16,4096]{1,0:T(8,128)(2,1)S(1)}, bf16[16,4096]{1,0:T(8,128)(2,1)S(1)}, u32[]{:S(2)}, u32[]{:S(2)}) collective-permute-start(bf16[16,4096]{1,0:T(8,128)(2,1)S(1)} %slice.16), channel_id=1, source_target_pairs={{0,4},{1,5},{4,8},{5,9},{8,12},{9,13},{12,14},{13,15},{14,10},{15,... | collective-permute-start | bytes 393224 | tf_op jit(solution)/shard_map/ppermute | solution.py:118
  42.3 8.3 %collective-permute-start.27 = (bf16[16,8192]{1,0:T(8,128)(2,1)S(1)}, bf16[16,8192]{1,0:T(8,128)(2,1)S(1)}, u32[]{:S(2)}, u32[]{:S(2)}) collective-permute-start(bf16[16,8192]{1,0:T(8,128)(2,1)S(1)} %collective-permute-done.26.refs_10_), channel_id=1, source_target_pairs={{0,1},{1,0},{2,3},{3,2},{4,5},{5,4},{6,7},{7,6},{8,9},{9,8},{10,11... | collective-permute-start | bytes 786440 | tf_op jit(solution)/shard_map/ppermute | solution.py:122
  42.3 8.7 %collective-permute-start.29 = (bf16[16,8192]{1,0:T(8,128)(2,1)S(1)}, bf16[16,8192]{1,0:T(8,128)(2,1)S(1)}, u32[]{:S(2)}, u32[]{:S(2)}) collective-permute-start(bf16[16,8192]{1,0:T(8,128)(2,1)S(1)} %collective-permute-done.28.refs_12_), channel_id=1, source_target_pairs={{0,1},{1,0},{2,3},{3,2},{4,5},{5,4},{6,7},{7,6},{8,9},{9,8},{10,11... | collective-permute-start | bytes 786440 | tf_op jit(solution)/shard_map/ppermute | solution.py:122
  42.8 38.1 %copy-start.40 = (s32[256]{0:T(256)S(1)}, s32[256]{0:T(256)}, u32[]{:S(2)}) copy-start(s32[256]{0:T(256)} %param.16) | copy-start | bytes 3076
  42.8 38.1 %copy-start = (bf16[8192,192]{0,1:T(8,128)(2,1)S(1)}, bf16[8192,192]{0,1:T(8,128)(2,1)}, u32[]{:S(2)}) copy-start(bf16[8192,192]{0,1:T(8,128)(2,1)} %param.14) | copy-start | bytes 9437188
  42.8 38.1 %copy-start.1 = (bf16[1792,192]{0,1:T(8,128)(2,1)S(1)}, bf16[1792,192]{0,1:T(8,128)(2,1)}, u32[]{:S(2)}) copy-start(bf16[1792,192]{0,1:T(8,128)(2,1)} %param.15) | copy-start | bytes 2064388
  42.8 38.1 %copy-start.7 = (bf16[16,8192]{1,0:T(8,128)(2,1)S(1)}, bf16[16,8192]{1,0:T(8,128)(2,1)}, u32[]{:S(2)}) copy-start(bf16[16,8192]{1,0:T(8,128)(2,1)} %refs_0_.4) | copy-start | bytes 786436
  45.0 5.0 %collective-permute-start.15 = (bf16[16,4096]{1,0:T(8,128)(2,1)S(1)}, bf16[16,4096]{1,0:T(8,128)(2,1)S(1)}, u32[]{:S(2)}, u32[]{:S(2)}) collective-permute-start(bf16[16,4096]{1,0:T(8,128)(2,1)S(1)} %slice.17), channel_id=1, source_target_pairs={{0,2},{1,3},{4,0},{5,1},{8,4},{9,5},{12,8},{13,9},{14,12},{15,13},... | collective-permute-start | bytes 393224 | tf_op jit(solution)/shard_map/ppermute | solution.py:118
  46.5 34.3 %copy-start.32 = (bf16[16,4096]{1,0:T(8,128)(2,1)}, bf16[16,4096]{1,0:T(8,128)(2,1)S(1)}, u32[]{:S(2)}) copy-start(bf16[16,4096]{1,0:T(8,128)(2,1)S(1)} %collective-permute-done.32.refs_16_) | copy-start | bytes 393220
  46.5 3.5 %collective-permute-start.31 = (bf16[16,4096]{1,0:T(8,128)(2,1)S(1)}, bf16[16,4096]{1,0:T(8,128)(2,1)S(1)}, u32[]{:S(2)}, u32[]{:S(2)}) collective-permute-start(bf16[16,4096]{1,0:T(8,128)(2,1)S(1)} %collective-permute-done.30.refs_14_), channel_id=1, source_target_pairs={{0,1},{1,0},{2,3},{3,2},{4,5},{5,4},{6,7},{7,6},{8,9},{9,8},{10,11... | collective-permute-start | bytes 393224 | tf_op jit(solution)/shard_map/ppermute | solution.py:122
  47.4 3.1 %collective-permute-start.33 = (bf16[16,4096]{1,0:T(8,128)(2,1)S(1)}, bf16[16,4096]{1,0:T(8,128)(2,1)S(1)}, u32[]{:S(2)}, u32[]{:S(2)}) collective-permute-start(bf16[16,4096]{1,0:T(8,128)(2,1)S(1)} %collective-permute-done.32.refs_16_), channel_id=1, source_target_pairs={{0,1},{1,0},{2,3},{3,2},{4,5},{5,4},{6,7},{7,6},{8,9},{9,8},{10,11... | collective-permute-start | bytes 393224 | tf_op jit(solution)/shard_map/ppermute | solution.py:122
  50.0 30.8 %collective-permute-start.8 = (bf16[16,8192]{1,0:T(8,128)(2,1)S(1)}, bf16[16,8192]{1,0:T(8,128)(2,1)S(1)}, u32[]{:S(2)}, u32[]{:S(2)}) collective-permute-start(bf16[16,8192]{1,0:T(8,128)(2,1)S(1)} %collective-permute-done.7.refs_8_), channel_id=1, source_target_pairs={{0,1},{1,0},{2,3},{3,2},{4,5},{5,4},{6,7},{7,6},{8,9},{9,8},{10,11... | collective-permute-start | bytes 786440 | tf_op jit(solution)/shard_map/ppermute | solution.py:122
  50.0 30.8 %copy-start.34 = (bf16[16,4096]{1,0:T(8,128)(2,1)}, bf16[16,4096]{1,0:T(8,128)(2,1)S(1)}, u32[]{:S(2)}) copy-start(bf16[16,4096]{1,0:T(8,128)(2,1)S(1)} %collective-permute-done.31.refs_15_) | copy-start | bytes 393220
  50.0 30.9 %collective-permute-start.10 = (bf16[16,8192]{1,0:T(8,128)(2,1)S(1)}, bf16[16,8192]{1,0:T(8,128)(2,1)S(1)}, u32[]{:S(2)}, u32[]{:S(2)}) collective-permute-start(bf16[16,8192]{1,0:T(8,128)(2,1)S(1)} %collective-permute-done.9.refs_10_), channel_id=1, source_target_pairs={{0,1},{1,0},{2,3},{3,2},{4,5},{5,4},{6,7},{7,6},{8,9},{9,8},{10,11... | collective-permute-start | bytes 786440 | tf_op jit(solution)/shard_map/ppermute | solution.py:122
  50.5 30.3 %copy-start.36 = (bf16[16,4096]{1,0:T(8,128)(2,1)}, bf16[16,4096]{1,0:T(8,128)(2,1)S(1)}, u32[]{:S(2)}) copy-start(bf16[16,4096]{1,0:T(8,128)(2,1)S(1)} %collective-permute-done.33.refs_17_) | copy-start | bytes 393220
  50.5 30.4 %collective-permute-start.12 = (bf16[16,8192]{1,0:T(8,128)(2,1)S(1)}, bf16[16,8192]{1,0:T(8,128)(2,1)S(1)}, u32[]{:S(2)}, u32[]{:S(2)}) collective-permute-start(bf16[16,8192]{1,0:T(8,128)(2,1)S(1)} %collective-permute-done.11.refs_12_), channel_id=1, source_target_pairs={{0,1},{1,0},{2,3},{3,2},{4,5},{5,4},{6,7},{7,6},{8,9},{9,8},{10,11... | collective-permute-start | bytes 786440 | tf_op jit(solution)/shard_map/ppermute | solution.py:122
  50.6 30.2 %copy-start.28 = (bf16[16,8192]{1,0:T(8,128)(2,1)}, bf16[16,8192]{1,0:T(8,128)(2,1)S(1)}, u32[]{:S(2)}) copy-start(bf16[16,8192]{1,0:T(8,128)(2,1)S(1)} %collective-permute-done.27.refs_11_) | copy-start | bytes 786436
  50.6 30.2 %collective-permute-start.14 = (bf16[16,4096]{1,0:T(8,128)(2,1)S(1)}, bf16[16,4096]{1,0:T(8,128)(2,1)S(1)}, u32[]{:S(2)}, u32[]{:S(2)}) collective-permute-start(bf16[16,4096]{1,0:T(8,128)(2,1)S(1)} %collective-permute-done.13.refs_14_), channel_id=1, source_target_pairs={{0,1},{1,0},{2,3},{3,2},{4,5},{5,4},{6,7},{7,6},{8,9},{9,8},{10,11... | collective-permute-start | bytes 393224 | tf_op jit(solution)/shard_map/ppermute | solution.py:122
  51.0 29.8 %copy-start.30 = (bf16[16,8192]{1,0:T(8,128)(2,1)}, bf16[16,8192]{1,0:T(8,128)(2,1)S(1)}, u32[]{:S(2)}) copy-start(bf16[16,8192]{1,0:T(8,128)(2,1)S(1)} %collective-permute-done.29.refs_13_) | copy-start | bytes 786436
  51.0 29.8 %collective-permute-start.16 = (bf16[16,4096]{1,0:T(8,128)(2,1)S(1)}, bf16[16,4096]{1,0:T(8,128)(2,1)S(1)}, u32[]{:S(2)}, u32[]{:S(2)}) collective-permute-start(bf16[16,4096]{1,0:T(8,128)(2,1)S(1)} %collective-permute-done.15.refs_16_), channel_id=1, source_target_pairs={{0,1},{1,0},{2,3},{3,2},{4,5},{5,4},{6,7},{7,6},{8,9},{9,8},{10,11... | collective-permute-start | bytes 393224 | tf_op jit(solution)/shard_map/ppermute | solution.py:122
  51.1 1.0 copy-start.8
  99.8 24.9 %all-to-all-start = ((f32[16,16,256]{2,1,0:T(8,128)}), f32[16,16,256]{2,1,0:T(8,128)S(1)}, u32[]{:S(2)}, u32[]{:S(2)}) async-start(f32[16,16,256]{2,1,0:T(8,128)} %shard_map.105), calls=%async_computation | async-start | bytes 524288 | tf_op jit(solution)/shard_map/all_to_all | solution.py:408
  105.6 1.0 copy-start.3
  106.6 0.9 copy-start.5
  107.5 0.9 copy-start.9
  108.5 0.9 copy-start.11
  109.4 0.9 copy-start.13
  110.4 0.9 copy-start.15
  111.3 0.9 copy-start.17
  124.7 1.0 copy-start.6
  (12 other events, 10.9 us)

commit v6 on v5

--- a/solution.py
+++ b/solution.py
@@ -10,6 +10,7 @@
 R = 64
 EX_TOK = 32
 TILE = 256
+PIECES = 4
 DEPTH = 2048
 SPLIT = 4
 MEBI = 1024 * 1024
@@ -122,8 +123,7 @@
     return lax.ppermute(block, "hid", [(h, h ^ 1) for h in range(2 * chips)])
 
 
-def gather_blocks(own, chips):
-    half = own.shape[1] // 2
+def gather_blocks(own, chips, last):
     places, blocks = [], []
 
     def found(offset, column, block):
@@ -139,8 +139,7 @@
         found(-step, 0, ahead)
         found(step, 0, behind)
     across = chips // 2
-    found(across, 0, ring_step(ahead[:, :half], chips, 1))
-    found(across, half, ring_step(behind[:, half:], chips, -1))
+    found(across, 0, ring_step(ahead if last > 0 else behind, chips, last))
     return places, blocks
 
 
@@ -168,18 +167,25 @@
 def forward_kernel(places, chips, *refs):
     count = len(places)
     blocks, refs = refs[:count], refs[count:]
-    gate_weight, up_weight, gate, up, gate_sum, up_sum, whole, sems = refs
+    gate_weight, up_weight, proj, gate, up, inputs, gate_sum, up_sum, whole, sems = refs
     n, k = pl.program_id(0), pl.program_id(1)
 
     @pl.when((n == 0) & (k == 0))
     def _():
         assemble(places, chips, blocks, whole, sems)
+        inputs[...] = jnp.zeros_like(inputs)
 
     depth = gate_weight.shape[0]
     x = whole[:, pl.ds(pl.multiple_of(k * depth, depth), depth)]
     gate_part = jnp.dot(x, gate_weight[...], preferred_element_type=jnp.float32)
     up_part = jnp.dot(x, up_weight[...], preferred_element_type=jnp.float32)
 
+    @pl.when(n < PIECES)
+    def _():
+        piece = depth // PIECES
+        part = pl.ds(pl.multiple_of(k * depth + n * piece, piece), piece)
+        inputs[...] += last_dot(proj[: 2 * R, part], whole[:, part])
+
     @pl.when(k == 0)
     def _():
         gate_sum[...] = gate_part
@@ -191,57 +197,30 @@
         up[...] = (up_sum[...] + up_part).T
 
 
-def forward(places, chips, blocks, gate_weight, up_weight, tile):
+def forward(places, chips, blocks, gate_weight, up_weight, proj, tile):
     depth, width = gate_weight.shape
     rows = blocks[0].shape[0] * chips * 2
     return pl.pallas_call(
         functools.partial(forward_kernel, places, chips),
         grid=(width // tile, 2),
-        out_shape=[jax.ShapeDtypeStruct((width, rows), jnp.float32)] * 2,
+        out_shape=[jax.ShapeDtypeStruct((width, rows), jnp.float32)] * 2
+        + [jax.ShapeDtypeStruct((2 * R, rows), jnp.float32)],
         in_specs=[pl.BlockSpec(memory_space=pl.ANY)] * len(blocks)
-        + [pl.BlockSpec((depth // 2, tile), lambda n, k: (k, n))] * 2,
-        out_specs=[pl.BlockSpec((tile, rows), lambda n, k: (n, 0))] * 2,
+        + [pl.BlockSpec((depth // 2, tile), lambda n, k: (k, n))] * 2
+        + [pl.BlockSpec((3 * R, depth), lambda n, k: (0, 0))],
+        out_specs=[pl.BlockSpec((tile, rows), lambda n, k: (n, 0))] * 2
+        + [pl.BlockSpec((2 * R, rows), lambda n, k: (0, 0))],
         scratch_shapes=[
             pltpu.VMEM((rows, tile), jnp.float32),
             pltpu.VMEM((rows, tile), jnp.float32),
             pltpu.VMEM((rows, depth), jnp.bfloat16),
             pltpu.SemaphoreType.DMA((len(blocks),)),
         ],
-        compiler_params=pltpu.CompilerParams(vmem_limit_bytes=20 * MEBI),
+        compiler_params=pltpu.CompilerParams(vmem_limit_bytes=28 * MEBI),
         cost_estimate=pl.CostEstimate(
             flops=4 * rows * depth * width, bytes_accessed=4 * depth * width, transcendentals=0
         ),
-    )(*blocks, gate_weight, up_weight)
-
-
-def inputs_kernel(places, chips, *refs):
-    count = len(places)
-    blocks, (proj, out, whole, sems) = refs[:count], refs[count:]
-    assemble(places, chips, blocks, whole, sems)
-    total = jnp.zeros(out.shape, jnp.float32)
-    for start in range(0, whole.shape[1], DEPTH):
-        part = pl.ds(start, DEPTH)
-        total += last_dot(proj[: 2 * R, part], whole[:, part])
-    out[...] = total
-
-
-def project_inputs(places, chips, blocks, proj):
-    rows, depth = blocks[0].shape[0] * chips * 2, proj.shape[1]
-    vmem = pl.BlockSpec(memory_space=pltpu.VMEM)
-    return pl.pallas_call(
-        functools.partial(inputs_kernel, places, chips),
-        out_shape=jax.ShapeDtypeStruct((2 * R, rows), jnp.float32),
-        in_specs=[pl.BlockSpec(memory_space=pl.ANY)] * len(blocks) + [vmem],
-        out_specs=vmem,
-        scratch_shapes=[
-            pltpu.VMEM((rows, depth), jnp.bfloat16),
-            pltpu.SemaphoreType.DMA((len(blocks),)),
-        ],
-        compiler_params=pltpu.CompilerParams(vmem_limit_bytes=24 * MEBI),
-        cost_estimate=pl.CostEstimate(
-            flops=16 * R * rows * depth, bytes_accessed=8 * R * depth, transcendentals=0
-        ),
-    )(*blocks, proj)
+    )(*blocks, gate_weight, up_weight, proj)
 
 
 def membership(ids, examples):
@@ -399,14 +378,15 @@
 ):
     chips = lax.axis_size("hid") // 2
     ids = example_ids[None, :]
-    places, token_blocks = gather_blocks(tokens, chips)
-    _, grad_blocks = gather_blocks(out_grad, chips)
-    gate, up = forward(places, chips, token_blocks, gate_weight, up_weight, TILE)
+    places, token_blocks = gather_blocks(tokens, chips, 1)
+    _, grad_blocks = gather_blocks(out_grad, chips, -1)
+    gate, up, inputs = forward(
+        places, chips, token_blocks, gate_weight, up_weight, proj_d.T, TILE
+    )
     send = backward(
         places, chips, grad_blocks, down_weight, [gate], [up], proj_d.T, proj_ff.T, ids, 1024, TILE
     )
     received = lax.all_to_all(send, "hid", 0, 0)
-    inputs = project_inputs(places, chips, token_blocks, proj_d.T)
     features, partial = finish(received, inputs, ids, test_features)
     scores = jnp.sum(lax.all_to_all(partial, "hid", 0, 0), axis=0)
     return features, scores

time: 143 us -> 130 us (0.909)
  local copies, waits for them, and re-layouts: 19.6 us -> 2.86 us
  blocking collectives: 13.7 us -> 26 us
  starting transfers between devices: 30.6 us -> 21.6 us
  waiting for transfers between devices: 25.5 us -> 28.9 us
  Pallas kernels: 50.9 us -> 48.6 us
    unnamed x82 -> x12, local copies, waits for them, and re-layouts: 19.6 us -> 2.86 us
    all_to_all x0 -> x1, blocking collectives: none -> 15.3 us  [local_ring(): received = lax.all_to_all(send, 'hid', 0, 0)]
    all_to_all x1 -> x0, starting transfers between devices: 5.81 us -> none  [local_ring(): received = lax.all_to_all(send, 'hid', 0, 0)]
    ppermute x16 -> x14, waiting for transfers between devices: 25.5 us -> 28.9 us  [ring_step(): return lax.ppermute(block, 'hid', pairs)]
    all_to_all x1, blocking collectives: 13.7 us -> 10.7 us  [local_ring(): scores = jnp.sum(lax.all_to_all(partial, 'hid', 0, 0), axis=0)]
    ppermute x16 -> x14, starting transfers between devices: 22.6 us -> 20 us  [ring_step(): return lax.ppermute(block, 'hid', pairs)]
    pallas_call x1 -> x0, Pallas kernels: 2.37 us -> none  [project_inputs(): pl.pallas_call(functools.partial(inputs_kernel, places, chips), out_shape...]
  transfers between devices with their start and end apart: 35 -> 30, of which waited for: 13 -> 12; matrix products, arithmetic and copies ran while one was open for 0% -> 0% of each run, Pallas kernels for 22% -> 23%
where the time goes in v6:
time: 130 us; the launch traced here: 129 us
  Pallas kernels  48.6 us (37%)
  waiting for transfers between devices  28.9 us (22%)
  blocking collectives  26 us (20%)
  starting transfers between devices  21.6 us (17%)
  local copies, waits for them, and re-layouts  2.86 us (2%)
    pallas_call x1, Pallas kernels, forward(): pl.pallas_call(functools.partial(forward_kernel, places, chips), grid=(wi...  29.7 us
    ppermute x14, waiting for transfers between devices, ring_step(): return lax.ppermute(block, 'hid', pairs)  28.9 us
    ppermute x14, starting transfers between devices, ring_step(): return lax.ppermute(block, 'hid', pairs)  20 us
    pallas_call x1, Pallas kernels, backward(): pl.pallas_call(functools.partial(backward_kernel, places, chips, examples...  17.8 us
    all_to_all x1, blocking collectives, local_ring(): received = lax.all_to_all(send, 'hid', 0, 0)  15.3 us
    all_to_all x1, blocking collectives, local_ring(): scores = jnp.sum(lax.all_to_all(partial, 'hid', 0, 0), axis=0)  10.7 us
    unnamed x12, local copies, waits for them, and re-layouts  2.86 us
  transfers between devices with their start and end apart: 30, of which 12 were waited for; matrix products, arithmetic and copies ran while one was open for 0% of the time, Pallas kernels for 23%

profile of v6, /device:TPU:0, one launch (start us, length us, event | category | flops | bytes accessed | tf_op | source)
XLA Modules:
  0.0 129.4 jit_solution(2331950838918975026)
XLA Ops:
  0.6 3.1 %collective-permute-start.16 = (bf16[16,8192]{1,0:T(8,128)(2,1)}, bf16[16,8192]{1,0:T(8,128)(2,1)S(1)}, u32[]{:S(2)}, u32[]{:S(2)}) collective-permute-start(bf16[16,8192]{1,0:T(8,128)(2,1)} %refs_0_.2), channel_id=1, source_target_pairs={{0,4},{1,5},{4,8},{5,9},{8,12},{9,13},{12,14},{13,15},{14,10},{15,... | collective-permute-start | bytes 786440 | tf_op jit(solution)/shard_map/ppermute | solution.py:119
  3.7 0.0 collective-permute-start.15
  3.7 0.1 collective-permute-start.18
  3.8 2.0 %collective-permute-start.1 = (bf16[16,8192]{1,0:T(8,128)(2,1)}, bf16[16,8192]{1,0:T(8,128)(2,1)S(1)}, u32[]{:S(2)}, u32[]{:S(2)}) collective-permute-start(bf16[16,8192]{1,0:T(8,128)(2,1)} %refs_0_.3), channel_id=1, source_target_pairs={{0,4},{1,5},{4,8},{5,9},{8,12},{9,13},{12,14},{13,15},{14,10},{15,... | collective-permute-start | bytes 786440 | tf_op jit(solution)/shard_map/ppermute | solution.py:119
  5.7 0.0 collective-permute-start
  5.7 5.2 %collective-permute-done.16.refs_2_ = bf16[16,8192]{1,0:T(8,128)(2,1)S(1)} collective-permute-done((bf16[16,8192]{1,0:T(8,128)(2,1)}, bf16[16,8192]{1,0:T(8,128)(2,1)S(1)}, u32[]{:S(2)}, u32[]{:S(2)}) %collective-permute-start.16) | collective-permute-done | bytes 262176 | tf_op jit(solution)/shard_map/ppermute | solution.py:119
  11.0 2.1 %collective-permute-start.3 = (bf16[16,8192]{1,0:T(8,128)(2,1)}, bf16[16,8192]{1,0:T(8,128)(2,1)S(1)}, u32[]{:S(2)}, u32[]{:S(2)}) collective-permute-start(bf16[16,8192]{1,0:T(8,128)(2,1)} %refs_0_.3), channel_id=1, source_target_pairs={{0,2},{1,3},{4,0},{5,1},{8,4},{9,5},{12,8},{13,9},{14,12},{15,13},... | collective-permute-start | bytes 786440 | tf_op jit(solution)/shard_map/ppermute | solution.py:119
  13.0 0.0 collective-permute-done.15.refs_1_
  13.0 0.1 collective-permute-start.20
  13.1 0.0 collective-permute-done.18.refs_4_
  13.1 0.0 collective-permute-start.17
  13.1 3.5 %collective-permute-done.1.refs_2_ = bf16[16,8192]{1,0:T(8,128)(2,1)S(1)} collective-permute-done((bf16[16,8192]{1,0:T(8,128)(2,1)}, bf16[16,8192]{1,0:T(8,128)(2,1)S(1)}, u32[]{:S(2)}, u32[]{:S(2)}) %collective-permute-start.1) | collective-permute-done | bytes 262176 | tf_op jit(solution)/shard_map/ppermute | solution.py:119
  16.6 2.1 %collective-permute-start.22 = (bf16[16,8192]{1,0:T(8,128)(2,1)S(1)}, bf16[16,8192]{1,0:T(8,128)(2,1)S(1)}, u32[]{:S(2)}, u32[]{:S(2)}) collective-permute-start(bf16[16,8192]{1,0:T(8,128)(2,1)S(1)} %collective-permute-done.18.refs_4_), channel_id=1, source_target_pairs={{0,2},{1,3},{4,0},{5,1},{8,4},{9,5},{12,8},{13,9},{14,12},{15,13},... | collective-permute-start | bytes 786440 | tf_op jit(solution)/shard_map/ppermute | solution.py:119
  18.6 0.0 collective-permute-done.refs_1_
  18.6 0.0 collective-permute-start.19
  18.6 0.2 collective-permute-done.3.refs_4_
  18.8 1.6 %collective-permute-start.5 = (bf16[16,8192]{1,0:T(8,128)(2,1)S(1)}, bf16[16,8192]{1,0:T(8,128)(2,1)S(1)}, u32[]{:S(2)}, u32[]{:S(2)}) collective-permute-start(bf16[16,8192]{1,0:T(8,128)(2,1)S(1)} %collective-permute-done.1.refs_2_), channel_id=1, source_target_pairs={{0,4},{1,5},{4,8},{5,9},{8,12},{9,13},{12,14},{13,15},{14,10},{15,... | collective-permute-start | bytes 786440 | tf_op jit(solution)/shard_map/ppermute | solution.py:119
  20.5 1.4 %collective-permute-done.20.refs_6_ = bf16[16,8192]{1,0:T(8,128)(2,1)S(1)} collective-permute-done((bf16[16,8192]{1,0:T(8,128)(2,1)S(1)}, bf16[16,8192]{1,0:T(8,128)(2,1)S(1)}, u32[]{:S(2)}, u32[]{:S(2)}) %collective-permute-start.20) | collective-permute-done | bytes 262176 | tf_op jit(solution)/shard_map/ppermute | solution.py:119
  21.9 0.0 collective-permute-start.2
  21.9 0.0 collective-permute-done.17.refs_3_
  21.9 1.3 collective-permute-start.7
  23.1 0.8 collective-permute-done.22.refs_8_
  23.9 0.0 collective-permute-start.4
  23.9 0.0 collective-permute-done.19.refs_5_
  23.9 1.6 %collective-permute-start.24 = (bf16[16,8192]{1,0:T(8,128)(2,1)S(1)}, bf16[16,8192]{1,0:T(8,128)(2,1)S(1)}, u32[]{:S(2)}, u32[]{:S(2)}) collective-permute-start(bf16[16,8192]{1,0:T(8,128)(2,1)S(1)} %collective-permute-done.20.refs_6_), channel_id=1, source_target_pairs={{0,4},{1,5},{4,8},{5,9},{8,12},{9,13},{12,14},{13,15},{14,10},{15,... | collective-permute-start | bytes 786440 | tf_op jit(solution)/shard_map/ppermute | solution.py:119
  25.5 2.2 %collective-permute-done.5.refs_6_ = bf16[16,8192]{1,0:T(8,128)(2,1)S(1)} collective-permute-done((bf16[16,8192]{1,0:T(8,128)(2,1)S(1)}, bf16[16,8192]{1,0:T(8,128)(2,1)S(1)}, u32[]{:S(2)}, u32[]{:S(2)}) %collective-permute-start.5) | collective-permute-done | bytes 262176 | tf_op jit(solution)/shard_map/ppermute | solution.py:119
  27.7 0.0 collective-permute-start.21
  27.7 0.0 collective-permute-done.2.refs_3_
  27.7 1.7 %collective-permute-start.26 = (bf16[16,8192]{1,0:T(8,128)(2,1)S(1)}, bf16[16,8192]{1,0:T(8,128)(2,1)S(1)}, u32[]{:S(2)}, u32[]{:S(2)}) collective-permute-start(bf16[16,8192]{1,0:T(8,128)(2,1)S(1)} %collective-permute-done.22.refs_8_), channel_id=1, source_target_pairs={{0,2},{1,3},{4,0},{5,1},{8,4},{9,5},{12,8},{13,9},{14,12},{15,13},... | collective-permute-start | bytes 786440 | tf_op jit(solution)/shard_map/ppermute | solution.py:119
  29.4 2.1 %collective-permute-done.7.refs_8_ = bf16[16,8192]{1,0:T(8,128)(2,1)S(1)} collective-permute-done((bf16[16,8192]{1,0:T(8,128)(2,1)S(1)}, bf16[16,8192]{1,0:T(8,128)(2,1)S(1)}, u32[]{:S(2)}, u32[]{:S(2)}) %collective-permute-start.7) | collective-permute-done | bytes 262176 | tf_op jit(solution)/shard_map/ppermute | solution.py:119
  31.5 0.0 collective-permute-start.23
  31.5 0.0 collective-permute-done.4.refs_5_
  31.5 0.3 collective-permute-start.11
  31.8 1.1 collective-permute-done.24.refs_10_
  33.0 1.4 %collective-permute-start.28 = (bf16[16,8192]{1,0:T(8,128)(2,1)S(1)}, bf16[16,8192]{1,0:T(8,128)(2,1)S(1)}, u32[]{:S(2)}, u32[]{:S(2)}) collective-permute-start(bf16[16,8192]{1,0:T(8,128)(2,1)S(1)} %collective-permute-done.24.refs_10_), channel_id=1, source_target_pairs={{0,4},{1,5},{4,8},{5,9},{8,12},{9,13},{12,14},{13,15},{14,10},{15,... | collective-permute-start | bytes 786440 | tf_op jit(solution)/shard_map/ppermute | solution.py:119
  34.4 1.6 %collective-permute-start.9 = (bf16[16,8192]{1,0:T(8,128)(2,1)S(1)}, bf16[16,8192]{1,0:T(8,128)(2,1)S(1)}, u32[]{:S(2)}, u32[]{:S(2)}) collective-permute-start(bf16[16,8192]{1,0:T(8,128)(2,1)S(1)} %collective-permute-done.5.refs_6_), channel_id=1, source_target_pairs={{0,4},{1,5},{4,8},{5,9},{8,12},{9,13},{12,14},{13,15},{14,10},{15,... | collective-permute-start | bytes 786440 | tf_op jit(solution)/shard_map/ppermute | solution.py:119
  36.0 1.1 collective-permute-done.26.refs_12_
  37.1 0.0 collective-permute-start.25
  37.1 0.0 collective-permute-done.23.refs_9_
  37.1 0.5 collective-permute-start.27
  37.6 4.9 %collective-permute-done.11.refs_12_ = bf16[16,8192]{1,0:T(8,128)(2,1)S(1)} collective-permute-done((bf16[16,8192]{1,0:T(8,128)(2,1)S(1)}, bf16[16,8192]{1,0:T(8,128)(2,1)S(1)}, u32[]{:S(2)}, u32[]{:S(2)}) %collective-permute-start.11) | collective-permute-done | bytes 262176 | tf_op jit(solution)/shard_map/ppermute | solution.py:119
  42.6 1.2 collective-permute-start.13
  43.7 2.9 %collective-permute-done.9.refs_10_ = bf16[16,8192]{1,0:T(8,128)(2,1)S(1)} collective-permute-done((bf16[16,8192]{1,0:T(8,128)(2,1)S(1)}, bf16[16,8192]{1,0:T(8,128)(2,1)S(1)}, u32[]{:S(2)}, u32[]{:S(2)}) %collective-permute-start.9) | collective-permute-done | bytes 262176 | tf_op jit(solution)/shard_map/ppermute | solution.py:119
  46.6 0.0 collective-permute-start.6
  46.6 0.0 collective-permute-done.25.refs_11_
  46.6 0.5 collective-permute-start.8
  47.1 0.0 collective-permute-done.27.refs_13_
  47.1 0.1 collective-permute-start.12
  47.2 3.5 %collective-permute-done.13.refs_14_ = bf16[16,8192]{1,0:T(8,128)(2,1)S(1)} collective-permute-done((bf16[16,8192]{1,0:T(8,128)(2,1)S(1)}, bf16[16,8192]{1,0:T(8,128)(2,1)S(1)}, u32[]{:S(2)}, u32[]{:S(2)}) %collective-permute-start.13) | collective-permute-done | bytes 262176 | tf_op jit(solution)/shard_map/ppermute | solution.py:119
  50.7 0.0 collective-permute-start.10
  50.7 0.0 collective-permute-done.29.refs_15_
  50.7 0.5 collective-permute-start.14
  51.2 1.9 %copy-done = bf16[8192,192]{0,1:T(8,128)(2,1)S(1)} copy-done((bf16[8192,192]{0,1:T(8,128)(2,1)S(1)}, bf16[8192,192]{0,1:T(8,128)(2,1)}, u32[]{:S(2)}) %copy-start) | copy-done | bytes 3145752
  53.1 0.9 copy-done.3
  54.1 29.7 %shard_map.104 = (f32[1792,256]{1,0:T(8,128)S(1)}, f32[1792,256]{1,0:T(8,128)S(1)}, f32[128,256]{1,0:T(8,128)S(1)}) custom-call(bf16[16,8192]{1,0:T(8,128)(2,1)S(1)} %copy-done.3, bf16[16,8192]{1,0:T(8,128)(2,1)S(1)} %collective-permute-done.15.refs_1_, bf16[16,8192]{1,0:T(8,128)(2,1)S(1)} %collective-permute-done.16.refs_2_, ...), custom_call_target="tpu_custom_call" | custom-call | flops 15032385536 | bytes 58720256 | tf_op jit(solution)/shard_map/pallas_call | solution.py:203
  83.7 0.0 collective-permute-done.6.refs_7_
  83.8 0.0 collective-permute-done.10.refs_11_
  83.8 0.0 collective-permute-done.12.refs_13_
  83.8 0.0 copy-start.2
  83.8 17.8 %shard_map.105 = f32[16,16,256]{2,1,0:T(8,128)S(1)} custom-call(bf16[16,8192]{1,0:T(8,128)(2,1)S(1)} %copy-done.4, bf16[16,8192]{1,0:T(8,128)(2,1)S(1)} %collective-permute-done.refs_1_, bf16[16,8192]{1,0:T(8,128)(2,1)S(1)} %collective-permute-done.1.refs_2_, bf16[16,8192]{1,0:T(8,128)(2,1)S(1)} %collective-permute-done.2.refs_3_, ...), custom_call_target="tpu_custom_call" | custom-call | flops 7516192768 | bytes 29360128 | tf_op jit(solution)/shard_map/pallas_call | solution.py:303
  101.6 15.3 %all_to_all.10.received = f32[16,16,256]{2,1,0:T(8,128)S(1)} all-to-all(f32[16,16,256]{2,1,0:T(8,128)S(1)} %shard_map.105), channel_id=1, replica_groups=mesh['groups'=2,'hid'=16,'mod'=1] {'hid'}, dimensions={0} | all-to-all | bytes 524288 | tf_op jit(solution)/shard_map/all_to_all | solution.py:389
  117.0 1.1 shard_map.106
  118.1 10.7 %all_to_all.11 = f32[16,8,256]{2,1,0:T(8,128)S(1)} all-to-all(f32[16,8,256]{2,1,0:T(8,128)S(1)} %get-tuple-element.11), channel_id=1, replica_groups=mesh['groups'=2,'hid'=16,'mod'=1] {'hid'}, dimensions={0} | all-to-all | bytes 262144 | tf_op jit(solution)/shard_map/all_to_all | solution.py:391
  128.8 0.6 reduce_sum.9
  (14 shorter events, 0.0 us)
Async XLA Ops:
  0.6 10.3 %collective-permute-start.16 = (bf16[16,8192]{1,0:T(8,128)(2,1)}, bf16[16,8192]{1,0:T(8,128)(2,1)S(1)}, u32[]{:S(2)}, u32[]{:S(2)}) collective-permute-start(bf16[16,8192]{1,0:T(8,128)(2,1)} %refs_0_.2), channel_id=1, source_target_pairs={{0,4},{1,5},{4,8},{5,9},{8,12},{9,13},{12,14},{13,15},{14,10},{15,... | collective-permute-start | bytes 786440 | tf_op jit(solution)/shard_map/ppermute | solution.py:119
  3.7 9.3 %collective-permute-start.15 = (bf16[16,8192]{1,0:T(8,128)(2,1)}, bf16[16,8192]{1,0:T(8,128)(2,1)S(1)}, u32[]{:S(2)}, u32[]{:S(2)}) collective-permute-start(bf16[16,8192]{1,0:T(8,128)(2,1)} %refs_0_.2), channel_id=1, source_target_pairs={{0,1},{1,0},{2,3},{3,2},{4,5},{5,4},{6,7},{7,6},{8,9},{9,8},{10,11... | collective-permute-start | bytes 786440 | tf_op jit(solution)/shard_map/ppermute | solution.py:123
  3.7 9.4 %collective-permute-start.18 = (bf16[16,8192]{1,0:T(8,128)(2,1)}, bf16[16,8192]{1,0:T(8,128)(2,1)S(1)}, u32[]{:S(2)}, u32[]{:S(2)}) collective-permute-start(bf16[16,8192]{1,0:T(8,128)(2,1)} %refs_0_.2), channel_id=1, source_target_pairs={{0,2},{1,3},{4,0},{5,1},{8,4},{9,5},{12,8},{13,9},{14,12},{15,13},... | collective-permute-start | bytes 786440 | tf_op jit(solution)/shard_map/ppermute | solution.py:119
  3.8 12.8 %collective-permute-start.1 = (bf16[16,8192]{1,0:T(8,128)(2,1)}, bf16[16,8192]{1,0:T(8,128)(2,1)S(1)}, u32[]{:S(2)}, u32[]{:S(2)}) collective-permute-start(bf16[16,8192]{1,0:T(8,128)(2,1)} %refs_0_.3), channel_id=1, source_target_pairs={{0,4},{1,5},{4,8},{5,9},{8,12},{9,13},{12,14},{13,15},{14,10},{15,... | collective-permute-start | bytes 786440 | tf_op jit(solution)/shard_map/ppermute | solution.py:119
  5.7 12.9 %collective-permute-start = (bf16[16,8192]{1,0:T(8,128)(2,1)}, bf16[16,8192]{1,0:T(8,128)(2,1)S(1)}, u32[]{:S(2)}, u32[]{:S(2)}) collective-permute-start(bf16[16,8192]{1,0:T(8,128)(2,1)} %refs_0_.3), channel_id=1, source_target_pairs={{0,1},{1,0},{2,3},{3,2},{4,5},{5,4},{6,7},{7,6},{8,9},{9,8},{10,11... | collective-permute-start | bytes 786440 | tf_op jit(solution)/shard_map/ppermute | solution.py:123
  11.0 7.9 %collective-permute-start.3 = (bf16[16,8192]{1,0:T(8,128)(2,1)}, bf16[16,8192]{1,0:T(8,128)(2,1)S(1)}, u32[]{:S(2)}, u32[]{:S(2)}) collective-permute-start(bf16[16,8192]{1,0:T(8,128)(2,1)} %refs_0_.3), channel_id=1, source_target_pairs={{0,2},{1,3},{4,0},{5,1},{8,4},{9,5},{12,8},{13,9},{14,12},{15,13},... | collective-permute-start | bytes 786440 | tf_op jit(solution)/shard_map/ppermute | solution.py:119
  13.0 8.8 %collective-permute-start.20 = (bf16[16,8192]{1,0:T(8,128)(2,1)S(1)}, bf16[16,8192]{1,0:T(8,128)(2,1)S(1)}, u32[]{:S(2)}, u32[]{:S(2)}) collective-permute-start(bf16[16,8192]{1,0:T(8,128)(2,1)S(1)} %collective-permute-done.16.refs_2_), channel_id=1, source_target_pairs={{0,4},{1,5},{4,8},{5,9},{8,12},{9,13},{12,14},{13,15},{14,10},{15,... | collective-permute-start | bytes 786440 | tf_op jit(solution)/shard_map/ppermute | solution.py:119
  13.1 8.7 %collective-permute-start.17 = (bf16[16,8192]{1,0:T(8,128)(2,1)S(1)}, bf16[16,8192]{1,0:T(8,128)(2,1)S(1)}, u32[]{:S(2)}, u32[]{:S(2)}) collective-permute-start(bf16[16,8192]{1,0:T(8,128)(2,1)S(1)} %collective-permute-done.16.refs_2_), channel_id=1, source_target_pairs={{0,1},{1,0},{2,3},{3,2},{4,5},{5,4},{6,7},{7,6},{8,9},{9,8},{10,11... | collective-permute-start | bytes 786440 | tf_op jit(solution)/shard_map/ppermute | solution.py:123
  16.6 7.3 %collective-permute-start.22 = (bf16[16,8192]{1,0:T(8,128)(2,1)S(1)}, bf16[16,8192]{1,0:T(8,128)(2,1)S(1)}, u32[]{:S(2)}, u32[]{:S(2)}) collective-permute-start(bf16[16,8192]{1,0:T(8,128)(2,1)S(1)} %collective-permute-done.18.refs_4_), channel_id=1, source_target_pairs={{0,2},{1,3},{4,0},{5,1},{8,4},{9,5},{12,8},{13,9},{14,12},{15,13},... | collective-permute-start | bytes 786440 | tf_op jit(solution)/shard_map/ppermute | solution.py:119
  18.6 5.2 %collective-permute-start.19 = (bf16[16,8192]{1,0:T(8,128)(2,1)S(1)}, bf16[16,8192]{1,0:T(8,128)(2,1)S(1)}, u32[]{:S(2)}, u32[]{:S(2)}) collective-permute-start(bf16[16,8192]{1,0:T(8,128)(2,1)S(1)} %collective-permute-done.18.refs_4_), channel_id=1, source_target_pairs={{0,1},{1,0},{2,3},{3,2},{4,5},{5,4},{6,7},{7,6},{8,9},{9,8},{10,11... | collective-permute-start | bytes 786440 | tf_op jit(solution)/shard_map/ppermute | solution.py:123
  18.8 8.9 %collective-permute-start.5 = (bf16[16,8192]{1,0:T(8,128)(2,1)S(1)}, bf16[16,8192]{1,0:T(8,128)(2,1)S(1)}, u32[]{:S(2)}, u32[]{:S(2)}) collective-permute-start(bf16[16,8192]{1,0:T(8,128)(2,1)S(1)} %collective-permute-done.1.refs_2_), channel_id=1, source_target_pairs={{0,4},{1,5},{4,8},{5,9},{8,12},{9,13},{12,14},{13,15},{14,10},{15,... | collective-permute-start | bytes 786440 | tf_op jit(solution)/shard_map/ppermute | solution.py:119
  21.9 5.8 %collective-permute-start.2 = (bf16[16,8192]{1,0:T(8,128)(2,1)S(1)}, bf16[16,8192]{1,0:T(8,128)(2,1)S(1)}, u32[]{:S(2)}, u32[]{:S(2)}) collective-permute-start(bf16[16,8192]{1,0:T(8,128)(2,1)S(1)} %collective-permute-done.1.refs_2_), channel_id=1, source_target_pairs={{0,1},{1,0},{2,3},{3,2},{4,5},{5,4},{6,7},{7,6},{8,9},{9,8},{10,11... | collective-permute-start | bytes 786440 | tf_op jit(solution)/shard_map/ppermute | solution.py:123
  21.9 9.6 %collective-permute-start.7 = (bf16[16,8192]{1,0:T(8,128)(2,1)S(1)}, bf16[16,8192]{1,0:T(8,128)(2,1)S(1)}, u32[]{:S(2)}, u32[]{:S(2)}) collective-permute-start(bf16[16,8192]{1,0:T(8,128)(2,1)S(1)} %collective-permute-done.3.refs_4_), channel_id=1, source_target_pairs={{0,2},{1,3},{4,0},{5,1},{8,4},{9,5},{12,8},{13,9},{14,12},{15,13},... | collective-permute-start | bytes 786440 | tf_op jit(solution)/shard_map/ppermute | solution.py:119
  23.9 7.6 %collective-permute-start.4 = (bf16[16,8192]{1,0:T(8,128)(2,1)S(1)}, bf16[16,8192]{1,0:T(8,128)(2,1)S(1)}, u32[]{:S(2)}, u32[]{:S(2)}) collective-permute-start(bf16[16,8192]{1,0:T(8,128)(2,1)S(1)} %collective-permute-done.3.refs_4_), channel_id=1, source_target_pairs={{0,1},{1,0},{2,3},{3,2},{4,5},{5,4},{6,7},{7,6},{8,9},{9,8},{10,11... | collective-permute-start | bytes 786440 | tf_op jit(solution)/shard_map/ppermute | solution.py:123
  23.9 9.1 %collective-permute-start.24 = (bf16[16,8192]{1,0:T(8,128)(2,1)S(1)}, bf16[16,8192]{1,0:T(8,128)(2,1)S(1)}, u32[]{:S(2)}, u32[]{:S(2)}) collective-permute-start(bf16[16,8192]{1,0:T(8,128)(2,1)S(1)} %collective-permute-done.20.refs_6_), channel_id=1, source_target_pairs={{0,4},{1,5},{4,8},{5,9},{8,12},{9,13},{12,14},{13,15},{14,10},{15,... | collective-permute-start | bytes 786440 | tf_op jit(solution)/shard_map/ppermute | solution.py:119
  27.7 6.7 %collective-permute-start.21 = (bf16[16,8192]{1,0:T(8,128)(2,1)S(1)}, bf16[16,8192]{1,0:T(8,128)(2,1)S(1)}, u32[]{:S(2)}, u32[]{:S(2)}) collective-permute-start(bf16[16,8192]{1,0:T(8,128)(2,1)S(1)} %collective-permute-done.20.refs_6_), channel_id=1, source_target_pairs={{0,1},{1,0},{2,3},{3,2},{4,5},{5,4},{6,7},{7,6},{8,9},{9,8},{10,11... | collective-permute-start | bytes 786440 | tf_op jit(solution)/shard_map/ppermute | solution.py:123
  27.7 9.4 %collective-permute-start.26 = (bf16[16,8192]{1,0:T(8,128)(2,1)S(1)}, bf16[16,8192]{1,0:T(8,128)(2,1)S(1)}, u32[]{:S(2)}, u32[]{:S(2)}) collective-permute-start(bf16[16,8192]{1,0:T(8,128)(2,1)S(1)} %collective-permute-done.22.refs_8_), channel_id=1, source_target_pairs={{0,2},{1,3},{4,0},{5,1},{8,4},{9,5},{12,8},{13,9},{14,12},{15,13},... | collective-permute-start | bytes 786440 | tf_op jit(solution)/shard_map/ppermute | solution.py:119
  31.5 5.6 %collective-permute-start.23 = (bf16[16,8192]{1,0:T(8,128)(2,1)S(1)}, bf16[16,8192]{1,0:T(8,128)(2,1)S(1)}, u32[]{:S(2)}, u32[]{:S(2)}) collective-permute-start(bf16[16,8192]{1,0:T(8,128)(2,1)S(1)} %collective-permute-done.22.refs_8_), channel_id=1, source_target_pairs={{0,1},{1,0},{2,3},{3,2},{4,5},{5,4},{6,7},{7,6},{8,9},{9,8},{10,11... | collective-permute-start | bytes 786440 | tf_op jit(solution)/shard_map/ppermute | solution.py:123
  31.5 11.0 %collective-permute-start.11 = (bf16[16,8192]{1,0:T(8,128)(2,1)S(1)}, bf16[16,8192]{1,0:T(8,128)(2,1)S(1)}, u32[]{:S(2)}, u32[]{:S(2)}) collective-permute-start(bf16[16,8192]{1,0:T(8,128)(2,1)S(1)} %collective-permute-done.7.refs_8_), channel_id=1, source_target_pairs={{0,2},{1,3},{4,0},{5,1},{8,4},{9,5},{12,8},{13,9},{14,12},{15,13},... | collective-permute-start | bytes 786440 | tf_op jit(solution)/shard_map/ppermute | solution.py:119
  33.0 10.7 %collective-permute-start.28 = (bf16[16,8192]{1,0:T(8,128)(2,1)S(1)}, bf16[16,8192]{1,0:T(8,128)(2,1)S(1)}, u32[]{:S(2)}, u32[]{:S(2)}) collective-permute-start(bf16[16,8192]{1,0:T(8,128)(2,1)S(1)} %collective-permute-done.24.refs_10_), channel_id=1, source_target_pairs={{0,4},{1,5},{4,8},{5,9},{8,12},{9,13},{12,14},{13,15},{14,10},{15,... | collective-permute-start | bytes 786440 | tf_op jit(solution)/shard_map/ppermute | solution.py:119
  34.4 12.2 %collective-permute-start.9 = (bf16[16,8192]{1,0:T(8,128)(2,1)S(1)}, bf16[16,8192]{1,0:T(8,128)(2,1)S(1)}, u32[]{:S(2)}, u32[]{:S(2)}) collective-permute-start(bf16[16,8192]{1,0:T(8,128)(2,1)S(1)} %collective-permute-done.5.refs_6_), channel_id=1, source_target_pairs={{0,4},{1,5},{4,8},{5,9},{8,12},{9,13},{12,14},{13,15},{14,10},{15,... | collective-permute-start | bytes 786440 | tf_op jit(solution)/shard_map/ppermute | solution.py:119
  37.1 9.5 %collective-permute-start.25 = (bf16[16,8192]{1,0:T(8,128)(2,1)S(1)}, bf16[16,8192]{1,0:T(8,128)(2,1)S(1)}, u32[]{:S(2)}, u32[]{:S(2)}) collective-permute-start(bf16[16,8192]{1,0:T(8,128)(2,1)S(1)} %collective-permute-done.24.refs_10_), channel_id=1, source_target_pairs={{0,1},{1,0},{2,3},{3,2},{4,5},{5,4},{6,7},{7,6},{8,9},{9,8},{10,11... | collective-permute-start | bytes 786440 | tf_op jit(solution)/shard_map/ppermute | solution.py:123
  37.1 10.0 %collective-permute-start.27 = (bf16[16,8192]{1,0:T(8,128)(2,1)S(1)}, bf16[16,8192]{1,0:T(8,128)(2,1)S(1)}, u32[]{:S(2)}, u32[]{:S(2)}) collective-permute-start(bf16[16,8192]{1,0:T(8,128)(2,1)S(1)} %collective-permute-done.26.refs_12_), channel_id=1, source_target_pairs={{0,1},{1,0},{2,3},{3,2},{4,5},{5,4},{6,7},{7,6},{8,9},{9,8},{10,11... | collective-permute-start | bytes 786440 | tf_op jit(solution)/shard_map/ppermute | solution.py:123
  42.6 8.1 %collective-permute-start.13 = (bf16[16,8192]{1,0:T(8,128)(2,1)S(1)}, bf16[16,8192]{1,0:T(8,128)(2,1)S(1)}, u32[]{:S(2)}, u32[]{:S(2)}) collective-permute-start(bf16[16,8192]{1,0:T(8,128)(2,1)S(1)} %collective-permute-done.11.refs_12_), channel_id=1, source_target_pairs={{0,2},{1,3},{4,0},{5,1},{8,4},{9,5},{12,8},{13,9},{14,12},{15,13},... | collective-permute-start | bytes 786440 | tf_op jit(solution)/shard_map/ppermute | solution.py:119
  43.7 7.0 %collective-permute-start.29 = (bf16[16,8192]{1,0:T(8,128)(2,1)S(1)}, bf16[16,8192]{1,0:T(8,128)(2,1)S(1)}, u32[]{:S(2)}, u32[]{:S(2)}) collective-permute-start(bf16[16,8192]{1,0:T(8,128)(2,1)S(1)} %collective-permute-done.28.refs_14_), channel_id=1, source_target_pairs={{0,1},{1,0},{2,3},{3,2},{4,5},{5,4},{6,7},{7,6},{8,9},{9,8},{10,11... | collective-permute-start | bytes 786440 | tf_op jit(solution)/shard_map/ppermute | solution.py:123
  46.6 37.1 %collective-permute-start.6 = (bf16[16,8192]{1,0:T(8,128)(2,1)S(1)}, bf16[16,8192]{1,0:T(8,128)(2,1)S(1)}, u32[]{:S(2)}, u32[]{:S(2)}) collective-permute-start(bf16[16,8192]{1,0:T(8,128)(2,1)S(1)} %collective-permute-done.5.refs_6_), channel_id=1, source_target_pairs={{0,1},{1,0},{2,3},{3,2},{4,5},{5,4},{6,7},{7,6},{8,9},{9,8},{10,11... | collective-permute-start | bytes 786440 | tf_op jit(solution)/shard_map/ppermute | solution.py:123
  46.6 37.1 %collective-permute-start.8 = (bf16[16,8192]{1,0:T(8,128)(2,1)S(1)}, bf16[16,8192]{1,0:T(8,128)(2,1)S(1)}, u32[]{:S(2)}, u32[]{:S(2)}) collective-permute-start(bf16[16,8192]{1,0:T(8,128)(2,1)S(1)} %collective-permute-done.7.refs_8_), channel_id=1, source_target_pairs={{0,1},{1,0},{2,3},{3,2},{4,5},{5,4},{6,7},{7,6},{8,9},{9,8},{10,11... | collective-permute-start | bytes 786440 | tf_op jit(solution)/shard_map/ppermute | solution.py:123
  47.1 36.6 %collective-permute-start.12 = (bf16[16,8192]{1,0:T(8,128)(2,1)S(1)}, bf16[16,8192]{1,0:T(8,128)(2,1)S(1)}, u32[]{:S(2)}, u32[]{:S(2)}) collective-permute-start(bf16[16,8192]{1,0:T(8,128)(2,1)S(1)} %collective-permute-done.11.refs_12_), channel_id=1, source_target_pairs={{0,1},{1,0},{2,3},{3,2},{4,5},{5,4},{6,7},{7,6},{8,9},{9,8},{10,11... | collective-permute-start | bytes 786440 | tf_op jit(solution)/shard_map/ppermute | solution.py:123
  50.7 33.1 %collective-permute-start.10 = (bf16[16,8192]{1,0:T(8,128)(2,1)S(1)}, bf16[16,8192]{1,0:T(8,128)(2,1)S(1)}, u32[]{:S(2)}, u32[]{:S(2)}) collective-permute-start(bf16[16,8192]{1,0:T(8,128)(2,1)S(1)} %collective-permute-done.9.refs_10_), channel_id=1, source_target_pairs={{0,1},{1,0},{2,3},{3,2},{4,5},{5,4},{6,7},{7,6},{8,9},{9,8},{10,11... | collective-permute-start | bytes 786440 | tf_op jit(solution)/shard_map/ppermute | solution.py:123
  50.7 33.1 %collective-permute-start.14 = (bf16[16,8192]{1,0:T(8,128)(2,1)S(1)}, bf16[16,8192]{1,0:T(8,128)(2,1)S(1)}, u32[]{:S(2)}, u32[]{:S(2)}) collective-permute-start(bf16[16,8192]{1,0:T(8,128)(2,1)S(1)} %collective-permute-done.13.refs_14_), channel_id=1, source_target_pairs={{0,1},{1,0},{2,3},{3,2},{4,5},{5,4},{6,7},{7,6},{8,9},{9,8},{10,11... | collective-permute-start | bytes 786440 | tf_op jit(solution)/shard_map/ppermute | solution.py:123
  51.2 1.9 %copy-start = (bf16[8192,192]{0,1:T(8,128)(2,1)S(1)}, bf16[8192,192]{0,1:T(8,128)(2,1)}, u32[]{:S(2)}) copy-start(bf16[8192,192]{0,1:T(8,128)(2,1)} %param.14) | copy-start | bytes 9437188
  53.1 0.9 copy-start.3
  54.1 29.7 %copy-start.1 = (bf16[1792,192]{0,1:T(8,128)(2,1)S(1)}, bf16[1792,192]{0,1:T(8,128)(2,1)}, u32[]{:S(2)}) copy-start(bf16[1792,192]{0,1:T(8,128)(2,1)} %param.15) | copy-start | bytes 2064388
  54.1 29.7 %copy-start.4 = (bf16[16,8192]{1,0:T(8,128)(2,1)S(1)}, bf16[16,8192]{1,0:T(8,128)(2,1)}, u32[]{:S(2)}) copy-start(bf16[16,8192]{1,0:T(8,128)(2,1)} %refs_0_.3) | copy-start | bytes 786436
  54.1 29.7 %copy-start.5 = (s32[256]{0:T(256)S(1)}, s32[256]{0:T(256)}, u32[]{:S(2)}) copy-start(s32[256]{0:T(256)} %param.16) | copy-start | bytes 3076
  83.8 33.2 %copy-start.2 = (bf16[256,768]{1,0:T(8,128)(2,1)S(1)}, bf16[256,768]{1,0:T(8,128)(2,1)}, u32[]{:S(2)}) copy-start(bf16[256,768]{1,0:T(8,128)(2,1)} %tests.1) | copy-start | bytes 1179652

commit v7 on v6

--- a/solution.py
+++ b/solution.py
@@ -124,23 +124,20 @@
 
 
 def gather_blocks(own, chips, last):
-    places, blocks = [], []
-
-    def found(offset, column, block):
-        for other in range(2):
-            places.append((offset, other, column))
-            blocks.append(core_swap(block, chips) if other else block)
-
-    found(0, 0, own)
+    offsets, blocks = [0], [own]
     ahead, behind = own, own
     for step in range(1, chips // 2):
         ahead = ring_step(ahead, chips, 1)
         behind = ring_step(behind, chips, -1)
-        found(-step, 0, ahead)
-        found(step, 0, behind)
-    across = chips // 2
-    found(across, 0, ring_step(ahead if last > 0 else behind, chips, last))
-    return places, blocks
+        offsets += [-step, step]
+        blocks += [ahead, behind]
+    offsets.append(chips // 2)
+    blocks.append(ring_step(ahead if last > 0 else behind, chips, last))
+    return [(offset, other, 0) for other in range(2) for offset in offsets], blocks
+
+
+def after(value, other):
+    return lax.optimization_barrier((value, other))[0]
 
 
 def assemble(places, chips, blocks, whole, sems):
@@ -380,9 +377,14 @@
     ids = example_ids[None, :]
     places, token_blocks = gather_blocks(tokens, chips, 1)
     _, grad_blocks = gather_blocks(out_grad, chips, -1)
+    token_blocks = token_blocks + [core_swap(block, chips) for block in token_blocks]
+    token_blocks[0] = after(token_blocks[0], grad_blocks[-2])
     gate, up, inputs = forward(
         places, chips, token_blocks, gate_weight, up_weight, proj_d.T, TILE
     )
+    early = [core_swap(block, chips) for block in grad_blocks[:-3]]
+    late = [core_swap(after(block, gate), chips) for block in grad_blocks[-3:]]
+    grad_blocks = grad_blocks + early + late
     send = backward(
         places, chips, grad_blocks, down_weight, [gate], [up], proj_d.T, proj_ff.T, ids, 1024, TILE
     )

time: 130 us -> 126 us (0.969)
  starting transfers between devices: 21.6 us -> 19.2 us
    ppermute x14, waiting for transfers between devices: 28.9 us -> 25.5 us  [ring_step(): return lax.ppermute(block, 'hid', pairs)]
    ppermute x14, starting transfers between devices: 20 us -> 16.9 us  [ring_step(): return lax.ppermute(block, 'hid', pairs)]
    ppermute x16, waiting for transfers between devices: 0.04 us -> 2.37 us  [core_swap(): return lax.ppermute(block, 'hid', [(h, h ^ 1) for h in range(2 * chips)])]
  transfers between devices with their start and end apart: 30 -> 30, of which waited for: 12 -> 14; matrix products, arithmetic and copies ran while one was open for 0% -> 0% of each run, Pallas kernels for 23% -> 24%
where the time goes in v7:
time: 126 us; the launch traced here: 125 us
  Pallas kernels  48.6 us (39%)
  waiting for transfers between devices  27.8 us (22%)
  blocking collectives  25.4 us (20%)
  starting transfers between devices  19.2 us (15%)
  local copies, waits for them, and re-layouts  2.86 us (2%)
    pallas_call x1, Pallas kernels, forward(): pl.pallas_call(functools.partial(forward_kernel, places, chips), grid=(wi...  29.7 us
    ppermute x14, waiting for transfers between devices, ring_step(): return lax.ppermute(block, 'hid', pairs)  25.5 us
    pallas_call x1, Pallas kernels, backward(): pl.pallas_call(functools.partial(backward_kernel, places, chips, examples...  17.8 us
    ppermute x14, starting transfers between devices, ring_step(): return lax.ppermute(block, 'hid', pairs)  16.9 us
    all_to_all x1, blocking collectives, local_ring(): received = lax.all_to_all(send, 'hid', 0, 0)  14.7 us
    all_to_all x1, blocking collectives, local_ring(): scores = jnp.sum(lax.all_to_all(partial, 'hid', 0, 0), axis=0)  10.7 us
    unnamed x12, local copies, waits for them, and re-layouts  2.86 us
  transfers between devices with their start and end apart: 30, of which 14 were waited for; matrix products, arithmetic and copies ran while one was open for 0% of the time, Pallas kernels for 24%

profile of v7, /device:TPU:0, one launch (start us, length us, event | category | flops | bytes accessed | tf_op | source)
XLA Modules:
  0.0 125.2 jit_solution(13810551731003522754)
XLA Ops:
  0.6 3.1 %collective-permute-start.12 = (bf16[16,8192]{1,0:T(8,128)(2,1)}, bf16[16,8192]{1,0:T(8,128)(2,1)S(1)}, u32[]{:S(2)}, u32[]{:S(2)}) collective-permute-start(bf16[16,8192]{1,0:T(8,128)(2,1)} %refs_0_.1), channel_id=1, source_target_pairs={{0,4},{1,5},{4,8},{5,9},{8,12},{9,13},{12,14},{13,15},{14,10},{15,... | collective-permute-start | bytes 786440 | tf_op jit(solution)/shard_map/ppermute | solution.py:119
  3.7 0.0 collective-permute-start.1
  3.7 1.9 %collective-permute-start.13 = (bf16[16,8192]{1,0:T(8,128)(2,1)}, bf16[16,8192]{1,0:T(8,128)(2,1)S(1)}, u32[]{:S(2)}, u32[]{:S(2)}) collective-permute-start(bf16[16,8192]{1,0:T(8,128)(2,1)} %refs_0_.1), channel_id=1, source_target_pairs={{0,2},{1,3},{4,0},{5,1},{8,4},{9,5},{12,8},{13,9},{14,12},{15,13},... | collective-permute-start | bytes 786440 | tf_op jit(solution)/shard_map/ppermute | solution.py:119
  5.6 0.0 collective-permute-start.19
  5.7 4.5 %collective-permute-done.12.refs_1_ = bf16[16,8192]{1,0:T(8,128)(2,1)S(1)} collective-permute-done((bf16[16,8192]{1,0:T(8,128)(2,1)}, bf16[16,8192]{1,0:T(8,128)(2,1)S(1)}, u32[]{:S(2)}, u32[]{:S(2)}) %collective-permute-start.12) | collective-permute-done | bytes 262176 | tf_op jit(solution)/shard_map/ppermute | solution.py:119
  10.1 1.8 %collective-permute-start.14 = (bf16[16,8192]{1,0:T(8,128)(2,1)S(1)}, bf16[16,8192]{1,0:T(8,128)(2,1)S(1)}, u32[]{:S(2)}, u32[]{:S(2)}) collective-permute-start(bf16[16,8192]{1,0:T(8,128)(2,1)S(1)} %collective-permute-done.12.refs_1_), channel_id=1, source_target_pairs={{0,4},{1,5},{4,8},{5,9},{8,12},{9,13},{12,14},{13,15},{14,10},{15,... | collective-permute-start | bytes 786440 | tf_op jit(solution)/shard_map/ppermute | solution.py:119
  12.0 1.6 %collective-permute-start = (bf16[16,8192]{1,0:T(8,128)(2,1)}, bf16[16,8192]{1,0:T(8,128)(2,1)S(1)}, u32[]{:S(2)}, u32[]{:S(2)}) collective-permute-start(bf16[16,8192]{1,0:T(8,128)(2,1)} %refs_0_.2), channel_id=1, source_target_pairs={{0,4},{1,5},{4,8},{5,9},{8,12},{9,13},{12,14},{13,15},{14,10},{15,... | collective-permute-start | bytes 786440 | tf_op jit(solution)/shard_map/ppermute | solution.py:119
  13.5 0.0 collective-permute-done.1.refs_2_
  13.5 0.4 collective-permute-start.3
  14.0 4.8 %collective-permute-done.13.refs_2_ = bf16[16,8192]{1,0:T(8,128)(2,1)S(1)} collective-permute-done((bf16[16,8192]{1,0:T(8,128)(2,1)}, bf16[16,8192]{1,0:T(8,128)(2,1)S(1)}, u32[]{:S(2)}, u32[]{:S(2)}) %collective-permute-start.13) | collective-permute-done | bytes 262176 | tf_op jit(solution)/shard_map/ppermute | solution.py:119
  18.8 0.0 collective-permute-start.15
  18.8 0.0 collective-permute-done.19.refs_8_
  18.8 0.0 collective-permute-start.20
  18.8 0.6 collective-permute-done.14.refs_3_
  19.4 1.8 %collective-permute-start.16 = (bf16[16,8192]{1,0:T(8,128)(2,1)S(1)}, bf16[16,8192]{1,0:T(8,128)(2,1)S(1)}, u32[]{:S(2)}, u32[]{:S(2)}) collective-permute-start(bf16[16,8192]{1,0:T(8,128)(2,1)S(1)} %collective-permute-done.14.refs_3_), channel_id=1, source_target_pairs={{0,4},{1,5},{4,8},{5,9},{8,12},{9,13},{12,14},{13,15},{14,10},{15,... | collective-permute-start | bytes 786440 | tf_op jit(solution)/shard_map/ppermute | solution.py:119
  21.2 3.1 %collective-permute-done.refs_1_ = bf16[16,8192]{1,0:T(8,128)(2,1)S(1)} collective-permute-done((bf16[16,8192]{1,0:T(8,128)(2,1)}, bf16[16,8192]{1,0:T(8,128)(2,1)S(1)}, u32[]{:S(2)}, u32[]{:S(2)}) %collective-permute-start) | collective-permute-done | bytes 262176 | tf_op jit(solution)/shard_map/ppermute | solution.py:119
  24.4 0.0 collective-permute-start.21
  24.4 0.0 collective-permute-done.3.refs_4_
  24.4 1.6 %collective-permute-start.2 = (bf16[16,8192]{1,0:T(8,128)(2,1)S(1)}, bf16[16,8192]{1,0:T(8,128)(2,1)S(1)}, u32[]{:S(2)}, u32[]{:S(2)}) collective-permute-start(bf16[16,8192]{1,0:T(8,128)(2,1)S(1)} %collective-permute-done.refs_1_), channel_id=1, source_target_pairs={{0,4},{1,5},{4,8},{5,9},{8,12},{9,13},{12,14},{13,15},{14,10},{15,... | collective-permute-start | bytes 786440 | tf_op jit(solution)/shard_map/ppermute | solution.py:119
  26.0 2.6 %collective-permute-done.15.refs_4_ = bf16[16,8192]{1,0:T(8,128)(2,1)S(1)} collective-permute-done((bf16[16,8192]{1,0:T(8,128)(2,1)S(1)}, bf16[16,8192]{1,0:T(8,128)(2,1)S(1)}, u32[]{:S(2)}, u32[]{:S(2)}) %collective-permute-start.15) | collective-permute-done | bytes 262176 | tf_op jit(solution)/shard_map/ppermute | solution.py:119
  28.5 0.3 collective-permute-start.5
  28.8 1.7 %collective-permute-start.17 = (bf16[16,8192]{1,0:T(8,128)(2,1)S(1)}, bf16[16,8192]{1,0:T(8,128)(2,1)S(1)}, u32[]{:S(2)}, u32[]{:S(2)}) collective-permute-start(bf16[16,8192]{1,0:T(8,128)(2,1)S(1)} %collective-permute-done.15.refs_4_), channel_id=1, source_target_pairs={{0,2},{1,3},{4,0},{5,1},{8,4},{9,5},{12,8},{13,9},{14,12},{15,13},... | collective-permute-start | bytes 786440 | tf_op jit(solution)/shard_map/ppermute | solution.py:119
  30.5 0.0 collective-permute-done.16.refs_5_
  30.5 0.7 collective-permute-start.18
  31.2 4.4 %collective-permute-done.2.refs_3_ = bf16[16,8192]{1,0:T(8,128)(2,1)S(1)} collective-permute-done((bf16[16,8192]{1,0:T(8,128)(2,1)S(1)}, bf16[16,8192]{1,0:T(8,128)(2,1)S(1)}, u32[]{:S(2)}, u32[]{:S(2)}) %collective-permute-start.2) | collective-permute-done | bytes 262176 | tf_op jit(solution)/shard_map/ppermute | solution.py:119
  35.6 0.0 collective-permute-start.23
  35.6 2.2 %collective-permute-done.5.refs_6_ = bf16[16,8192]{1,0:T(8,128)(2,1)S(1)} collective-permute-done((bf16[16,8192]{1,0:T(8,128)(2,1)S(1)}, bf16[16,8192]{1,0:T(8,128)(2,1)S(1)}, u32[]{:S(2)}, u32[]{:S(2)}) %collective-permute-start.5) | collective-permute-done | bytes 262176 | tf_op jit(solution)/shard_map/ppermute | solution.py:119
  37.8 0.0 collective-permute-start.24
  37.8 3.2 %collective-permute-done.17.refs_6_ = bf16[16,8192]{1,0:T(8,128)(2,1)S(1)} collective-permute-done((bf16[16,8192]{1,0:T(8,128)(2,1)S(1)}, bf16[16,8192]{1,0:T(8,128)(2,1)S(1)}, u32[]{:S(2)}, u32[]{:S(2)}) %collective-permute-start.17) | collective-permute-done | bytes 262176 | tf_op jit(solution)/shard_map/ppermute | solution.py:119
  41.0 0.0 collective-permute-start.25
  41.0 0.0 collective-permute-done.18.refs_7_
  41.0 0.5 collective-permute-start.26
  41.5 0.0 collective-permute-done.22.refs_11_
  41.5 0.1 collective-permute-start.7
  41.6 0.0 collective-permute-done.23.refs_12_
  41.6 0.4 collective-permute-start.8
  42.0 0.0 collective-permute-done.24.refs_13_
  42.0 0.1 collective-permute-start.9
  42.1 0.4 collective-permute-done.25.refs_14_
  42.5 1.6 %collective-permute-start.4 = (bf16[16,8192]{1,0:T(8,128)(2,1)S(1)}, bf16[16,8192]{1,0:T(8,128)(2,1)S(1)}, u32[]{:S(2)}, u32[]{:S(2)}) collective-permute-start(bf16[16,8192]{1,0:T(8,128)(2,1)S(1)} %collective-permute-done.2.refs_3_), channel_id=1, source_target_pairs={{0,4},{1,5},{4,8},{5,9},{8,12},{9,13},{12,14},{13,15},{14,10},{15,... | collective-permute-start | bytes 786440 | tf_op jit(solution)/shard_map/ppermute | solution.py:119
  44.1 0.4 collective-permute-start.6
  44.6 1.9 %copy-done = bf16[8192,192]{0,1:T(8,128)(2,1)S(1)} copy-done((bf16[8192,192]{0,1:T(8,128)(2,1)S(1)}, bf16[8192,192]{0,1:T(8,128)(2,1)}, u32[]{:S(2)}) %copy-start) | copy-done | bytes 3145752
  46.5 0.9 copy-done.3
  47.4 29.7 %shard_map.104 = (f32[1792,256]{1,0:T(8,128)S(1)}, f32[1792,256]{1,0:T(8,128)S(1)}, f32[128,256]{1,0:T(8,128)S(1)}) custom-call(bf16[16,8192]{1,0:T(8,128)(2,1)S(1)} %copy-done.3, bf16[16,8192]{1,0:T(8,128)(2,1)S(1)} %collective-permute-done.12.refs_1_, bf16[16,8192]{1,0:T(8,128)(2,1)S(1)} %collective-permute-done.13.refs_2_, ...), custom_call_target="tpu_custom_call" | custom-call | flops 15032385536 | bytes 58720256 | tf_op jit(solution)/shard_map/pallas_call | solution.py:200
  77.1 0.0 collective-permute-done.6.refs_7_
  77.1 0.1 collective-permute-start.10
  77.2 0.5 collective-permute-start.11
  77.7 0.0 collective-permute-done.7.refs_8_
  77.7 0.1 collective-permute-start.29
  77.8 0.0 collective-permute-done.8.refs_9_
  77.8 0.4 collective-permute-start.28
  78.2 0.0 collective-permute-done.9.refs_10_
  78.2 0.1 collective-permute-start.27
  78.3 0.4 collective-permute-done.10.refs_11_
  78.7 0.4 collective-permute-done.11.refs_12_
  79.1 0.4 collective-permute-done.29.refs_15_
  79.5 0.4 collective-permute-done.28.refs_14_
  79.8 0.4 collective-permute-done.27.refs_13_
  80.2 0.0 copy-start.2
  80.2 17.8 %shard_map.105 = f32[16,16,256]{2,1,0:T(8,128)S(1)} custom-call(bf16[16,8192]{1,0:T(8,128)(2,1)S(1)} %copy-done.4, bf16[16,8192]{1,0:T(8,128)(2,1)S(1)} %collective-permute-done.refs_1_, bf16[16,8192]{1,0:T(8,128)(2,1)S(1)} %collective-permute-done.1.refs_2_, bf16[16,8192]{1,0:T(8,128)(2,1)S(1)} %collective-permute-done.2.refs_3_, ...), custom_call_target="tpu_custom_call" | custom-call | flops 7516192768 | bytes 29360128 | tf_op jit(solution)/shard_map/pallas_call | solution.py:300
  98.0 14.7 %all_to_all.10.received = f32[16,16,256]{2,1,0:T(8,128)S(1)} all-to-all(f32[16,16,256]{2,1,0:T(8,128)S(1)} %shard_map.105), channel_id=1, replica_groups=mesh['groups'=2,'hid'=16,'mod'=1] {'hid'}, dimensions={0} | all-to-all | bytes 524288 | tf_op jit(solution)/shard_map/all_to_all | solution.py:391
  112.8 1.1 shard_map.106
  113.9 10.7 %all_to_all.11 = f32[16,8,256]{2,1,0:T(8,128)S(1)} all-to-all(f32[16,8,256]{2,1,0:T(8,128)S(1)} %get-tuple-element.19), channel_id=1, replica_groups=mesh['groups'=2,'hid'=16,'mod'=1] {'hid'}, dimensions={0} | all-to-all | bytes 262144 | tf_op jit(solution)/shard_map/all_to_all | solution.py:393
  124.6 0.6 reduce_sum.9
  (14 shorter events, 0.0 us)
Async XLA Ops:
  0.6 9.5 %collective-permute-start.12 = (bf16[16,8192]{1,0:T(8,128)(2,1)}, bf16[16,8192]{1,0:T(8,128)(2,1)S(1)}, u32[]{:S(2)}, u32[]{:S(2)}) collective-permute-start(bf16[16,8192]{1,0:T(8,128)(2,1)} %refs_0_.1), channel_id=1, source_target_pairs={{0,4},{1,5},{4,8},{5,9},{8,12},{9,13},{12,14},{13,15},{14,10},{15,... | collective-permute-start | bytes 786440 | tf_op jit(solution)/shard_map/ppermute | solution.py:119
  3.7 9.8 %collective-permute-start.1 = (bf16[16,8192]{1,0:T(8,128)(2,1)}, bf16[16,8192]{1,0:T(8,128)(2,1)S(1)}, u32[]{:S(2)}, u32[]{:S(2)}) collective-permute-start(bf16[16,8192]{1,0:T(8,128)(2,1)} %refs_0_.2), channel_id=1, source_target_pairs={{0,2},{1,3},{4,0},{5,1},{8,4},{9,5},{12,8},{13,9},{14,12},{15,13},... | collective-permute-start | bytes 786440 | tf_op jit(solution)/shard_map/ppermute | solution.py:119
  3.7 15.1 %collective-permute-start.13 = (bf16[16,8192]{1,0:T(8,128)(2,1)}, bf16[16,8192]{1,0:T(8,128)(2,1)S(1)}, u32[]{:S(2)}, u32[]{:S(2)}) collective-permute-start(bf16[16,8192]{1,0:T(8,128)(2,1)} %refs_0_.1), channel_id=1, source_target_pairs={{0,2},{1,3},{4,0},{5,1},{8,4},{9,5},{12,8},{13,9},{14,12},{15,13},... | collective-permute-start | bytes 786440 | tf_op jit(solution)/shard_map/ppermute | solution.py:119
  5.6 13.1 %collective-permute-start.19 = (bf16[16,8192]{1,0:T(8,128)(2,1)}, bf16[16,8192]{1,0:T(8,128)(2,1)S(1)}, u32[]{:S(2)}, u32[]{:S(2)}) collective-permute-start(bf16[16,8192]{1,0:T(8,128)(2,1)} %refs_0_.1), channel_id=1, source_target_pairs={{0,1},{1,0},{2,3},{3,2},{4,5},{5,4},{6,7},{7,6},{8,9},{9,8},{10,11... | collective-permute-start | bytes 786440 | tf_op jit(solution)/shard_map/ppermute | solution.py:123
  10.1 9.2 %collective-permute-start.14 = (bf16[16,8192]{1,0:T(8,128)(2,1)S(1)}, bf16[16,8192]{1,0:T(8,128)(2,1)S(1)}, u32[]{:S(2)}, u32[]{:S(2)}) collective-permute-start(bf16[16,8192]{1,0:T(8,128)(2,1)S(1)} %collective-permute-done.12.refs_1_), channel_id=1, source_target_pairs={{0,4},{1,5},{4,8},{5,9},{8,12},{9,13},{12,14},{13,15},{14,10},{15,... | collective-permute-start | bytes 786440 | tf_op jit(solution)/shard_map/ppermute | solution.py:119
  12.0 12.4 %collective-permute-start = (bf16[16,8192]{1,0:T(8,128)(2,1)}, bf16[16,8192]{1,0:T(8,128)(2,1)S(1)}, u32[]{:S(2)}, u32[]{:S(2)}) collective-permute-start(bf16[16,8192]{1,0:T(8,128)(2,1)} %refs_0_.2), channel_id=1, source_target_pairs={{0,4},{1,5},{4,8},{5,9},{8,12},{9,13},{12,14},{13,15},{14,10},{15,... | collective-permute-start | bytes 786440 | tf_op jit(solution)/shard_map/ppermute | solution.py:119
  13.5 10.8 %collective-permute-start.3 = (bf16[16,8192]{1,0:T(8,128)(2,1)S(1)}, bf16[16,8192]{1,0:T(8,128)(2,1)S(1)}, u32[]{:S(2)}, u32[]{:S(2)}) collective-permute-start(bf16[16,8192]{1,0:T(8,128)(2,1)S(1)} %collective-permute-done.1.refs_2_), channel_id=1, source_target_pairs={{0,2},{1,3},{4,0},{5,1},{8,4},{9,5},{12,8},{13,9},{14,12},{15,13},... | collective-permute-start | bytes 786440 | tf_op jit(solution)/shard_map/ppermute | solution.py:119
  18.8 9.8 %collective-permute-start.15 = (bf16[16,8192]{1,0:T(8,128)(2,1)S(1)}, bf16[16,8192]{1,0:T(8,128)(2,1)S(1)}, u32[]{:S(2)}, u32[]{:S(2)}) collective-permute-start(bf16[16,8192]{1,0:T(8,128)(2,1)S(1)} %collective-permute-done.13.refs_2_), channel_id=1, source_target_pairs={{0,2},{1,3},{4,0},{5,1},{8,4},{9,5},{12,8},{13,9},{14,12},{15,13},... | collective-permute-start | bytes 786440 | tf_op jit(solution)/shard_map/ppermute | solution.py:119
  18.8 10.1 %collective-permute-start.20 = (bf16[16,8192]{1,0:T(8,128)(2,1)S(1)}, bf16[16,8192]{1,0:T(8,128)(2,1)S(1)}, u32[]{:S(2)}, u32[]{:S(2)}) collective-permute-start(bf16[16,8192]{1,0:T(8,128)(2,1)S(1)} %collective-permute-done.12.refs_1_), channel_id=1, source_target_pairs={{0,1},{1,0},{2,3},{3,2},{4,5},{5,4},{6,7},{7,6},{8,9},{9,8},{10,11... | collective-permute-start | bytes 786440 | tf_op jit(solution)/shard_map/ppermute | solution.py:123
  19.4 11.1 %collective-permute-start.16 = (bf16[16,8192]{1,0:T(8,128)(2,1)S(1)}, bf16[16,8192]{1,0:T(8,128)(2,1)S(1)}, u32[]{:S(2)}, u32[]{:S(2)}) collective-permute-start(bf16[16,8192]{1,0:T(8,128)(2,1)S(1)} %collective-permute-done.14.refs_3_), channel_id=1, source_target_pairs={{0,4},{1,5},{4,8},{5,9},{8,12},{9,13},{12,14},{13,15},{14,10},{15,... | collective-permute-start | bytes 786440 | tf_op jit(solution)/shard_map/ppermute | solution.py:119
  24.4 6.8 %collective-permute-start.21 = (bf16[16,8192]{1,0:T(8,128)(2,1)S(1)}, bf16[16,8192]{1,0:T(8,128)(2,1)S(1)}, u32[]{:S(2)}, u32[]{:S(2)}) collective-permute-start(bf16[16,8192]{1,0:T(8,128)(2,1)S(1)} %collective-permute-done.13.refs_2_), channel_id=1, source_target_pairs={{0,1},{1,0},{2,3},{3,2},{4,5},{5,4},{6,7},{7,6},{8,9},{9,8},{10,11... | collective-permute-start | bytes 786440 | tf_op jit(solution)/shard_map/ppermute | solution.py:123
  24.4 11.2 %collective-permute-start.2 = (bf16[16,8192]{1,0:T(8,128)(2,1)S(1)}, bf16[16,8192]{1,0:T(8,128)(2,1)S(1)}, u32[]{:S(2)}, u32[]{:S(2)}) collective-permute-start(bf16[16,8192]{1,0:T(8,128)(2,1)S(1)} %collective-permute-done.refs_1_), channel_id=1, source_target_pairs={{0,4},{1,5},{4,8},{5,9},{8,12},{9,13},{12,14},{13,15},{14,10},{15,... | collective-permute-start | bytes 786440 | tf_op jit(solution)/shard_map/ppermute | solution.py:119
  28.5 9.2 %collective-permute-start.5 = (bf16[16,8192]{1,0:T(8,128)(2,1)S(1)}, bf16[16,8192]{1,0:T(8,128)(2,1)S(1)}, u32[]{:S(2)}, u32[]{:S(2)}) collective-permute-start(bf16[16,8192]{1,0:T(8,128)(2,1)S(1)} %collective-permute-done.3.refs_4_), channel_id=1, source_target_pairs={{0,2},{1,3},{4,0},{5,1},{8,4},{9,5},{12,8},{13,9},{14,12},{15,13},... | collective-permute-start | bytes 786440 | tf_op jit(solution)/shard_map/ppermute | solution.py:119
  28.8 12.2 %collective-permute-start.17 = (bf16[16,8192]{1,0:T(8,128)(2,1)S(1)}, bf16[16,8192]{1,0:T(8,128)(2,1)S(1)}, u32[]{:S(2)}, u32[]{:S(2)}) collective-permute-start(bf16[16,8192]{1,0:T(8,128)(2,1)S(1)} %collective-permute-done.15.refs_4_), channel_id=1, source_target_pairs={{0,2},{1,3},{4,0},{5,1},{8,4},{9,5},{12,8},{13,9},{14,12},{15,13},... | collective-permute-start | bytes 786440 | tf_op jit(solution)/shard_map/ppermute | solution.py:119
  30.5 10.5 %collective-permute-start.18 = (bf16[16,8192]{1,0:T(8,128)(2,1)S(1)}, bf16[16,8192]{1,0:T(8,128)(2,1)S(1)}, u32[]{:S(2)}, u32[]{:S(2)}) collective-permute-start(bf16[16,8192]{1,0:T(8,128)(2,1)S(1)} %collective-permute-done.16.refs_5_), channel_id=1, source_target_pairs={{0,4},{1,5},{4,8},{5,9},{8,12},{9,13},{12,14},{13,15},{14,10},{15,... | collective-permute-start | bytes 786440 | tf_op jit(solution)/shard_map/ppermute | solution.py:119
  31.2 10.4 %collective-permute-start.22 = (bf16[16,8192]{1,0:T(8,128)(2,1)S(1)}, bf16[16,8192]{1,0:T(8,128)(2,1)S(1)}, u32[]{:S(2)}, u32[]{:S(2)}) collective-permute-start(bf16[16,8192]{1,0:T(8,128)(2,1)S(1)} %collective-permute-done.14.refs_3_), channel_id=1, source_target_pairs={{0,1},{1,0},{2,3},{3,2},{4,5},{5,4},{6,7},{7,6},{8,9},{9,8},{10,11... | collective-permute-start | bytes 786440 | tf_op jit(solution)/shard_map/ppermute | solution.py:123
  35.6 6.0 %collective-permute-start.23 = (bf16[16,8192]{1,0:T(8,128)(2,1)S(1)}, bf16[16,8192]{1,0:T(8,128)(2,1)S(1)}, u32[]{:S(2)}, u32[]{:S(2)}) collective-permute-start(bf16[16,8192]{1,0:T(8,128)(2,1)S(1)} %collective-permute-done.15.refs_4_), channel_id=1, source_target_pairs={{0,1},{1,0},{2,3},{3,2},{4,5},{5,4},{6,7},{7,6},{8,9},{9,8},{10,11... | collective-permute-start | bytes 786440 | tf_op jit(solution)/shard_map/ppermute | solution.py:123
  37.8 4.3 %collective-permute-start.24 = (bf16[16,8192]{1,0:T(8,128)(2,1)S(1)}, bf16[16,8192]{1,0:T(8,128)(2,1)S(1)}, u32[]{:S(2)}, u32[]{:S(2)}) collective-permute-start(bf16[16,8192]{1,0:T(8,128)(2,1)S(1)} %collective-permute-done.16.refs_5_), channel_id=1, source_target_pairs={{0,1},{1,0},{2,3},{3,2},{4,5},{5,4},{6,7},{7,6},{8,9},{9,8},{10,11... | collective-permute-start | bytes 786440 | tf_op jit(solution)/shard_map/ppermute | solution.py:123
  41.0 1.5 %collective-permute-start.25 = (bf16[16,8192]{1,0:T(8,128)(2,1)S(1)}, bf16[16,8192]{1,0:T(8,128)(2,1)S(1)}, u32[]{:S(2)}, u32[]{:S(2)}) collective-permute-start(bf16[16,8192]{1,0:T(8,128)(2,1)S(1)} %collective-permute-done.17.refs_6_), channel_id=1, source_target_pairs={{0,1},{1,0},{2,3},{3,2},{4,5},{5,4},{6,7},{7,6},{8,9},{9,8},{10,11... | collective-permute-start | bytes 786440 | tf_op jit(solution)/shard_map/ppermute | solution.py:123
  41.0 3.1 %collective-permute-start.26 = (bf16[16,8192]{1,0:T(8,128)(2,1)S(1)}, bf16[16,8192]{1,0:T(8,128)(2,1)S(1)}, u32[]{:S(2)}, u32[]{:S(2)}) collective-permute-start(bf16[16,8192]{1,0:T(8,128)(2,1)S(1)} %collective-permute-done.18.refs_7_), channel_id=1, source_target_pairs={{0,1},{1,0},{2,3},{3,2},{4,5},{5,4},{6,7},{7,6},{8,9},{9,8},{10,11... | collective-permute-start | bytes 786440 | tf_op jit(solution)/shard_map/ppermute | solution.py:123
  41.5 36.2 %collective-permute-start.7 = (bf16[16,8192]{1,0:T(8,128)(2,1)}, bf16[16,8192]{1,0:T(8,128)(2,1)S(1)}, u32[]{:S(2)}, u32[]{:S(2)}) collective-permute-start(bf16[16,8192]{1,0:T(8,128)(2,1)} %refs_0_.2), channel_id=1, source_target_pairs={{0,1},{1,0},{2,3},{3,2},{4,5},{5,4},{6,7},{7,6},{8,9},{9,8},{10,11... | collective-permute-start | bytes 786440 | tf_op jit(solution)/shard_map/ppermute | solution.py:123
  41.6 36.2 %collective-permute-start.8 = (bf16[16,8192]{1,0:T(8,128)(2,1)S(1)}, bf16[16,8192]{1,0:T(8,128)(2,1)S(1)}, u32[]{:S(2)}, u32[]{:S(2)}) collective-permute-start(bf16[16,8192]{1,0:T(8,128)(2,1)S(1)} %collective-permute-done.refs_1_), channel_id=1, source_target_pairs={{0,1},{1,0},{2,3},{3,2},{4,5},{5,4},{6,7},{7,6},{8,9},{9,8},{10,11... | collective-permute-start | bytes 786440 | tf_op jit(solution)/shard_map/ppermute | solution.py:123
  42.0 36.2 %collective-permute-start.9 = (bf16[16,8192]{1,0:T(8,128)(2,1)S(1)}, bf16[16,8192]{1,0:T(8,128)(2,1)S(1)}, u32[]{:S(2)}, u32[]{:S(2)}) collective-permute-start(bf16[16,8192]{1,0:T(8,128)(2,1)S(1)} %collective-permute-done.1.refs_2_), channel_id=1, source_target_pairs={{0,1},{1,0},{2,3},{3,2},{4,5},{5,4},{6,7},{7,6},{8,9},{9,8},{10,11... | collective-permute-start | bytes 786440 | tf_op jit(solution)/shard_map/ppermute | solution.py:123
  42.5 34.6 %collective-permute-start.4 = (bf16[16,8192]{1,0:T(8,128)(2,1)S(1)}, bf16[16,8192]{1,0:T(8,128)(2,1)S(1)}, u32[]{:S(2)}, u32[]{:S(2)}) collective-permute-start(bf16[16,8192]{1,0:T(8,128)(2,1)S(1)} %collective-permute-done.2.refs_3_), channel_id=1, source_target_pairs={{0,4},{1,5},{4,8},{5,9},{8,12},{9,13},{12,14},{13,15},{14,10},{15,... | collective-permute-start | bytes 786440 | tf_op jit(solution)/shard_map/ppermute | solution.py:119
  44.1 33.0 %collective-permute-start.6 = (bf16[16,8192]{1,0:T(8,128)(2,1)S(1)}, bf16[16,8192]{1,0:T(8,128)(2,1)S(1)}, u32[]{:S(2)}, u32[]{:S(2)}) collective-permute-start(bf16[16,8192]{1,0:T(8,128)(2,1)S(1)} %collective-permute-done.5.refs_6_), channel_id=1, source_target_pairs={{0,2},{1,3},{4,0},{5,1},{8,4},{9,5},{12,8},{13,9},{14,12},{15,13},... | collective-permute-start | bytes 786440 | tf_op jit(solution)/shard_map/ppermute | solution.py:119
  44.6 1.9 %copy-start = (bf16[8192,192]{0,1:T(8,128)(2,1)S(1)}, bf16[8192,192]{0,1:T(8,128)(2,1)}, u32[]{:S(2)}) copy-start(bf16[8192,192]{0,1:T(8,128)(2,1)} %param.14) | copy-start | bytes 9437188
  46.5 0.9 copy-start.3
  47.4 32.8 %copy-start.1 = (bf16[1792,192]{0,1:T(8,128)(2,1)S(1)}, bf16[1792,192]{0,1:T(8,128)(2,1)}, u32[]{:S(2)}) copy-start(bf16[1792,192]{0,1:T(8,128)(2,1)} %param.15) | copy-start | bytes 2064388
  47.4 32.8 %copy-start.4 = (bf16[16,8192]{1,0:T(8,128)(2,1)S(1)}, bf16[16,8192]{1,0:T(8,128)(2,1)}, u32[]{:S(2)}) copy-start(bf16[16,8192]{1,0:T(8,128)(2,1)} %refs_0_.2) | copy-start | bytes 786436
  47.4 32.8 %copy-start.5 = (s32[256]{0:T(256)S(1)}, s32[256]{0:T(256)}, u32[]{:S(2)}) copy-start(s32[256]{0:T(256)} %param.16) | copy-start | bytes 3076
  77.1 1.6 %collective-permute-start.10 = (bf16[16,8192]{1,0:T(8,128)(2,1)S(1)}, bf16[16,8192]{1,0:T(8,128)(2,1)S(1)}, u32[]{:S(2)}, u32[]{:S(2)}) collective-permute-start(bf16[16,8192]{1,0:T(8,128)(2,1)S(1)} %collective-permute-done.2.refs_3_), channel_id=1, source_target_pairs={{0,1},{1,0},{2,3},{3,2},{4,5},{5,4},{6,7},{7,6},{8,9},{9,8},{10,11... | collective-permute-start | bytes 786440 | tf_op jit(solution)/shard_map/ppermute | solution.py:123
  77.2 1.9 %collective-permute-start.11 = (bf16[16,8192]{1,0:T(8,128)(2,1)S(1)}, bf16[16,8192]{1,0:T(8,128)(2,1)S(1)}, u32[]{:S(2)}, u32[]{:S(2)}) collective-permute-start(bf16[16,8192]{1,0:T(8,128)(2,1)S(1)} %collective-permute-done.3.refs_4_), channel_id=1, source_target_pairs={{0,1},{1,0},{2,3},{3,2},{4,5},{5,4},{6,7},{7,6},{8,9},{9,8},{10,11... | collective-permute-start | bytes 786440 | tf_op jit(solution)/shard_map/ppermute | solution.py:123
  77.7 1.8 %collective-permute-start.29 = (bf16[16,8192]{1,0:T(8,128)(2,1)S(1)}, bf16[16,8192]{1,0:T(8,128)(2,1)S(1)}, u32[]{:S(2)}, u32[]{:S(2)}) collective-permute-start(bf16[16,8192]{1,0:T(8,128)(2,1)S(1)} %collective-permute-done.6.refs_7_), channel_id=1, source_target_pairs={{0,1},{1,0},{2,3},{3,2},{4,5},{5,4},{6,7},{7,6},{8,9},{9,8},{10,11... | collective-permute-start | bytes 786440 | tf_op jit(solution)/shard_map/ppermute | solution.py:123
  77.8 2.1 %collective-permute-start.28 = (bf16[16,8192]{1,0:T(8,128)(2,1)S(1)}, bf16[16,8192]{1,0:T(8,128)(2,1)S(1)}, u32[]{:S(2)}, u32[]{:S(2)}) collective-permute-start(bf16[16,8192]{1,0:T(8,128)(2,1)S(1)} %collective-permute-done.5.refs_6_), channel_id=1, source_target_pairs={{0,1},{1,0},{2,3},{3,2},{4,5},{5,4},{6,7},{7,6},{8,9},{9,8},{10,11... | collective-permute-start | bytes 786440 | tf_op jit(solution)/shard_map/ppermute | solution.py:123
  78.2 2.0 %collective-permute-start.27 = (bf16[16,8192]{1,0:T(8,128)(2,1)S(1)}, bf16[16,8192]{1,0:T(8,128)(2,1)S(1)}, u32[]{:S(2)}, u32[]{:S(2)}) collective-permute-start(bf16[16,8192]{1,0:T(8,128)(2,1)S(1)} %collective-permute-done.4.refs_5_), channel_id=1, source_target_pairs={{0,1},{1,0},{2,3},{3,2},{4,5},{5,4},{6,7},{7,6},{8,9},{9,8},{10,11... | collective-permute-start | bytes 786440 | tf_op jit(solution)/shard_map/ppermute | solution.py:123
  80.2 32.6 %copy-start.2 = (bf16[256,768]{1,0:T(8,128)(2,1)S(1)}, bf16[256,768]{1,0:T(8,128)(2,1)}, u32[]{:S(2)}) copy-start(bf16[256,768]{1,0:T(8,128)(2,1)} %tests.1) | copy-start | bytes 1179652

commit v8 on v7

--- a/solution.py
+++ b/solution.py
@@ -181,7 +181,7 @@
     def _():
         piece = depth // PIECES
         part = pl.ds(pl.multiple_of(k * depth + n * piece, piece), piece)
-        inputs[...] += last_dot(proj[: 2 * R, part], whole[:, part])
+        inputs[...] += last_dot(proj[: 2 * R, :], whole[:, part])
 
     @pl.when(k == 0)
     def _():
@@ -204,7 +204,12 @@
         + [jax.ShapeDtypeStruct((2 * R, rows), jnp.float32)],
         in_specs=[pl.BlockSpec(memory_space=pl.ANY)] * len(blocks)
         + [pl.BlockSpec((depth // 2, tile), lambda n, k: (k, n))] * 2
-        + [pl.BlockSpec((3 * R, depth), lambda n, k: (0, 0))],
+        + [
+            pl.BlockSpec(
+                (3 * R, depth // (2 * PIECES)),
+                lambda n, k: (0, k * PIECES + jnp.minimum(n, PIECES - 1)),
+            )
+        ],
         out_specs=[pl.BlockSpec((tile, rows), lambda n, k: (n, 0))] * 2
         + [pl.BlockSpec((2 * R, rows), lambda n, k: (0, 0))],
         scratch_shapes=[
@@ -231,13 +236,16 @@
     )
 
 
-def backward_kernel(places, chips, examples, tile, parts, *refs):
+def backward_kernel(places, chips, examples, tile, *refs):
     count = len(places)
     blocks, refs = refs[:count], refs[count:]
     weights, refs = refs[:SPLIT], refs[SPLIT:]
     proj, proj_ff, ids = refs[:3]
-    gates, ups = refs[3 : 3 + parts], refs[3 + parts : 3 + 2 * parts]
-    ready, whole, spread, flipped, sums, sems = refs[3 + 2 * parts :]
+    gate_up, (ready, whole, spread, flipped, sums, gate, up, sems, late) = refs[3:5], refs[5:]
+    fetches = [
+        pltpu.make_async_copy(source, target, late.at[index])
+        for index, (source, target) in enumerate(zip(gate_up, (gate, up)))
+    ]
     step = pl.program_id(0)
     hid = 2 * chips
     shares = R // hid
@@ -245,6 +253,8 @@
     @pl.when(step == 0)
     def _():
         assemble(places, chips, blocks, whole, sems)
+        for fetch in fetches:
+            fetch.start()
         spread[...] = jnp.zeros_like(spread)
         flipped[...] = jnp.zeros_like(flipped)
 
@@ -259,20 +269,17 @@
     @pl.when(step == pl.num_programs(0) - 1)
     def _():
         sums[...] = jnp.zeros_like(sums)
-        start = 0
-        for gate, up in zip(gates, ups):
-            for local in range(0, gate.shape[0], tile):
-                part = pl.ds(local, tile)
-                hidden, gate_grad, up_grad = pointwise(
-                    gate[part, :], up[part, :], spread[start : start + tile, :]
+        for fetch in fetches:
+            fetch.wait()
+        for start in range(0, gate.shape[0], tile):
+            part = pl.ds(start, tile)
+            hidden, gate_grad, up_grad = pointwise(gate[part, :], up[part, :], spread[part, :])
+            for m, value in enumerate((gate_grad, up_grad, hidden)):
+                sums[m * R : (m + 1) * R, :] += jnp.dot(
+                    proj_ff[m * R : (m + 1) * R, start : start + tile],
+                    value,
+                    preferred_element_type=jnp.float32,
                 )
-                for m, value in enumerate((gate_grad, up_grad, hidden)):
-                    sums[m * R : (m + 1) * R, :] += jnp.dot(
-                        proj_ff[m * R : (m + 1) * R, start : start + tile],
-                        value,
-                        preferred_element_type=jnp.float32,
-                    )
-                start += tile
         for m in range(2):
             for p in range(hid):
                 own = sums[m * R + p * shares : m * R + (p + 1) * shares, :]
@@ -287,7 +294,7 @@
             ready[:, 2 * shares :, j * R : (j + 1) * R] = product.reshape(hid, examples, R)
 
 
-def backward(places, chips, blocks, weight, gates, ups, proj, proj_ff, ids, depth_tile, tile):
+def backward(places, chips, blocks, weight, gate, up, proj, proj_ff, ids, depth_tile, tile):
     rows = blocks[0].shape[0] * chips * 2
     width, depth = weight.shape
     hid = 2 * chips
@@ -298,7 +305,7 @@
         return pl.BlockSpec(shape, lambda k: (0,) * len(shape))
 
     return pl.pallas_call(
-        functools.partial(backward_kernel, places, chips, examples, tile, len(gates)),
+        functools.partial(backward_kernel, places, chips, examples, tile),
         grid=(depth // depth_tile,),
         out_shape=jax.ShapeDtypeStruct((hid, deep, rows), jnp.float32),
         in_specs=[pl.BlockSpec(memory_space=pl.ANY)] * len(blocks)
@@ -311,20 +318,23 @@
             stay(3 * R, width),
             stay(1, rows),
         ]
-        + [stay(*value.shape) for value in (*gates, *ups)],
+        + [pl.BlockSpec(memory_space=pl.ANY)] * 2,
         out_specs=stay(hid, deep, rows),
         scratch_shapes=[
             pltpu.VMEM((rows, depth), jnp.bfloat16),
             pltpu.VMEM((width, rows), jnp.float32),
             pltpu.VMEM((rows // 128, R, 128), jnp.float32),
             pltpu.VMEM((3 * R, rows), jnp.float32),
+            pltpu.VMEM((width, rows), jnp.float32),
+            pltpu.VMEM((width, rows), jnp.float32),
             pltpu.SemaphoreType.DMA((len(blocks),)),
+            pltpu.SemaphoreType.DMA((2,)),
         ],
         compiler_params=pltpu.CompilerParams(vmem_limit_bytes=32 * MEBI),
         cost_estimate=pl.CostEstimate(
             flops=2 * rows * depth * width, bytes_accessed=2 * depth * width, transcendentals=0
         ),
-    )(*blocks, *[weight] * SPLIT, proj, proj_ff, ids, *gates, *ups)
+    )(*blocks, *[weight] * SPLIT, proj, proj_ff, ids, gate, up)
 
 
 def features_kernel(hid, received, inputs, ids, tests, features, partial):
@@ -386,7 +396,7 @@
     late = [core_swap(after(block, gate), chips) for block in grad_blocks[-3:]]
     grad_blocks = grad_blocks + early + late
     send = backward(
-        places, chips, grad_blocks, down_weight, [gate], [up], proj_d.T, proj_ff.T, ids, 1024, TILE
+        places, chips, grad_blocks, down_weight, gate, up, proj_d.T, proj_ff.T, ids, 1024, TILE
     )
     received = lax.all_to_all(send, "hid", 0, 0)
     features, partial = finish(received, inputs, ids, test_features)

time: 126 us -> 126 us (level)
  no operation moved by 1% of the time
where the time goes in v8:
time: 126 us
  Pallas kernels  48.9 us (39%)
  waiting for transfers between devices  27.8 us (22%)
  blocking collectives  25.4 us (20%)
  starting transfers between devices  19.2 us (15%)
  local copies, waits for them, and re-layouts  2.86 us (2%)
    pallas_call x1, Pallas kernels, forward(): pl.pallas_call(functools.partial(forward_kernel, places, chips), grid=(wi...  29.7 us
    ppermute x14, waiting for transfers between devices, ring_step(): return lax.ppermute(block, 'hid', pairs)  25.5 us
    pallas_call x1, Pallas kernels, backward(): pl.pallas_call(functools.partial(backward_kernel, places, chips, examples...  18.1 us
    ppermute x14, starting transfers between devices, ring_step(): return lax.ppermute(block, 'hid', pairs)  16.9 us
    all_to_all x1, blocking collectives, local_ring(): received = lax.all_to_all(send, 'hid', 0, 0)  14.7 us
    all_to_all x1, blocking collectives, local_ring(): scores = jnp.sum(lax.all_to_all(partial, 'hid', 0, 0), axis=0)  10.7 us
    unnamed x12, local copies, waits for them, and re-layouts  2.86 us
  transfers between devices with their start and end apart: 30, of which 14 were waited for; matrix products, arithmetic and copies ran while one was open for 0% of the time, Pallas kernels for 24%

profile of v8, /device:TPU:0, one launch (start us, length us, event | category | flops | bytes accessed | tf_op | source)
XLA Modules:
  0.0 125.5 jit_solution(5324208764509193123)
XLA Ops:
  0.6 3.1 %collective-permute-start.12 = (bf16[16,8192]{1,0:T(8,128)(2,1)}, bf16[16,8192]{1,0:T(8,128)(2,1)S(1)}, u32[]{:S(2)}, u32[]{:S(2)}) collective-permute-start(bf16[16,8192]{1,0:T(8,128)(2,1)} %refs_0_.1), channel_id=1, source_target_pairs={{0,4},{1,5},{4,8},{5,9},{8,12},{9,13},{12,14},{13,15},{14,10},{15,... | collective-permute-start | bytes 786440 | tf_op jit(solution)/shard_map/ppermute | solution.py:119
  3.7 0.0 collective-permute-start.1
  3.7 1.9 %collective-permute-start.13 = (bf16[16,8192]{1,0:T(8,128)(2,1)}, bf16[16,8192]{1,0:T(8,128)(2,1)S(1)}, u32[]{:S(2)}, u32[]{:S(2)}) collective-permute-start(bf16[16,8192]{1,0:T(8,128)(2,1)} %refs_0_.1), channel_id=1, source_target_pairs={{0,2},{1,3},{4,0},{5,1},{8,4},{9,5},{12,8},{13,9},{14,12},{15,13},... | collective-permute-start | bytes 786440 | tf_op jit(solution)/shard_map/ppermute | solution.py:119
  5.6 0.0 collective-permute-start.19
  5.7 4.5 %collective-permute-done.12.refs_1_ = bf16[16,8192]{1,0:T(8,128)(2,1)S(1)} collective-permute-done((bf16[16,8192]{1,0:T(8,128)(2,1)}, bf16[16,8192]{1,0:T(8,128)(2,1)S(1)}, u32[]{:S(2)}, u32[]{:S(2)}) %collective-permute-start.12) | collective-permute-done | bytes 262176 | tf_op jit(solution)/shard_map/ppermute | solution.py:119
  10.1 1.8 %collective-permute-start.14 = (bf16[16,8192]{1,0:T(8,128)(2,1)S(1)}, bf16[16,8192]{1,0:T(8,128)(2,1)S(1)}, u32[]{:S(2)}, u32[]{:S(2)}) collective-permute-start(bf16[16,8192]{1,0:T(8,128)(2,1)S(1)} %collective-permute-done.12.refs_1_), channel_id=1, source_target_pairs={{0,4},{1,5},{4,8},{5,9},{8,12},{9,13},{12,14},{13,15},{14,10},{15,... | collective-permute-start | bytes 786440 | tf_op jit(solution)/shard_map/ppermute | solution.py:119
  12.0 1.6 %collective-permute-start = (bf16[16,8192]{1,0:T(8,128)(2,1)}, bf16[16,8192]{1,0:T(8,128)(2,1)S(1)}, u32[]{:S(2)}, u32[]{:S(2)}) collective-permute-start(bf16[16,8192]{1,0:T(8,128)(2,1)} %refs_0_.2), channel_id=1, source_target_pairs={{0,4},{1,5},{4,8},{5,9},{8,12},{9,13},{12,14},{13,15},{14,10},{15,... | collective-permute-start | bytes 786440 | tf_op jit(solution)/shard_map/ppermute | solution.py:119
  13.5 0.0 collective-permute-done.1.refs_2_
  13.5 0.4 collective-permute-start.3
  14.0 4.8 %collective-permute-done.13.refs_2_ = bf16[16,8192]{1,0:T(8,128)(2,1)S(1)} collective-permute-done((bf16[16,8192]{1,0:T(8,128)(2,1)}, bf16[16,8192]{1,0:T(8,128)(2,1)S(1)}, u32[]{:S(2)}, u32[]{:S(2)}) %collective-permute-start.13) | collective-permute-done | bytes 262176 | tf_op jit(solution)/shard_map/ppermute | solution.py:119
  18.8 0.0 collective-permute-start.15
  18.8 0.0 collective-permute-done.19.refs_8_
  18.8 0.0 collective-permute-start.20
  18.8 0.6 collective-permute-done.14.refs_3_
  19.4 1.8 %collective-permute-start.16 = (bf16[16,8192]{1,0:T(8,128)(2,1)S(1)}, bf16[16,8192]{1,0:T(8,128)(2,1)S(1)}, u32[]{:S(2)}, u32[]{:S(2)}) collective-permute-start(bf16[16,8192]{1,0:T(8,128)(2,1)S(1)} %collective-permute-done.14.refs_3_), channel_id=1, source_target_pairs={{0,4},{1,5},{4,8},{5,9},{8,12},{9,13},{12,14},{13,15},{14,10},{15,... | collective-permute-start | bytes 786440 | tf_op jit(solution)/shard_map/ppermute | solution.py:119
  21.2 3.1 %collective-permute-done.refs_1_ = bf16[16,8192]{1,0:T(8,128)(2,1)S(1)} collective-permute-done((bf16[16,8192]{1,0:T(8,128)(2,1)}, bf16[16,8192]{1,0:T(8,128)(2,1)S(1)}, u32[]{:S(2)}, u32[]{:S(2)}) %collective-permute-start) | collective-permute-done | bytes 262176 | tf_op jit(solution)/shard_map/ppermute | solution.py:119
  24.4 0.0 collective-permute-start.21
  24.4 0.0 collective-permute-done.3.refs_4_
  24.4 1.6 %collective-permute-start.2 = (bf16[16,8192]{1,0:T(8,128)(2,1)S(1)}, bf16[16,8192]{1,0:T(8,128)(2,1)S(1)}, u32[]{:S(2)}, u32[]{:S(2)}) collective-permute-start(bf16[16,8192]{1,0:T(8,128)(2,1)S(1)} %collective-permute-done.refs_1_), channel_id=1, source_target_pairs={{0,4},{1,5},{4,8},{5,9},{8,12},{9,13},{12,14},{13,15},{14,10},{15,... | collective-permute-start | bytes 786440 | tf_op jit(solution)/shard_map/ppermute | solution.py:119
  26.0 2.6 %collective-permute-done.15.refs_4_ = bf16[16,8192]{1,0:T(8,128)(2,1)S(1)} collective-permute-done((bf16[16,8192]{1,0:T(8,128)(2,1)S(1)}, bf16[16,8192]{1,0:T(8,128)(2,1)S(1)}, u32[]{:S(2)}, u32[]{:S(2)}) %collective-permute-start.15) | collective-permute-done | bytes 262176 | tf_op jit(solution)/shard_map/ppermute | solution.py:119
  28.5 0.3 collective-permute-start.5
  28.8 1.7 %collective-permute-start.17 = (bf16[16,8192]{1,0:T(8,128)(2,1)S(1)}, bf16[16,8192]{1,0:T(8,128)(2,1)S(1)}, u32[]{:S(2)}, u32[]{:S(2)}) collective-permute-start(bf16[16,8192]{1,0:T(8,128)(2,1)S(1)} %collective-permute-done.15.refs_4_), channel_id=1, source_target_pairs={{0,2},{1,3},{4,0},{5,1},{8,4},{9,5},{12,8},{13,9},{14,12},{15,13},... | collective-permute-start | bytes 786440 | tf_op jit(solution)/shard_map/ppermute | solution.py:119
  30.5 0.0 collective-permute-done.16.refs_5_
  30.5 0.7 collective-permute-start.18
  31.2 4.4 %collective-permute-done.2.refs_3_ = bf16[16,8192]{1,0:T(8,128)(2,1)S(1)} collective-permute-done((bf16[16,8192]{1,0:T(8,128)(2,1)S(1)}, bf16[16,8192]{1,0:T(8,128)(2,1)S(1)}, u32[]{:S(2)}, u32[]{:S(2)}) %collective-permute-start.2) | collective-permute-done | bytes 262176 | tf_op jit(solution)/shard_map/ppermute | solution.py:119
  35.6 0.0 collective-permute-start.23
  35.6 2.2 %collective-permute-done.5.refs_6_ = bf16[16,8192]{1,0:T(8,128)(2,1)S(1)} collective-permute-done((bf16[16,8192]{1,0:T(8,128)(2,1)S(1)}, bf16[16,8192]{1,0:T(8,128)(2,1)S(1)}, u32[]{:S(2)}, u32[]{:S(2)}) %collective-permute-start.5) | collective-permute-done | bytes 262176 | tf_op jit(solution)/shard_map/ppermute | solution.py:119
  37.8 0.0 collective-permute-start.24
  37.8 3.2 %collective-permute-done.17.refs_6_ = bf16[16,8192]{1,0:T(8,128)(2,1)S(1)} collective-permute-done((bf16[16,8192]{1,0:T(8,128)(2,1)S(1)}, bf16[16,8192]{1,0:T(8,128)(2,1)S(1)}, u32[]{:S(2)}, u32[]{:S(2)}) %collective-permute-start.17) | collective-permute-done | bytes 262176 | tf_op jit(solution)/shard_map/ppermute | solution.py:119
  41.0 0.0 collective-permute-start.25
  41.0 0.0 collective-permute-done.18.refs_7_
  41.0 0.5 collective-permute-start.26
  41.5 0.0 collective-permute-done.22.refs_11_
  41.5 0.1 collective-permute-start.7
  41.6 0.0 collective-permute-done.23.refs_12_
  41.6 0.4 collective-permute-start.8
  42.0 0.0 collective-permute-done.24.refs_13_
  42.0 0.1 collective-permute-start.9
  42.1 0.4 collective-permute-done.25.refs_14_
  42.5 1.6 %collective-permute-start.4 = (bf16[16,8192]{1,0:T(8,128)(2,1)S(1)}, bf16[16,8192]{1,0:T(8,128)(2,1)S(1)}, u32[]{:S(2)}, u32[]{:S(2)}) collective-permute-start(bf16[16,8192]{1,0:T(8,128)(2,1)S(1)} %collective-permute-done.2.refs_3_), channel_id=1, source_target_pairs={{0,4},{1,5},{4,8},{5,9},{8,12},{9,13},{12,14},{13,15},{14,10},{15,... | collective-permute-start | bytes 786440 | tf_op jit(solution)/shard_map/ppermute | solution.py:119
  44.1 0.4 collective-permute-start.6
  44.6 1.9 %copy-done = bf16[8192,192]{0,1:T(8,128)(2,1)S(1)} copy-done((bf16[8192,192]{0,1:T(8,128)(2,1)S(1)}, bf16[8192,192]{0,1:T(8,128)(2,1)}, u32[]{:S(2)}) %copy-start) | copy-done | bytes 3145752
  46.5 0.9 copy-done.3
  47.4 29.7 %shard_map.104 = (f32[1792,256]{1,0:T(8,128)S(1)}, f32[1792,256]{1,0:T(8,128)S(1)}, f32[128,256]{1,0:T(8,128)S(1)}) custom-call(bf16[16,8192]{1,0:T(8,128)(2,1)S(1)} %copy-done.3, bf16[16,8192]{1,0:T(8,128)(2,1)S(1)} %collective-permute-done.12.refs_1_, bf16[16,8192]{1,0:T(8,128)(2,1)S(1)} %collective-permute-done.13.refs_2_, ...), custom_call_target="tpu_custom_call" | custom-call | flops 15032385536 | bytes 58720256 | tf_op jit(solution)/shard_map/pallas_call | solution.py:200
  77.2 0.0 collective-permute-done.6.refs_7_
  77.2 0.1 collective-permute-start.10
  77.3 0.5 collective-permute-start.11
  77.8 0.0 collective-permute-done.7.refs_8_
  77.8 0.1 collective-permute-start.29
  77.8 0.0 collective-permute-done.8.refs_9_
  77.8 0.4 collective-permute-start.28
  78.3 0.0 collective-permute-done.9.refs_10_
  78.3 0.1 collective-permute-start.27
  78.4 0.4 collective-permute-done.10.refs_11_
  78.8 0.4 collective-permute-done.11.refs_12_
  79.1 0.4 collective-permute-done.29.refs_15_
  79.5 0.4 collective-permute-done.28.refs_14_
  79.9 0.4 collective-permute-done.27.refs_13_
  80.3 0.0 copy-start.2
  80.3 18.1 %shard_map.105 = f32[16,16,256]{2,1,0:T(8,128)S(1)} custom-call(bf16[16,8192]{1,0:T(8,128)(2,1)S(1)} %copy-done.4, bf16[16,8192]{1,0:T(8,128)(2,1)S(1)} %collective-permute-done.refs_1_, bf16[16,8192]{1,0:T(8,128)(2,1)S(1)} %collective-permute-done.1.refs_2_, bf16[16,8192]{1,0:T(8,128)(2,1)S(1)} %collective-permute-done.2.refs_3_, ...), custom_call_target="tpu_custom_call" | custom-call | flops 7516192768 | bytes 29360128 | tf_op jit(solution)/shard_map/pallas_call | solution.py:307
  98.4 14.7 %all_to_all.10.received = f32[16,16,256]{2,1,0:T(8,128)S(1)} all-to-all(f32[16,16,256]{2,1,0:T(8,128)S(1)} %shard_map.105), channel_id=1, replica_groups=mesh['groups'=2,'hid'=16,'mod'=1] {'hid'}, dimensions={0} | all-to-all | bytes 524288 | tf_op jit(solution)/shard_map/all_to_all | solution.py:401
  113.1 1.1 shard_map.106
  114.2 10.7 %all_to_all.11 = f32[16,8,256]{2,1,0:T(8,128)S(1)} all-to-all(f32[16,8,256]{2,1,0:T(8,128)S(1)} %get-tuple-element.19), channel_id=1, replica_groups=mesh['groups'=2,'hid'=16,'mod'=1] {'hid'}, dimensions={0} | all-to-all | bytes 262144 | tf_op jit(solution)/shard_map/all_to_all | solution.py:403
  124.9 0.6 reduce_sum.9
  (14 shorter events, 0.0 us)
Async XLA Ops:
  0.6 9.5 %collective-permute-start.12 = (bf16[16,8192]{1,0:T(8,128)(2,1)}, bf16[16,8192]{1,0:T(8,128)(2,1)S(1)}, u32[]{:S(2)}, u32[]{:S(2)}) collective-permute-start(bf16[16,8192]{1,0:T(8,128)(2,1)} %refs_0_.1), channel_id=1, source_target_pairs={{0,4},{1,5},{4,8},{5,9},{8,12},{9,13},{12,14},{13,15},{14,10},{15,... | collective-permute-start | bytes 786440 | tf_op jit(solution)/shard_map/ppermute | solution.py:119
  3.7 9.8 %collective-permute-start.1 = (bf16[16,8192]{1,0:T(8,128)(2,1)}, bf16[16,8192]{1,0:T(8,128)(2,1)S(1)}, u32[]{:S(2)}, u32[]{:S(2)}) collective-permute-start(bf16[16,8192]{1,0:T(8,128)(2,1)} %refs_0_.2), channel_id=1, source_target_pairs={{0,2},{1,3},{4,0},{5,1},{8,4},{9,5},{12,8},{13,9},{14,12},{15,13},... | collective-permute-start | bytes 786440 | tf_op jit(solution)/shard_map/ppermute | solution.py:119
  3.7 15.1 %collective-permute-start.13 = (bf16[16,8192]{1,0:T(8,128)(2,1)}, bf16[16,8192]{1,0:T(8,128)(2,1)S(1)}, u32[]{:S(2)}, u32[]{:S(2)}) collective-permute-start(bf16[16,8192]{1,0:T(8,128)(2,1)} %refs_0_.1), channel_id=1, source_target_pairs={{0,2},{1,3},{4,0},{5,1},{8,4},{9,5},{12,8},{13,9},{14,12},{15,13},... | collective-permute-start | bytes 786440 | tf_op jit(solution)/shard_map/ppermute | solution.py:119
  5.6 13.1 %collective-permute-start.19 = (bf16[16,8192]{1,0:T(8,128)(2,1)}, bf16[16,8192]{1,0:T(8,128)(2,1)S(1)}, u32[]{:S(2)}, u32[]{:S(2)}) collective-permute-start(bf16[16,8192]{1,0:T(8,128)(2,1)} %refs_0_.1), channel_id=1, source_target_pairs={{0,1},{1,0},{2,3},{3,2},{4,5},{5,4},{6,7},{7,6},{8,9},{9,8},{10,11... | collective-permute-start | bytes 786440 | tf_op jit(solution)/shard_map/ppermute | solution.py:123
  10.1 9.2 %collective-permute-start.14 = (bf16[16,8192]{1,0:T(8,128)(2,1)S(1)}, bf16[16,8192]{1,0:T(8,128)(2,1)S(1)}, u32[]{:S(2)}, u32[]{:S(2)}) collective-permute-start(bf16[16,8192]{1,0:T(8,128)(2,1)S(1)} %collective-permute-done.12.refs_1_), channel_id=1, source_target_pairs={{0,4},{1,5},{4,8},{5,9},{8,12},{9,13},{12,14},{13,15},{14,10},{15,... | collective-permute-start | bytes 786440 | tf_op jit(solution)/shard_map/ppermute | solution.py:119
  12.0 12.4 %collective-permute-start = (bf16[16,8192]{1,0:T(8,128)(2,1)}, bf16[16,8192]{1,0:T(8,128)(2,1)S(1)}, u32[]{:S(2)}, u32[]{:S(2)}) collective-permute-start(bf16[16,8192]{1,0:T(8,128)(2,1)} %refs_0_.2), channel_id=1, source_target_pairs={{0,4},{1,5},{4,8},{5,9},{8,12},{9,13},{12,14},{13,15},{14,10},{15,... | collective-permute-start | bytes 786440 | tf_op jit(solution)/shard_map/ppermute | solution.py:119
  13.5 10.8 %collective-permute-start.3 = (bf16[16,8192]{1,0:T(8,128)(2,1)S(1)}, bf16[16,8192]{1,0:T(8,128)(2,1)S(1)}, u32[]{:S(2)}, u32[]{:S(2)}) collective-permute-start(bf16[16,8192]{1,0:T(8,128)(2,1)S(1)} %collective-permute-done.1.refs_2_), channel_id=1, source_target_pairs={{0,2},{1,3},{4,0},{5,1},{8,4},{9,5},{12,8},{13,9},{14,12},{15,13},... | collective-permute-start | bytes 786440 | tf_op jit(solution)/shard_map/ppermute | solution.py:119
  18.8 9.8 %collective-permute-start.15 = (bf16[16,8192]{1,0:T(8,128)(2,1)S(1)}, bf16[16,8192]{1,0:T(8,128)(2,1)S(1)}, u32[]{:S(2)}, u32[]{:S(2)}) collective-permute-start(bf16[16,8192]{1,0:T(8,128)(2,1)S(1)} %collective-permute-done.13.refs_2_), channel_id=1, source_target_pairs={{0,2},{1,3},{4,0},{5,1},{8,4},{9,5},{12,8},{13,9},{14,12},{15,13},... | collective-permute-start | bytes 786440 | tf_op jit(solution)/shard_map/ppermute | solution.py:119
  18.8 10.1 %collective-permute-start.20 = (bf16[16,8192]{1,0:T(8,128)(2,1)S(1)}, bf16[16,8192]{1,0:T(8,128)(2,1)S(1)}, u32[]{:S(2)}, u32[]{:S(2)}) collective-permute-start(bf16[16,8192]{1,0:T(8,128)(2,1)S(1)} %collective-permute-done.12.refs_1_), channel_id=1, source_target_pairs={{0,1},{1,0},{2,3},{3,2},{4,5},{5,4},{6,7},{7,6},{8,9},{9,8},{10,11... | collective-permute-start | bytes 786440 | tf_op jit(solution)/shard_map/ppermute | solution.py:123
  19.4 11.1 %collective-permute-start.16 = (bf16[16,8192]{1,0:T(8,128)(2,1)S(1)}, bf16[16,8192]{1,0:T(8,128)(2,1)S(1)}, u32[]{:S(2)}, u32[]{:S(2)}) collective-permute-start(bf16[16,8192]{1,0:T(8,128)(2,1)S(1)} %collective-permute-done.14.refs_3_), channel_id=1, source_target_pairs={{0,4},{1,5},{4,8},{5,9},{8,12},{9,13},{12,14},{13,15},{14,10},{15,... | collective-permute-start | bytes 786440 | tf_op jit(solution)/shard_map/ppermute | solution.py:119
  24.4 6.8 %collective-permute-start.21 = (bf16[16,8192]{1,0:T(8,128)(2,1)S(1)}, bf16[16,8192]{1,0:T(8,128)(2,1)S(1)}, u32[]{:S(2)}, u32[]{:S(2)}) collective-permute-start(bf16[16,8192]{1,0:T(8,128)(2,1)S(1)} %collective-permute-done.13.refs_2_), channel_id=1, source_target_pairs={{0,1},{1,0},{2,3},{3,2},{4,5},{5,4},{6,7},{7,6},{8,9},{9,8},{10,11... | collective-permute-start | bytes 786440 | tf_op jit(solution)/shard_map/ppermute | solution.py:123
  24.4 11.2 %collective-permute-start.2 = (bf16[16,8192]{1,0:T(8,128)(2,1)S(1)}, bf16[16,8192]{1,0:T(8,128)(2,1)S(1)}, u32[]{:S(2)}, u32[]{:S(2)}) collective-permute-start(bf16[16,8192]{1,0:T(8,128)(2,1)S(1)} %collective-permute-done.refs_1_), channel_id=1, source_target_pairs={{0,4},{1,5},{4,8},{5,9},{8,12},{9,13},{12,14},{13,15},{14,10},{15,... | collective-permute-start | bytes 786440 | tf_op jit(solution)/shard_map/ppermute | solution.py:119
  28.5 9.2 %collective-permute-start.5 = (bf16[16,8192]{1,0:T(8,128)(2,1)S(1)}, bf16[16,8192]{1,0:T(8,128)(2,1)S(1)}, u32[]{:S(2)}, u32[]{:S(2)}) collective-permute-start(bf16[16,8192]{1,0:T(8,128)(2,1)S(1)} %collective-permute-done.3.refs_4_), channel_id=1, source_target_pairs={{0,2},{1,3},{4,0},{5,1},{8,4},{9,5},{12,8},{13,9},{14,12},{15,13},... | collective-permute-start | bytes 786440 | tf_op jit(solution)/shard_map/ppermute | solution.py:119
  28.8 12.2 %collective-permute-start.17 = (bf16[16,8192]{1,0:T(8,128)(2,1)S(1)}, bf16[16,8192]{1,0:T(8,128)(2,1)S(1)}, u32[]{:S(2)}, u32[]{:S(2)}) collective-permute-start(bf16[16,8192]{1,0:T(8,128)(2,1)S(1)} %collective-permute-done.15.refs_4_), channel_id=1, source_target_pairs={{0,2},{1,3},{4,0},{5,1},{8,4},{9,5},{12,8},{13,9},{14,12},{15,13},... | collective-permute-start | bytes 786440 | tf_op jit(solution)/shard_map/ppermute | solution.py:119
  30.5 10.5 %collective-permute-start.18 = (bf16[16,8192]{1,0:T(8,128)(2,1)S(1)}, bf16[16,8192]{1,0:T(8,128)(2,1)S(1)}, u32[]{:S(2)}, u32[]{:S(2)}) collective-permute-start(bf16[16,8192]{1,0:T(8,128)(2,1)S(1)} %collective-permute-done.16.refs_5_), channel_id=1, source_target_pairs={{0,4},{1,5},{4,8},{5,9},{8,12},{9,13},{12,14},{13,15},{14,10},{15,... | collective-permute-start | bytes 786440 | tf_op jit(solution)/shard_map/ppermute | solution.py:119
  31.2 10.4 %collective-permute-start.22 = (bf16[16,8192]{1,0:T(8,128)(2,1)S(1)}, bf16[16,8192]{1,0:T(8,128)(2,1)S(1)}, u32[]{:S(2)}, u32[]{:S(2)}) collective-permute-start(bf16[16,8192]{1,0:T(8,128)(2,1)S(1)} %collective-permute-done.14.refs_3_), channel_id=1, source_target_pairs={{0,1},{1,0},{2,3},{3,2},{4,5},{5,4},{6,7},{7,6},{8,9},{9,8},{10,11... | collective-permute-start | bytes 786440 | tf_op jit(solution)/shard_map/ppermute | solution.py:123
  35.6 6.0 %collective-permute-start.23 = (bf16[16,8192]{1,0:T(8,128)(2,1)S(1)}, bf16[16,8192]{1,0:T(8,128)(2,1)S(1)}, u32[]{:S(2)}, u32[]{:S(2)}) collective-permute-start(bf16[16,8192]{1,0:T(8,128)(2,1)S(1)} %collective-permute-done.15.refs_4_), channel_id=1, source_target_pairs={{0,1},{1,0},{2,3},{3,2},{4,5},{5,4},{6,7},{7,6},{8,9},{9,8},{10,11... | collective-permute-start | bytes 786440 | tf_op jit(solution)/shard_map/ppermute | solution.py:123
  37.8 4.3 %collective-permute-start.24 = (bf16[16,8192]{1,0:T(8,128)(2,1)S(1)}, bf16[16,8192]{1,0:T(8,128)(2,1)S(1)}, u32[]{:S(2)}, u32[]{:S(2)}) collective-permute-start(bf16[16,8192]{1,0:T(8,128)(2,1)S(1)} %collective-permute-done.16.refs_5_), channel_id=1, source_target_pairs={{0,1},{1,0},{2,3},{3,2},{4,5},{5,4},{6,7},{7,6},{8,9},{9,8},{10,11... | collective-permute-start | bytes 786440 | tf_op jit(solution)/shard_map/ppermute | solution.py:123
  41.0 1.5 %collective-permute-start.25 = (bf16[16,8192]{1,0:T(8,128)(2,1)S(1)}, bf16[16,8192]{1,0:T(8,128)(2,1)S(1)}, u32[]{:S(2)}, u32[]{:S(2)}) collective-permute-start(bf16[16,8192]{1,0:T(8,128)(2,1)S(1)} %collective-permute-done.17.refs_6_), channel_id=1, source_target_pairs={{0,1},{1,0},{2,3},{3,2},{4,5},{5,4},{6,7},{7,6},{8,9},{9,8},{10,11... | collective-permute-start | bytes 786440 | tf_op jit(solution)/shard_map/ppermute | solution.py:123
  41.0 3.1 %collective-permute-start.26 = (bf16[16,8192]{1,0:T(8,128)(2,1)S(1)}, bf16[16,8192]{1,0:T(8,128)(2,1)S(1)}, u32[]{:S(2)}, u32[]{:S(2)}) collective-permute-start(bf16[16,8192]{1,0:T(8,128)(2,1)S(1)} %collective-permute-done.18.refs_7_), channel_id=1, source_target_pairs={{0,1},{1,0},{2,3},{3,2},{4,5},{5,4},{6,7},{7,6},{8,9},{9,8},{10,11... | collective-permute-start | bytes 786440 | tf_op jit(solution)/shard_map/ppermute | solution.py:123
  41.5 36.2 %collective-permute-start.7 = (bf16[16,8192]{1,0:T(8,128)(2,1)}, bf16[16,8192]{1,0:T(8,128)(2,1)S(1)}, u32[]{:S(2)}, u32[]{:S(2)}) collective-permute-start(bf16[16,8192]{1,0:T(8,128)(2,1)} %refs_0_.2), channel_id=1, source_target_pairs={{0,1},{1,0},{2,3},{3,2},{4,5},{5,4},{6,7},{7,6},{8,9},{9,8},{10,11... | collective-permute-start | bytes 786440 | tf_op jit(solution)/shard_map/ppermute | solution.py:123
  41.6 36.2 %collective-permute-start.8 = (bf16[16,8192]{1,0:T(8,128)(2,1)S(1)}, bf16[16,8192]{1,0:T(8,128)(2,1)S(1)}, u32[]{:S(2)}, u32[]{:S(2)}) collective-permute-start(bf16[16,8192]{1,0:T(8,128)(2,1)S(1)} %collective-permute-done.refs_1_), channel_id=1, source_target_pairs={{0,1},{1,0},{2,3},{3,2},{4,5},{5,4},{6,7},{7,6},{8,9},{9,8},{10,11... | collective-permute-start | bytes 786440 | tf_op jit(solution)/shard_map/ppermute | solution.py:123
  42.0 36.2 %collective-permute-start.9 = (bf16[16,8192]{1,0:T(8,128)(2,1)S(1)}, bf16[16,8192]{1,0:T(8,128)(2,1)S(1)}, u32[]{:S(2)}, u32[]{:S(2)}) collective-permute-start(bf16[16,8192]{1,0:T(8,128)(2,1)S(1)} %collective-permute-done.1.refs_2_), channel_id=1, source_target_pairs={{0,1},{1,0},{2,3},{3,2},{4,5},{5,4},{6,7},{7,6},{8,9},{9,8},{10,11... | collective-permute-start | bytes 786440 | tf_op jit(solution)/shard_map/ppermute | solution.py:123
  42.5 34.7 %collective-permute-start.4 = (bf16[16,8192]{1,0:T(8,128)(2,1)S(1)}, bf16[16,8192]{1,0:T(8,128)(2,1)S(1)}, u32[]{:S(2)}, u32[]{:S(2)}) collective-permute-start(bf16[16,8192]{1,0:T(8,128)(2,1)S(1)} %collective-permute-done.2.refs_3_), channel_id=1, source_target_pairs={{0,4},{1,5},{4,8},{5,9},{8,12},{9,13},{12,14},{13,15},{14,10},{15,... | collective-permute-start | bytes 786440 | tf_op jit(solution)/shard_map/ppermute | solution.py:119
  44.1 33.0 %collective-permute-start.6 = (bf16[16,8192]{1,0:T(8,128)(2,1)S(1)}, bf16[16,8192]{1,0:T(8,128)(2,1)S(1)}, u32[]{:S(2)}, u32[]{:S(2)}) collective-permute-start(bf16[16,8192]{1,0:T(8,128)(2,1)S(1)} %collective-permute-done.5.refs_6_), channel_id=1, source_target_pairs={{0,2},{1,3},{4,0},{5,1},{8,4},{9,5},{12,8},{13,9},{14,12},{15,13},... | collective-permute-start | bytes 786440 | tf_op jit(solution)/shard_map/ppermute | solution.py:119
  44.6 1.9 %copy-start = (bf16[8192,192]{0,1:T(8,128)(2,1)S(1)}, bf16[8192,192]{0,1:T(8,128)(2,1)}, u32[]{:S(2)}) copy-start(bf16[8192,192]{0,1:T(8,128)(2,1)} %param.14) | copy-start | bytes 9437188
  46.5 0.9 copy-start.3
  47.4 32.9 %copy-start.1 = (bf16[1792,192]{0,1:T(8,128)(2,1)S(1)}, bf16[1792,192]{0,1:T(8,128)(2,1)}, u32[]{:S(2)}) copy-start(bf16[1792,192]{0,1:T(8,128)(2,1)} %param.15) | copy-start | bytes 2064388
  47.4 32.9 %copy-start.4 = (bf16[16,8192]{1,0:T(8,128)(2,1)S(1)}, bf16[16,8192]{1,0:T(8,128)(2,1)}, u32[]{:S(2)}) copy-start(bf16[16,8192]{1,0:T(8,128)(2,1)} %refs_0_.2) | copy-start | bytes 786436
  47.4 32.9 %copy-start.5 = (s32[256]{0:T(256)S(1)}, s32[256]{0:T(256)}, u32[]{:S(2)}) copy-start(s32[256]{0:T(256)} %param.16) | copy-start | bytes 3076
  77.2 1.6 %collective-permute-start.10 = (bf16[16,8192]{1,0:T(8,128)(2,1)S(1)}, bf16[16,8192]{1,0:T(8,128)(2,1)S(1)}, u32[]{:S(2)}, u32[]{:S(2)}) collective-permute-start(bf16[16,8192]{1,0:T(8,128)(2,1)S(1)} %collective-permute-done.2.refs_3_), channel_id=1, source_target_pairs={{0,1},{1,0},{2,3},{3,2},{4,5},{5,4},{6,7},{7,6},{8,9},{9,8},{10,11... | collective-permute-start | bytes 786440 | tf_op jit(solution)/shard_map/ppermute | solution.py:123
  77.3 1.9 %collective-permute-start.11 = (bf16[16,8192]{1,0:T(8,128)(2,1)S(1)}, bf16[16,8192]{1,0:T(8,128)(2,1)S(1)}, u32[]{:S(2)}, u32[]{:S(2)}) collective-permute-start(bf16[16,8192]{1,0:T(8,128)(2,1)S(1)} %collective-permute-done.3.refs_4_), channel_id=1, source_target_pairs={{0,1},{1,0},{2,3},{3,2},{4,5},{5,4},{6,7},{7,6},{8,9},{9,8},{10,11... | collective-permute-start | bytes 786440 | tf_op jit(solution)/shard_map/ppermute | solution.py:123
  77.8 1.8 %collective-permute-start.29 = (bf16[16,8192]{1,0:T(8,128)(2,1)S(1)}, bf16[16,8192]{1,0:T(8,128)(2,1)S(1)}, u32[]{:S(2)}, u32[]{:S(2)}) collective-permute-start(bf16[16,8192]{1,0:T(8,128)(2,1)S(1)} %collective-permute-done.6.refs_7_), channel_id=1, source_target_pairs={{0,1},{1,0},{2,3},{3,2},{4,5},{5,4},{6,7},{7,6},{8,9},{9,8},{10,11... | collective-permute-start | bytes 786440 | tf_op jit(solution)/shard_map/ppermute | solution.py:123
  77.8 2.1 %collective-permute-start.28 = (bf16[16,8192]{1,0:T(8,128)(2,1)S(1)}, bf16[16,8192]{1,0:T(8,128)(2,1)S(1)}, u32[]{:S(2)}, u32[]{:S(2)}) collective-permute-start(bf16[16,8192]{1,0:T(8,128)(2,1)S(1)} %collective-permute-done.5.refs_6_), channel_id=1, source_target_pairs={{0,1},{1,0},{2,3},{3,2},{4,5},{5,4},{6,7},{7,6},{8,9},{9,8},{10,11... | collective-permute-start | bytes 786440 | tf_op jit(solution)/shard_map/ppermute | solution.py:123
  78.3 2.0 %collective-permute-start.27 = (bf16[16,8192]{1,0:T(8,128)(2,1)S(1)}, bf16[16,8192]{1,0:T(8,128)(2,1)S(1)}, u32[]{:S(2)}, u32[]{:S(2)}) collective-permute-start(bf16[16,8192]{1,0:T(8,128)(2,1)S(1)} %collective-permute-done.4.refs_5_), channel_id=1, source_target_pairs={{0,1},{1,0},{2,3},{3,2},{4,5},{5,4},{6,7},{7,6},{8,9},{9,8},{10,11... | collective-permute-start | bytes 786440 | tf_op jit(solution)/shard_map/ppermute | solution.py:123
  80.3 32.8 %copy-start.2 = (bf16[256,768]{1,0:T(8,128)(2,1)S(1)}, bf16[256,768]{1,0:T(8,128)(2,1)}, u32[]{:S(2)}) copy-start(bf16[256,768]{1,0:T(8,128)(2,1)} %tests.1) | copy-start | bytes 1179652

commit v9 on v7

--- a/solution.py
+++ b/solution.py
@@ -320,7 +320,7 @@
             pltpu.VMEM((3 * R, rows), jnp.float32),
             pltpu.SemaphoreType.DMA((len(blocks),)),
         ],
-        compiler_params=pltpu.CompilerParams(vmem_limit_bytes=32 * MEBI),
+        compiler_params=pltpu.CompilerParams(vmem_limit_bytes=44 * MEBI),
         cost_estimate=pl.CostEstimate(
             flops=2 * rows * depth * width, bytes_accessed=2 * depth * width, transcendentals=0
         ),
@@ -386,7 +386,7 @@
     late = [core_swap(after(block, gate), chips) for block in grad_blocks[-3:]]
     grad_blocks = grad_blocks + early + late
     send = backward(
-        places, chips, grad_blocks, down_weight, [gate], [up], proj_d.T, proj_ff.T, ids, 1024, TILE
+        places, chips, grad_blocks, down_weight, [gate], [up], proj_d.T, proj_ff.T, ids, 2048, TILE
     )
     received = lax.all_to_all(send, "hid", 0, 0)
     features, partial = finish(received, inputs, ids, test_features)

time: 126 us -> 124 us (0.984)
  no operation moved by 1% of the time
where the time goes in v9:
time: 124 us
  Pallas kernels  47.5 us (38%)
  waiting for transfers between devices  27.8 us (22%)
  blocking collectives  25.4 us (20%)
  starting transfers between devices  19.2 us (15%)
  local copies, waits for them, and re-layouts  2.86 us (2%)
    pallas_call x1, Pallas kernels, forward(): pl.pallas_call(functools.partial(forward_kernel, places, chips), grid=(wi...  29.7 us
    ppermute x14, waiting for transfers between devices, ring_step(): return lax.ppermute(block, 'hid', pairs)  25.5 us
    ppermute x14, starting transfers between devices, ring_step(): return lax.ppermute(block, 'hid', pairs)  16.9 us
    pallas_call x1, Pallas kernels, backward(): pl.pallas_call(functools.partial(backward_kernel, places, chips, examples...  16.7 us
    all_to_all x1, blocking collectives, local_ring(): received = lax.all_to_all(send, 'hid', 0, 0)  14.7 us
    all_to_all x1, blocking collectives, local_ring(): scores = jnp.sum(lax.all_to_all(partial, 'hid', 0, 0), axis=0)  10.7 us
    unnamed x12, local copies, waits for them, and re-layouts  2.86 us
  transfers between devices with their start and end apart: 30, of which 14 were waited for; matrix products, arithmetic and copies ran while one was open for 0% of the time, Pallas kernels for 24%

profile of v9, /device:TPU:0, one launch (start us, length us, event | category | flops | bytes accessed | tf_op | source)
XLA Modules:
  0.0 124.1 jit_solution(3666095361793132626)
XLA Ops:
  0.6 3.1 %collective-permute-start.12 = (bf16[16,8192]{1,0:T(8,128)(2,1)}, bf16[16,8192]{1,0:T(8,128)(2,1)S(1)}, u32[]{:S(2)}, u32[]{:S(2)}) collective-permute-start(bf16[16,8192]{1,0:T(8,128)(2,1)} %refs_0_.1), channel_id=1, source_target_pairs={{0,4},{1,5},{4,8},{5,9},{8,12},{9,13},{12,14},{13,15},{14,10},{15,... | collective-permute-start | bytes 786440 | tf_op jit(solution)/shard_map/ppermute | solution.py:119
  3.7 0.0 collective-permute-start.1
  3.7 1.9 %collective-permute-start.13 = (bf16[16,8192]{1,0:T(8,128)(2,1)}, bf16[16,8192]{1,0:T(8,128)(2,1)S(1)}, u32[]{:S(2)}, u32[]{:S(2)}) collective-permute-start(bf16[16,8192]{1,0:T(8,128)(2,1)} %refs_0_.1), channel_id=1, source_target_pairs={{0,2},{1,3},{4,0},{5,1},{8,4},{9,5},{12,8},{13,9},{14,12},{15,13},... | collective-permute-start | bytes 786440 | tf_op jit(solution)/shard_map/ppermute | solution.py:119
  5.6 0.0 collective-permute-start.19
  5.7 4.5 %collective-permute-done.12.refs_1_ = bf16[16,8192]{1,0:T(8,128)(2,1)S(1)} collective-permute-done((bf16[16,8192]{1,0:T(8,128)(2,1)}, bf16[16,8192]{1,0:T(8,128)(2,1)S(1)}, u32[]{:S(2)}, u32[]{:S(2)}) %collective-permute-start.12) | collective-permute-done | bytes 262176 | tf_op jit(solution)/shard_map/ppermute | solution.py:119
  10.1 1.8 %collective-permute-start.14 = (bf16[16,8192]{1,0:T(8,128)(2,1)S(1)}, bf16[16,8192]{1,0:T(8,128)(2,1)S(1)}, u32[]{:S(2)}, u32[]{:S(2)}) collective-permute-start(bf16[16,8192]{1,0:T(8,128)(2,1)S(1)} %collective-permute-done.12.refs_1_), channel_id=1, source_target_pairs={{0,4},{1,5},{4,8},{5,9},{8,12},{9,13},{12,14},{13,15},{14,10},{15,... | collective-permute-start | bytes 786440 | tf_op jit(solution)/shard_map/ppermute | solution.py:119
  12.0 1.6 %collective-permute-start = (bf16[16,8192]{1,0:T(8,128)(2,1)}, bf16[16,8192]{1,0:T(8,128)(2,1)S(1)}, u32[]{:S(2)}, u32[]{:S(2)}) collective-permute-start(bf16[16,8192]{1,0:T(8,128)(2,1)} %refs_0_.2), channel_id=1, source_target_pairs={{0,4},{1,5},{4,8},{5,9},{8,12},{9,13},{12,14},{13,15},{14,10},{15,... | collective-permute-start | bytes 786440 | tf_op jit(solution)/shard_map/ppermute | solution.py:119
  13.5 0.0 collective-permute-done.1.refs_2_
  13.5 0.4 collective-permute-start.3
  14.0 4.8 %collective-permute-done.13.refs_2_ = bf16[16,8192]{1,0:T(8,128)(2,1)S(1)} collective-permute-done((bf16[16,8192]{1,0:T(8,128)(2,1)}, bf16[16,8192]{1,0:T(8,128)(2,1)S(1)}, u32[]{:S(2)}, u32[]{:S(2)}) %collective-permute-start.13) | collective-permute-done | bytes 262176 | tf_op jit(solution)/shard_map/ppermute | solution.py:119
  18.8 0.0 collective-permute-start.15
  18.8 0.0 collective-permute-done.19.refs_8_
  18.8 0.0 collective-permute-start.20
  18.8 0.6 collective-permute-done.14.refs_3_
  19.4 1.8 %collective-permute-start.16 = (bf16[16,8192]{1,0:T(8,128)(2,1)S(1)}, bf16[16,8192]{1,0:T(8,128)(2,1)S(1)}, u32[]{:S(2)}, u32[]{:S(2)}) collective-permute-start(bf16[16,8192]{1,0:T(8,128)(2,1)S(1)} %collective-permute-done.14.refs_3_), channel_id=1, source_target_pairs={{0,4},{1,5},{4,8},{5,9},{8,12},{9,13},{12,14},{13,15},{14,10},{15,... | collective-permute-start | bytes 786440 | tf_op jit(solution)/shard_map/ppermute | solution.py:119
  21.2 3.1 %collective-permute-done.refs_1_ = bf16[16,8192]{1,0:T(8,128)(2,1)S(1)} collective-permute-done((bf16[16,8192]{1,0:T(8,128)(2,1)}, bf16[16,8192]{1,0:T(8,128)(2,1)S(1)}, u32[]{:S(2)}, u32[]{:S(2)}) %collective-permute-start) | collective-permute-done | bytes 262176 | tf_op jit(solution)/shard_map/ppermute | solution.py:119
  24.4 0.0 collective-permute-start.21
  24.4 0.0 collective-permute-done.3.refs_4_
  24.4 1.6 %collective-permute-start.2 = (bf16[16,8192]{1,0:T(8,128)(2,1)S(1)}, bf16[16,8192]{1,0:T(8,128)(2,1)S(1)}, u32[]{:S(2)}, u32[]{:S(2)}) collective-permute-start(bf16[16,8192]{1,0:T(8,128)(2,1)S(1)} %collective-permute-done.refs_1_), channel_id=1, source_target_pairs={{0,4},{1,5},{4,8},{5,9},{8,12},{9,13},{12,14},{13,15},{14,10},{15,... | collective-permute-start | bytes 786440 | tf_op jit(solution)/shard_map/ppermute | solution.py:119
  26.0 2.6 %collective-permute-done.15.refs_4_ = bf16[16,8192]{1,0:T(8,128)(2,1)S(1)} collective-permute-done((bf16[16,8192]{1,0:T(8,128)(2,1)S(1)}, bf16[16,8192]{1,0:T(8,128)(2,1)S(1)}, u32[]{:S(2)}, u32[]{:S(2)}) %collective-permute-start.15) | collective-permute-done | bytes 262176 | tf_op jit(solution)/shard_map/ppermute | solution.py:119
  28.5 0.3 collective-permute-start.5
  28.8 1.7 %collective-permute-start.17 = (bf16[16,8192]{1,0:T(8,128)(2,1)S(1)}, bf16[16,8192]{1,0:T(8,128)(2,1)S(1)}, u32[]{:S(2)}, u32[]{:S(2)}) collective-permute-start(bf16[16,8192]{1,0:T(8,128)(2,1)S(1)} %collective-permute-done.15.refs_4_), channel_id=1, source_target_pairs={{0,2},{1,3},{4,0},{5,1},{8,4},{9,5},{12,8},{13,9},{14,12},{15,13},... | collective-permute-start | bytes 786440 | tf_op jit(solution)/shard_map/ppermute | solution.py:119
  30.5 0.0 collective-permute-done.16.refs_5_
  30.5 0.7 collective-permute-start.18
  31.2 4.4 %collective-permute-done.2.refs_3_ = bf16[16,8192]{1,0:T(8,128)(2,1)S(1)} collective-permute-done((bf16[16,8192]{1,0:T(8,128)(2,1)S(1)}, bf16[16,8192]{1,0:T(8,128)(2,1)S(1)}, u32[]{:S(2)}, u32[]{:S(2)}) %collective-permute-start.2) | collective-permute-done | bytes 262176 | tf_op jit(solution)/shard_map/ppermute | solution.py:119
  35.6 0.0 collective-permute-start.23
  35.6 2.2 %collective-permute-done.5.refs_6_ = bf16[16,8192]{1,0:T(8,128)(2,1)S(1)} collective-permute-done((bf16[16,8192]{1,0:T(8,128)(2,1)S(1)}, bf16[16,8192]{1,0:T(8,128)(2,1)S(1)}, u32[]{:S(2)}, u32[]{:S(2)}) %collective-permute-start.5) | collective-permute-done | bytes 262176 | tf_op jit(solution)/shard_map/ppermute | solution.py:119
  37.8 0.0 collective-permute-start.24
  37.8 3.2 %collective-permute-done.17.refs_6_ = bf16[16,8192]{1,0:T(8,128)(2,1)S(1)} collective-permute-done((bf16[16,8192]{1,0:T(8,128)(2,1)S(1)}, bf16[16,8192]{1,0:T(8,128)(2,1)S(1)}, u32[]{:S(2)}, u32[]{:S(2)}) %collective-permute-start.17) | collective-permute-done | bytes 262176 | tf_op jit(solution)/shard_map/ppermute | solution.py:119
  41.0 0.0 collective-permute-start.25
  41.0 0.0 collective-permute-done.18.refs_7_
  41.0 0.5 collective-permute-start.26
  41.5 0.0 collective-permute-done.22.refs_11_
  41.5 0.1 collective-permute-start.7
  41.6 0.0 collective-permute-done.23.refs_12_
  41.6 0.4 collective-permute-start.8
  42.0 0.0 collective-permute-done.24.refs_13_
  42.0 0.1 collective-permute-start.9
  42.1 0.4 collective-permute-done.25.refs_14_
  42.5 1.6 %collective-permute-start.4 = (bf16[16,8192]{1,0:T(8,128)(2,1)S(1)}, bf16[16,8192]{1,0:T(8,128)(2,1)S(1)}, u32[]{:S(2)}, u32[]{:S(2)}) collective-permute-start(bf16[16,8192]{1,0:T(8,128)(2,1)S(1)} %collective-permute-done.2.refs_3_), channel_id=1, source_target_pairs={{0,4},{1,5},{4,8},{5,9},{8,12},{9,13},{12,14},{13,15},{14,10},{15,... | collective-permute-start | bytes 786440 | tf_op jit(solution)/shard_map/ppermute | solution.py:119
  44.1 0.4 collective-permute-start.6
  44.6 1.9 %copy-done = bf16[8192,192]{0,1:T(8,128)(2,1)S(1)} copy-done((bf16[8192,192]{0,1:T(8,128)(2,1)S(1)}, bf16[8192,192]{0,1:T(8,128)(2,1)}, u32[]{:S(2)}) %copy-start) | copy-done | bytes 3145752
  46.5 0.9 copy-done.3
  47.4 29.7 %shard_map.104 = (f32[1792,256]{1,0:T(8,128)S(1)}, f32[1792,256]{1,0:T(8,128)S(1)}, f32[128,256]{1,0:T(8,128)S(1)}) custom-call(bf16[16,8192]{1,0:T(8,128)(2,1)S(1)} %copy-done.3, bf16[16,8192]{1,0:T(8,128)(2,1)S(1)} %collective-permute-done.12.refs_1_, bf16[16,8192]{1,0:T(8,128)(2,1)S(1)} %collective-permute-done.13.refs_2_, ...), custom_call_target="tpu_custom_call" | custom-call | flops 15032385536 | bytes 58720256 | tf_op jit(solution)/shard_map/pallas_call | solution.py:200
  77.1 0.0 collective-permute-done.6.refs_7_
  77.1 0.1 collective-permute-start.10
  77.2 0.5 collective-permute-start.11
  77.7 0.0 collective-permute-done.7.refs_8_
  77.7 0.1 collective-permute-start.29
  77.8 0.0 collective-permute-done.8.refs_9_
  77.8 0.4 collective-permute-start.28
  78.2 0.0 collective-permute-done.9.refs_10_
  78.2 0.1 collective-permute-start.27
  78.3 0.4 collective-permute-done.10.refs_11_
  78.7 0.4 collective-permute-done.11.refs_12_
  79.1 0.4 collective-permute-done.29.refs_15_
  79.5 0.4 collective-permute-done.28.refs_14_
  79.8 0.4 collective-permute-done.27.refs_13_
  80.2 0.0 copy-start.2
  80.2 16.7 %shard_map.105 = f32[16,16,256]{2,1,0:T(8,128)S(1)} custom-call(bf16[16,8192]{1,0:T(8,128)(2,1)S(1)} %copy-done.4, bf16[16,8192]{1,0:T(8,128)(2,1)S(1)} %collective-permute-done.refs_1_, bf16[16,8192]{1,0:T(8,128)(2,1)S(1)} %collective-permute-done.1.refs_2_, bf16[16,8192]{1,0:T(8,128)(2,1)S(1)} %collective-permute-done.2.refs_3_, ...), custom_call_target="tpu_custom_call" | custom-call | flops 7516192768 | bytes 29360128 | tf_op jit(solution)/shard_map/pallas_call | solution.py:300
  97.0 14.7 %all_to_all.10.received = f32[16,16,256]{2,1,0:T(8,128)S(1)} all-to-all(f32[16,16,256]{2,1,0:T(8,128)S(1)} %shard_map.105), channel_id=1, replica_groups=mesh['groups'=2,'hid'=16,'mod'=1] {'hid'}, dimensions={0} | all-to-all | bytes 524288 | tf_op jit(solution)/shard_map/all_to_all | solution.py:391
  111.7 1.1 shard_map.106
  112.8 10.7 %all_to_all.11 = f32[16,8,256]{2,1,0:T(8,128)S(1)} all-to-all(f32[16,8,256]{2,1,0:T(8,128)S(1)} %get-tuple-element.19), channel_id=1, replica_groups=mesh['groups'=2,'hid'=16,'mod'=1] {'hid'}, dimensions={0} | all-to-all | bytes 262144 | tf_op jit(solution)/shard_map/all_to_all | solution.py:393
  123.5 0.6 reduce_sum.9
  (14 shorter events, 0.0 us)
Async XLA Ops:
  0.6 9.5 %collective-permute-start.12 = (bf16[16,8192]{1,0:T(8,128)(2,1)}, bf16[16,8192]{1,0:T(8,128)(2,1)S(1)}, u32[]{:S(2)}, u32[]{:S(2)}) collective-permute-start(bf16[16,8192]{1,0:T(8,128)(2,1)} %refs_0_.1), channel_id=1, source_target_pairs={{0,4},{1,5},{4,8},{5,9},{8,12},{9,13},{12,14},{13,15},{14,10},{15,... | collective-permute-start | bytes 786440 | tf_op jit(solution)/shard_map/ppermute | solution.py:119
  3.7 9.8 %collective-permute-start.1 = (bf16[16,8192]{1,0:T(8,128)(2,1)}, bf16[16,8192]{1,0:T(8,128)(2,1)S(1)}, u32[]{:S(2)}, u32[]{:S(2)}) collective-permute-start(bf16[16,8192]{1,0:T(8,128)(2,1)} %refs_0_.2), channel_id=1, source_target_pairs={{0,2},{1,3},{4,0},{5,1},{8,4},{9,5},{12,8},{13,9},{14,12},{15,13},... | collective-permute-start | bytes 786440 | tf_op jit(solution)/shard_map/ppermute | solution.py:119
  3.7 15.1 %collective-permute-start.13 = (bf16[16,8192]{1,0:T(8,128)(2,1)}, bf16[16,8192]{1,0:T(8,128)(2,1)S(1)}, u32[]{:S(2)}, u32[]{:S(2)}) collective-permute-start(bf16[16,8192]{1,0:T(8,128)(2,1)} %refs_0_.1), channel_id=1, source_target_pairs={{0,2},{1,3},{4,0},{5,1},{8,4},{9,5},{12,8},{13,9},{14,12},{15,13},... | collective-permute-start | bytes 786440 | tf_op jit(solution)/shard_map/ppermute | solution.py:119
  5.6 13.1 %collective-permute-start.19 = (bf16[16,8192]{1,0:T(8,128)(2,1)}, bf16[16,8192]{1,0:T(8,128)(2,1)S(1)}, u32[]{:S(2)}, u32[]{:S(2)}) collective-permute-start(bf16[16,8192]{1,0:T(8,128)(2,1)} %refs_0_.1), channel_id=1, source_target_pairs={{0,1},{1,0},{2,3},{3,2},{4,5},{5,4},{6,7},{7,6},{8,9},{9,8},{10,11... | collective-permute-start | bytes 786440 | tf_op jit(solution)/shard_map/ppermute | solution.py:123
  10.1 9.2 %collective-permute-start.14 = (bf16[16,8192]{1,0:T(8,128)(2,1)S(1)}, bf16[16,8192]{1,0:T(8,128)(2,1)S(1)}, u32[]{:S(2)}, u32[]{:S(2)}) collective-permute-start(bf16[16,8192]{1,0:T(8,128)(2,1)S(1)} %collective-permute-done.12.refs_1_), channel_id=1, source_target_pairs={{0,4},{1,5},{4,8},{5,9},{8,12},{9,13},{12,14},{13,15},{14,10},{15,... | collective-permute-start | bytes 786440 | tf_op jit(solution)/shard_map/ppermute | solution.py:119
  12.0 12.4 %collective-permute-start = (bf16[16,8192]{1,0:T(8,128)(2,1)}, bf16[16,8192]{1,0:T(8,128)(2,1)S(1)}, u32[]{:S(2)}, u32[]{:S(2)}) collective-permute-start(bf16[16,8192]{1,0:T(8,128)(2,1)} %refs_0_.2), channel_id=1, source_target_pairs={{0,4},{1,5},{4,8},{5,9},{8,12},{9,13},{12,14},{13,15},{14,10},{15,... | collective-permute-start | bytes 786440 | tf_op jit(solution)/shard_map/ppermute | solution.py:119
  13.5 10.8 %collective-permute-start.3 = (bf16[16,8192]{1,0:T(8,128)(2,1)S(1)}, bf16[16,8192]{1,0:T(8,128)(2,1)S(1)}, u32[]{:S(2)}, u32[]{:S(2)}) collective-permute-start(bf16[16,8192]{1,0:T(8,128)(2,1)S(1)} %collective-permute-done.1.refs_2_), channel_id=1, source_target_pairs={{0,2},{1,3},{4,0},{5,1},{8,4},{9,5},{12,8},{13,9},{14,12},{15,13},... | collective-permute-start | bytes 786440 | tf_op jit(solution)/shard_map/ppermute | solution.py:119
  18.8 9.8 %collective-permute-start.15 = (bf16[16,8192]{1,0:T(8,128)(2,1)S(1)}, bf16[16,8192]{1,0:T(8,128)(2,1)S(1)}, u32[]{:S(2)}, u32[]{:S(2)}) collective-permute-start(bf16[16,8192]{1,0:T(8,128)(2,1)S(1)} %collective-permute-done.13.refs_2_), channel_id=1, source_target_pairs={{0,2},{1,3},{4,0},{5,1},{8,4},{9,5},{12,8},{13,9},{14,12},{15,13},... | collective-permute-start | bytes 786440 | tf_op jit(solution)/shard_map/ppermute | solution.py:119
  18.8 10.1 %collective-permute-start.20 = (bf16[16,8192]{1,0:T(8,128)(2,1)S(1)}, bf16[16,8192]{1,0:T(8,128)(2,1)S(1)}, u32[]{:S(2)}, u32[]{:S(2)}) collective-permute-start(bf16[16,8192]{1,0:T(8,128)(2,1)S(1)} %collective-permute-done.12.refs_1_), channel_id=1, source_target_pairs={{0,1},{1,0},{2,3},{3,2},{4,5},{5,4},{6,7},{7,6},{8,9},{9,8},{10,11... | collective-permute-start | bytes 786440 | tf_op jit(solution)/shard_map/ppermute | solution.py:123
  19.4 11.1 %collective-permute-start.16 = (bf16[16,8192]{1,0:T(8,128)(2,1)S(1)}, bf16[16,8192]{1,0:T(8,128)(2,1)S(1)}, u32[]{:S(2)}, u32[]{:S(2)}) collective-permute-start(bf16[16,8192]{1,0:T(8,128)(2,1)S(1)} %collective-permute-done.14.refs_3_), channel_id=1, source_target_pairs={{0,4},{1,5},{4,8},{5,9},{8,12},{9,13},{12,14},{13,15},{14,10},{15,... | collective-permute-start | bytes 786440 | tf_op jit(solution)/shard_map/ppermute | solution.py:119
  24.4 6.8 %collective-permute-start.21 = (bf16[16,8192]{1,0:T(8,128)(2,1)S(1)}, bf16[16,8192]{1,0:T(8,128)(2,1)S(1)}, u32[]{:S(2)}, u32[]{:S(2)}) collective-permute-start(bf16[16,8192]{1,0:T(8,128)(2,1)S(1)} %collective-permute-done.13.refs_2_), channel_id=1, source_target_pairs={{0,1},{1,0},{2,3},{3,2},{4,5},{5,4},{6,7},{7,6},{8,9},{9,8},{10,11... | collective-permute-start | bytes 786440 | tf_op jit(solution)/shard_map/ppermute | solution.py:123
  24.4 11.2 %collective-permute-start.2 = (bf16[16,8192]{1,0:T(8,128)(2,1)S(1)}, bf16[16,8192]{1,0:T(8,128)(2,1)S(1)}, u32[]{:S(2)}, u32[]{:S(2)}) collective-permute-start(bf16[16,8192]{1,0:T(8,128)(2,1)S(1)} %collective-permute-done.refs_1_), channel_id=1, source_target_pairs={{0,4},{1,5},{4,8},{5,9},{8,12},{9,13},{12,14},{13,15},{14,10},{15,... | collective-permute-start | bytes 786440 | tf_op jit(solution)/shard_map/ppermute | solution.py:119
  28.5 9.2 %collective-permute-start.5 = (bf16[16,8192]{1,0:T(8,128)(2,1)S(1)}, bf16[16,8192]{1,0:T(8,128)(2,1)S(1)}, u32[]{:S(2)}, u32[]{:S(2)}) collective-permute-start(bf16[16,8192]{1,0:T(8,128)(2,1)S(1)} %collective-permute-done.3.refs_4_), channel_id=1, source_target_pairs={{0,2},{1,3},{4,0},{5,1},{8,4},{9,5},{12,8},{13,9},{14,12},{15,13},... | collective-permute-start | bytes 786440 | tf_op jit(solution)/shard_map/ppermute | solution.py:119
  28.8 12.2 %collective-permute-start.17 = (bf16[16,8192]{1,0:T(8,128)(2,1)S(1)}, bf16[16,8192]{1,0:T(8,128)(2,1)S(1)}, u32[]{:S(2)}, u32[]{:S(2)}) collective-permute-start(bf16[16,8192]{1,0:T(8,128)(2,1)S(1)} %collective-permute-done.15.refs_4_), channel_id=1, source_target_pairs={{0,2},{1,3},{4,0},{5,1},{8,4},{9,5},{12,8},{13,9},{14,12},{15,13},... | collective-permute-start | bytes 786440 | tf_op jit(solution)/shard_map/ppermute | solution.py:119
  30.5 10.5 %collective-permute-start.18 = (bf16[16,8192]{1,0:T(8,128)(2,1)S(1)}, bf16[16,8192]{1,0:T(8,128)(2,1)S(1)}, u32[]{:S(2)}, u32[]{:S(2)}) collective-permute-start(bf16[16,8192]{1,0:T(8,128)(2,1)S(1)} %collective-permute-done.16.refs_5_), channel_id=1, source_target_pairs={{0,4},{1,5},{4,8},{5,9},{8,12},{9,13},{12,14},{13,15},{14,10},{15,... | collective-permute-start | bytes 786440 | tf_op jit(solution)/shard_map/ppermute | solution.py:119
  31.2 10.4 %collective-permute-start.22 = (bf16[16,8192]{1,0:T(8,128)(2,1)S(1)}, bf16[16,8192]{1,0:T(8,128)(2,1)S(1)}, u32[]{:S(2)}, u32[]{:S(2)}) collective-permute-start(bf16[16,8192]{1,0:T(8,128)(2,1)S(1)} %collective-permute-done.14.refs_3_), channel_id=1, source_target_pairs={{0,1},{1,0},{2,3},{3,2},{4,5},{5,4},{6,7},{7,6},{8,9},{9,8},{10,11... | collective-permute-start | bytes 786440 | tf_op jit(solution)/shard_map/ppermute | solution.py:123
  35.6 6.0 %collective-permute-start.23 = (bf16[16,8192]{1,0:T(8,128)(2,1)S(1)}, bf16[16,8192]{1,0:T(8,128)(2,1)S(1)}, u32[]{:S(2)}, u32[]{:S(2)}) collective-permute-start(bf16[16,8192]{1,0:T(8,128)(2,1)S(1)} %collective-permute-done.15.refs_4_), channel_id=1, source_target_pairs={{0,1},{1,0},{2,3},{3,2},{4,5},{5,4},{6,7},{7,6},{8,9},{9,8},{10,11... | collective-permute-start | bytes 786440 | tf_op jit(solution)/shard_map/ppermute | solution.py:123
  37.8 4.3 %collective-permute-start.24 = (bf16[16,8192]{1,0:T(8,128)(2,1)S(1)}, bf16[16,8192]{1,0:T(8,128)(2,1)S(1)}, u32[]{:S(2)}, u32[]{:S(2)}) collective-permute-start(bf16[16,8192]{1,0:T(8,128)(2,1)S(1)} %collective-permute-done.16.refs_5_), channel_id=1, source_target_pairs={{0,1},{1,0},{2,3},{3,2},{4,5},{5,4},{6,7},{7,6},{8,9},{9,8},{10,11... | collective-permute-start | bytes 786440 | tf_op jit(solution)/shard_map/ppermute | solution.py:123
  41.0 1.5 %collective-permute-start.25 = (bf16[16,8192]{1,0:T(8,128)(2,1)S(1)}, bf16[16,8192]{1,0:T(8,128)(2,1)S(1)}, u32[]{:S(2)}, u32[]{:S(2)}) collective-permute-start(bf16[16,8192]{1,0:T(8,128)(2,1)S(1)} %collective-permute-done.17.refs_6_), channel_id=1, source_target_pairs={{0,1},{1,0},{2,3},{3,2},{4,5},{5,4},{6,7},{7,6},{8,9},{9,8},{10,11... | collective-permute-start | bytes 786440 | tf_op jit(solution)/shard_map/ppermute | solution.py:123
  41.0 3.1 %collective-permute-start.26 = (bf16[16,8192]{1,0:T(8,128)(2,1)S(1)}, bf16[16,8192]{1,0:T(8,128)(2,1)S(1)}, u32[]{:S(2)}, u32[]{:S(2)}) collective-permute-start(bf16[16,8192]{1,0:T(8,128)(2,1)S(1)} %collective-permute-done.18.refs_7_), channel_id=1, source_target_pairs={{0,1},{1,0},{2,3},{3,2},{4,5},{5,4},{6,7},{7,6},{8,9},{9,8},{10,11... | collective-permute-start | bytes 786440 | tf_op jit(solution)/shard_map/ppermute | solution.py:123
  41.5 36.2 %collective-permute-start.7 = (bf16[16,8192]{1,0:T(8,128)(2,1)}, bf16[16,8192]{1,0:T(8,128)(2,1)S(1)}, u32[]{:S(2)}, u32[]{:S(2)}) collective-permute-start(bf16[16,8192]{1,0:T(8,128)(2,1)} %refs_0_.2), channel_id=1, source_target_pairs={{0,1},{1,0},{2,3},{3,2},{4,5},{5,4},{6,7},{7,6},{8,9},{9,8},{10,11... | collective-permute-start | bytes 786440 | tf_op jit(solution)/shard_map/ppermute | solution.py:123
  41.6 36.2 %collective-permute-start.8 = (bf16[16,8192]{1,0:T(8,128)(2,1)S(1)}, bf16[16,8192]{1,0:T(8,128)(2,1)S(1)}, u32[]{:S(2)}, u32[]{:S(2)}) collective-permute-start(bf16[16,8192]{1,0:T(8,128)(2,1)S(1)} %collective-permute-done.refs_1_), channel_id=1, source_target_pairs={{0,1},{1,0},{2,3},{3,2},{4,5},{5,4},{6,7},{7,6},{8,9},{9,8},{10,11... | collective-permute-start | bytes 786440 | tf_op jit(solution)/shard_map/ppermute | solution.py:123
  42.0 36.2 %collective-permute-start.9 = (bf16[16,8192]{1,0:T(8,128)(2,1)S(1)}, bf16[16,8192]{1,0:T(8,128)(2,1)S(1)}, u32[]{:S(2)}, u32[]{:S(2)}) collective-permute-start(bf16[16,8192]{1,0:T(8,128)(2,1)S(1)} %collective-permute-done.1.refs_2_), channel_id=1, source_target_pairs={{0,1},{1,0},{2,3},{3,2},{4,5},{5,4},{6,7},{7,6},{8,9},{9,8},{10,11... | collective-permute-start | bytes 786440 | tf_op jit(solution)/shard_map/ppermute | solution.py:123
  42.5 34.6 %collective-permute-start.4 = (bf16[16,8192]{1,0:T(8,128)(2,1)S(1)}, bf16[16,8192]{1,0:T(8,128)(2,1)S(1)}, u32[]{:S(2)}, u32[]{:S(2)}) collective-permute-start(bf16[16,8192]{1,0:T(8,128)(2,1)S(1)} %collective-permute-done.2.refs_3_), channel_id=1, source_target_pairs={{0,4},{1,5},{4,8},{5,9},{8,12},{9,13},{12,14},{13,15},{14,10},{15,... | collective-permute-start | bytes 786440 | tf_op jit(solution)/shard_map/ppermute | solution.py:119
  44.1 33.0 %collective-permute-start.6 = (bf16[16,8192]{1,0:T(8,128)(2,1)S(1)}, bf16[16,8192]{1,0:T(8,128)(2,1)S(1)}, u32[]{:S(2)}, u32[]{:S(2)}) collective-permute-start(bf16[16,8192]{1,0:T(8,128)(2,1)S(1)} %collective-permute-done.5.refs_6_), channel_id=1, source_target_pairs={{0,2},{1,3},{4,0},{5,1},{8,4},{9,5},{12,8},{13,9},{14,12},{15,13},... | collective-permute-start | bytes 786440 | tf_op jit(solution)/shard_map/ppermute | solution.py:119
  44.6 1.9 %copy-start = (bf16[8192,192]{0,1:T(8,128)(2,1)S(1)}, bf16[8192,192]{0,1:T(8,128)(2,1)}, u32[]{:S(2)}) copy-start(bf16[8192,192]{0,1:T(8,128)(2,1)} %param.14) | copy-start | bytes 9437188
  46.5 0.9 copy-start.3
  47.4 32.8 %copy-start.1 = (bf16[1792,192]{0,1:T(8,128)(2,1)S(1)}, bf16[1792,192]{0,1:T(8,128)(2,1)}, u32[]{:S(2)}) copy-start(bf16[1792,192]{0,1:T(8,128)(2,1)} %param.15) | copy-start | bytes 2064388
  47.4 32.8 %copy-start.4 = (bf16[16,8192]{1,0:T(8,128)(2,1)S(1)}, bf16[16,8192]{1,0:T(8,128)(2,1)}, u32[]{:S(2)}) copy-start(bf16[16,8192]{1,0:T(8,128)(2,1)} %refs_0_.2) | copy-start | bytes 786436
  47.4 32.8 %copy-start.5 = (s32[256]{0:T(256)S(1)}, s32[256]{0:T(256)}, u32[]{:S(2)}) copy-start(s32[256]{0:T(256)} %param.16) | copy-start | bytes 3076
  77.1 1.6 %collective-permute-start.10 = (bf16[16,8192]{1,0:T(8,128)(2,1)S(1)}, bf16[16,8192]{1,0:T(8,128)(2,1)S(1)}, u32[]{:S(2)}, u32[]{:S(2)}) collective-permute-start(bf16[16,8192]{1,0:T(8,128)(2,1)S(1)} %collective-permute-done.2.refs_3_), channel_id=1, source_target_pairs={{0,1},{1,0},{2,3},{3,2},{4,5},{5,4},{6,7},{7,6},{8,9},{9,8},{10,11... | collective-permute-start | bytes 786440 | tf_op jit(solution)/shard_map/ppermute | solution.py:123
  77.2 1.9 %collective-permute-start.11 = (bf16[16,8192]{1,0:T(8,128)(2,1)S(1)}, bf16[16,8192]{1,0:T(8,128)(2,1)S(1)}, u32[]{:S(2)}, u32[]{:S(2)}) collective-permute-start(bf16[16,8192]{1,0:T(8,128)(2,1)S(1)} %collective-permute-done.3.refs_4_), channel_id=1, source_target_pairs={{0,1},{1,0},{2,3},{3,2},{4,5},{5,4},{6,7},{7,6},{8,9},{9,8},{10,11... | collective-permute-start | bytes 786440 | tf_op jit(solution)/shard_map/ppermute | solution.py:123
  77.7 1.8 %collective-permute-start.29 = (bf16[16,8192]{1,0:T(8,128)(2,1)S(1)}, bf16[16,8192]{1,0:T(8,128)(2,1)S(1)}, u32[]{:S(2)}, u32[]{:S(2)}) collective-permute-start(bf16[16,8192]{1,0:T(8,128)(2,1)S(1)} %collective-permute-done.6.refs_7_), channel_id=1, source_target_pairs={{0,1},{1,0},{2,3},{3,2},{4,5},{5,4},{6,7},{7,6},{8,9},{9,8},{10,11... | collective-permute-start | bytes 786440 | tf_op jit(solution)/shard_map/ppermute | solution.py:123
  77.8 2.1 %collective-permute-start.28 = (bf16[16,8192]{1,0:T(8,128)(2,1)S(1)}, bf16[16,8192]{1,0:T(8,128)(2,1)S(1)}, u32[]{:S(2)}, u32[]{:S(2)}) collective-permute-start(bf16[16,8192]{1,0:T(8,128)(2,1)S(1)} %collective-permute-done.5.refs_6_), channel_id=1, source_target_pairs={{0,1},{1,0},{2,3},{3,2},{4,5},{5,4},{6,7},{7,6},{8,9},{9,8},{10,11... | collective-permute-start | bytes 786440 | tf_op jit(solution)/shard_map/ppermute | solution.py:123
  78.2 2.0 %collective-permute-start.27 = (bf16[16,8192]{1,0:T(8,128)(2,1)S(1)}, bf16[16,8192]{1,0:T(8,128)(2,1)S(1)}, u32[]{:S(2)}, u32[]{:S(2)}) collective-permute-start(bf16[16,8192]{1,0:T(8,128)(2,1)S(1)} %collective-permute-done.4.refs_5_), channel_id=1, source_target_pairs={{0,1},{1,0},{2,3},{3,2},{4,5},{5,4},{6,7},{7,6},{8,9},{9,8},{10,11... | collective-permute-start | bytes 786440 | tf_op jit(solution)/shard_map/ppermute | solution.py:123
  80.2 31.5 %copy-start.2 = (bf16[256,768]{1,0:T(8,128)(2,1)S(1)}, bf16[256,768]{1,0:T(8,128)(2,1)}, u32[]{:S(2)}) copy-start(bf16[256,768]{1,0:T(8,128)(2,1)} %tests.1) | copy-start | bytes 1179652
